TPU v7x, 512 devices: a whole 4x8x8 slice. The times are simulated.
512 devices in a mesh: ctx: 64 (over y, z), head: 8 (over x, core).
Axes of the slice: x: 4, y: 8, z: 8, core: 2. Of those that a mesh axis runs over, the one named last changes fastest.
Arguments:
- g_conv: bfloat16 [1536, 16384], P('head', 'ctx'), may hold values from -6 to 6
- pre: bfloat16 [2, 1536, 16384], P(None, 'head', 'ctx'), may hold values from -6 to 6
- kernel: float32 [31, 1536], P(None, 'head'), may hold values from -1 to 1
- w_point: bfloat16 [2, 1536, 1536], P(None, 'head'), may hold values from -0.15625 to 0.15625
- g_out: bfloat16 [1536, 16384], P('head', 'ctx'), may hold values from -6 to 6
- w_out: bfloat16 [1536, 1536], P('head'), may hold values from -0.15625 to 0.15625
- queries: bfloat16 [16384, 1536], P('ctx', 'head'), may hold values from -24 to 24
- keys: bfloat16 [16384, 1536], P('ctx', 'head'), may hold values from -24 to 24
- values: bfloat16 [16384, 1536], P('ctx', 'head'), may hold values from -6 to 6
- block_mask: int32 [128, 4, 2], P('ctx'), may hold values from 0 to 1
- counts: int32 [64], P('ctx'), may hold values from 1 to 256, 12288 in all
Outputs:
- stream_grad: bfloat16 [16384, 1536], P('ctx', 'head')
- grad_queries: bfloat16 [16384, 1536], P('ctx', 'head')
- grad_keys: bfloat16 [16384, 1536], P('ctx', 'head')
- grad_values: bfloat16 [16384, 1536], P('ctx', 'head')
Inputs may be any that keep to these rules, and one draw needn't show every extreme that they name: `counts`: the largest count equals 256.
All inputs are finite; a program needn't handle non-finite values. No bound on the sum of `counts` on one device may be relied on, other than what follows from the above.
Results may differ from a plain program's by a relative error of at most 0.02.
Values may be sent and summed in bfloat16 or wider, within the bound.
No kernel may reach another device: no remote copies, remote signals or barrier semaphores. Data moves between devices by JAX's collectives and lax.ppermute only.
A program may use at most 64 MiB of HBM per device.

v0:
```python
import math

import jax
import jax.numpy as jnp
from jax import lax
from jax.sharding import PartitionSpec as P

HEAD_DIM = 64
KW = 31
LINKS = 4
HALF = 15


def with_halo(x, sides, width):
    for axis, dim in sides:
        count, length = (lax.axis_size(axis), x.shape[dim])
        up = [(i, (i + 1) % count) for i in range(count - 1)]
        down = [(j, i) for i, j in up]
        last = lax.slice_in_dim(x, length - width, length, axis=dim)
        initial = lax.slice_in_dim(x, 0, width, axis=dim)
        before = lax.ppermute(last, axis, up)
        after = lax.ppermute(initial, axis, down)
        x = jnp.concatenate([before, x, after], axis=dim)
    return x


def shifted(value, axis, steps):
    count = lax.axis_size(axis)
    pairs = [(source, (source + steps) % count) for source in range(count)]
    return lax.ppermute(value, axis, pairs)


def link_allowed(query_valid, key_valid, link_mask, is_local):
    blocks = link_mask > 0
    if is_local:
        blocks = blocks | jnp.eye(blocks.shape[0], dtype=bool)
    block_count = blocks.shape[0]
    width = query_valid.shape[0] // block_count
    element = jnp.broadcast_to(blocks[:, None, :, None], (block_count, width, block_count, width))
    element = element.reshape(block_count * width, block_count * width)
    return element & query_valid[:, None] & key_valid[None, :]


def link_grads(
    query_heads,
    grad_heads,
    key_heads,
    value_heads,
    allowed,
    row_max,
    row_sum,
    row_delta,
    score_scale,
):
    scores = (
        jnp.einsum("qhd,khd->hqk", query_heads, key_heads, preferred_element_type=jnp.float32)
        * score_scale
    )
    probs = jnp.where(allowed[None], jnp.exp(scores - row_max[..., None]) / row_sum[..., None], 0.0)
    dprob = jnp.einsum("qhd,khd->hqk", grad_heads, value_heads, preferred_element_type=jnp.float32)
    dscore = (probs * (dprob - row_delta[..., None])).astype(jnp.bfloat16)
    return (dscore, probs.astype(jnp.bfloat16))


def per_device(
    g_conv, pre, kernel, w_point, g_out, w_out, queries, keys, values, block_mask, counts
):
    row_count = queries.shape[0]
    columns = queries.shape[1]
    head_count = columns // HEAD_DIM
    score_scale = 1.0 / math.sqrt(HEAD_DIM)
    padded = with_halo(g_conv, (("ctx", 1),), HALF)
    conv_grad = jnp.zeros((columns, row_count), jnp.float32)
    for tap_index in range(KW):
        first_row = 2 * HALF - tap_index
        conv_grad = conv_grad + kernel[tap_index][:, None] * padded[
            :, first_row : first_row + row_count
        ].astype(jnp.float32)
    pre_wide = pre.astype(jnp.float32)
    gate = jax.nn.sigmoid(pre_wide[1])
    grad_value = conv_grad * gate
    grad_gate = conv_grad * pre_wide[0] * gate * (1.0 - gate)
    pre_grad = (
        jnp.stack([grad_value, grad_gate], axis=0)
        .astype(jnp.bfloat16)
        .reshape(2 * columns, row_count)
    )
    point_grad = lax.dot_general(
        pre_grad,
        w_point.reshape(2 * columns, w_point.shape[2]),
        (((0,), (0,)), ((), ())),
        preferred_element_type=jnp.float32,
    )
    g_rows = g_out.astype(jnp.float32).T
    piece = lax.psum_scatter(
        point_grad.astype(jnp.bfloat16), "head", scatter_dimension=1, tiled=True
    ).astype(jnp.float32)
    stream_grad = (g_rows + piece).astype(jnp.bfloat16)
    stream_full = lax.all_gather(stream_grad, "head", axis=1, tiled=True)
    positions = jnp.arange(row_count, dtype=jnp.int32)
    query_valid = positions < counts[0]
    head_grad = lax.dot_general(
        stream_full, w_out, (((1,), (1,)), ((), ())), preferred_element_type=jnp.float32
    )
    head_grad = jnp.where(query_valid[:, None], head_grad, 0.0).astype(jnp.bfloat16)

    def split(array):
        return array.reshape(array.shape[0], head_count, HEAD_DIM)

    query_heads = split(queries)
    grad_heads = split(head_grad)
    offsets = [0, 1, -1, lax.axis_size("ctx") // 2]
    remote = [(keys, values, counts)]
    for offset in offsets[1:]:
        remote.append(shifted((keys, values, counts), "ctx", offset))
    row_max = jnp.full((head_count, row_count), -1e30, jnp.float32)
    row_sum = jnp.zeros((head_count, row_count), jnp.float32)
    weighted = jnp.zeros((head_count, row_count), jnp.float32)
    allowed_list = []
    for link_index in range(LINKS):
        far_keys, far_values, far_counts = remote[link_index]
        allowed = link_allowed(
            query_valid, positions < far_counts[0], block_mask[:, link_index, :], link_index == 0
        )
        allowed_list.append(allowed)
        scores = (
            jnp.einsum(
                "qhd,khd->hqk", query_heads, split(far_keys), preferred_element_type=jnp.float32
            )
            * score_scale
        )
        new_max = jnp.maximum(row_max, jnp.max(jnp.where(allowed[None], scores, -1e30), axis=-1))
        expo = jnp.where(allowed[None], jnp.exp(scores - new_max[..., None]), 0.0)
        factor = jnp.exp(row_max - new_max)
        dprob = jnp.einsum(
            "qhd,khd->hqk", grad_heads, split(far_values), preferred_element_type=jnp.float32
        )
        row_sum = row_sum * factor + jnp.sum(expo, axis=-1)
        weighted = weighted * factor + jnp.sum(expo * dprob, axis=-1)
        row_max = new_max
    row_sum = row_sum + (1.0 - query_valid.astype(jnp.float32))[None, :]
    row_delta = weighted / row_sum
    grad_query = jnp.zeros((row_count, head_count, HEAD_DIM), jnp.float32)
    key_total = jnp.zeros((row_count, head_count, HEAD_DIM), jnp.float32)
    value_total = jnp.zeros((row_count, head_count, HEAD_DIM), jnp.float32)
    for link_index in range(LINKS):
        far_keys, far_values, far_counts = remote[link_index]
        dscore, probs_low = link_grads(
            query_heads,
            grad_heads,
            split(far_keys),
            split(far_values),
            allowed_list[link_index],
            row_max,
            row_sum,
            row_delta,
            score_scale,
        )
        grad_query = (
            grad_query
            + jnp.einsum(
                "hqk,khd->qhd", dscore, split(far_keys), preferred_element_type=jnp.float32
            )
            * score_scale
        )
        key_term = (
            jnp.einsum("hqk,qhd->khd", dscore, query_heads, preferred_element_type=jnp.float32)
            * score_scale
        )
        value_term = jnp.einsum(
            "hqk,qhd->khd", probs_low, grad_heads, preferred_element_type=jnp.float32
        )
        if link_index > 0:
            key_term, value_term = (
                shifted(key_term.astype(jnp.bfloat16), "ctx", -offsets[link_index]).astype(
                    key_term.dtype
                ),
                shifted(value_term.astype(jnp.bfloat16), "ctx", -offsets[link_index]).astype(
                    value_term.dtype
                ),
            )
        key_total = key_total + key_term
        value_total = value_total + value_term
    grad_queries = grad_query.reshape(row_count, columns).astype(jnp.bfloat16)
    grad_keys = key_total.reshape(row_count, columns).astype(jnp.bfloat16)
    grad_values = value_total.reshape(row_count, columns).astype(jnp.bfloat16)
    return (stream_grad, grad_queries, grad_keys, grad_values)


def solution(mesh):
    in_specs = (
        P("head", "ctx"),
        P(None, "head", "ctx"),
        P(None, "head"),
        P(None, "head", None),
        P("head", "ctx"),
        P("head", None),
        P("ctx", "head"),
        P("ctx", "head"),
        P("ctx", "head"),
        P("ctx", None, None),
        P("ctx"),
    )
    out_specs = (P("ctx", "head"), P("ctx", "head"), P("ctx", "head"), P("ctx", "head"))
    return jax.shard_map(
        per_device, mesh=mesh, in_specs=in_specs, out_specs=out_specs, check_vma=False
    )
```

profile of v0, /device:TPU:1, one launch (start us, length us, event | category | flops | bytes accessed | tf_op | source)
XLA Modules:
  0.0 173.3 jit_solution(2334303911334602970)
XLA Ops:
  7.2 5.0 %collective-permute-start.2 = (s32[1]{0:T(128)}, s32[1]{0:T(128)}, u32[]{:S(2)}, u32[]{:S(2)}) collective-permute-start(s32[1]{0:T(128)} %param.21), channel_id=1, source_target_pairs={{0,8},{8,16},{16,24},{24,32},{32,40},{40,48},{48,56},{56,64},{64,7... | collective-permute-start | bytes 20 | tf_op jit(solution)/shard_map/ppermute | solution.py:30
  12.2 7.5 %collective-permute-start.6 = (s32[1]{0:T(128)}, s32[1]{0:T(128)}, u32[]{:S(2)}, u32[]{:S(2)}) collective-permute-start(s32[1]{0:T(128)} %param.21), channel_id=1, source_target_pairs={{0,256},{8,264},{16,272},{24,280},{32,288},{40,296},{48,304},{56,3... | collective-permute-start | bytes 20 | tf_op jit(solution)/shard_map/ppermute | solution.py:30
  19.7 8.5 %collective-permute-start.4 = (s32[1]{0:T(128)}, s32[1]{0:T(128)}, u32[]{:S(2)}, u32[]{:S(2)}) collective-permute-start(s32[1]{0:T(128)} %param.21), channel_id=1, source_target_pairs={{0,504},{8,0},{16,8},{24,16},{32,24},{40,32},{48,40},{56,48},{64,5... | collective-permute-start | bytes 20 | tf_op jit(solution)/shard_map/ppermute | solution.py:30
  28.2 1.9 %collective-permute-start.3 = (bf16[256,192]{0,1:T(8,128)(2,1)}, bf16[256,192]{0,1:T(8,128)(2,1)S(1)}, u32[]{:S(2)}, u32[]{:S(2)}) collective-permute-start(bf16[256,192]{0,1:T(8,128)(2,1)} %param.18), channel_id=1, source_target_pairs={{0,8},{8,16},{16,24},{24,32},{32,40},{40,48},{48,56},{56,64},{64,7... | collective-permute-start | bytes 294920 | tf_op jit(solution)/shard_map/ppermute | solution.py:30
  30.1 4.8 %collective-permute-start.7 = (bf16[256,192]{0,1:T(8,128)(2,1)}, bf16[256,192]{0,1:T(8,128)(2,1)}, u32[]{:S(2)}, u32[]{:S(2)}) collective-permute-start(bf16[256,192]{0,1:T(8,128)(2,1)} %param.18), channel_id=1, source_target_pairs={{0,256},{8,264},{16,272},{24,280},{32,288},{40,296},{48,304},{56,3... | collective-permute-start | bytes 294920 | tf_op jit(solution)/shard_map/ppermute | solution.py:30
  42.0 6.7 %collective-permute-start.5 = (bf16[256,192]{0,1:T(8,128)(2,1)}, bf16[256,192]{0,1:T(8,128)(2,1)}, u32[]{:S(2)}, u32[]{:S(2)}) collective-permute-start(bf16[256,192]{0,1:T(8,128)(2,1)} %param.18), channel_id=1, source_target_pairs={{0,504},{8,0},{16,8},{24,16},{32,24},{40,32},{48,40},{56,48},{64,5... | collective-permute-start | bytes 294920 | tf_op jit(solution)/shard_map/ppermute | solution.py:30
  49.4 1.3 collective-permute-start
  51.4 2.8 %collective-permute-done = bf16[192,15]{1,0:T(8,128)(2,1)S(1)} collective-permute-done((bf16[192,15]{1,0:T(8,128)(2,1)S(1)}, bf16[192,15]{1,0:T(8,128)(2,1)S(1)}, u32[]{:S(2)}, u32[]{:S(2)}) %collective-permute-start) | collective-permute-done | bytes 5792 | tf_op jit(solution)/shard_map/ppermute | solution.py:22
  54.2 1.6 collective-permute-start.1
  55.9 1.1 collective-permute-done.1
  57.0 3.7 %collective-permute-start.8 = (bf16[256,192]{0,1:T(8,128)(2,1)}, bf16[256,192]{0,1:T(8,128)(2,1)}, u32[]{:S(2)}, u32[]{:S(2)}) collective-permute-start(bf16[256,192]{0,1:T(8,128)(2,1)} %param.19), channel_id=1, source_target_pairs={{0,8},{8,16},{16,24},{24,32},{32,40},{40,48},{48,56},{56,64},{64,7... | collective-permute-start | bytes 294920 | tf_op jit(solution)/shard_map/ppermute | solution.py:30
  60.7 2.1 %fusion.40 = (bf16[1,192,256]{2,1,0:T(8,128)(2,1)S(1)}, f32[192,256]{1,0:T(8,128)S(1)}) fusion(f32[2,192,256]{2,1,0:T(8,128)S(1)} %convert_element_type.242, bf16[192,256]{1,0:T(8,128)(2,1)S(1)} %copy-done.10, bf16[192,15]{1,0:T(8,128)(2,1)S(1)} %collective-permute-done.1, f32[192]{0:T(256)S(1)} %bitcast.201, f32[192]{0:T(256)S(1)} %bitcast.202, ...), kind=kLoop, calls=%fused_computation.114 | loop fusion | flops 6979584 | bytes 2093952 | tf_op jit(solution)/shard_map/stack | solution.py:84
  62.9 1.5 fusion
  64.5 8.2 %collective-permute-start.10 = (bf16[256,192]{0,1:T(8,128)(2,1)}, bf16[256,192]{0,1:T(8,128)(2,1)}, u32[]{:S(2)}, u32[]{:S(2)}) collective-permute-start(bf16[256,192]{0,1:T(8,128)(2,1)} %param.19), channel_id=1, source_target_pairs={{0,256},{8,264},{16,272},{24,280},{32,288},{40,296},{48,304},{56,3... | collective-permute-start | bytes 294920 | tf_op jit(solution)/shard_map/ppermute | solution.py:30
  76.4 6.7 %collective-permute-start.9 = (bf16[256,192]{0,1:T(8,128)(2,1)}, bf16[256,192]{0,1:T(8,128)(2,1)}, u32[]{:S(2)}, u32[]{:S(2)}) collective-permute-start(bf16[256,192]{0,1:T(8,128)(2,1)} %param.19), channel_id=1, source_target_pairs={{0,504},{8,0},{16,8},{24,16},{32,24},{40,32},{48,40},{56,48},{64,5... | collective-permute-start | bytes 294920 | tf_op jit(solution)/shard_map/ppermute | solution.py:30
  83.5 1.3 select_reduce_fusion.1
  84.7 2.2 %select_reduce_fusion = (f32[3,256]{1,0:T(4,128)S(1)}, f32[3,256,256]{1,2,0:T(8,128)}) fusion(pred[256,256]{0,1:T(8,128)(4,1)} %copy.34, bf16[256,3,64]{0,2,1:T(8,128)(2,1)} %bitcast.166, bf16[256,3,64]{0,2,1:T(8,128)(2,1)} %bitcast.45), kind=kOutput, calls=%fused_computation.47 | convolution fusion | flops 25754880 | bytes 1051648 | tf_op jit(solution)/shard_map/qhd,khd->hqk/dot_general | solution.py:127
  87.5 15.4 %reduce-scatter.2.cloned.1.call-done = bf16[256,192]{0,1:T(8,128)(2,1)} async-done(((bf16[256,1536]{0,1:T(8,128)(2,1)}), bf16[256,192]{0,1:T(8,128)(2,1)}) %reduce-scatter.2.cloned.1.call-update) | async-done | bytes 98320 | tf_op jit(solution)/shard_map/reduce_scatter | solution.py:95
  104.0 15.7 %all_gather.3 = bf16[256,1536]{0,1:T(8,128)(2,1)S(1)} all-gather(bf16[256,192]{0,1:T(8,128)(2,1)S(1)} %fusion.37), channel_id=1, replica_groups=mesh['ctx'=64,'head'=8] {'head'}, dimensions={1}, use_global_device_ids=true | all-gather | bytes 884736 | tf_op jit(solution)/shard_map/all_gather | solution.py:99
  120.0 1.3 fusion.17
  121.3 1.3 fusion.16
  122.7 1.3 select_reduce_fusion.4
  124.0 1.3 fusion.15
  127.4 1.1 fusion.68
  129.1 7.1 %collective-permute-start.13 = (bf16[256,3,64]{0,2,1:T(8,128)(2,1)S(1)}, bf16[256,3,64]{0,2,1:T(8,128)(2,1)S(1)}, u32[]{:S(2)}, u32[]{:S(2)}) collective-permute-start(bf16[256,3,64]{0,2,1:T(8,128)(2,1)S(1)} %fusion.9), channel_id=1, source_target_pairs={{0,256},{8,264},{16,272},{24,280},{32,288},{40,296},{48,304},{56,3... | collective-permute-start | bytes 294920 | tf_op jit(solution)/shard_map/ppermute | solution.py:30
  136.2 5.6 %collective-permute-start.11 = (bf16[256,3,64]{0,2,1:T(8,128)(2,1)S(1)}, bf16[256,3,64]{0,2,1:T(8,128)(2,1)S(1)}, u32[]{:S(2)}, u32[]{:S(2)}) collective-permute-start(bf16[256,3,64]{0,2,1:T(8,128)(2,1)S(1)} %fusion.11), channel_id=1, source_target_pairs={{0,504},{8,0},{16,8},{24,16},{32,24},{40,32},{48,40},{56,48},{64,5... | collective-permute-start | bytes 294920 | tf_op jit(solution)/shard_map/ppermute | solution.py:30
  141.9 1.9 %collective-permute-start.12 = (bf16[256,3,64]{0,2,1:T(8,128)(2,1)S(1)}, bf16[256,3,64]{0,2,1:T(8,128)(2,1)S(1)}, u32[]{:S(2)}, u32[]{:S(2)}) collective-permute-start(bf16[256,3,64]{0,2,1:T(8,128)(2,1)S(1)} %fusion.10), channel_id=1, source_target_pairs={{0,8},{8,16},{16,24},{24,32},{32,40},{40,48},{48,56},{56,64},{64,7... | collective-permute-start | bytes 294920 | tf_op jit(solution)/shard_map/ppermute | solution.py:30
  144.2 4.2 %collective-permute-start.16 = (bf16[256,3,64]{0,2,1:T(8,128)(2,1)S(1)}, bf16[256,3,64]{0,2,1:T(8,128)(2,1)S(1)}, u32[]{:S(2)}, u32[]{:S(2)}) collective-permute-start(bf16[256,3,64]{0,2,1:T(8,128)(2,1)S(1)} %fusion.14), channel_id=1, source_target_pairs={{0,256},{8,264},{16,272},{24,280},{32,288},{40,296},{48,304},{56,3... | collective-permute-start | bytes 294920 | tf_op jit(solution)/shard_map/ppermute | solution.py:30
  148.4 6.7 %collective-permute-start.14 = (bf16[256,3,64]{0,2,1:T(8,128)(2,1)S(1)}, bf16[256,3,64]{0,2,1:T(8,128)(2,1)S(1)}, u32[]{:S(2)}, u32[]{:S(2)}) collective-permute-start(bf16[256,3,64]{0,2,1:T(8,128)(2,1)S(1)} %fusion.12), channel_id=1, source_target_pairs={{0,504},{8,0},{16,8},{24,16},{32,24},{40,32},{48,40},{56,48},{64,5... | collective-permute-start | bytes 294920 | tf_op jit(solution)/shard_map/ppermute | solution.py:30
  155.1 1.7 %fusion.8 = bf16[3,256,64]{1,2,0:T(8,128)(2,1)} fusion(f32[3,256,64]{1,2,0:T(8,128)S(1)} %fusion.68, f32[3,256,64]{1,2,0:T(8,128)S(1)} %convolution_add_fusion.1, bf16[256,3,64]{0,2,1:T(8,128)(2,1)} %bitcast.43, bf16[3,256,256]{1,2,0:T(8,128)(2,1)S(1)} %get-tuple-element.56), kind=kOutput, calls=%fused_computation.21 | convolution fusion | flops 25362432 | bytes 983040 | tf_op jit(solution)/shard_map/hqk,khd->qhd/dot_general | solution.py:161
  156.9 1.9 %collective-permute-start.15 = (bf16[256,3,64]{0,2,1:T(8,128)(2,1)S(1)}, bf16[256,3,64]{0,2,1:T(8,128)(2,1)S(1)}, u32[]{:S(2)}, u32[]{:S(2)}) collective-permute-start(bf16[256,3,64]{0,2,1:T(8,128)(2,1)S(1)} %fusion.13), channel_id=1, source_target_pairs={{0,8},{8,16},{16,24},{24,32},{32,40},{40,48},{48,56},{56,64},{64,7... | collective-permute-start | bytes 294920 | tf_op jit(solution)/shard_map/ppermute | solution.py:30
  159.7 5.8 %collective-permute-done.15 = bf16[256,3,64]{0,2,1:T(8,128)(2,1)S(1)} collective-permute-done((bf16[256,3,64]{0,2,1:T(8,128)(2,1)S(1)}, bf16[256,3,64]{0,2,1:T(8,128)(2,1)S(1)}, u32[]{:S(2)}, u32[]{:S(2)}) %collective-permute-start.15) | collective-permute-done | bytes 98336 | tf_op jit(solution)/shard_map/ppermute | solution.py:30
  (98 shorter events, 18.9 us)
Async XLA Ops:
  7.2 55.8 %copy-start = (bf16[2,192,1536]{2,1,0:T(8,128)(2,1)S(1)}, bf16[2,192,1536]{2,1,0:T(8,128)(2,1)}, u32[]{:S(2)}) copy-start(bf16[2,192,1536]{2,1,0:T(8,128)(2,1)} %param.14) | copy-start | bytes 3538948
  7.2 53.5 %copy-start.10 = (bf16[192,256]{1,0:T(8,128)(2,1)S(1)}, bf16[192,256]{1,0:T(8,128)(2,1)}, u32[]{:S(2)}) copy-start(bf16[192,256]{1,0:T(8,128)(2,1)} %param.11) | copy-start | bytes 294916
  7.2 95.7 %reduce-scatter.2.cloned.1.call-start = ((), (), s32[]{:S(2)}) async-start(), calls=%async_computation.1 | async-start | bytes 884736 | tf_op jit(solution)/shard_map/reduce_scatter | solution.py:95
  7.2 34.8 %collective-permute-start.2 = (s32[1]{0:T(128)}, s32[1]{0:T(128)}, u32[]{:S(2)}, u32[]{:S(2)}) collective-permute-start(s32[1]{0:T(128)} %param.21), channel_id=1, source_target_pairs={{0,8},{8,16},{16,24},{24,32},{32,40},{40,48},{48,56},{56,64},{64,7... | collective-permute-start | bytes 20 | tf_op jit(solution)/shard_map/ppermute | solution.py:30
  12.2 37.2 %collective-permute-start.6 = (s32[1]{0:T(128)}, s32[1]{0:T(128)}, u32[]{:S(2)}, u32[]{:S(2)}) collective-permute-start(s32[1]{0:T(128)} %param.21), channel_id=1, source_target_pairs={{0,256},{8,264},{16,272},{24,280},{32,288},{40,296},{48,304},{56,3... | collective-permute-start | bytes 20 | tf_op jit(solution)/shard_map/ppermute | solution.py:30
  19.7 44.8 %collective-permute-start.4 = (s32[1]{0:T(128)}, s32[1]{0:T(128)}, u32[]{:S(2)}, u32[]{:S(2)}) collective-permute-start(s32[1]{0:T(128)} %param.21), channel_id=1, source_target_pairs={{0,504},{8,0},{16,8},{24,16},{32,24},{40,32},{48,40},{56,48},{64,5... | collective-permute-start | bytes 20 | tf_op jit(solution)/shard_map/ppermute | solution.py:30
  28.2 48.2 %collective-permute-start.3 = (bf16[256,192]{0,1:T(8,128)(2,1)}, bf16[256,192]{0,1:T(8,128)(2,1)S(1)}, u32[]{:S(2)}, u32[]{:S(2)}) collective-permute-start(bf16[256,192]{0,1:T(8,128)(2,1)} %param.18), channel_id=1, source_target_pairs={{0,8},{8,16},{16,24},{24,32},{32,40},{40,48},{48,56},{56,64},{64,7... | collective-permute-start | bytes 294920 | tf_op jit(solution)/shard_map/ppermute | solution.py:30
  30.1 54.7 %collective-permute-start.7 = (bf16[256,192]{0,1:T(8,128)(2,1)}, bf16[256,192]{0,1:T(8,128)(2,1)}, u32[]{:S(2)}, u32[]{:S(2)}) collective-permute-start(bf16[256,192]{0,1:T(8,128)(2,1)} %param.18), channel_id=1, source_target_pairs={{0,256},{8,264},{16,272},{24,280},{32,288},{40,296},{48,304},{56,3... | collective-permute-start | bytes 294920 | tf_op jit(solution)/shard_map/ppermute | solution.py:30
  39.3 34.5 %copy-start.18 = (pred[256]{0:T(512)(128)(4,1)}, pred[256]{0:T(512)(128)(4,1)S(1)}, u32[]{:S(2)}) copy-start(pred[256]{0:T(512)(128)(4,1)S(1)} %iota_compare_fusion.3) | copy-start | bytes 772
  42.0 41.4 %collective-permute-start.5 = (bf16[256,192]{0,1:T(8,128)(2,1)}, bf16[256,192]{0,1:T(8,128)(2,1)}, u32[]{:S(2)}, u32[]{:S(2)}) collective-permute-start(bf16[256,192]{0,1:T(8,128)(2,1)} %param.18), channel_id=1, source_target_pairs={{0,504},{8,0},{16,8},{24,16},{32,24},{40,32},{48,40},{56,48},{64,5... | collective-permute-start | bytes 294920 | tf_op jit(solution)/shard_map/ppermute | solution.py:30
  49.4 4.8 %collective-permute-start = (bf16[192,15]{1,0:T(8,128)(2,1)S(1)}, bf16[192,15]{1,0:T(8,128)(2,1)S(1)}, u32[]{:S(2)}, u32[]{:S(2)}) collective-permute-start(bf16[192,15]{1,0:T(8,128)(2,1)S(1)} %get-tuple-element.21), channel_id=1, source_target_pairs={{8,0},{16,8},{24,16},{32,24},{40,32},{48,40},{56,48},{64,56},{72,6... | collective-permute-start | bytes 17288 | tf_op jit(solution)/shard_map/ppermute | solution.py:22
  54.2 2.8 %collective-permute-start.1 = (bf16[192,15]{1,0:T(8,128)(2,1)S(1)}, bf16[192,15]{1,0:T(8,128)(2,1)S(1)}, u32[]{:S(2)}, u32[]{:S(2)}) collective-permute-start(bf16[192,15]{1,0:T(8,128)(2,1)S(1)} %get-tuple-element.22), channel_id=1, source_target_pairs={{0,8},{8,16},{16,24},{24,32},{32,40},{40,48},{48,56},{56,64},{64,7... | collective-permute-start | bytes 17288 | tf_op jit(solution)/shard_map/ppermute | solution.py:21
  57.0 64.3 %collective-permute-start.8 = (bf16[256,192]{0,1:T(8,128)(2,1)}, bf16[256,192]{0,1:T(8,128)(2,1)}, u32[]{:S(2)}, u32[]{:S(2)}) collective-permute-start(bf16[256,192]{0,1:T(8,128)(2,1)} %param.19), channel_id=1, source_target_pairs={{0,8},{8,16},{16,24},{24,32},{32,40},{40,48},{48,56},{56,64},{64,7... | collective-permute-start | bytes 294920 | tf_op jit(solution)/shard_map/ppermute | solution.py:30
  64.5 9.8 %copy-start.2 = (bf16[256,192]{0,1:T(8,128)(2,1)S(1)}, bf16[256,192]{0,1:T(8,128)(2,1)}, u32[]{:S(2)}) copy-start(bf16[256,192]{0,1:T(8,128)(2,1)} %param.17) | copy-start | bytes 294916
  64.5 9.8 %copy-start.15 = (bf16[256,192]{0,1:T(8,128)(2,1)S(1)}, bf16[256,192]{0,1:T(8,128)(2,1)}, u32[]{:S(2)}) copy-start(bf16[256,192]{0,1:T(8,128)(2,1)} %param.18) | copy-start | bytes 294916
  64.5 58.2 %collective-permute-start.10 = (bf16[256,192]{0,1:T(8,128)(2,1)}, bf16[256,192]{0,1:T(8,128)(2,1)}, u32[]{:S(2)}, u32[]{:S(2)}) collective-permute-start(bf16[256,192]{0,1:T(8,128)(2,1)} %param.19), channel_id=1, source_target_pairs={{0,256},{8,264},{16,272},{24,280},{32,288},{40,296},{48,304},{56,3... | collective-permute-start | bytes 294920 | tf_op jit(solution)/shard_map/ppermute | solution.py:30
  74.3 8.8 %copy-start.4 = (pred[256,256]{0,1:T(8,128)(4,1)}, pred[256,256]{0,1:T(8,128)(4,1)S(1)}, u32[]{:S(2)}) copy-start(pred[256,256]{0,1:T(8,128)(4,1)S(1)} %copy.31) | copy-start | bytes 196612
  76.4 7.1 %copy-start.8 = (pred[256,256]{0,1:T(8,128)(4,1)}, pred[256,256]{0,1:T(8,128)(4,1)S(1)}, u32[]{:S(2)}) copy-start(pred[256,256]{0,1:T(8,128)(4,1)S(1)} %copy.32) | copy-start | bytes 196612
  76.4 7.1 %copy-start.12 = (bf16[256,192]{0,1:T(8,128)(2,1)}, bf16[256,192]{0,1:T(8,128)(2,1)S(1)}, u32[]{:S(2)}) copy-start(bf16[256,192]{0,1:T(8,128)(2,1)S(1)} %collective-permute-done.3) | copy-start | bytes 294916
  76.4 43.6 %collective-permute-start.9 = (bf16[256,192]{0,1:T(8,128)(2,1)}, bf16[256,192]{0,1:T(8,128)(2,1)}, u32[]{:S(2)}, u32[]{:S(2)}) collective-permute-start(bf16[256,192]{0,1:T(8,128)(2,1)} %param.19), channel_id=1, source_target_pairs={{0,504},{8,0},{16,8},{24,16},{32,24},{40,32},{48,40},{56,48},{64,5... | collective-permute-start | bytes 294920 | tf_op jit(solution)/shard_map/ppermute | solution.py:30
  102.9 16.7 %copy-start.11 = (bf16[192,1536]{1,0:T(8,128)(2,1)S(1)}, bf16[192,1536]{1,0:T(8,128)(2,1)}, u32[]{:S(2)}) copy-start(bf16[192,1536]{1,0:T(8,128)(2,1)} %param.16) | copy-start | bytes 1769476
  102.9 16.7 %copy-start.19 = (pred[256]{0:T(512)(128)(4,1)S(1)}, pred[256]{0:T(512)(128)(4,1)}, u32[]{:S(2)}) copy-start(pred[256]{0:T(512)(128)(4,1)} %copy-done.18) | copy-start | bytes 772
  103.9 16.0 %copy-start.14 = (bf16[256,192]{0,1:T(8,128)(2,1)}, bf16[256,192]{0,1:T(8,128)(2,1)S(1)}, u32[]{:S(2)}) copy-start(bf16[256,192]{0,1:T(8,128)(2,1)S(1)} %fusion.37) | copy-start | bytes 294916
  103.9 16.0 %copy-start.7 = (pred[256,256]{0,1:T(8,128)(4,1)S(1)}, pred[256,256]{0,1:T(8,128)(4,1)}, u32[]{:S(2)}) copy-start(pred[256,256]{0,1:T(8,128)(4,1)} %copy.33) | copy-start | bytes 196612
  127.2 16.6 %copy-start.16 = (bf16[256,192]{0,1:T(8,128)(2,1)S(1)}, bf16[256,192]{0,1:T(8,128)(2,1)}, u32[]{:S(2)}) copy-start(bf16[256,192]{0,1:T(8,128)(2,1)} %param.18) | copy-start | bytes 294916
  127.4 16.6 %copy-start.13 = (bf16[256,192]{0,1:T(8,128)(2,1)S(1)}, bf16[256,192]{0,1:T(8,128)(2,1)}, u32[]{:S(2)}) copy-start(bf16[256,192]{0,1:T(8,128)(2,1)} %copy-done.12) | copy-start | bytes 294916
  129.1 27.8 %collective-permute-start.13 = (bf16[256,3,64]{0,2,1:T(8,128)(2,1)S(1)}, bf16[256,3,64]{0,2,1:T(8,128)(2,1)S(1)}, u32[]{:S(2)}, u32[]{:S(2)}) collective-permute-start(bf16[256,3,64]{0,2,1:T(8,128)(2,1)S(1)} %fusion.9), channel_id=1, source_target_pairs={{0,256},{8,264},{16,272},{24,280},{32,288},{40,296},{48,304},{56,3... | collective-permute-start | bytes 294920 | tf_op jit(solution)/shard_map/ppermute | solution.py:30
  136.2 22.6 %collective-permute-start.11 = (bf16[256,3,64]{0,2,1:T(8,128)(2,1)S(1)}, bf16[256,3,64]{0,2,1:T(8,128)(2,1)S(1)}, u32[]{:S(2)}, u32[]{:S(2)}) collective-permute-start(bf16[256,3,64]{0,2,1:T(8,128)(2,1)S(1)} %fusion.11), channel_id=1, source_target_pairs={{0,504},{8,0},{16,8},{24,16},{32,24},{40,32},{48,40},{56,48},{64,5... | collective-permute-start | bytes 294920 | tf_op jit(solution)/shard_map/ppermute | solution.py:30
  141.9 16.9 %collective-permute-start.12 = (bf16[256,3,64]{0,2,1:T(8,128)(2,1)S(1)}, bf16[256,3,64]{0,2,1:T(8,128)(2,1)S(1)}, u32[]{:S(2)}, u32[]{:S(2)}) collective-permute-start(bf16[256,3,64]{0,2,1:T(8,128)(2,1)S(1)} %fusion.10), channel_id=1, source_target_pairs={{0,8},{8,16},{16,24},{24,32},{32,40},{40,48},{48,56},{56,64},{64,7... | collective-permute-start | bytes 294920 | tf_op jit(solution)/shard_map/ppermute | solution.py:30
  144.2 15.5 %collective-permute-start.16 = (bf16[256,3,64]{0,2,1:T(8,128)(2,1)S(1)}, bf16[256,3,64]{0,2,1:T(8,128)(2,1)S(1)}, u32[]{:S(2)}, u32[]{:S(2)}) collective-permute-start(bf16[256,3,64]{0,2,1:T(8,128)(2,1)S(1)} %fusion.14), channel_id=1, source_target_pairs={{0,256},{8,264},{16,272},{24,280},{32,288},{40,296},{48,304},{56,3... | collective-permute-start | bytes 294920 | tf_op jit(solution)/shard_map/ppermute | solution.py:30
  148.4 11.3 %collective-permute-start.14 = (bf16[256,3,64]{0,2,1:T(8,128)(2,1)S(1)}, bf16[256,3,64]{0,2,1:T(8,128)(2,1)S(1)}, u32[]{:S(2)}, u32[]{:S(2)}) collective-permute-start(bf16[256,3,64]{0,2,1:T(8,128)(2,1)S(1)} %fusion.12), channel_id=1, source_target_pairs={{0,504},{8,0},{16,8},{24,16},{32,24},{40,32},{48,40},{56,48},{64,5... | collective-permute-start | bytes 294920 | tf_op jit(solution)/shard_map/ppermute | solution.py:30
  156.9 8.7 %collective-permute-start.15 = (bf16[256,3,64]{0,2,1:T(8,128)(2,1)S(1)}, bf16[256,3,64]{0,2,1:T(8,128)(2,1)S(1)}, u32[]{:S(2)}, u32[]{:S(2)}) collective-permute-start(bf16[256,3,64]{0,2,1:T(8,128)(2,1)S(1)} %fusion.13), channel_id=1, source_target_pairs={{0,8},{8,16},{16,24},{24,32},{32,40},{40,48},{48,56},{56,64},{64,7... | collective-permute-start | bytes 294920 | tf_op jit(solution)/shard_map/ppermute | solution.py:30
  (7 other events, 9.1 us)
Sparse Core Ops, SparseCore 0:
  64.6 38.2 reduce-scatter.1
where the time goes:
time: 175 us; the launch traced here: 173 us
  starting transfers between devices  83.2 us (48%)
  waiting for transfers between devices  25.2 us (14%)
  matrix products  18 us (10%)
  blocking collectives  15.7 us (9%)
  between operations  15.3 us (9%)
  other arithmetic  9.56 us (5%)
  local copies, waits for them, and re-layouts  6.39 us (4%)
    ppermute x15, starting transfers between devices, shifted(): return lax.ppermute(value, axis, pairs)  80.3 us
    all_gather x1, blocking collectives, per_device(): stream_full = lax.all_gather(stream_grad, 'head', axis=1, tiled=True)  15.7 us
    reduce_scatter x1, waiting for transfers between devices, per_device(): lax.psum_scatter(point_grad.astype(jnp.bfloat16), 'head', scatter_dimensi...  15.4 us
    ppermute x15, waiting for transfers between devices, shifted(): return lax.ppermute(value, axis, pairs)  5.84 us
    dot_general x3, matrix products, per_device(): jnp.einsum('qhd,khd->hqk', grad_heads, split(far_values), preferred_eleme...  3.88 us
    dot_general x3, matrix products, per_device(): jnp.einsum('qhd,khd->hqk', query_heads, split(far_keys), preferred_elemen...  3.77 us
  transfers between devices with their start and end apart: 18, of which 4 were waited for; matrix products, arithmetic and copies ran while one was open for 15% of the time, Pallas kernels for 0%

commit v1 on v0

v1 whole, which is shorter than its diff:
```python
import functools
import math

import jax
import jax.numpy as jnp
from jax import lax
from jax.experimental import pallas as pl
from jax.experimental.pallas import tpu as pltpu
from jax.sharding import PartitionSpec as P

HEAD_DIM = 64
KW = 31
LINKS = 4
HALF = 15
LANES = 128
META = 16
NEG = -1e30
SCALE = 1.0 / math.sqrt(HEAD_DIM)
SCALE2 = SCALE * math.log2(math.e)
MIRROR = (0, 2, 1, 3)
VMEM = pl.BlockSpec(memory_space=pltpu.VMEM)
HBM = pl.BlockSpec(memory_space=pltpu.HBM)
SMEM = pl.BlockSpec(memory_space=pltpu.SMEM)
F32 = jnp.float32
BF16 = jnp.bfloat16


def call(body, out_shapes, args, specs, flops, moved, exps=0, scratch=()):
    return pl.pallas_call(
        body,
        out_shape=out_shapes,
        in_specs=specs,
        out_specs=jax.tree.map(lambda _: VMEM, out_shapes),
        scratch_shapes=list(scratch),
        compiler_params=pltpu.CompilerParams(vmem_limit_bytes=24 * 1024 * 1024),
        cost_estimate=pl.CostEstimate(flops=flops, bytes_accessed=moved, transcendentals=exps),
    )(*args)


def dot_tn(a, b):
    return lax.dot_general(a, b, (((0,), (0,)), ((), ())), preferred_element_type=F32)


def dot_nt(a, b):
    return lax.dot_general(a, b, (((1,), (1,)), ((), ())), preferred_element_type=F32)


def dot_nn(a, b):
    return lax.dot_general(a, b, (((1,), (0,)), ((), ())), preferred_element_type=F32)


def prep_body(
    mask_ref,
    count_ref,
    keys_ref,
    values_ref,
    queries_ref,
    g_ref,
    pre_ref,
    taps_ref,
    w_ref,
    out_ref,
    conv_ref,
    gate_ref,
    taps_out,
    w_out,
    x_ref,
    g_low,
    pre_low,
    taps_low,
    w_low,
    sems,
):
    columns, rows = keys_ref.shape
    copies = [
        pltpu.make_async_copy(g_ref, g_low, sems.at[0]),
        pltpu.make_async_copy(taps_ref, taps_low, sems.at[1]),
        pltpu.make_async_copy(pre_ref, pre_low, sems.at[2]),
        pltpu.make_async_copy(w_ref, w_low, sems.at[3]),
        pltpu.make_async_copy(keys_ref, out_ref.at[pl.ds(0, columns)], sems.at[4]),
        pltpu.make_async_copy(values_ref, out_ref.at[pl.ds(columns, columns)], sems.at[5]),
        pltpu.make_async_copy(queries_ref, out_ref.at[pl.ds(2 * columns, columns)], sems.at[6]),
    ]
    for copy in copies:
        copy.start()
    row = lax.broadcasted_iota(jnp.int32, (META, rows), 0)
    first = lax.broadcasted_iota(jnp.int32, (META, rows), 1) < rows // 2
    meta = jnp.where(row == 0, count_ref[0].astype(F32), 0.0)
    for j in range(LINKS):
        for kb in range(2):
            picked = []
            for qb in range(2):
                bit = (mask_ref[qb, j, kb] > 0).astype(F32)
                if j == 0 and qb == kb:
                    bit = jnp.maximum(bit, 1.0)
                picked.append(bit)
            meta = jnp.where(row == 1 + 2 * j + kb, jnp.where(first, picked[0], picked[1]), meta)
    out_ref[3 * columns :, :] = meta.astype(BF16)
    copies[0].wait()
    x_ref[:, 0:LANES] = jnp.zeros((columns, LANES), F32)
    x_ref[:, LANES : LANES + rows] = g_low[...].astype(F32)
    x_ref[:, LANES + rows :] = jnp.zeros((columns, LANES), F32)
    copies[1].wait()
    taps = jnp.concatenate([taps_low[...], jnp.zeros((LANES - KW, columns), F32)], axis=0)
    taps_out[...] = taps.T
    copies[2].wait()
    step = 32

    def block(i, carry):
        at = pl.ds(pl.multiple_of(i * step, step), step)
        x = x_ref[at, :]
        wide = x.shape[1]
        moved = [pltpu.roll(x, (16 - 8 * a) % wide, 1)[:, LANES:] for a in range(4)]
        acc = jnp.zeros((step, wide - LANES), F32)
        for b in range(8):
            part = 0.0
            for a in range(4):
                k = 31 - 8 * a - b
                if k < KW:
                    part = part + taps_out[at, k : k + 1] * moved[a]
            acc = acc + (pltpu.roll(part, wide - LANES - b, 1) if b else part)
        conv_ref[at, :] = acc[:, :rows]
        value = pre_low[0, at, :].astype(F32)
        gate = jax.nn.sigmoid(pre_low[1, at, :].astype(F32))
        gate_ref[0, at, :] = gate
        gate_ref[1, at, :] = value * gate * (1.0 - gate)
        return carry

    lax.fori_loop(0, columns // step, block, 0)
    copies[3].wait()
    model = w_ref.shape[1]
    for at in range(0, model, LANES):
        w_out[at : at + LANES, :] = w_low[:, at : at + LANES].T
    for copy in copies[4:]:
        copy.wait()


def meta_of(ref, columns):
    return ref[3 * columns : 3 * columns + META, :].astype(F32)


def limits(query_meta, key_count, link):
    lane = lax.broadcasted_iota(jnp.int32, query_meta[0:1].shape, 1).astype(F32)
    valid = lane < query_meta[0:1]
    return [
        jnp.where(valid & (query_meta[1 + 2 * link + kb : 2 + 2 * link + kb] > 0.5), key_count, 0.0)
        for kb in range(2)
    ]


def masked(scores, limit_rows):
    rows = scores.shape[0]
    half = rows // 2
    parts = []
    for kb in range(2):
        index = lax.broadcasted_iota(jnp.int32, (half, scores.shape[1]), 0).astype(F32) + kb * half
        parts.append(
            jnp.where(index < limit_rows[kb], scores[kb * half : (kb + 1) * half], NEG)
        )
    return jnp.concatenate(parts, axis=0)


def conv_body(columns, before_ref, after_ref, conv_ref, gate_ref, taps_ref, w_ref, out_ref, low_ref):
    rows = conv_ref.shape[1]
    step = 64
    for at in range(0, columns, step):
        here = slice(at, at + step)
        lane = lax.broadcasted_iota(jnp.int32, (step, LANES), 1)
        before = jnp.where(lane >= LANES - HALF, before_ref[here, rows - LANES :].astype(F32), 0.0)
        after = jnp.where(lane < HALF, after_ref[here, :LANES].astype(F32), 0.0)
        left = jnp.zeros((step, LANES), F32)
        right = jnp.zeros((step, LANES), F32)
        for m in range(1, HALF + 1):
            left = left + taps_ref[here, HALF + m : HALF + m + 1] * pltpu.roll(before, m, 1)
            right = right + taps_ref[here, HALF - m : HALF - m + 1] * pltpu.roll(after, LANES - m, 1)
        left = jnp.where(lane < HALF, left, 0.0)
        right = jnp.where(lane >= LANES - HALF, right, 0.0)
        grad = conv_ref[here, :] + jnp.concatenate([left, right], axis=1)
        low_ref[here, :] = (grad * gate_ref[0, here, :]).astype(BF16)
        low_ref[columns + at : columns + at + step, :] = (grad * gate_ref[1, here, :]).astype(BF16)
    model = w_ref.shape[0]
    chunk = 256 if model % 256 == 0 else LANES
    low = low_ref[...]
    for at in range(0, model, chunk):
        out_ref[at : at + chunk, :] = dot_nn(w_ref[at : at + chunk, :], low).astype(BF16)


def softmax_of(refs, own_meta, columns, links, h, top):
    lo, hi = h * HEAD_DIM, (h + 1) * HEAD_DIM
    query = refs[0][2 * columns + lo : 2 * columns + hi, :]
    scores = []
    for ref, link in zip(refs[1:], links):
        limit = limits(own_meta, meta_of(ref, columns)[0:1], link)
        scores.append(masked(dot_tn(ref[lo:hi, :], query) * SCALE2, limit))
    top = functools.reduce(jnp.maximum, [jnp.max(s, axis=0, keepdims=True) for s in scores], top)
    total = jnp.zeros_like(top)
    mixed = jnp.zeros((HEAD_DIM, top.shape[1]), F32)
    for ref, score in zip(refs[1:], scores):
        expo = jnp.exp2(score - top)
        total = total + jnp.sum(expo, axis=0, keepdims=True)
        mixed = mixed + dot_nn(ref[columns + lo : columns + hi, :], expo.astype(BF16))
    return top, total, mixed


def softmax_body(columns, own_ref, one_ref, two_ref, out_ref):
    own_meta = meta_of(own_ref, columns)
    heads = columns // HEAD_DIM
    start = jnp.full(own_meta[0:1].shape, NEG, F32)
    out_ref[columns:, :] = jnp.zeros((8, own_ref.shape[1]), F32)
    for h in range(heads):
        top, total, mixed = softmax_of(
            (own_ref, own_ref, one_ref, two_ref), own_meta, columns, (0, 1, 2), h, start
        )
        out_ref[h * HEAD_DIM : (h + 1) * HEAD_DIM, :] = mixed
        out_ref[columns + h : columns + h + 1, :] = top
        out_ref[columns + heads + h : columns + heads + h + 1, :] = total


def pieces(value, count):
    found = []
    for _ in range(count):
        low = value.astype(BF16).astype(F32)
        found.append(low)
        value = value - low
    return found


def grad_body(columns, w_ref, stream_ref, own_ref, far_ref, soft_ref, out_ref):
    head_grad = dot_nn(w_ref[...], stream_ref[...])
    own_meta = meta_of(own_ref, columns)
    heads = columns // HEAD_DIM
    lane = lax.broadcasted_iota(jnp.int32, own_meta[0:1].shape, 1).astype(F32)
    valid = lane < own_meta[0:1]
    low = jnp.where(valid, head_grad, 0.0).astype(BF16)
    out_ref[0:columns, :] = low
    rows = []
    for h in range(heads):
        lo, hi = h * HEAD_DIM, (h + 1) * HEAD_DIM
        old_top = soft_ref[columns + h : columns + h + 1, :]
        top, total, mixed = softmax_of((own_ref, far_ref), own_meta, columns, (3,), h, old_top)
        factor = jnp.exp2(old_top - top)
        total = total + factor * soft_ref[columns + heads + h : columns + heads + h + 1, :]
        mixed = (mixed + factor * soft_ref[lo:hi, :]) / total
        delta = jnp.sum(low[lo:hi].astype(F32) * mixed, axis=0, keepdims=True)
        rows += pieces(jnp.where(valid, top + jnp.log2(total), -NEG), 3)
        rows += pieces(jnp.where(valid, delta, 0.0), 2)
    index = lax.broadcasted_iota(jnp.int32, (META, own_meta.shape[1]), 0)
    meta = jnp.zeros((META, own_meta.shape[1]), F32)
    for i, row in enumerate(rows):
        meta = jnp.where(index == i, row, meta)
    out_ref[columns:, :] = meta.astype(BF16)


def stats_of(ref, columns, h):
    meta = ref[columns : columns + META, :].astype(F32)
    at = 5 * h
    lse = (meta[at : at + 1] + meta[at + 1 : at + 2]) + meta[at + 2 : at + 3]
    delta = meta[at + 3 : at + 4] + meta[at + 4 : at + 5]
    return lse, delta


def tile(key, value, query, grad, lse, delta, limit):
    probs = jnp.exp2(masked(dot_tn(key, query) * SCALE2 - lse, limit))
    dscore = (probs * (dot_tn(value, grad) - delta)).astype(BF16)
    return probs.astype(BF16), dscore


def local_body(columns, own_ref, one_ref, two_ref, far_ref, grad_ref, query_out, acc_out):
    refs = (own_ref, one_ref, two_ref, far_ref)
    own_meta = meta_of(own_ref, columns)
    limit = [limits(own_meta, meta_of(refs[j], columns)[0:1], j) for j in range(LINKS)]
    for h in range(columns // HEAD_DIM):
        lo, hi = h * HEAD_DIM, (h + 1) * HEAD_DIM
        query = own_ref[2 * columns + lo : 2 * columns + hi, :]
        grad = grad_ref[lo:hi, :]
        lse, delta = stats_of(grad_ref, columns, h)
        total = jnp.zeros((HEAD_DIM, own_ref.shape[1]), F32)
        for j in range(LINKS):
            key = refs[j][lo:hi, :]
            value = refs[j][columns + lo : columns + hi, :]
            probs, dscore = tile(key, value, query, grad, lse, delta, limit[j])
            total = total + dot_nn(key, dscore)
            if j == 0:
                acc_out[lo:hi, :] = dot_nt(query, dscore)
                acc_out[columns + lo : columns + hi, :] = dot_nt(grad, probs)
        query_out[lo:hi, :] = (total * SCALE).astype(BF16)


def remote_terms(columns, links, own_ref, span_refs, grad_refs, h):
    lo, hi = h * HEAD_DIM, (h + 1) * HEAD_DIM
    key = own_ref[lo:hi, :]
    value = own_ref[columns + lo : columns + hi, :]
    count = meta_of(own_ref, columns)[0:1]
    key_term = value_term = 0.0
    for link, span_ref, grad_ref in zip(links, span_refs, grad_refs):
        query = span_ref[2 * columns + lo : 2 * columns + hi, :]
        grad = grad_ref[lo:hi, :]
        lse, delta = stats_of(grad_ref, columns, h)
        limit = limits(meta_of(span_ref, columns), count, link)
        probs, dscore = tile(key, value, query, grad, lse, delta, limit)
        key_term = key_term + dot_nt(query, dscore)
        value_term = value_term + dot_nt(grad, probs)
    return key_term, value_term


def near_body(columns, own_ref, one_ref, two_ref, grad_one_ref, grad_two_ref, acc_ref, acc_out):
    for h in range(columns // HEAD_DIM):
        lo, hi = h * HEAD_DIM, (h + 1) * HEAD_DIM
        key_term, value_term = remote_terms(
            columns,
            (MIRROR[1], MIRROR[2]),
            own_ref,
            (one_ref, two_ref),
            (grad_one_ref, grad_two_ref),
            h,
        )
        acc_out[lo:hi, :] = acc_ref[lo:hi, :] + key_term
        acc_out[columns + lo : columns + hi, :] = acc_ref[columns + lo : columns + hi, :] + value_term


def far_body(columns, own_ref, far_ref, grad_far_ref, acc_ref, key_out, value_out):
    for h in range(columns // HEAD_DIM):
        lo, hi = h * HEAD_DIM, (h + 1) * HEAD_DIM
        key_term, value_term = remote_terms(
            columns, (MIRROR[3],), own_ref, (far_ref,), (grad_far_ref,), h
        )
        key_out[lo:hi, :] = ((acc_ref[lo:hi, :] + key_term) * SCALE).astype(BF16)
        value_out[lo:hi, :] = (acc_ref[columns + lo : columns + hi, :] + value_term).astype(BF16)


def shifted(value, steps):
    count = lax.axis_size("ctx")
    pairs = [(source, (source + steps) % count) for source in range(count)]
    return lax.ppermute(value, "ctx", pairs)


def per_device(
    g_conv, pre, kernel, w_point, g_out, w_out, queries, keys, values, block_mask, counts
):
    columns, row_count = g_conv.shape
    model = w_point.shape[2]
    groups = lax.axis_size("head")
    spans = lax.axis_size("ctx")
    shape = jax.ShapeDtypeStruct
    queries, keys, values = (queries.T, keys.T, values.T)
    message = 3 * columns + META
    square = 2 * columns * row_count * row_count

    up = [(i, i + 1) for i in range(spans - 1)]
    before = lax.ppermute(g_conv, "ctx", up)
    after = lax.ppermute(g_conv, "ctx", [(j, i) for i, j in up])
    flat = (columns, row_count)
    own, conv, gate, taps, w_turned = call(
        prep_body,
        (
            shape((message, row_count), BF16),
            shape(flat, F32),
            shape((2,) + flat, F32),
            shape((columns, LANES), F32),
            shape((model, 2 * columns), BF16),
        ),
        (
            block_mask,
            counts,
            keys,
            values,
            queries,
            g_conv,
            pre,
            kernel,
            w_point.reshape(2 * columns, model),
        ),
        [SMEM] * 2 + [HBM] * 7,
        2 * KW * columns * row_count,
        8 * columns * model + 8 * message * row_count,
        columns * row_count,
        (
            pltpu.VMEM((columns, row_count + 2 * LANES), F32),
            pltpu.VMEM(flat, BF16),
            pltpu.VMEM((2,) + flat, BF16),
            pltpu.VMEM((KW, columns), F32),
            pltpu.VMEM((2 * columns, model), BF16),
            pltpu.SemaphoreType.DMA((7,)),
        ),
    )
    offsets = [0, 1, -1, spans // 2]
    far = shifted(own, offsets[3])
    point_grad = call(
        functools.partial(conv_body, columns),
        shape((model, row_count), BF16),
        (before, after, conv, gate, taps, w_turned),
        [VMEM] * 6,
        4 * columns * model * row_count,
        4 * columns * model,
        0,
        (pltpu.VMEM((2 * columns, row_count), BF16),),
    )
    parts = lax.all_to_all(
        point_grad.reshape(groups, columns, row_count), "head", 0, 0, tiled=False
    )
    later, _ = lax.optimization_barrier((own, point_grad))
    one, two = [shifted(later, offset) for offset in offsets[1:3]]
    soft = call(
        functools.partial(softmax_body, columns),
        shape((columns + 8, row_count), F32),
        (own, one, two),
        [VMEM] * 3,
        6 * square,
        6 * message * row_count,
        3 * columns // HEAD_DIM * row_count * row_count,
    )
    piece = jnp.sum(parts.astype(F32), axis=0)
    stream_grad = (g_out.astype(F32) + piece).astype(BF16)
    stream_full = lax.all_gather(stream_grad, "head", axis=0, tiled=True)
    grad = call(
        functools.partial(grad_body, columns),
        shape((columns + META, row_count), BF16),
        (w_out, stream_full, own, far, soft),
        [VMEM] * 5,
        2 * columns * model * row_count + 2 * square,
        2 * model * (columns + row_count),
        columns // HEAD_DIM * row_count * row_count,
    )
    grad_one, grad_two, grad_far = [shifted(grad, offset) for offset in offsets[1:]]
    grad_queries, acc = call(
        functools.partial(local_body, columns),
        (shape((columns, row_count), BF16), shape((2 * columns, row_count), F32)),
        (own, one, two, far, grad),
        [VMEM] * 5,
        3 * LINKS * square,
        8 * message * row_count,
        LINKS * columns // HEAD_DIM * row_count * row_count,
    )
    acc = call(
        functools.partial(near_body, columns),
        shape((2 * columns, row_count), F32),
        (own, one, two, grad_one, grad_two, acc),
        [VMEM] * 6,
        8 * square,
        8 * message * row_count,
        2 * columns // HEAD_DIM * row_count * row_count,
    )
    grad_keys, grad_values = call(
        functools.partial(far_body, columns),
        (shape((columns, row_count), BF16), shape((columns, row_count), BF16)),
        (own, far, grad_far, acc),
        [VMEM] * 4,
        4 * square,
        8 * message * row_count,
        columns // HEAD_DIM * row_count * row_count,
    )
    return (stream_grad.T, grad_queries.T, grad_keys.T, grad_values.T)


def solution(mesh):
    in_specs = (
        P("head", "ctx"),
        P(None, "head", "ctx"),
        P(None, "head"),
        P(None, "head", None),
        P("head", "ctx"),
        P("head", None),
        P("ctx", "head"),
        P("ctx", "head"),
        P("ctx", "head"),
        P("ctx", None, None),
        P("ctx"),
    )
    out_specs = (P("ctx", "head"), P("ctx", "head"), P("ctx", "head"), P("ctx", "head"))
    return jax.shard_map(
        per_device, mesh=mesh, in_specs=in_specs, out_specs=out_specs, check_vma=False
    )
```

time: 175 us -> 105 us (0.60)
  starting transfers between devices: 83.2 us -> 41.8 us
  Pallas kernels: 0 us -> 18.7 us
  matrix products: 18 us -> 0 us
  waiting for transfers between devices: 25.2 us -> 7.76 us
  between operations: 15.3 us -> 1.45 us
  blocking collectives: 15.7 us -> 27.1 us
  other arithmetic: 9.56 us -> 0.13 us
    ppermute x17 -> x8, starting transfers between devices: 83.2 us -> 35 us  [the longest x6 28.9 us: shifted(): return lax.ppermute(value, 'ctx', pairs)]
    pallas_call x0 -> x7, Pallas kernels: none -> 18.7 us  [call(): pl.pallas_call(body, out_shape=out_shapes, in_specs=specs, out_specs=jax....]
    dot_general x22 -> x0, matrix products: 18 us -> none  [the longest x3 3.88 us: per_device(): jnp.einsum('qhd,khd->hqk', grad_heads, split(far_values), preferred_eleme...]
    reduce_scatter x1 -> x0, waiting for transfers between devices: 15.4 us -> none  [per_device(): lax.psum_scatter(point_grad.astype(jnp.bfloat16), 'head', scatter_dimensi...]
    all_gather x1, blocking collectives: 15.7 us -> 27.1 us  [per_device(): stream_full = lax.all_gather(stream_grad, 'head', axis=0, tiled=True)]
    all_to_all x0 -> x1, starting transfers between devices: none -> 6.79 us  [per_device(): lax.all_to_all(point_grad.reshape(groups, columns, row_count), 'head', 0,...]
    unnamed x43 -> x21, local copies, waits for them, and re-layouts: 1.03 us -> 7.31 us
    slice x3 -> x0, local copies, waits for them, and re-layouts: 2.9 us -> none  [the longest x2 2 us: per_device(): kernel[tap_index][:, None]]
  transfers between devices with their start and end apart: 18 -> 9, of which waited for: 4 -> 2; matrix products, arithmetic and copies ran while one was open for 15% -> 1% of each run, Pallas kernels for 0% -> 13%
where the time goes in v1:
time: 105 us; the launch traced here: 104 us
  starting transfers between devices  41.8 us (40%)
  blocking collectives  27.1 us (26%)
  Pallas kernels  18.7 us (18%)
  waiting for transfers between devices  7.76 us (7%)
  local copies, waits for them, and re-layouts  7.31 us (7%)
  between operations  1.45 us (1%)
    ppermute x6, starting transfers between devices, shifted(): return lax.ppermute(value, 'ctx', pairs)  28.9 us
    all_gather x1, blocking collectives, per_device(): stream_full = lax.all_gather(stream_grad, 'head', axis=0, tiled=True)  27.1 us
    pallas_call x7, Pallas kernels, call(): pl.pallas_call(body, out_shape=out_shapes, in_specs=specs, out_specs=jax....  18.7 us
    ppermute x6, waiting for transfers between devices, shifted(): return lax.ppermute(value, 'ctx', pairs)  7.75 us
    unnamed x21, local copies, waits for them, and re-layouts  7.31 us
    all_to_all x1, starting transfers between devices, per_device(): lax.all_to_all(point_grad.reshape(groups, columns, row_count), 'head', 0,...  6.79 us
    ppermute x1, starting transfers between devices, per_device(): before = lax.ppermute(g_conv, 'ctx', up)  4.83 us
  transfers between devices with their start and end apart: 9, of which 2 were waited for; matrix products, arithmetic and copies ran while one was open for 1% of the time, Pallas kernels for 13%

profile of v1, /device:TPU:1, one launch (start us, length us, event | category | flops | bytes accessed | tf_op | source)
XLA Modules:
  0.0 104.2 jit_solution(3142279779383544998)
XLA Ops:
  0.6 4.8 %collective-permute-start = (bf16[192,256]{1,0:T(8,128)(2,1)}, bf16[192,256]{1,0:T(8,128)(2,1)S(1)}, u32[]{:S(2)}, u32[]{:S(2)}) collective-permute-start(bf16[192,256]{1,0:T(8,128)(2,1)} %g_ref.1), channel_id=1, source_target_pairs={{0,8},{8,16},{16,24},{24,32},{32,40},{40,48},{48,56},{56,64},{64,7... | collective-permute-start | bytes 294920 | tf_op jit(solution)/shard_map/ppermute | solution.py:350
  5.5 1.3 %collective-permute-start.1 = (bf16[192,256]{1,0:T(8,128)(2,1)}, bf16[192,256]{1,0:T(8,128)(2,1)S(1)}, u32[]{:S(2)}, u32[]{:S(2)}) collective-permute-start(bf16[192,256]{1,0:T(8,128)(2,1)} %g_ref.1), channel_id=1, source_target_pairs={{8,0},{16,8},{24,16},{32,24},{40,32},{48,40},{56,48},{64,56},{72,6... | collective-permute-start | bytes 294920 | tf_op jit(solution)/shard_map/ppermute | solution.py:351
  7.4 0.8 copy.15.mask_ref
  8.2 1.3 %copy-done = bf16[2,192,1536]{2,1,0:T(8,128)(2,1)S(1)} copy-done((bf16[2,192,1536]{2,1,0:T(8,128)(2,1)S(1)}, bf16[2,192,1536]{2,1,0:T(8,128)(2,1)}, u32[]{:S(2)}) %copy-start) | copy-done | bytes 1179672
  9.5 0.9 copy-done.2
  10.4 0.9 copy-done.3
  11.3 0.9 copy-done.4
  12.2 0.9 copy-done.5
  13.1 0.9 copy-done.6
  14.0 0.8 copy-done.7
  14.7 6.8 %shard_map.138 = (bf16[592,256]{1,0:T(8,128)(2,1)S(1)}, f32[192,256]{1,0:T(8,128)S(1)}, f32[2,192,256]{2,1,0:T(8,128)S(1)}, f32[192,128]{1,0:T(8,128)S(1)}, bf16[1536,384]{1,0:T(8,128)(2,1)S(1)}) custom-call(s32[2,4,2]{2,1,0:T(4,128)S(1)} %copy.15.mask_ref, s32[1]{0:T(128)S(6)} %copy.16.count_ref, bf16[192,256]{1,0:T(8,128)(2,1)S(1)} %bitcast.10, ...), custom_call_target="tpu_custom_call" | custom-call | flops 3047424 | bytes 3571712 | tf_op jit(solution)/shard_map/pallas_call | solution.py:29
  21.6 0.0 collective-permute-done.1.after_ref
  21.6 3.0 %shard_map.139 = bf16[1536,256]{1,0:T(8,128)(2,1)} custom-call(bf16[192,256]{1,0:T(8,128)(2,1)S(1)} %collective-permute-done.before_ref, bf16[192,256]{1,0:T(8,128)(2,1)S(1)} %collective-permute-done.1.after_ref, f32[192,256]{1,0:T(8,128)S(1)} %get-tuple-element.14.conv_ref, f32[2,192,256]{2,1,0:T(8,128)S(1)} %get-tuple-element.15.gate_ref, ...), custom_call_target="tpu_custom_call" | custom-call | flops 301989888 | bytes 1179648 | tf_op jit(solution)/shard_map/pallas_call | solution.py:29
  24.6 6.8 %all-to-all-start = ((bf16[8,192,256]{2,1,0:T(8,128)(2,1)}), bf16[8,192,256]{2,1,0:T(8,128)(2,1)S(1)}, u32[]{:S(2)}, u32[]{:S(2)}) async-start(bf16[8,192,256]{2,1,0:T(8,128)(2,1)} %bitcast.4), calls=%async_computation | async-start | bytes 1572864 | tf_op jit(solution)/shard_map/all_to_all | solution.py:398
  31.4 12.4 %collective-permute-start.3 = (bf16[592,256]{1,0:T(8,128)(2,1)S(1)}, bf16[592,256]{1,0:T(8,128)(2,1)S(1)}, u32[]{:S(2)}, u32[]{:S(2)}) collective-permute-start(bf16[592,256]{1,0:T(8,128)(2,1)S(1)} %get-tuple-element.19.own_ref), channel_id=1, source_target_pairs={{0,504},{8,0},{16,8},{24,16},{32,24},{40,32},{48,40},{56,48},{64,5... | collective-permute-start | bytes 909320 | tf_op jit(solution)/shard_map/ppermute | solution.py:334
  43.8 1.9 %collective-permute-start.2 = (bf16[592,256]{1,0:T(8,128)(2,1)S(1)}, bf16[592,256]{1,0:T(8,128)(2,1)S(1)}, u32[]{:S(2)}, u32[]{:S(2)}) collective-permute-start(bf16[592,256]{1,0:T(8,128)(2,1)S(1)} %get-tuple-element.19.own_ref), channel_id=1, source_target_pairs={{0,8},{8,16},{16,24},{24,32},{32,40},{40,48},{48,56},{56,64},{64,7... | collective-permute-start | bytes 909320 | tf_op jit(solution)/shard_map/ppermute | solution.py:334
  45.7 4.4 %collective-permute-start.4 = (bf16[592,256]{1,0:T(8,128)(2,1)S(1)}, bf16[592,256]{1,0:T(8,128)(2,1)S(1)}, u32[]{:S(2)}, u32[]{:S(2)}) collective-permute-start(bf16[592,256]{1,0:T(8,128)(2,1)S(1)} %get-tuple-element.19.own_ref), channel_id=1, source_target_pairs={{0,256},{8,264},{16,272},{24,280},{32,288},{40,296},{48,304},{56,3... | collective-permute-start | bytes 909320 | tf_op jit(solution)/shard_map/ppermute | solution.py:334
  50.2 0.2 collective-permute-done.3.two_ref
  50.4 7.5 %collective-permute-done.2.one_ref = bf16[592,256]{1,0:T(8,128)(2,1)S(1)} collective-permute-done((bf16[592,256]{1,0:T(8,128)(2,1)S(1)}, bf16[592,256]{1,0:T(8,128)(2,1)S(1)}, u32[]{:S(2)}, u32[]{:S(2)}) %collective-permute-start.2) | collective-permute-done | bytes 303136 | tf_op jit(solution)/shard_map/ppermute | solution.py:334
  57.9 1.5 %shard_map.140.soft_ref = f32[200,256]{1,0:T(8,128)S(1)} custom-call(bf16[592,256]{1,0:T(8,128)(2,1)S(1)} %get-tuple-element.19.own_ref, bf16[592,256]{1,0:T(8,128)(2,1)S(1)} %collective-permute-done.2.one_ref, bf16[592,256]{1,0:T(8,128)(2,1)S(1)} %collective-permute-done.3.two_ref), custom_call_target="tpu_custom_call" | custom-call | flops 150994944 | bytes 909312 | tf_op jit(solution)/shard_map/pallas_call | solution.py:29
  59.5 0.0 copy-start.1
  59.5 0.0 all-to-all-done
  59.5 0.1 convert_reduce_fusion
  59.6 0.0 copy-start.8
  59.7 27.1 %all_gather.3.stream_ref = bf16[1536,256]{1,0:T(8,128)(2,1)S(1)} all-gather(bf16[192,256]{1,0:T(8,128)(2,1)S(1)} %add_convert_fusion), channel_id=1, replica_groups=mesh['ctx'=64,'head'=8] {'head'}, dimensions={0}, use_global_device_ids=true | all-gather | bytes 884736 | tf_op jit(solution)/shard_map/all_gather | solution.py:414
  86.8 1.0 shard_map.141.grad_ref
  87.8 1.9 %collective-permute-start.7 = (bf16[208,256]{1,0:T(8,128)(2,1)S(1)}, bf16[208,256]{1,0:T(8,128)(2,1)S(1)}, u32[]{:S(2)}, u32[]{:S(2)}) collective-permute-start(bf16[208,256]{1,0:T(8,128)(2,1)S(1)} %shard_map.141.grad_ref), channel_id=1, source_target_pairs={{0,504},{8,0},{16,8},{24,16},{32,24},{40,32},{48,40},{56,48},{64,5... | collective-permute-start | bytes 319496 | tf_op jit(solution)/shard_map/ppermute | solution.py:334
  89.7 3.4 %collective-permute-start.6 = (bf16[208,256]{1,0:T(8,128)(2,1)S(1)}, bf16[208,256]{1,0:T(8,128)(2,1)S(1)}, u32[]{:S(2)}, u32[]{:S(2)}) collective-permute-start(bf16[208,256]{1,0:T(8,128)(2,1)S(1)} %shard_map.141.grad_ref), channel_id=1, source_target_pairs={{0,8},{8,16},{16,24},{24,32},{32,40},{40,48},{48,56},{56,64},{64,7... | collective-permute-start | bytes 319496 | tf_op jit(solution)/shard_map/ppermute | solution.py:334
  93.1 4.8 %collective-permute-start.5 = (bf16[208,256]{1,0:T(8,128)(2,1)S(1)}, bf16[208,256]{1,0:T(8,128)(2,1)S(1)}, u32[]{:S(2)}, u32[]{:S(2)}) collective-permute-start(bf16[208,256]{1,0:T(8,128)(2,1)S(1)} %shard_map.141.grad_ref), channel_id=1, source_target_pairs={{0,256},{8,264},{16,272},{24,280},{32,288},{40,296},{48,304},{56,3... | collective-permute-start | bytes 319496 | tf_op jit(solution)/shard_map/ppermute | solution.py:334
  97.9 3.4 %shard_map.142 = (bf16[192,256]{1,0:T(8,128)(2,1)}, f32[384,256]{1,0:T(8,128)S(1)}) custom-call(bf16[592,256]{1,0:T(8,128)(2,1)S(1)} %get-tuple-element.19.own_ref, bf16[592,256]{1,0:T(8,128)(2,1)S(1)} %collective-permute-done.2.one_ref, bf16[592,256]{1,0:T(8,128)(2,1)S(1)} %collective-permute-done.3.two_ref, ...), custom_call_target="tpu_custom_call" | custom-call | flops 301989888 | bytes 1212416 | tf_op jit(solution)/shard_map/pallas_call | solution.py:29
  101.4 1.3 %shard_map.143.acc_ref = f32[384,256]{1,0:T(8,128)S(1)} custom-call(bf16[592,256]{1,0:T(8,128)(2,1)S(1)} %get-tuple-element.19.own_ref, bf16[592,256]{1,0:T(8,128)(2,1)S(1)} %collective-permute-done.2.one_ref, bf16[592,256]{1,0:T(8,128)(2,1)S(1)} %collective-permute-done.3.two_ref, bf16[208,256]{1,0:T(8,128)(2,1)S(1)} %collective-permute-done.6.grad_one_ref, ...), custom_call_target="tpu_custom_call" | custom-call | flops 201326592 | bytes 1212416 | tf_op jit(solution)/shard_map/pallas_call | solution.py:29
  102.7 1.5 %shard_map.144 = (bf16[192,256]{1,0:T(8,128)(2,1)}, bf16[192,256]{1,0:T(8,128)(2,1)}) custom-call(bf16[592,256]{1,0:T(8,128)(2,1)S(1)} %get-tuple-element.19.own_ref, bf16[592,256]{1,0:T(8,128)(2,1)S(1)} %collective-permute-done.4.far_ref, bf16[208,256]{1,0:T(8,128)(2,1)S(1)} %collective-permute-done.5.grad_far_ref, f32[384,256]{1,0:T(8,128)S(1)} %shard_map.143.acc_ref), custom_call_target="tpu_custom_call" | custom-call | flops 100663296 | bytes 1212416 | tf_op jit(solution)/shard_map/pallas_call | solution.py:29
  (17 shorter events, 0.1 us)
Async XLA Ops:
  0.6 20.9 %collective-permute-start = (bf16[192,256]{1,0:T(8,128)(2,1)}, bf16[192,256]{1,0:T(8,128)(2,1)S(1)}, u32[]{:S(2)}, u32[]{:S(2)}) collective-permute-start(bf16[192,256]{1,0:T(8,128)(2,1)} %g_ref.1), channel_id=1, source_target_pairs={{0,8},{8,16},{16,24},{24,32},{32,40},{40,48},{48,56},{56,64},{64,7... | collective-permute-start | bytes 294920 | tf_op jit(solution)/shard_map/ppermute | solution.py:350
  5.5 16.1 %collective-permute-start.1 = (bf16[192,256]{1,0:T(8,128)(2,1)}, bf16[192,256]{1,0:T(8,128)(2,1)S(1)}, u32[]{:S(2)}, u32[]{:S(2)}) collective-permute-start(bf16[192,256]{1,0:T(8,128)(2,1)} %g_ref.1), channel_id=1, source_target_pairs={{8,0},{16,8},{24,16},{32,24},{40,32},{48,40},{56,48},{64,56},{72,6... | collective-permute-start | bytes 294920 | tf_op jit(solution)/shard_map/ppermute | solution.py:351
  8.2 1.3 %copy-start = (bf16[2,192,1536]{2,1,0:T(8,128)(2,1)S(1)}, bf16[2,192,1536]{2,1,0:T(8,128)(2,1)}, u32[]{:S(2)}) copy-start(bf16[2,192,1536]{2,1,0:T(8,128)(2,1)} %param.14) | copy-start | bytes 3538948
  9.5 0.9 copy-start.2
  10.4 0.9 copy-start.3
  11.3 0.9 copy-start.4
  12.2 0.9 copy-start.5
  13.1 0.9 copy-start.6
  14.0 0.8 copy-start.7
  24.6 34.9 %all-to-all-start = ((bf16[8,192,256]{2,1,0:T(8,128)(2,1)}), bf16[8,192,256]{2,1,0:T(8,128)(2,1)S(1)}, u32[]{:S(2)}, u32[]{:S(2)}) async-start(bf16[8,192,256]{2,1,0:T(8,128)(2,1)} %bitcast.4), calls=%async_computation | async-start | bytes 1572864 | tf_op jit(solution)/shard_map/all_to_all | solution.py:398
  31.4 28.2 %copy-start.9 = (bf16[192,256]{1,0:T(8,128)(2,1)S(1)}, bf16[192,256]{1,0:T(8,128)(2,1)}, u32[]{:S(2)}) copy-start(bf16[192,256]{1,0:T(8,128)(2,1)} %param.15) | copy-start | bytes 294916
  31.4 19.0 %collective-permute-start.3 = (bf16[592,256]{1,0:T(8,128)(2,1)S(1)}, bf16[592,256]{1,0:T(8,128)(2,1)S(1)}, u32[]{:S(2)}, u32[]{:S(2)}) collective-permute-start(bf16[592,256]{1,0:T(8,128)(2,1)S(1)} %get-tuple-element.19.own_ref), channel_id=1, source_target_pairs={{0,504},{8,0},{16,8},{24,16},{32,24},{40,32},{48,40},{56,48},{64,5... | collective-permute-start | bytes 909320 | tf_op jit(solution)/shard_map/ppermute | solution.py:334
  43.8 14.1 %collective-permute-start.2 = (bf16[592,256]{1,0:T(8,128)(2,1)S(1)}, bf16[592,256]{1,0:T(8,128)(2,1)S(1)}, u32[]{:S(2)}, u32[]{:S(2)}) collective-permute-start(bf16[592,256]{1,0:T(8,128)(2,1)S(1)} %get-tuple-element.19.own_ref), channel_id=1, source_target_pairs={{0,8},{8,16},{16,24},{24,32},{32,40},{40,48},{48,56},{56,64},{64,7... | collective-permute-start | bytes 909320 | tf_op jit(solution)/shard_map/ppermute | solution.py:334
  45.7 41.0 %collective-permute-start.4 = (bf16[592,256]{1,0:T(8,128)(2,1)S(1)}, bf16[592,256]{1,0:T(8,128)(2,1)S(1)}, u32[]{:S(2)}, u32[]{:S(2)}) collective-permute-start(bf16[592,256]{1,0:T(8,128)(2,1)S(1)} %get-tuple-element.19.own_ref), channel_id=1, source_target_pairs={{0,256},{8,264},{16,272},{24,280},{32,288},{40,296},{48,304},{56,3... | collective-permute-start | bytes 909320 | tf_op jit(solution)/shard_map/ppermute | solution.py:334
  59.5 27.3 %copy-start.1 = (bf16[192,1536]{1,0:T(8,128)(2,1)S(1)}, bf16[192,1536]{1,0:T(8,128)(2,1)}, u32[]{:S(2)}) copy-start(bf16[192,1536]{1,0:T(8,128)(2,1)} %w_ref.1) | copy-start | bytes 1769476
  59.6 28.1 %copy-start.8 = (bf16[192,256]{1,0:T(8,128)(2,1)}, bf16[192,256]{1,0:T(8,128)(2,1)S(1)}, u32[]{:S(2)}) copy-start(bf16[192,256]{1,0:T(8,128)(2,1)S(1)} %add_convert_fusion) | copy-start | bytes 294916
  87.8 13.6 %collective-permute-start.7 = (bf16[208,256]{1,0:T(8,128)(2,1)S(1)}, bf16[208,256]{1,0:T(8,128)(2,1)S(1)}, u32[]{:S(2)}, u32[]{:S(2)}) collective-permute-start(bf16[208,256]{1,0:T(8,128)(2,1)S(1)} %shard_map.141.grad_ref), channel_id=1, source_target_pairs={{0,504},{8,0},{16,8},{24,16},{32,24},{40,32},{48,40},{56,48},{64,5... | collective-permute-start | bytes 319496 | tf_op jit(solution)/shard_map/ppermute | solution.py:334
  89.7 11.6 %collective-permute-start.6 = (bf16[208,256]{1,0:T(8,128)(2,1)S(1)}, bf16[208,256]{1,0:T(8,128)(2,1)S(1)}, u32[]{:S(2)}, u32[]{:S(2)}) collective-permute-start(bf16[208,256]{1,0:T(8,128)(2,1)S(1)} %shard_map.141.grad_ref), channel_id=1, source_target_pairs={{0,8},{8,16},{16,24},{24,32},{32,40},{40,48},{48,56},{56,64},{64,7... | collective-permute-start | bytes 319496 | tf_op jit(solution)/shard_map/ppermute | solution.py:334
  93.1 9.6 %collective-permute-start.5 = (bf16[208,256]{1,0:T(8,128)(2,1)S(1)}, bf16[208,256]{1,0:T(8,128)(2,1)S(1)}, u32[]{:S(2)}, u32[]{:S(2)}) collective-permute-start(bf16[208,256]{1,0:T(8,128)(2,1)S(1)} %shard_map.141.grad_ref), channel_id=1, source_target_pairs={{0,256},{8,264},{16,272},{24,280},{32,288},{40,296},{48,304},{56,3... | collective-permute-start | bytes 319496 | tf_op jit(solution)/shard_map/ppermute | solution.py:334

commit v2 on v1

--- a/solution.py
+++ b/solution.py
@@ -14,6 +14,7 @@
 HALF = 15
 LANES = 128
 META = 16
+BIG = 58
 NEG = -1e30
 SCALE = 1.0 / math.sqrt(HEAD_DIM)
 SCALE2 = SCALE * math.log2(math.e)
@@ -25,14 +26,14 @@
 BF16 = jnp.bfloat16
 
 
-def call(body, out_shapes, args, specs, flops, moved, exps=0, scratch=()):
+def call(body, out_shapes, args, specs, flops, moved, exps=0, scratch=(), mib=24):
     return pl.pallas_call(
         body,
         out_shape=out_shapes,
         in_specs=specs,
         out_specs=jax.tree.map(lambda _: VMEM, out_shapes),
         scratch_shapes=list(scratch),
-        compiler_params=pltpu.CompilerParams(vmem_limit_bytes=24 * 1024 * 1024),
+        compiler_params=pltpu.CompilerParams(vmem_limit_bytes=mib * 1024 * 1024),
         cost_estimate=pl.CostEstimate(flops=flops, bytes_accessed=moved, transcendentals=exps),
     )(*args)
 
@@ -49,37 +50,11 @@
     return lax.dot_general(a, b, (((1,), (0,)), ((), ())), preferred_element_type=F32)
 
 
-def prep_body(
-    mask_ref,
-    count_ref,
-    keys_ref,
-    values_ref,
-    queries_ref,
-    g_ref,
-    pre_ref,
-    taps_ref,
-    w_ref,
-    out_ref,
-    conv_ref,
-    gate_ref,
-    taps_out,
-    w_out,
-    x_ref,
-    g_low,
-    pre_low,
-    taps_low,
-    w_low,
-    sems,
-):
+def pack_body(mask_ref, count_ref, keys_ref, values_ref, queries_ref, out_ref, sems):
     columns, rows = keys_ref.shape
     copies = [
-        pltpu.make_async_copy(g_ref, g_low, sems.at[0]),
-        pltpu.make_async_copy(taps_ref, taps_low, sems.at[1]),
-        pltpu.make_async_copy(pre_ref, pre_low, sems.at[2]),
-        pltpu.make_async_copy(w_ref, w_low, sems.at[3]),
-        pltpu.make_async_copy(keys_ref, out_ref.at[pl.ds(0, columns)], sems.at[4]),
-        pltpu.make_async_copy(values_ref, out_ref.at[pl.ds(columns, columns)], sems.at[5]),
-        pltpu.make_async_copy(queries_ref, out_ref.at[pl.ds(2 * columns, columns)], sems.at[6]),
+        pltpu.make_async_copy(ref, out_ref.at[pl.ds(i * columns, columns)], sems.at[i])
+        for i, ref in enumerate((keys_ref, values_ref, queries_ref))
     ]
     for copy in copies:
         copy.start()
@@ -96,14 +71,28 @@
                 picked.append(bit)
             meta = jnp.where(row == 1 + 2 * j + kb, jnp.where(first, picked[0], picked[1]), meta)
     out_ref[3 * columns :, :] = meta.astype(BF16)
-    copies[0].wait()
+    for copy in copies:
+        copy.wait()
+
+
+def own_conv_body(
+    g_ref, pre_ref, taps_ref, conv_ref, gate_ref, taps_out, x_ref, g_low, pre_low, taps_low, sems
+):
+    columns, rows = g_ref.shape
+    copies = [
+        pltpu.make_async_copy(g_ref, g_low, sems.at[0]),
+        pltpu.make_async_copy(taps_ref, taps_low, sems.at[1]),
+        pltpu.make_async_copy(pre_ref, pre_low, sems.at[2]),
+    ]
+    for copy in copies:
+        copy.start()
     x_ref[:, 0:LANES] = jnp.zeros((columns, LANES), F32)
+    x_ref[:, LANES + rows :] = jnp.zeros((columns, LANES), F32)
+    for copy in copies:
+        copy.wait()
     x_ref[:, LANES : LANES + rows] = g_low[...].astype(F32)
-    x_ref[:, LANES + rows :] = jnp.zeros((columns, LANES), F32)
-    copies[1].wait()
     taps = jnp.concatenate([taps_low[...], jnp.zeros((LANES - KW, columns), F32)], axis=0)
     taps_out[...] = taps.T
-    copies[2].wait()
     step = 32
 
     def block(i, carry):
@@ -127,12 +116,6 @@
         return carry
 
     lax.fori_loop(0, columns // step, block, 0)
-    copies[3].wait()
-    model = w_ref.shape[1]
-    for at in range(0, model, LANES):
-        w_out[at : at + LANES, :] = w_low[:, at : at + LANES].T
-    for copy in copies[4:]:
-        copy.wait()
 
 
 def meta_of(ref, columns):
@@ -160,7 +143,21 @@
     return jnp.concatenate(parts, axis=0)
 
 
-def conv_body(columns, before_ref, after_ref, conv_ref, gate_ref, taps_ref, w_ref, out_ref, low_ref):
+def edge_body(
+    columns,
+    before_ref,
+    after_ref,
+    conv_ref,
+    gate_ref,
+    taps_ref,
+    w_ref,
+    out_ref,
+    low_ref,
+    w_low,
+    sem,
+):
+    copy = pltpu.make_async_copy(w_ref, w_low, sem)
+    copy.start()
     rows = conv_ref.shape[1]
     step = 64
     for at in range(0, columns, step):
@@ -178,11 +175,12 @@
         grad = conv_ref[here, :] + jnp.concatenate([left, right], axis=1)
         low_ref[here, :] = (grad * gate_ref[0, here, :]).astype(BF16)
         low_ref[columns + at : columns + at + step, :] = (grad * gate_ref[1, here, :]).astype(BF16)
-    model = w_ref.shape[0]
+    copy.wait()
+    model = w_ref.shape[1]
     chunk = 256 if model % 256 == 0 else LANES
     low = low_ref[...]
     for at in range(0, model, chunk):
-        out_ref[at : at + chunk, :] = dot_nn(w_ref[at : at + chunk, :], low).astype(BF16)
+        out_ref[at : at + chunk, :] = dot_tn(w_low[:, at : at + chunk], low).astype(BF16)
 
 
 def softmax_of(refs, own_meta, columns, links, h, top):
@@ -350,55 +348,55 @@
     before = lax.ppermute(g_conv, "ctx", up)
     after = lax.ppermute(g_conv, "ctx", [(j, i) for i, j in up])
     flat = (columns, row_count)
-    own, conv, gate, taps, w_turned = call(
-        prep_body,
-        (
-            shape((message, row_count), BF16),
-            shape(flat, F32),
-            shape((2,) + flat, F32),
-            shape((columns, LANES), F32),
-            shape((model, 2 * columns), BF16),
-        ),
-        (
-            block_mask,
-            counts,
-            keys,
-            values,
-            queries,
-            g_conv,
-            pre,
-            kernel,
-            w_point.reshape(2 * columns, model),
-        ),
-        [SMEM] * 2 + [HBM] * 7,
+    own = call(
+        pack_body,
+        shape((message, row_count), BF16),
+        (block_mask, counts, keys, values, queries),
+        [SMEM] * 2 + [HBM] * 3,
+        0,
+        4 * message * row_count,
+        0,
+        (pltpu.SemaphoreType.DMA((3,)),),
+        mib=BIG,
+    )
+    offsets = [0, 1, -1, spans // 2]
+    far = shifted(own, offsets[3])
+    conv, gate, taps = call(
+        own_conv_body,
+        (shape(flat, F32), shape((2,) + flat, F32), shape((columns, LANES), F32)),
+        (g_conv, pre, kernel),
+        [HBM] * 3,
         2 * KW * columns * row_count,
-        8 * columns * model + 8 * message * row_count,
+        20 * columns * row_count,
         columns * row_count,
         (
             pltpu.VMEM((columns, row_count + 2 * LANES), F32),
             pltpu.VMEM(flat, BF16),
             pltpu.VMEM((2,) + flat, BF16),
             pltpu.VMEM((KW, columns), F32),
-            pltpu.VMEM((2 * columns, model), BF16),
-            pltpu.SemaphoreType.DMA((7,)),
+            pltpu.SemaphoreType.DMA((3,)),
         ),
-    )
-    offsets = [0, 1, -1, spans // 2]
-    far = shifted(own, offsets[3])
+        mib=BIG,
+    )
     point_grad = call(
-        functools.partial(conv_body, columns),
+        functools.partial(edge_body, columns),
         shape((model, row_count), BF16),
-        (before, after, conv, gate, taps, w_turned),
-        [VMEM] * 6,
+        (before, after, conv, gate, taps, w_point.reshape(2 * columns, model)),
+        [VMEM] * 5 + [HBM],
         4 * columns * model * row_count,
         4 * columns * model,
         0,
-        (pltpu.VMEM((2 * columns, row_count), BF16),),
+        (
+            pltpu.VMEM((2 * columns, row_count), BF16),
+            pltpu.VMEM((2 * columns, model), BF16),
+            pltpu.SemaphoreType.DMA,
+        ),
+        mib=BIG,
     )
     parts = lax.all_to_all(
         point_grad.reshape(groups, columns, row_count), "head", 0, 0, tiled=False
     )
-    later, _ = lax.optimization_barrier((own, point_grad))
+    later, far, _ = lax.optimization_barrier((own, far, point_grad))
     one, two = [shifted(later, offset) for offset in offsets[1:3]]
     soft = call(
         functools.partial(softmax_body, columns),

time: 105 us -> 114 us (1.086)
  starting transfers between devices: 41.8 us -> 55 us
  blocking collectives: 27.1 us -> 15.6 us
  waiting for transfers between devices: 7.76 us -> 14.6 us
  local copies, waits for them, and re-layouts: 7.31 us -> 2.33 us
  Pallas kernels: 18.7 us -> 23.2 us
    ppermute x6, starting transfers between devices: 28.9 us -> 42 us  [shifted(): return lax.ppermute(value, 'ctx', pairs)]
    all_gather x1, blocking collectives: 27.1 us -> 15.6 us  [per_device(): stream_full = lax.all_gather(stream_grad, 'head', axis=0, tiled=True)]
    ppermute x6, waiting for transfers between devices: 7.75 us -> 14.6 us  [shifted(): return lax.ppermute(value, 'ctx', pairs)]
    unnamed x21 -> x17, local copies, waits for them, and re-layouts: 7.31 us -> 2.33 us
    pallas_call x7 -> x8, Pallas kernels: 18.7 us -> 23.2 us  [call(): pl.pallas_call(body, out_shape=out_shapes, in_specs=specs, out_specs=jax....]
  transfers between devices with their start and end apart: 9 -> 9, of which waited for: 2 -> 3; matrix products, arithmetic and copies ran while one was open for 1% -> 1% of each run, Pallas kernels for 13% -> 14%
where the time goes in v2:
time: 114 us; the launch traced here: 112 us
  starting transfers between devices  55 us (48%)
  Pallas kernels  23.2 us (20%)
  blocking collectives  15.6 us (14%)
  waiting for transfers between devices  14.6 us (13%)
  local copies, waits for them, and re-layouts  2.33 us (2%)
  between operations  1.5 us (1%)
    ppermute x6, starting transfers between devices, shifted(): return lax.ppermute(value, 'ctx', pairs)  42 us
    pallas_call x8, Pallas kernels, call(): pl.pallas_call(body, out_shape=out_shapes, in_specs=specs, out_specs=jax....  23.2 us
    all_gather x1, blocking collectives, per_device(): stream_full = lax.all_gather(stream_grad, 'head', axis=0, tiled=True)  15.6 us
    ppermute x6, waiting for transfers between devices, shifted(): return lax.ppermute(value, 'ctx', pairs)  14.6 us
    all_to_all x1, starting transfers between devices, per_device(): lax.all_to_all(point_grad.reshape(groups, columns, row_count), 'head', 0,...  6.8 us
    ppermute x1, starting transfers between devices, per_device(): before = lax.ppermute(g_conv, 'ctx', up)  4.83 us
    unnamed x17, local copies, waits for them, and re-layouts  2.33 us
  transfers between devices with their start and end apart: 9, of which 3 were waited for; matrix products, arithmetic and copies ran while one was open for 1% of the time, Pallas kernels for 14%

profile of v2, /device:TPU:1, one launch (start us, length us, event | category | flops | bytes accessed | tf_op | source)
XLA Modules:
  0.0 112.3 jit_solution(5757512944800677186)
XLA Ops:
  0.6 4.8 %collective-permute-start = (bf16[192,256]{1,0:T(8,128)(2,1)}, bf16[192,256]{1,0:T(8,128)(2,1)S(1)}, u32[]{:S(2)}, u32[]{:S(2)}) collective-permute-start(bf16[192,256]{1,0:T(8,128)(2,1)} %g_ref.1), channel_id=1, source_target_pairs={{0,8},{8,16},{16,24},{24,32},{32,40},{40,48},{48,56},{56,64},{64,7... | collective-permute-start | bytes 294920 | tf_op jit(solution)/shard_map/ppermute | solution.py:348
  5.5 1.3 %collective-permute-start.1 = (bf16[192,256]{1,0:T(8,128)(2,1)}, bf16[192,256]{1,0:T(8,128)(2,1)S(1)}, u32[]{:S(2)}, u32[]{:S(2)}) collective-permute-start(bf16[192,256]{1,0:T(8,128)(2,1)} %g_ref.1), channel_id=1, source_target_pairs={{8,0},{16,8},{24,16},{32,24},{40,32},{48,40},{56,48},{64,56},{72,6... | collective-permute-start | bytes 294920 | tf_op jit(solution)/shard_map/ppermute | solution.py:349
  6.8 6.5 %shard_map.138 = (f32[192,256]{1,0:T(8,128)}, f32[2,192,256]{2,1,0:T(8,128)}, f32[192,128]{1,0:T(8,128)}) custom-call(bf16[192,256]{1,0:T(8,128)(2,1)} %g_ref.1, bf16[2,192,256]{2,1,0:T(8,128)(2,1)} %pre_ref.1, f32[31,192]{1,0:T(8,128)} %taps_ref.1), custom_call_target="tpu_custom_call" | custom-call | flops 3047424 | bytes 983040 | tf_op jit(solution)/shard_map/pallas_call | solution.py:30
  13.3 0.0 copy-start.4
  13.3 0.0 copy-start.5
  13.3 0.6 copy-done.4
  13.9 0.0 copy-done.5
  13.9 5.3 %shard_map.139 = bf16[1536,256]{1,0:T(8,128)(2,1)} custom-call(bf16[192,256]{1,0:T(8,128)(2,1)} %copy-done.4, bf16[192,256]{1,0:T(8,128)(2,1)} %copy-done.5, f32[192,256]{1,0:T(8,128)} %get-tuple-element.13.conv_ref, f32[2,192,256]{2,1,0:T(8,128)} %get-tuple-element.14.gate_ref, f32[192,128]{1,0:T(8,128)} %get-tuple-element.15.taps_ref, ...), custom_call_target="tpu_custom_call" | custom-call | flops 301989888 | bytes 1179648 | tf_op jit(solution)/shard_map/pallas_call | solution.py:30
  19.3 0.0 copy-start.7
  19.3 6.8 %all-to-all-start = ((bf16[8,192,256]{2,1,0:T(8,128)(2,1)}), bf16[8,192,256]{2,1,0:T(8,128)(2,1)S(1)}, u32[]{:S(2)}, u32[]{:S(2)}) async-start(bf16[8,192,256]{2,1,0:T(8,128)(2,1)} %bitcast.9), calls=%async_computation | async-start | bytes 1572864 | tf_op jit(solution)/shard_map/all_to_all | solution.py:396
  26.1 0.7 copy.15.mask_ref
  27.4 0.0 copy-start.6
  27.4 2.6 %shard_map.140.own_ref = bf16[592,256]{1,0:T(8,128)(2,1)} custom-call(s32[2,4,2]{2,1,0:T(4,128)} %copy.15.mask_ref, s32[1]{0:T(128)S(6)} %copy.16.count_ref, bf16[192,256]{1,0:T(8,128)(2,1)} %bitcast.12, bf16[192,256]{1,0:T(8,128)(2,1)} %bitcast.13, bf16[192,256]{1,0:T(8,128)(2,1)} %bitcast.14), custom_call_target="tpu_custom_call" | custom-call | bytes 606208 | tf_op jit(solution)/shard_map/pallas_call | solution.py:30
  30.0 13.1 %collective-permute-start.2 = (bf16[592,256]{1,0:T(8,128)(2,1)}, bf16[592,256]{1,0:T(8,128)(2,1)S(1)}, u32[]{:S(2)}, u32[]{:S(2)}) collective-permute-start(bf16[592,256]{1,0:T(8,128)(2,1)} %shard_map.140.own_ref), channel_id=1, source_target_pairs={{0,256},{8,264},{16,272},{24,280},{32,288},{40,296},{48,304},{56,3... | collective-permute-start | bytes 909320 | tf_op jit(solution)/shard_map/ppermute | solution.py:332
  43.1 8.5 %collective-permute-done.2.far_ref = bf16[592,256]{1,0:T(8,128)(2,1)S(1)} collective-permute-done((bf16[592,256]{1,0:T(8,128)(2,1)}, bf16[592,256]{1,0:T(8,128)(2,1)S(1)}, u32[]{:S(2)}, u32[]{:S(2)}) %collective-permute-start.2) | collective-permute-done | bytes 303136 | tf_op jit(solution)/shard_map/ppermute | solution.py:332
  51.6 2.6 %collective-permute-start.3 = (bf16[592,256]{1,0:T(8,128)(2,1)}, bf16[592,256]{1,0:T(8,128)(2,1)S(1)}, u32[]{:S(2)}, u32[]{:S(2)}) collective-permute-start(bf16[592,256]{1,0:T(8,128)(2,1)} %shard_map.140.own_ref), channel_id=1, source_target_pairs={{0,8},{8,16},{16,24},{24,32},{32,40},{40,48},{48,56},{56,64},{64,7... | collective-permute-start | bytes 909320 | tf_op jit(solution)/shard_map/ppermute | solution.py:332
  54.2 11.4 %collective-permute-start.4 = (bf16[592,256]{1,0:T(8,128)(2,1)}, bf16[592,256]{1,0:T(8,128)(2,1)S(1)}, u32[]{:S(2)}, u32[]{:S(2)}) collective-permute-start(bf16[592,256]{1,0:T(8,128)(2,1)} %shard_map.140.own_ref), channel_id=1, source_target_pairs={{0,504},{8,0},{16,8},{24,16},{32,24},{40,32},{48,40},{56,48},{64,5... | collective-permute-start | bytes 909320 | tf_op jit(solution)/shard_map/ppermute | solution.py:332
  65.6 5.1 %collective-permute-done.3.one_ref = bf16[592,256]{1,0:T(8,128)(2,1)S(1)} collective-permute-done((bf16[592,256]{1,0:T(8,128)(2,1)}, bf16[592,256]{1,0:T(8,128)(2,1)S(1)}, u32[]{:S(2)}, u32[]{:S(2)}) %collective-permute-start.3) | collective-permute-done | bytes 303136 | tf_op jit(solution)/shard_map/ppermute | solution.py:332
  70.7 1.0 collective-permute-done.4.two_ref
  71.7 1.0 copy-done
  72.6 1.6 %shard_map.141.soft_ref = f32[200,256]{1,0:T(8,128)S(1)} custom-call(bf16[592,256]{1,0:T(8,128)(2,1)S(1)} %copy-done, bf16[592,256]{1,0:T(8,128)(2,1)S(1)} %collective-permute-done.3.one_ref, bf16[592,256]{1,0:T(8,128)(2,1)S(1)} %collective-permute-done.4.two_ref), custom_call_target="tpu_custom_call" | custom-call | flops 150994944 | bytes 909312 | tf_op jit(solution)/shard_map/pallas_call | solution.py:30
  74.2 0.0 copy-start.2
  74.2 0.1 convert_reduce_fusion
  74.4 0.0 copy-start.3
  74.4 15.6 %all_gather.3.stream_ref = bf16[1536,256]{1,0:T(8,128)(2,1)S(1)} all-gather(bf16[192,256]{1,0:T(8,128)(2,1)S(1)} %add_convert_fusion), channel_id=1, replica_groups=mesh['ctx'=64,'head'=8] {'head'}, dimensions={0}, use_global_device_ids=true | all-gather | bytes 884736 | tf_op jit(solution)/shard_map/all_gather | solution.py:412
  90.0 1.0 shard_map.142.grad_ref
  91.0 1.9 %collective-permute-start.6 = (bf16[208,256]{1,0:T(8,128)(2,1)S(1)}, bf16[208,256]{1,0:T(8,128)(2,1)S(1)}, u32[]{:S(2)}, u32[]{:S(2)}) collective-permute-start(bf16[208,256]{1,0:T(8,128)(2,1)S(1)} %shard_map.142.grad_ref), channel_id=1, source_target_pairs={{0,8},{8,16},{16,24},{24,32},{32,40},{40,48},{48,56},{56,64},{64,7... | collective-permute-start | bytes 319496 | tf_op jit(solution)/shard_map/ppermute | solution.py:332
  92.9 7.3 %collective-permute-start.7 = (bf16[208,256]{1,0:T(8,128)(2,1)S(1)}, bf16[208,256]{1,0:T(8,128)(2,1)S(1)}, u32[]{:S(2)}, u32[]{:S(2)}) collective-permute-start(bf16[208,256]{1,0:T(8,128)(2,1)S(1)} %shard_map.142.grad_ref), channel_id=1, source_target_pairs={{0,504},{8,0},{16,8},{24,16},{32,24},{40,32},{48,40},{56,48},{64,5... | collective-permute-start | bytes 319496 | tf_op jit(solution)/shard_map/ppermute | solution.py:332
  100.2 5.7 %collective-permute-start.5 = (bf16[208,256]{1,0:T(8,128)(2,1)S(1)}, bf16[208,256]{1,0:T(8,128)(2,1)S(1)}, u32[]{:S(2)}, u32[]{:S(2)}) collective-permute-start(bf16[208,256]{1,0:T(8,128)(2,1)S(1)} %shard_map.142.grad_ref), channel_id=1, source_target_pairs={{0,256},{8,264},{16,272},{24,280},{32,288},{40,296},{48,304},{56,3... | collective-permute-start | bytes 319496 | tf_op jit(solution)/shard_map/ppermute | solution.py:332
  106.0 3.4 %shard_map.143 = (bf16[192,256]{1,0:T(8,128)(2,1)}, f32[384,256]{1,0:T(8,128)S(1)}) custom-call(bf16[592,256]{1,0:T(8,128)(2,1)S(1)} %copy-done.1, bf16[592,256]{1,0:T(8,128)(2,1)S(1)} %collective-permute-done.3.one_ref, bf16[592,256]{1,0:T(8,128)(2,1)S(1)} %collective-permute-done.4.two_ref, bf16[592,256]{1,0:T(8,128)(2,1)S(1)} %collective-permute-done.2.far_ref, ...), custom_call_target="tpu_custom_call" | custom-call | flops 301989888 | bytes 1212416 | tf_op jit(solution)/shard_map/pallas_call | solution.py:30
  109.4 1.3 %shard_map.144.acc_ref = f32[384,256]{1,0:T(8,128)S(1)} custom-call(bf16[592,256]{1,0:T(8,128)(2,1)S(1)} %copy-done.1, bf16[592,256]{1,0:T(8,128)(2,1)S(1)} %collective-permute-done.3.one_ref, bf16[592,256]{1,0:T(8,128)(2,1)S(1)} %collective-permute-done.4.two_ref, bf16[208,256]{1,0:T(8,128)(2,1)S(1)} %collective-permute-done.6.grad_one_ref, ...), custom_call_target="tpu_custom_call" | custom-call | flops 201326592 | bytes 1212416 | tf_op jit(solution)/shard_map/pallas_call | solution.py:30
  110.7 1.5 %shard_map.145 = (bf16[192,256]{1,0:T(8,128)(2,1)}, bf16[192,256]{1,0:T(8,128)(2,1)}) custom-call(bf16[592,256]{1,0:T(8,128)(2,1)S(1)} %copy-done.1, bf16[592,256]{1,0:T(8,128)(2,1)S(1)} %collective-permute-done.2.far_ref, bf16[208,256]{1,0:T(8,128)(2,1)S(1)} %collective-permute-done.5.grad_far_ref, f32[384,256]{1,0:T(8,128)S(1)} %shard_map.144.acc_ref), custom_call_target="tpu_custom_call" | custom-call | flops 100663296 | bytes 1212416 | tf_op jit(solution)/shard_map/pallas_call | solution.py:30
  (14 shorter events, 0.1 us)
Async XLA Ops:
  0.6 12.6 %collective-permute-start = (bf16[192,256]{1,0:T(8,128)(2,1)}, bf16[192,256]{1,0:T(8,128)(2,1)S(1)}, u32[]{:S(2)}, u32[]{:S(2)}) collective-permute-start(bf16[192,256]{1,0:T(8,128)(2,1)} %g_ref.1), channel_id=1, source_target_pairs={{0,8},{8,16},{16,24},{24,32},{32,40},{40,48},{48,56},{56,64},{64,7... | collective-permute-start | bytes 294920 | tf_op jit(solution)/shard_map/ppermute | solution.py:348
  5.5 7.8 %collective-permute-start.1 = (bf16[192,256]{1,0:T(8,128)(2,1)}, bf16[192,256]{1,0:T(8,128)(2,1)S(1)}, u32[]{:S(2)}, u32[]{:S(2)}) collective-permute-start(bf16[192,256]{1,0:T(8,128)(2,1)} %g_ref.1), channel_id=1, source_target_pairs={{8,0},{16,8},{24,16},{32,24},{40,32},{48,40},{56,48},{64,56},{72,6... | collective-permute-start | bytes 294920 | tf_op jit(solution)/shard_map/ppermute | solution.py:349
  13.3 0.6 copy-start.4
  13.3 0.7 copy-start.5
  19.3 6.8 %copy-start.7 = (s32[2,4,2]{1,2,0:T(2,128)S(1)}, s32[2,4,2]{1,2,0:T(2,128)}, u32[]{:S(2)}) copy-start(s32[2,4,2]{1,2,0:T(2,128)} %param.20) | copy-start | bytes 196
  19.3 54.9 %all-to-all-start = ((bf16[8,192,256]{2,1,0:T(8,128)(2,1)}), bf16[8,192,256]{2,1,0:T(8,128)(2,1)S(1)}, u32[]{:S(2)}, u32[]{:S(2)}) async-start(bf16[8,192,256]{2,1,0:T(8,128)(2,1)} %bitcast.9), calls=%async_computation | async-start | bytes 1572864 | tf_op jit(solution)/shard_map/all_to_all | solution.py:396
  27.4 46.9 %copy-start.6 = (bf16[192,256]{1,0:T(8,128)(2,1)S(1)}, bf16[192,256]{1,0:T(8,128)(2,1)}, u32[]{:S(2)}) copy-start(bf16[192,256]{1,0:T(8,128)(2,1)} %param.15) | copy-start | bytes 294916
  30.0 21.6 %collective-permute-start.2 = (bf16[592,256]{1,0:T(8,128)(2,1)}, bf16[592,256]{1,0:T(8,128)(2,1)S(1)}, u32[]{:S(2)}, u32[]{:S(2)}) collective-permute-start(bf16[592,256]{1,0:T(8,128)(2,1)} %shard_map.140.own_ref), channel_id=1, source_target_pairs={{0,256},{8,264},{16,272},{24,280},{32,288},{40,296},{48,304},{56,3... | collective-permute-start | bytes 909320 | tf_op jit(solution)/shard_map/ppermute | solution.py:332
  51.6 19.1 %collective-permute-start.3 = (bf16[592,256]{1,0:T(8,128)(2,1)}, bf16[592,256]{1,0:T(8,128)(2,1)S(1)}, u32[]{:S(2)}, u32[]{:S(2)}) collective-permute-start(bf16[592,256]{1,0:T(8,128)(2,1)} %shard_map.140.own_ref), channel_id=1, source_target_pairs={{0,8},{8,16},{16,24},{24,32},{32,40},{40,48},{48,56},{56,64},{64,7... | collective-permute-start | bytes 909320 | tf_op jit(solution)/shard_map/ppermute | solution.py:332
  54.2 17.4 %collective-permute-start.4 = (bf16[592,256]{1,0:T(8,128)(2,1)}, bf16[592,256]{1,0:T(8,128)(2,1)S(1)}, u32[]{:S(2)}, u32[]{:S(2)}) collective-permute-start(bf16[592,256]{1,0:T(8,128)(2,1)} %shard_map.140.own_ref), channel_id=1, source_target_pairs={{0,504},{8,0},{16,8},{24,16},{32,24},{40,32},{48,40},{56,48},{64,5... | collective-permute-start | bytes 909320 | tf_op jit(solution)/shard_map/ppermute | solution.py:332
  71.7 1.0 copy-start
  74.2 15.8 %copy-start.1 = (bf16[592,256]{1,0:T(8,128)(2,1)S(1)}, bf16[592,256]{1,0:T(8,128)(2,1)}, u32[]{:S(2)}) copy-start(bf16[592,256]{1,0:T(8,128)(2,1)} %shard_map.140.own_ref) | copy-start | bytes 909316
  74.2 15.8 %copy-start.2 = (bf16[192,1536]{1,0:T(8,128)(2,1)S(1)}, bf16[192,1536]{1,0:T(8,128)(2,1)}, u32[]{:S(2)}) copy-start(bf16[192,1536]{1,0:T(8,128)(2,1)} %w_ref.1) | copy-start | bytes 1769476
  74.4 16.6 %copy-start.3 = (bf16[192,256]{1,0:T(8,128)(2,1)}, bf16[192,256]{1,0:T(8,128)(2,1)S(1)}, u32[]{:S(2)}) copy-start(bf16[192,256]{1,0:T(8,128)(2,1)S(1)} %add_convert_fusion) | copy-start | bytes 294916
  91.0 18.4 %collective-permute-start.6 = (bf16[208,256]{1,0:T(8,128)(2,1)S(1)}, bf16[208,256]{1,0:T(8,128)(2,1)S(1)}, u32[]{:S(2)}, u32[]{:S(2)}) collective-permute-start(bf16[208,256]{1,0:T(8,128)(2,1)S(1)} %shard_map.142.grad_ref), channel_id=1, source_target_pairs={{0,8},{8,16},{16,24},{24,32},{32,40},{40,48},{48,56},{56,64},{64,7... | collective-permute-start | bytes 319496 | tf_op jit(solution)/shard_map/ppermute | solution.py:332
  92.9 16.5 %collective-permute-start.7 = (bf16[208,256]{1,0:T(8,128)(2,1)S(1)}, bf16[208,256]{1,0:T(8,128)(2,1)S(1)}, u32[]{:S(2)}, u32[]{:S(2)}) collective-permute-start(bf16[208,256]{1,0:T(8,128)(2,1)S(1)} %shard_map.142.grad_ref), channel_id=1, source_target_pairs={{0,504},{8,0},{16,8},{24,16},{32,24},{40,32},{48,40},{56,48},{64,5... | collective-permute-start | bytes 319496 | tf_op jit(solution)/shard_map/ppermute | solution.py:332
  100.2 10.5 %collective-permute-start.5 = (bf16[208,256]{1,0:T(8,128)(2,1)S(1)}, bf16[208,256]{1,0:T(8,128)(2,1)S(1)}, u32[]{:S(2)}, u32[]{:S(2)}) collective-permute-start(bf16[208,256]{1,0:T(8,128)(2,1)S(1)} %shard_map.142.grad_ref), channel_id=1, source_target_pairs={{0,256},{8,264},{16,272},{24,280},{32,288},{40,296},{48,304},{56,3... | collective-permute-start | bytes 319496 | tf_op jit(solution)/shard_map/ppermute | solution.py:332

commit v3 on v2

--- a/solution.py
+++ b/solution.py
@@ -50,14 +50,11 @@
     return lax.dot_general(a, b, (((1,), (0,)), ((), ())), preferred_element_type=F32)
 
 
-def pack_body(mask_ref, count_ref, keys_ref, values_ref, queries_ref, out_ref, sems):
+def pack_body(mask_ref, count_ref, keys_ref, values_ref, queries_ref, out_ref):
     columns, rows = keys_ref.shape
-    copies = [
-        pltpu.make_async_copy(ref, out_ref.at[pl.ds(i * columns, columns)], sems.at[i])
-        for i, ref in enumerate((keys_ref, values_ref, queries_ref))
-    ]
-    for copy in copies:
-        copy.start()
+    out_ref[0:columns, :] = keys_ref[...]
+    out_ref[columns : 2 * columns, :] = values_ref[...]
+    out_ref[2 * columns : 3 * columns, :] = queries_ref[...]
     row = lax.broadcasted_iota(jnp.int32, (META, rows), 0)
     first = lax.broadcasted_iota(jnp.int32, (META, rows), 1) < rows // 2
     meta = jnp.where(row == 0, count_ref[0].astype(F32), 0.0)
@@ -69,53 +66,72 @@
                 if j == 0 and qb == kb:
                     bit = jnp.maximum(bit, 1.0)
                 picked.append(bit)
-            meta = jnp.where(row == 1 + 2 * j + kb, jnp.where(first, picked[0], picked[1]), meta)
+            meta = jnp.where(
+                row == 1 + 2 * j + kb, jnp.where(first, picked[0], picked[1]), meta
+            )
     out_ref[3 * columns :, :] = meta.astype(BF16)
-    for copy in copies:
-        copy.wait()
-
-
-def own_conv_body(
-    g_ref, pre_ref, taps_ref, conv_ref, gate_ref, taps_out, x_ref, g_low, pre_low, taps_low, sems
+
+
+def conv_body(
+    columns,
+    before_ref,
+    after_ref,
+    g_ref,
+    pre_ref,
+    taps_ref,
+    w_ref,
+    out_ref,
+    x_ref,
+    moved_ref,
+    g_low,
+    pre_low,
+    taps_low,
+    w_low,
+    sum_ref,
+    low_ref,
+    sems,
 ):
-    columns, rows = g_ref.shape
     copies = [
         pltpu.make_async_copy(g_ref, g_low, sems.at[0]),
         pltpu.make_async_copy(taps_ref, taps_low, sems.at[1]),
         pltpu.make_async_copy(pre_ref, pre_low, sems.at[2]),
+        pltpu.make_async_copy(w_ref, w_low, sems.at[3]),
     ]
     for copy in copies:
         copy.start()
-    x_ref[:, 0:LANES] = jnp.zeros((columns, LANES), F32)
-    x_ref[:, LANES + rows :] = jnp.zeros((columns, LANES), F32)
-    for copy in copies:
-        copy.wait()
-    x_ref[:, LANES : LANES + rows] = g_low[...].astype(F32)
-    taps = jnp.concatenate([taps_low[...], jnp.zeros((LANES - KW, columns), F32)], axis=0)
-    taps_out[...] = taps.T
+    rows = g_ref.shape[1]
+    pad = 16
+    x_ref[0:pad, :] = before_ref[:, rows - LANES :].astype(F32).T[LANES - pad :, :]
+    x_ref[pad + rows :, :] = after_ref[:, :LANES].astype(F32).T[:pad, :]
+    copies[0].wait()
+    copies[1].wait()
+    x_ref[pad : pad + rows, :] = g_low[...].astype(F32).T
+    for shift in range(8):
+        moved_ref[shift] = x_ref[shift : shift + rows + 24, :]
     step = 32
 
     def block(i, carry):
-        at = pl.ds(pl.multiple_of(i * step, step), step)
-        x = x_ref[at, :]
-        wide = x.shape[1]
-        moved = [pltpu.roll(x, (16 - 8 * a) % wide, 1)[:, LANES:] for a in range(4)]
-        acc = jnp.zeros((step, wide - LANES), F32)
-        for b in range(8):
-            part = 0.0
-            for a in range(4):
-                k = 31 - 8 * a - b
-                if k < KW:
-                    part = part + taps_out[at, k : k + 1] * moved[a]
-            acc = acc + (pltpu.roll(part, wide - LANES - b, 1) if b else part)
-        conv_ref[at, :] = acc[:, :rows]
-        value = pre_low[0, at, :].astype(F32)
-        gate = jax.nn.sigmoid(pre_low[1, at, :].astype(F32))
-        gate_ref[0, at, :] = gate
-        gate_ref[1, at, :] = value * gate * (1.0 - gate)
+        at = pl.multiple_of(i * step, step)
+        acc = jnp.zeros((step, columns), F32)
+        for k in range(KW):
+            a, shift = divmod(31 - k, 8)
+            acc = acc + taps_low[k : k + 1, :] * moved_ref[shift, pl.ds(at + 8 * a, step), :]
+        sum_ref[pl.ds(at, step), :] = acc
         return carry
 
-    lax.fori_loop(0, columns // step, block, 0)
+    lax.fori_loop(0, rows // step, block, 0)
+    grad = sum_ref[...].T
+    copies[2].wait()
+    value = pre_low[0].astype(F32)
+    gate = jax.nn.sigmoid(pre_low[1].astype(F32))
+    low_ref[0:columns, :] = (grad * gate).astype(BF16)
+    low_ref[columns:, :] = (grad * value * gate * (1.0 - gate)).astype(BF16)
+    copies[3].wait()
+    low = low_ref[...].T
+    model = w_ref.shape[1]
+    chunk = 256 if model % 256 == 0 else LANES
+    for at in range(0, model, chunk):
+        out_ref[at : at + chunk, :] = dot_nn(low, w_low[:, at : at + chunk]).astype(BF16).T
 
 
 def meta_of(ref, columns):
@@ -141,46 +157,6 @@
             jnp.where(index < limit_rows[kb], scores[kb * half : (kb + 1) * half], NEG)
         )
     return jnp.concatenate(parts, axis=0)
-
-
-def edge_body(
-    columns,
-    before_ref,
-    after_ref,
-    conv_ref,
-    gate_ref,
-    taps_ref,
-    w_ref,
-    out_ref,
-    low_ref,
-    w_low,
-    sem,
-):
-    copy = pltpu.make_async_copy(w_ref, w_low, sem)
-    copy.start()
-    rows = conv_ref.shape[1]
-    step = 64
-    for at in range(0, columns, step):
-        here = slice(at, at + step)
-        lane = lax.broadcasted_iota(jnp.int32, (step, LANES), 1)
-        before = jnp.where(lane >= LANES - HALF, before_ref[here, rows - LANES :].astype(F32), 0.0)
-        after = jnp.where(lane < HALF, after_ref[here, :LANES].astype(F32), 0.0)
-        left = jnp.zeros((step, LANES), F32)
-        right = jnp.zeros((step, LANES), F32)
-        for m in range(1, HALF + 1):
-            left = left + taps_ref[here, HALF + m : HALF + m + 1] * pltpu.roll(before, m, 1)
-            right = right + taps_ref[here, HALF - m : HALF - m + 1] * pltpu.roll(after, LANES - m, 1)
-        left = jnp.where(lane < HALF, left, 0.0)
-        right = jnp.where(lane >= LANES - HALF, right, 0.0)
-        grad = conv_ref[here, :] + jnp.concatenate([left, right], axis=1)
-        low_ref[here, :] = (grad * gate_ref[0, here, :]).astype(BF16)
-        low_ref[columns + at : columns + at + step, :] = (grad * gate_ref[1, here, :]).astype(BF16)
-    copy.wait()
-    model = w_ref.shape[1]
-    chunk = 256 if model % 256 == 0 else LANES
-    low = low_ref[...]
-    for at in range(0, model, chunk):
-        out_ref[at : at + chunk, :] = dot_tn(w_low[:, at : at + chunk], low).astype(BF16)
 
 
 def softmax_of(refs, own_meta, columns, links, h, top):
@@ -352,52 +328,39 @@
         pack_body,
         shape((message, row_count), BF16),
         (block_mask, counts, keys, values, queries),
-        [SMEM] * 2 + [HBM] * 3,
+        [SMEM] * 2 + [VMEM] * 3,
         0,
         4 * message * row_count,
-        0,
-        (pltpu.SemaphoreType.DMA((3,)),),
-        mib=BIG,
     )
     offsets = [0, 1, -1, spans // 2]
-    far = shifted(own, offsets[3])
-    conv, gate, taps = call(
-        own_conv_body,
-        (shape(flat, F32), shape((2,) + flat, F32), shape((columns, LANES), F32)),
-        (g_conv, pre, kernel),
-        [HBM] * 3,
-        2 * KW * columns * row_count,
-        20 * columns * row_count,
+    point_grad = call(
+        functools.partial(conv_body, columns),
+        shape((model, row_count), BF16),
+        (before, after, g_conv, pre, kernel, w_point.reshape(2 * columns, model)),
+        [VMEM] * 2 + [HBM] * 4,
+        4 * columns * model * row_count,
+        4 * columns * model,
         columns * row_count,
         (
-            pltpu.VMEM((columns, row_count + 2 * LANES), F32),
+            pltpu.VMEM((row_count + 32, columns), F32),
+            pltpu.VMEM((8, row_count + 24, columns), F32),
             pltpu.VMEM(flat, BF16),
             pltpu.VMEM((2,) + flat, BF16),
             pltpu.VMEM((KW, columns), F32),
-            pltpu.SemaphoreType.DMA((3,)),
+            pltpu.VMEM((2 * columns, model), BF16),
+            pltpu.VMEM((row_count, columns), F32),
+            pltpu.VMEM((2 * columns, row_count), BF16),
+            pltpu.SemaphoreType.DMA((4,)),
         ),
         mib=BIG,
     )
-    point_grad = call(
-        functools.partial(edge_body, columns),
-        shape((model, row_count), BF16),
-        (before, after, conv, gate, taps, w_point.reshape(2 * columns, model)),
-        [VMEM] * 5 + [HBM],
-        4 * columns * model * row_count,
-        4 * columns * model,
-        0,
-        (
-            pltpu.VMEM((2 * columns, row_count), BF16),
-            pltpu.VMEM((2 * columns, model), BF16),
-            pltpu.SemaphoreType.DMA,
-        ),
-        mib=BIG,
-    )
     parts = lax.all_to_all(
         point_grad.reshape(groups, columns, row_count), "head", 0, 0, tiled=False
     )
-    later, far, _ = lax.optimization_barrier((own, far, point_grad))
-    one, two = [shifted(later, offset) for offset in offsets[1:3]]
+    own, _ = lax.optimization_barrier((own, point_grad))
+    one, two = [shifted(own, offset) for offset in offsets[1:3]]
+    later, one, two = lax.optimization_barrier((own, one, two))
+    far = shifted(later, offsets[3])
     soft = call(
         functools.partial(softmax_body, columns),
         shape((columns + 8, row_count), F32),

time: 114 us -> 92.8 us (0.81); the launches traced: 112 us -> 92.3 us
  Pallas kernels: 23.2 us -> 14.4 us
  starting transfers between devices: 55 us -> 46.7 us
  local copies, waits for them, and re-layouts: 2.33 us -> 0.78 us
    ppermute x6, starting transfers between devices: 42 us -> 33.2 us  [shifted(): return lax.ppermute(value, 'ctx', pairs)]
    pallas_call x8 -> x7, Pallas kernels: 23.2 us -> 14.4 us  [call(): pl.pallas_call(body, out_shape=out_shapes, in_specs=specs, out_specs=jax....]
    ppermute x6, waiting for transfers between devices: 14.6 us -> 9.06 us  [shifted(): return lax.ppermute(value, 'ctx', pairs)]
    ppermute x1, waiting for transfers between devices: 0.01 us -> 4.27 us  [per_device(): after = lax.ppermute(g_conv, 'ctx', [(j, i) for i, j in up])]
    unnamed x17 -> x19, local copies, waits for them, and re-layouts: 2.33 us -> 0.78 us
  transfers between devices with their start and end apart: 9 -> 9, of which waited for: 3 -> 5; matrix products, arithmetic and copies ran while one was open for 1% -> 0% of each run, Pallas kernels for 14% -> 8%
where the time goes in v3:
time: 92.8 us; the launch traced here: 92.3 us
  starting transfers between devices  46.7 us (50%)
  blocking collectives  14.8 us (16%)
  Pallas kernels  14.4 us (16%)
  waiting for transfers between devices  14 us (15%)
  between operations  1.5 us (2%)
    ppermute x6, starting transfers between devices, shifted(): return lax.ppermute(value, 'ctx', pairs)  33.2 us
    all_gather x1, blocking collectives, per_device(): stream_full = lax.all_gather(stream_grad, 'head', axis=0, tiled=True)  14.8 us
    pallas_call x7, Pallas kernels, call(): pl.pallas_call(body, out_shape=out_shapes, in_specs=specs, out_specs=jax....  14.4 us
    ppermute x6, waiting for transfers between devices, shifted(): return lax.ppermute(value, 'ctx', pairs)  9.06 us
    all_to_all x1, starting transfers between devices, per_device(): lax.all_to_all(point_grad.reshape(groups, columns, row_count), 'head', 0,...  7.45 us
    ppermute x1, starting transfers between devices, per_device(): before = lax.ppermute(g_conv, 'ctx', up)  4.83 us
    ppermute x1, waiting for transfers between devices, per_device(): after = lax.ppermute(g_conv, 'ctx', [(j, i) for i, j in up])  4.27 us
  transfers between devices with their start and end apart: 9, of which 5 were waited for; matrix products, arithmetic and copies ran while one was open for 0% of the time, Pallas kernels for 8%

profile of v3, /device:TPU:1, one launch (start us, length us, event | category | flops | bytes accessed | tf_op | source)
XLA Modules:
  0.0 92.3 jit_solution(8770648327623061348)
XLA Ops:
  0.6 4.8 %collective-permute-start = (bf16[192,256]{1,0:T(8,128)(2,1)}, bf16[192,256]{1,0:T(8,128)(2,1)S(1)}, u32[]{:S(2)}, u32[]{:S(2)}) collective-permute-start(bf16[192,256]{1,0:T(8,128)(2,1)} %g_ref.1), channel_id=1, source_target_pairs={{0,8},{8,16},{16,24},{24,32},{32,40},{40,48},{48,56},{56,64},{64,7... | collective-permute-start | bytes 294920 | tf_op jit(solution)/shard_map/ppermute | solution.py:324
  5.5 1.3 %collective-permute-start.1 = (bf16[192,256]{1,0:T(8,128)(2,1)}, bf16[192,256]{1,0:T(8,128)(2,1)S(1)}, u32[]{:S(2)}, u32[]{:S(2)}) collective-permute-start(bf16[192,256]{1,0:T(8,128)(2,1)} %g_ref.1), channel_id=1, source_target_pairs={{8,0},{16,8},{24,16},{32,24},{40,32},{48,40},{56,48},{64,56},{72,6... | collective-permute-start | bytes 294920 | tf_op jit(solution)/shard_map/ppermute | solution.py:325
  6.8 0.6 collective-permute-done.before_ref
  7.4 4.3 %collective-permute-done.1.after_ref = bf16[192,256]{1,0:T(8,128)(2,1)S(1)} collective-permute-done((bf16[192,256]{1,0:T(8,128)(2,1)}, bf16[192,256]{1,0:T(8,128)(2,1)S(1)}, u32[]{:S(2)}, u32[]{:S(2)}) %collective-permute-start.1) | collective-permute-done | bytes 98336 | tf_op jit(solution)/shard_map/ppermute | solution.py:325
  11.7 0.6 copy-done.6
  12.3 4.9 %shard_map.138 = bf16[1536,256]{1,0:T(8,128)(2,1)} custom-call(bf16[192,256]{1,0:T(8,128)(2,1)} %copy-done.5, bf16[192,256]{1,0:T(8,128)(2,1)} %copy-done.6, bf16[192,256]{1,0:T(8,128)(2,1)} %g_ref.1, bf16[2,192,256]{2,1,0:T(8,128)(2,1)} %pre_ref.1, f32[31,192]{1,0:T(8,128)} %taps_ref.1, bf16[384,1536]{1,0:T(8,128)(2,1)} %bitcast.13), custom_call_target="tpu_custom_call" | custom-call | flops 301989888 | bytes 1179648 | tf_op jit(solution)/shard_map/pallas_call | solution.py:30
  17.2 0.0 copy-start.8
  17.2 0.0 copy-start.1
  17.2 0.0 copy-start.2
  17.3 0.0 copy-start.3
  17.3 7.4 %all-to-all-start = ((bf16[8,192,256]{2,1,0:T(8,128)(2,1)}), bf16[8,192,256]{2,1,0:T(8,128)(2,1)S(1)}, u32[]{:S(2)}, u32[]{:S(2)}) async-start(bf16[8,192,256]{2,1,0:T(8,128)(2,1)} %bitcast.12), calls=%async_computation | async-start | bytes 1572864 | tf_op jit(solution)/shard_map/all_to_all | solution.py:357
  24.7 0.1 copy.15.mask_ref
  25.5 0.6 shard_map.139.own_ref
  26.1 0.0 copy-start.7
  26.1 3.0 %collective-permute-start.2 = (bf16[592,256]{1,0:T(8,128)(2,1)S(1)}, bf16[592,256]{1,0:T(8,128)(2,1)S(1)}, u32[]{:S(2)}, u32[]{:S(2)}) collective-permute-start(bf16[592,256]{1,0:T(8,128)(2,1)S(1)} %shard_map.139.own_ref), channel_id=1, source_target_pairs={{0,8},{8,16},{16,24},{24,32},{32,40},{40,48},{48,56},{56,64},{64,7... | collective-permute-start | bytes 909320 | tf_op jit(solution)/shard_map/ppermute | solution.py:308
  29.1 8.5 %collective-permute-start.3 = (bf16[592,256]{1,0:T(8,128)(2,1)S(1)}, bf16[592,256]{1,0:T(8,128)(2,1)S(1)}, u32[]{:S(2)}, u32[]{:S(2)}) collective-permute-start(bf16[592,256]{1,0:T(8,128)(2,1)S(1)} %shard_map.139.own_ref), channel_id=1, source_target_pairs={{0,504},{8,0},{16,8},{24,16},{32,24},{40,32},{48,40},{56,48},{64,5... | collective-permute-start | bytes 909320 | tf_op jit(solution)/shard_map/ppermute | solution.py:308
  37.6 5.6 %collective-permute-done.2.one_ref = bf16[592,256]{1,0:T(8,128)(2,1)S(1)} collective-permute-done((bf16[592,256]{1,0:T(8,128)(2,1)S(1)}, bf16[592,256]{1,0:T(8,128)(2,1)S(1)}, u32[]{:S(2)}, u32[]{:S(2)}) %collective-permute-start.2) | collective-permute-done | bytes 303136 | tf_op jit(solution)/shard_map/ppermute | solution.py:308
  43.2 1.0 %collective-permute-done.3.two_ref = bf16[592,256]{1,0:T(8,128)(2,1)S(1)} collective-permute-done((bf16[592,256]{1,0:T(8,128)(2,1)S(1)}, bf16[592,256]{1,0:T(8,128)(2,1)S(1)}, u32[]{:S(2)}, u32[]{:S(2)}) %collective-permute-start.3) | collective-permute-done | bytes 303136 | tf_op jit(solution)/shard_map/ppermute | solution.py:308
  44.2 8.0 %collective-permute-start.4 = (bf16[592,256]{1,0:T(8,128)(2,1)S(1)}, bf16[592,256]{1,0:T(8,128)(2,1)S(1)}, u32[]{:S(2)}, u32[]{:S(2)}) collective-permute-start(bf16[592,256]{1,0:T(8,128)(2,1)S(1)} %shard_map.139.own_ref), channel_id=1, source_target_pairs={{0,256},{8,264},{16,272},{24,280},{32,288},{40,296},{48,304},{56,3... | collective-permute-start | bytes 909320 | tf_op jit(solution)/shard_map/ppermute | solution.py:308
  52.2 1.5 %shard_map.140.soft_ref = f32[200,256]{1,0:T(8,128)S(1)} custom-call(bf16[592,256]{1,0:T(8,128)(2,1)S(1)} %shard_map.139.own_ref, bf16[592,256]{1,0:T(8,128)(2,1)S(1)} %collective-permute-done.2.one_ref, bf16[592,256]{1,0:T(8,128)(2,1)S(1)} %collective-permute-done.3.two_ref), custom_call_target="tpu_custom_call" | custom-call | flops 150994944 | bytes 909312 | tf_op jit(solution)/shard_map/pallas_call | solution.py:30
  53.8 0.0 copy-start
  53.8 0.1 convert_reduce_fusion
  54.0 0.0 copy-start.4
  54.0 14.8 %all_gather.3.stream_ref = bf16[1536,256]{1,0:T(8,128)(2,1)S(1)} all-gather(bf16[192,256]{1,0:T(8,128)(2,1)S(1)} %add_convert_fusion), channel_id=1, replica_groups=mesh['ctx'=64,'head'=8] {'head'}, dimensions={0}, use_global_device_ids=true | all-gather | bytes 884736 | tf_op jit(solution)/shard_map/all_gather | solution.py:375
  68.8 1.0 %shard_map.141.grad_ref = bf16[208,256]{1,0:T(8,128)(2,1)S(1)} custom-call(bf16[192,1536]{1,0:T(8,128)(2,1)S(1)} %copy-done, bf16[1536,256]{1,0:T(8,128)(2,1)S(1)} %all_gather.3.stream_ref, bf16[592,256]{1,0:T(8,128)(2,1)S(1)} %shard_map.139.own_ref, bf16[592,256]{1,0:T(8,128)(2,1)S(1)} %collective-permute-done.4.far_ref, f32[200,256]{1,0:T(8,128)S(1)} %shard_map.140.soft_ref), custom_call_target="tpu_custom_call" | custom-call | flops 201326592 | bytes 1376256 | tf_op jit(solution)/shard_map/pallas_call | solution.py:30
  69.8 1.9 %collective-permute-start.6 = (bf16[208,256]{1,0:T(8,128)(2,1)S(1)}, bf16[208,256]{1,0:T(8,128)(2,1)S(1)}, u32[]{:S(2)}, u32[]{:S(2)}) collective-permute-start(bf16[208,256]{1,0:T(8,128)(2,1)S(1)} %shard_map.141.grad_ref), channel_id=1, source_target_pairs={{0,8},{8,16},{16,24},{24,32},{32,40},{40,48},{48,56},{56,64},{64,7... | collective-permute-start | bytes 319496 | tf_op jit(solution)/shard_map/ppermute | solution.py:308
  71.7 7.4 %collective-permute-start.7 = (bf16[208,256]{1,0:T(8,128)(2,1)S(1)}, bf16[208,256]{1,0:T(8,128)(2,1)S(1)}, u32[]{:S(2)}, u32[]{:S(2)}) collective-permute-start(bf16[208,256]{1,0:T(8,128)(2,1)S(1)} %shard_map.141.grad_ref), channel_id=1, source_target_pairs={{0,504},{8,0},{16,8},{24,16},{32,24},{40,32},{48,40},{56,48},{64,5... | collective-permute-start | bytes 319496 | tf_op jit(solution)/shard_map/ppermute | solution.py:308
  79.1 4.4 %collective-permute-start.5 = (bf16[208,256]{1,0:T(8,128)(2,1)S(1)}, bf16[208,256]{1,0:T(8,128)(2,1)S(1)}, u32[]{:S(2)}, u32[]{:S(2)}) collective-permute-start(bf16[208,256]{1,0:T(8,128)(2,1)S(1)} %shard_map.141.grad_ref), channel_id=1, source_target_pairs={{0,256},{8,264},{16,272},{24,280},{32,288},{40,296},{48,304},{56,3... | collective-permute-start | bytes 319496 | tf_op jit(solution)/shard_map/ppermute | solution.py:308
  83.5 3.4 %shard_map.142 = (bf16[192,256]{1,0:T(8,128)(2,1)}, f32[384,256]{1,0:T(8,128)S(1)}) custom-call(bf16[592,256]{1,0:T(8,128)(2,1)S(1)} %shard_map.139.own_ref, bf16[592,256]{1,0:T(8,128)(2,1)S(1)} %collective-permute-done.2.one_ref, bf16[592,256]{1,0:T(8,128)(2,1)S(1)} %collective-permute-done.3.two_ref, bf16[592,256]{1,0:T(8,128)(2,1)S(1)} %collective-permute-done.4.far_ref, ...), custom_call_target="tpu_custom_call" | custom-call | flops 301989888 | bytes 1212416 | tf_op jit(solution)/shard_map/pallas_call | solution.py:30
  86.9 1.3 %shard_map.143.acc_ref = f32[384,256]{1,0:T(8,128)S(1)} custom-call(bf16[592,256]{1,0:T(8,128)(2,1)S(1)} %shard_map.139.own_ref, bf16[592,256]{1,0:T(8,128)(2,1)S(1)} %collective-permute-done.2.one_ref, bf16[592,256]{1,0:T(8,128)(2,1)S(1)} %collective-permute-done.3.two_ref, bf16[208,256]{1,0:T(8,128)(2,1)S(1)} %collective-permute-done.6.grad_one_ref, ...), custom_call_target="tpu_custom_call" | custom-call | flops 201326592 | bytes 1212416 | tf_op jit(solution)/shard_map/pallas_call | solution.py:30
  88.3 2.5 %collective-permute-done.5.grad_far_ref = bf16[208,256]{1,0:T(8,128)(2,1)S(1)} collective-permute-done((bf16[208,256]{1,0:T(8,128)(2,1)S(1)}, bf16[208,256]{1,0:T(8,128)(2,1)S(1)}, u32[]{:S(2)}, u32[]{:S(2)}) %collective-permute-start.5) | collective-permute-done | bytes 106528 | tf_op jit(solution)/shard_map/ppermute | solution.py:308
  90.7 1.6 %shard_map.144 = (bf16[192,256]{1,0:T(8,128)(2,1)}, bf16[192,256]{1,0:T(8,128)(2,1)}) custom-call(bf16[592,256]{1,0:T(8,128)(2,1)S(1)} %shard_map.139.own_ref, bf16[592,256]{1,0:T(8,128)(2,1)S(1)} %collective-permute-done.4.far_ref, bf16[208,256]{1,0:T(8,128)(2,1)S(1)} %collective-permute-done.5.grad_far_ref, f32[384,256]{1,0:T(8,128)S(1)} %shard_map.143.acc_ref), custom_call_target="tpu_custom_call" | custom-call | flops 100663296 | bytes 1212416 | tf_op jit(solution)/shard_map/pallas_call | solution.py:30
  (15 shorter events, 0.1 us)
Async XLA Ops:
  0.6 6.8 %collective-permute-start = (bf16[192,256]{1,0:T(8,128)(2,1)}, bf16[192,256]{1,0:T(8,128)(2,1)S(1)}, u32[]{:S(2)}, u32[]{:S(2)}) collective-permute-start(bf16[192,256]{1,0:T(8,128)(2,1)} %g_ref.1), channel_id=1, source_target_pairs={{0,8},{8,16},{16,24},{24,32},{32,40},{40,48},{48,56},{56,64},{64,7... | collective-permute-start | bytes 294920 | tf_op jit(solution)/shard_map/ppermute | solution.py:324
  5.5 6.2 %collective-permute-start.1 = (bf16[192,256]{1,0:T(8,128)(2,1)}, bf16[192,256]{1,0:T(8,128)(2,1)S(1)}, u32[]{:S(2)}, u32[]{:S(2)}) collective-permute-start(bf16[192,256]{1,0:T(8,128)(2,1)} %g_ref.1), channel_id=1, source_target_pairs={{8,0},{16,8},{24,16},{32,24},{40,32},{48,40},{56,48},{64,56},{72,6... | collective-permute-start | bytes 294920 | tf_op jit(solution)/shard_map/ppermute | solution.py:325
  7.4 4.3 %copy-start.5 = (bf16[192,256]{1,0:T(8,128)(2,1)}, bf16[192,256]{1,0:T(8,128)(2,1)S(1)}, u32[]{:S(2)}) copy-start(bf16[192,256]{1,0:T(8,128)(2,1)S(1)} %collective-permute-done.before_ref) | copy-start | bytes 294916
  11.7 0.6 copy-start.6
  17.2 7.5 %copy-start.8 = (s32[2,4,2]{1,2,0:T(2,128)S(1)}, s32[2,4,2]{1,2,0:T(2,128)}, u32[]{:S(2)}) copy-start(s32[2,4,2]{1,2,0:T(2,128)} %param.20) | copy-start | bytes 196
  17.2 8.2 %copy-start.1 = (bf16[256,192]{0,1:T(8,128)(2,1)S(1)}, bf16[256,192]{0,1:T(8,128)(2,1)}, u32[]{:S(2)}) copy-start(bf16[256,192]{0,1:T(8,128)(2,1)} %param.18) | copy-start | bytes 294916
  17.2 8.2 %copy-start.2 = (bf16[256,192]{0,1:T(8,128)(2,1)S(1)}, bf16[256,192]{0,1:T(8,128)(2,1)}, u32[]{:S(2)}) copy-start(bf16[256,192]{0,1:T(8,128)(2,1)} %param.19) | copy-start | bytes 294916
  17.3 8.2 %copy-start.3 = (bf16[256,192]{0,1:T(8,128)(2,1)S(1)}, bf16[256,192]{0,1:T(8,128)(2,1)}, u32[]{:S(2)}) copy-start(bf16[256,192]{0,1:T(8,128)(2,1)} %param.17) | copy-start | bytes 294916
  17.3 36.5 %all-to-all-start = ((bf16[8,192,256]{2,1,0:T(8,128)(2,1)}), bf16[8,192,256]{2,1,0:T(8,128)(2,1)S(1)}, u32[]{:S(2)}, u32[]{:S(2)}) async-start(bf16[8,192,256]{2,1,0:T(8,128)(2,1)} %bitcast.12), calls=%async_computation | async-start | bytes 1572864 | tf_op jit(solution)/shard_map/all_to_all | solution.py:357
  26.1 27.8 %copy-start.7 = (bf16[192,256]{1,0:T(8,128)(2,1)S(1)}, bf16[192,256]{1,0:T(8,128)(2,1)}, u32[]{:S(2)}) copy-start(bf16[192,256]{1,0:T(8,128)(2,1)} %param.15) | copy-start | bytes 294916
  26.1 17.1 %collective-permute-start.2 = (bf16[592,256]{1,0:T(8,128)(2,1)S(1)}, bf16[592,256]{1,0:T(8,128)(2,1)S(1)}, u32[]{:S(2)}, u32[]{:S(2)}) collective-permute-start(bf16[592,256]{1,0:T(8,128)(2,1)S(1)} %shard_map.139.own_ref), channel_id=1, source_target_pairs={{0,8},{8,16},{16,24},{24,32},{32,40},{40,48},{48,56},{56,64},{64,7... | collective-permute-start | bytes 909320 | tf_op jit(solution)/shard_map/ppermute | solution.py:308
  29.1 15.1 %collective-permute-start.3 = (bf16[592,256]{1,0:T(8,128)(2,1)S(1)}, bf16[592,256]{1,0:T(8,128)(2,1)S(1)}, u32[]{:S(2)}, u32[]{:S(2)}) collective-permute-start(bf16[592,256]{1,0:T(8,128)(2,1)S(1)} %shard_map.139.own_ref), channel_id=1, source_target_pairs={{0,504},{8,0},{16,8},{24,16},{32,24},{40,32},{48,40},{56,48},{64,5... | collective-permute-start | bytes 909320 | tf_op jit(solution)/shard_map/ppermute | solution.py:308
  44.2 24.6 %collective-permute-start.4 = (bf16[592,256]{1,0:T(8,128)(2,1)S(1)}, bf16[592,256]{1,0:T(8,128)(2,1)S(1)}, u32[]{:S(2)}, u32[]{:S(2)}) collective-permute-start(bf16[592,256]{1,0:T(8,128)(2,1)S(1)} %shard_map.139.own_ref), channel_id=1, source_target_pairs={{0,256},{8,264},{16,272},{24,280},{32,288},{40,296},{48,304},{56,3... | collective-permute-start | bytes 909320 | tf_op jit(solution)/shard_map/ppermute | solution.py:308
  53.8 15.0 %copy-start = (bf16[192,1536]{1,0:T(8,128)(2,1)S(1)}, bf16[192,1536]{1,0:T(8,128)(2,1)}, u32[]{:S(2)}) copy-start(bf16[192,1536]{1,0:T(8,128)(2,1)} %w_ref.1) | copy-start | bytes 1769476
  54.0 15.8 %copy-start.4 = (bf16[192,256]{1,0:T(8,128)(2,1)}, bf16[192,256]{1,0:T(8,128)(2,1)S(1)}, u32[]{:S(2)}) copy-start(bf16[192,256]{1,0:T(8,128)(2,1)S(1)} %add_convert_fusion) | copy-start | bytes 294916
  69.8 17.2 %collective-permute-start.6 = (bf16[208,256]{1,0:T(8,128)(2,1)S(1)}, bf16[208,256]{1,0:T(8,128)(2,1)S(1)}, u32[]{:S(2)}, u32[]{:S(2)}) collective-permute-start(bf16[208,256]{1,0:T(8,128)(2,1)S(1)} %shard_map.141.grad_ref), channel_id=1, source_target_pairs={{0,8},{8,16},{16,24},{24,32},{32,40},{40,48},{48,56},{56,64},{64,7... | collective-permute-start | bytes 319496 | tf_op jit(solution)/shard_map/ppermute | solution.py:308
  71.7 15.2 %collective-permute-start.7 = (bf16[208,256]{1,0:T(8,128)(2,1)S(1)}, bf16[208,256]{1,0:T(8,128)(2,1)S(1)}, u32[]{:S(2)}, u32[]{:S(2)}) collective-permute-start(bf16[208,256]{1,0:T(8,128)(2,1)S(1)} %shard_map.141.grad_ref), channel_id=1, source_target_pairs={{0,504},{8,0},{16,8},{24,16},{32,24},{40,32},{48,40},{56,48},{64,5... | collective-permute-start | bytes 319496 | tf_op jit(solution)/shard_map/ppermute | solution.py:308
  79.1 11.6 %collective-permute-start.5 = (bf16[208,256]{1,0:T(8,128)(2,1)S(1)}, bf16[208,256]{1,0:T(8,128)(2,1)S(1)}, u32[]{:S(2)}, u32[]{:S(2)}) collective-permute-start(bf16[208,256]{1,0:T(8,128)(2,1)S(1)} %shard_map.141.grad_ref), channel_id=1, source_target_pairs={{0,256},{8,264},{16,272},{24,280},{32,288},{40,296},{48,304},{56,3... | collective-permute-start | bytes 319496 | tf_op jit(solution)/shard_map/ppermute | solution.py:308

commit v4 on v3

--- a/solution.py
+++ b/solution.py
@@ -15,6 +15,7 @@
 LANES = 128
 META = 16
 BIG = 58
+PAD = 16
 NEG = -1e30
 SCALE = 1.0 / math.sqrt(HEAD_DIM)
 SCALE2 = SCALE * math.log2(math.e)
@@ -72,23 +73,20 @@
     out_ref[3 * columns :, :] = meta.astype(BF16)
 
 
-def conv_body(
-    columns,
-    before_ref,
-    after_ref,
+def own_conv_body(
     g_ref,
     pre_ref,
     taps_ref,
     w_ref,
-    out_ref,
+    sum_out,
+    gate_out,
+    w_out,
     x_ref,
     moved_ref,
     g_low,
     pre_low,
     taps_low,
     w_low,
-    sum_ref,
-    low_ref,
     sems,
 ):
     copies = [
@@ -99,13 +97,12 @@
     ]
     for copy in copies:
         copy.start()
-    rows = g_ref.shape[1]
-    pad = 16
-    x_ref[0:pad, :] = before_ref[:, rows - LANES :].astype(F32).T[LANES - pad :, :]
-    x_ref[pad + rows :, :] = after_ref[:, :LANES].astype(F32).T[:pad, :]
+    columns, rows = g_ref.shape
+    x_ref[0:PAD, :] = jnp.zeros((PAD, columns), F32)
+    x_ref[PAD + rows :, :] = jnp.zeros((PAD, columns), F32)
     copies[0].wait()
     copies[1].wait()
-    x_ref[pad : pad + rows, :] = g_low[...].astype(F32).T
+    x_ref[PAD : PAD + rows, :] = g_low[...].astype(F32).T
     for shift in range(8):
         moved_ref[shift] = x_ref[shift : shift + rows + 24, :]
     step = 32
@@ -114,24 +111,46 @@
         at = pl.multiple_of(i * step, step)
         acc = jnp.zeros((step, columns), F32)
         for k in range(KW):
-            a, shift = divmod(31 - k, 8)
+            a, shift = divmod(PAD + HALF - k, 8)
             acc = acc + taps_low[k : k + 1, :] * moved_ref[shift, pl.ds(at + 8 * a, step), :]
-        sum_ref[pl.ds(at, step), :] = acc
+        sum_out[pl.ds(at, step), :] = acc
         return carry
 
     lax.fori_loop(0, rows // step, block, 0)
-    grad = sum_ref[...].T
     copies[2].wait()
     value = pre_low[0].astype(F32)
     gate = jax.nn.sigmoid(pre_low[1].astype(F32))
-    low_ref[0:columns, :] = (grad * gate).astype(BF16)
-    low_ref[columns:, :] = (grad * value * gate * (1.0 - gate)).astype(BF16)
+    gate_out[0] = gate.T
+    gate_out[1] = (value * gate * (1.0 - gate)).T
     copies[3].wait()
-    low = low_ref[...].T
+    for half in range(2):
+        for at in range(0, w_ref.shape[2], LANES):
+            w_out[half, at : at + LANES, :] = w_low[half, :, at : at + LANES].T
+
+
+def edge_body(before_ref, after_ref, sum_ref, gate_ref, taps_ref, w_ref, out_ref, head, tail):
+    rows, columns = sum_ref.shape
+    blank = jnp.zeros((PAD, columns), F32)
+    head[0:PAD, :] = before_ref[:, rows - LANES :].astype(F32).T[LANES - PAD :, :]
+    head[PAD:, :] = blank
+    tail[0:PAD, :] = blank
+    tail[PAD:, :] = after_ref[:, :LANES].astype(F32).T[:PAD, :]
+    first, last = blank, blank
+    for d in range(1, HALF + 1):
+        first = first + taps_ref[HALF + d : HALF + d + 1, :] * head[PAD - d : 2 * PAD - d, :]
+        last = last + taps_ref[HALF - d : HALF - d + 1, :] * tail[d : PAD + d, :]
+    grad = jnp.concatenate(
+        [sum_ref[0:PAD, :] + first, sum_ref[PAD : rows - PAD, :], sum_ref[rows - PAD :, :] + last],
+        axis=0,
+    )
+    low = [(grad * gate_ref[half]).astype(BF16) for half in range(2)]
     model = w_ref.shape[1]
     chunk = 256 if model % 256 == 0 else LANES
     for at in range(0, model, chunk):
-        out_ref[at : at + chunk, :] = dot_nn(low, w_low[:, at : at + chunk]).astype(BF16).T
+        here = slice(at, at + chunk)
+        out_ref[here, :] = (
+            dot_nt(w_ref[0, here, :], low[0]) + dot_nt(w_ref[1, here, :], low[1])
+        ).astype(BF16)
 
 
 def meta_of(ref, columns):
@@ -159,37 +178,6 @@
     return jnp.concatenate(parts, axis=0)
 
 
-def softmax_of(refs, own_meta, columns, links, h, top):
-    lo, hi = h * HEAD_DIM, (h + 1) * HEAD_DIM
-    query = refs[0][2 * columns + lo : 2 * columns + hi, :]
-    scores = []
-    for ref, link in zip(refs[1:], links):
-        limit = limits(own_meta, meta_of(ref, columns)[0:1], link)
-        scores.append(masked(dot_tn(ref[lo:hi, :], query) * SCALE2, limit))
-    top = functools.reduce(jnp.maximum, [jnp.max(s, axis=0, keepdims=True) for s in scores], top)
-    total = jnp.zeros_like(top)
-    mixed = jnp.zeros((HEAD_DIM, top.shape[1]), F32)
-    for ref, score in zip(refs[1:], scores):
-        expo = jnp.exp2(score - top)
-        total = total + jnp.sum(expo, axis=0, keepdims=True)
-        mixed = mixed + dot_nn(ref[columns + lo : columns + hi, :], expo.astype(BF16))
-    return top, total, mixed
-
-
-def softmax_body(columns, own_ref, one_ref, two_ref, out_ref):
-    own_meta = meta_of(own_ref, columns)
-    heads = columns // HEAD_DIM
-    start = jnp.full(own_meta[0:1].shape, NEG, F32)
-    out_ref[columns:, :] = jnp.zeros((8, own_ref.shape[1]), F32)
-    for h in range(heads):
-        top, total, mixed = softmax_of(
-            (own_ref, own_ref, one_ref, two_ref), own_meta, columns, (0, 1, 2), h, start
-        )
-        out_ref[h * HEAD_DIM : (h + 1) * HEAD_DIM, :] = mixed
-        out_ref[columns + h : columns + h + 1, :] = top
-        out_ref[columns + heads + h : columns + heads + h + 1, :] = total
-
-
 def pieces(value, count):
     found = []
     for _ in range(count):
@@ -199,25 +187,37 @@
     return found
 
 
-def grad_body(columns, w_ref, stream_ref, own_ref, far_ref, soft_ref, out_ref):
-    head_grad = dot_nn(w_ref[...], stream_ref[...])
+def grad_body(
+    columns, w_ref, stream_ref, own_ref, one_ref, two_ref, far_ref, out_ref, tile_out, inverse_out
+):
+    refs = (own_ref, one_ref, two_ref, far_ref)
     own_meta = meta_of(own_ref, columns)
-    heads = columns // HEAD_DIM
     lane = lax.broadcasted_iota(jnp.int32, own_meta[0:1].shape, 1).astype(F32)
     valid = lane < own_meta[0:1]
-    low = jnp.where(valid, head_grad, 0.0).astype(BF16)
+    limit = [limits(own_meta, meta_of(refs[j], columns)[0:1], j) for j in range(LINKS)]
+    low = jnp.where(valid, dot_nn(w_ref[...], stream_ref[...]), 0.0).astype(BF16)
     out_ref[0:columns, :] = low
     rows = []
-    for h in range(heads):
+    inverse_out[...] = jnp.zeros(inverse_out.shape, F32)
+    for h in range(columns // HEAD_DIM):
         lo, hi = h * HEAD_DIM, (h + 1) * HEAD_DIM
-        old_top = soft_ref[columns + h : columns + h + 1, :]
-        top, total, mixed = softmax_of((own_ref, far_ref), own_meta, columns, (3,), h, old_top)
-        factor = jnp.exp2(old_top - top)
-        total = total + factor * soft_ref[columns + heads + h : columns + heads + h + 1, :]
-        mixed = (mixed + factor * soft_ref[lo:hi, :]) / total
-        delta = jnp.sum(low[lo:hi].astype(F32) * mixed, axis=0, keepdims=True)
+        query = own_ref[2 * columns + lo : 2 * columns + hi, :]
+        scores = [
+            masked(dot_tn(refs[j][lo:hi, :], query) * SCALE2, limit[j]) for j in range(LINKS)
+        ]
+        top = functools.reduce(jnp.maximum, [jnp.max(s, axis=0, keepdims=True) for s in scores])
+        total = jnp.zeros_like(top)
+        mixed = jnp.zeros((HEAD_DIM, own_ref.shape[1]), F32)
+        for j in range(LINKS):
+            expo = jnp.exp2(scores[j] - top)
+            tile_out[LINKS * h + j] = expo
+            total = total + jnp.sum(expo, axis=0, keepdims=True)
+            mixed = mixed + dot_nn(refs[j][columns + lo : columns + hi, :], expo.astype(BF16))
+        inverse = jnp.where(valid, 1.0 / total, 0.0)
+        inverse_out[h : h + 1, :] = inverse
+        delta = jnp.sum(low[lo:hi].astype(F32) * mixed, axis=0, keepdims=True) * inverse
         rows += pieces(jnp.where(valid, top + jnp.log2(total), -NEG), 3)
-        rows += pieces(jnp.where(valid, delta, 0.0), 2)
+        rows += pieces(delta, 2)
     index = lax.broadcasted_iota(jnp.int32, (META, own_meta.shape[1]), 0)
     meta = jnp.zeros((META, own_meta.shape[1]), F32)
     for i, row in enumerate(rows):
@@ -239,24 +239,34 @@
     return probs.astype(BF16), dscore
 
 
-def local_body(columns, own_ref, one_ref, two_ref, far_ref, grad_ref, query_out, acc_out):
+def local_body(
+    columns,
+    own_ref,
+    one_ref,
+    two_ref,
+    far_ref,
+    grad_ref,
+    tile_ref,
+    inverse_ref,
+    query_out,
+    acc_out,
+):
     refs = (own_ref, one_ref, two_ref, far_ref)
-    own_meta = meta_of(own_ref, columns)
-    limit = [limits(own_meta, meta_of(refs[j], columns)[0:1], j) for j in range(LINKS)]
     for h in range(columns // HEAD_DIM):
         lo, hi = h * HEAD_DIM, (h + 1) * HEAD_DIM
-        query = own_ref[2 * columns + lo : 2 * columns + hi, :]
         grad = grad_ref[lo:hi, :]
-        lse, delta = stats_of(grad_ref, columns, h)
+        inverse = inverse_ref[h : h + 1, :]
+        _, delta = stats_of(grad_ref, columns, h)
         total = jnp.zeros((HEAD_DIM, own_ref.shape[1]), F32)
         for j in range(LINKS):
-            key = refs[j][lo:hi, :]
             value = refs[j][columns + lo : columns + hi, :]
-            probs, dscore = tile(key, value, query, grad, lse, delta, limit[j])
-            total = total + dot_nn(key, dscore)
+            probs = tile_ref[LINKS * h + j] * inverse
+            dscore = (probs * (dot_tn(value, grad) - delta)).astype(BF16)
+            total = total + dot_nn(refs[j][lo:hi, :], dscore)
             if j == 0:
+                query = own_ref[2 * columns + lo : 2 * columns + hi, :]
                 acc_out[lo:hi, :] = dot_nt(query, dscore)
-                acc_out[columns + lo : columns + hi, :] = dot_nt(grad, probs)
+                acc_out[columns + lo : columns + hi, :] = dot_nt(grad, probs.astype(BF16))
         query_out[lo:hi, :] = (total * SCALE).astype(BF16)
 
 
@@ -333,64 +343,65 @@
         4 * message * row_count,
     )
     offsets = [0, 1, -1, spans // 2]
-    point_grad = call(
-        functools.partial(conv_body, columns),
-        shape((model, row_count), BF16),
-        (before, after, g_conv, pre, kernel, w_point.reshape(2 * columns, model)),
-        [VMEM] * 2 + [HBM] * 4,
-        4 * columns * model * row_count,
-        4 * columns * model,
+    conv, gate, w_turned = call(
+        own_conv_body,
+        (
+            shape((row_count, columns), F32),
+            shape((2, row_count, columns), F32),
+            shape((2, model, columns), BF16),
+        ),
+        (g_conv, pre, kernel, w_point),
+        [HBM] * 4,
+        2 * KW * columns * row_count,
+        8 * columns * model,
         columns * row_count,
         (
-            pltpu.VMEM((row_count + 32, columns), F32),
+            pltpu.VMEM((row_count + 2 * PAD, columns), F32),
             pltpu.VMEM((8, row_count + 24, columns), F32),
             pltpu.VMEM(flat, BF16),
             pltpu.VMEM((2,) + flat, BF16),
             pltpu.VMEM((KW, columns), F32),
-            pltpu.VMEM((2 * columns, model), BF16),
-            pltpu.VMEM((row_count, columns), F32),
-            pltpu.VMEM((2 * columns, row_count), BF16),
+            pltpu.VMEM((2, columns, model), BF16),
             pltpu.SemaphoreType.DMA((4,)),
         ),
         mib=BIG,
     )
+    point_grad = call(
+        edge_body,
+        shape((model, row_count), BF16),
+        (before, after, conv, gate, kernel, w_turned),
+        [VMEM] * 6,
+        4 * columns * model * row_count,
+        4 * columns * model,
+        0,
+        (pltpu.VMEM((2 * PAD, columns), F32), pltpu.VMEM((2 * PAD, columns), F32)),
+    )
     parts = lax.all_to_all(
         point_grad.reshape(groups, columns, row_count), "head", 0, 0, tiled=False
     )
     own, _ = lax.optimization_barrier((own, point_grad))
-    one, two = [shifted(own, offset) for offset in offsets[1:3]]
-    later, one, two = lax.optimization_barrier((own, one, two))
-    far = shifted(later, offsets[3])
-    soft = call(
-        functools.partial(softmax_body, columns),
-        shape((columns + 8, row_count), F32),
-        (own, one, two),
-        [VMEM] * 3,
-        6 * square,
-        6 * message * row_count,
-        3 * columns // HEAD_DIM * row_count * row_count,
-    )
+    one, two, far = [shifted(own, offset) for offset in offsets[1:]]
     piece = jnp.sum(parts.astype(F32), axis=0)
     stream_grad = (g_out.astype(F32) + piece).astype(BF16)
     stream_full = lax.all_gather(stream_grad, "head", axis=0, tiled=True)
-    grad = call(
+    tiles = (LINKS * columns // HEAD_DIM, row_count, row_count)
+    grad, tile, inverse = call(
         functools.partial(grad_body, columns),
-        shape((columns + META, row_count), BF16),
-        (w_out, stream_full, own, far, soft),
-        [VMEM] * 5,
-        2 * columns * model * row_count + 2 * square,
+        (shape((columns + META, row_count), BF16), shape(tiles, F32), shape((8, row_count), F32)),
+        (w_out, stream_full, own, one, two, far),
+        [VMEM] * 6,
+        2 * columns * model * row_count + 2 * LINKS * square,
         2 * model * (columns + row_count),
-        columns // HEAD_DIM * row_count * row_count,
+        LINKS * columns // HEAD_DIM * row_count * row_count,
     )
     grad_one, grad_two, grad_far = [shifted(grad, offset) for offset in offsets[1:]]
     grad_queries, acc = call(
         functools.partial(local_body, columns),
         (shape((columns, row_count), BF16), shape((2 * columns, row_count), F32)),
-        (own, one, two, far, grad),
-        [VMEM] * 5,
+        (own, one, two, far, grad, tile, inverse),
+        [VMEM] * 7,
         3 * LINKS * square,
         8 * message * row_count,
-        LINKS * columns // HEAD_DIM * row_count * row_count,
     )
     acc = call(
         functools.partial(near_body, columns),

time: 92.8 us -> 86.6 us (0.933)
  the two profiles are of different devices: /device:TPU:1 before, /device:TPU:2 now
where the time goes in v4:
time: 86.6 us; the launch traced here: 86 us
  starting transfers between devices  43.5 us (50%)
  Pallas kernels  14.1 us (16%)
  blocking collectives  13.5 us (16%)
  waiting for transfers between devices  9.11 us (11%)
  local copies, waits for them, and re-layouts  4.29 us (5%)
  between operations  1.52 us (2%)
    ppermute x6, starting transfers between devices, shifted(): return lax.ppermute(value, 'ctx', pairs)  31.7 us
    pallas_call x7, Pallas kernels, call(): pl.pallas_call(body, out_shape=out_shapes, in_specs=specs, out_specs=jax....  14.1 us
    all_gather x1, blocking collectives, per_device(): stream_full = lax.all_gather(stream_grad, 'head', axis=0, tiled=True)  13.5 us
    ppermute x6, waiting for transfers between devices, shifted(): return lax.ppermute(value, 'ctx', pairs)  7.37 us
    all_to_all x1, starting transfers between devices, per_device(): lax.all_to_all(point_grad.reshape(groups, columns, row_count), 'head', 0,...  6.16 us
    unnamed x23, local copies, waits for them, and re-layouts  4.29 us
    ppermute x1, starting transfers between devices, per_device(): before = lax.ppermute(g_conv, 'ctx', up)  4.28 us
    ppermute x1, waiting for transfers between devices, per_device(): after = lax.ppermute(g_conv, 'ctx', [(j, i) for i, j in up])  1.74 us
  transfers between devices with their start and end apart: 9, of which 3 were waited for; matrix products, arithmetic and copies ran while one was open for 0% of the time, Pallas kernels for 10%

profile of v4, /device:TPU:2, one launch (start us, length us, event | category | flops | bytes accessed | tf_op | source)
XLA Modules:
  0.0 86.0 jit_solution(12007703594653096852)
XLA Ops:
  0.6 4.3 %collective-permute-start = (bf16[192,256]{1,0:T(8,128)(2,1)}, bf16[192,256]{1,0:T(8,128)(2,1)S(1)}, u32[]{:S(2)}, u32[]{:S(2)}) collective-permute-start(bf16[192,256]{1,0:T(8,128)(2,1)} %g_ref.1), channel_id=1, source_target_pairs={{0,8},{8,16},{16,24},{24,32},{32,40},{40,48},{48,56},{56,64},{64,7... | collective-permute-start | bytes 294920 | tf_op jit(solution)/shard_map/ppermute | solution.py:334
  4.9 1.3 %collective-permute-start.1 = (bf16[192,256]{1,0:T(8,128)(2,1)}, bf16[192,256]{1,0:T(8,128)(2,1)S(1)}, u32[]{:S(2)}, u32[]{:S(2)}) collective-permute-start(bf16[192,256]{1,0:T(8,128)(2,1)} %g_ref.1), channel_id=1, source_target_pairs={{8,0},{16,8},{24,16},{32,24},{40,32},{48,40},{56,48},{64,56},{72,6... | collective-permute-start | bytes 294920 | tf_op jit(solution)/shard_map/ppermute | solution.py:335
  6.2 4.0 %shard_map.138 = (f32[256,192]{1,0:T(8,128)}, f32[2,256,192]{2,1,0:T(8,128)}, bf16[2,1536,192]{2,1,0:T(8,128)(2,1)}) custom-call(bf16[192,256]{1,0:T(8,128)(2,1)} %g_ref.1, bf16[2,192,256]{2,1,0:T(8,128)(2,1)} %pre_ref.1, f32[31,192]{1,0:T(8,128)} %taps_ref.3, bf16[2,192,1536]{2,1,0:T(8,128)(2,1)} %w_ref.2), custom_call_target="tpu_custom_call" | custom-call | flops 3047424 | bytes 2359296 | tf_op jit(solution)/shard_map/pallas_call | solution.py:31
  10.3 1.7 %collective-permute-done.1.after_ref = bf16[192,256]{1,0:T(8,128)(2,1)S(1)} collective-permute-done((bf16[192,256]{1,0:T(8,128)(2,1)}, bf16[192,256]{1,0:T(8,128)(2,1)S(1)}, u32[]{:S(2)}, u32[]{:S(2)}) %collective-permute-start.1) | collective-permute-done | bytes 98336 | tf_op jit(solution)/shard_map/ppermute | solution.py:335
  12.0 1.4 %copy-done = bf16[2,1536,192]{2,1,0:T(8,128)(2,1)S(1)} copy-done((bf16[2,1536,192]{2,1,0:T(8,128)(2,1)S(1)}, bf16[2,1536,192]{2,1,0:T(8,128)(2,1)}, u32[]{:S(2)}) %copy-start) | copy-done | bytes 1179672
  13.4 1.0 %copy-done.2 = f32[2,256,192]{2,1,0:T(8,128)S(1)} copy-done((f32[2,256,192]{2,1,0:T(8,128)S(1)}, f32[2,256,192]{2,1,0:T(8,128)}, u32[]{:S(2)}) %copy-start.2) | copy-done | bytes 393240
  14.5 0.9 %copy-done.3 = f32[256,192]{1,0:T(8,128)S(1)} copy-done((f32[256,192]{1,0:T(8,128)S(1)}, f32[256,192]{1,0:T(8,128)}, u32[]{:S(2)}) %copy-start.3) | copy-done | bytes 196632
  15.4 0.8 copy-done.4
  16.2 1.7 %shard_map.139 = bf16[1536,256]{1,0:T(8,128)(2,1)} custom-call(bf16[192,256]{1,0:T(8,128)(2,1)S(1)} %collective-permute-done.before_ref, bf16[192,256]{1,0:T(8,128)(2,1)S(1)} %collective-permute-done.1.after_ref, f32[256,192]{1,0:T(8,128)S(1)} %copy-done.3, f32[2,256,192]{2,1,0:T(8,128)S(1)} %copy-done.2, f32[31,192]{1,0:T(8,128)S(1)} %copy-done.4, ...), custom_call_target="tpu_custom_call" | custom-call | flops 301989888 | bytes 1179648 | tf_op jit(solution)/shard_map/pallas_call | solution.py:31
  17.8 0.0 copy-start.9
  17.8 6.2 %all-to-all-start = ((bf16[8,192,256]{2,1,0:T(8,128)(2,1)}), bf16[8,192,256]{2,1,0:T(8,128)(2,1)S(1)}, u32[]{:S(2)}, u32[]{:S(2)}) async-start(bf16[8,192,256]{2,1,0:T(8,128)(2,1)} %bitcast), calls=%async_computation | async-start | bytes 1572864 | tf_op jit(solution)/shard_map/all_to_all | solution.py:379
  24.7 0.1 copy.15.mask_ref
  24.8 0.6 shard_map.140.own_ref
  25.5 12.0 %collective-permute-start.4 = (bf16[592,256]{1,0:T(8,128)(2,1)S(1)}, bf16[592,256]{1,0:T(8,128)(2,1)S(1)}, u32[]{:S(2)}, u32[]{:S(2)}) collective-permute-start(bf16[592,256]{1,0:T(8,128)(2,1)S(1)} %shard_map.140.own_ref), channel_id=1, source_target_pairs={{0,256},{8,264},{16,272},{24,280},{32,288},{40,296},{48,304},{56,3... | collective-permute-start | bytes 909320 | tf_op jit(solution)/shard_map/ppermute | solution.py:318
  37.5 6.0 %collective-permute-start.3 = (bf16[592,256]{1,0:T(8,128)(2,1)S(1)}, bf16[592,256]{1,0:T(8,128)(2,1)S(1)}, u32[]{:S(2)}, u32[]{:S(2)}) collective-permute-start(bf16[592,256]{1,0:T(8,128)(2,1)S(1)} %shard_map.140.own_ref), channel_id=1, source_target_pairs={{0,504},{8,0},{16,8},{24,16},{32,24},{40,32},{48,40},{56,48},{64,5... | collective-permute-start | bytes 909320 | tf_op jit(solution)/shard_map/ppermute | solution.py:318
  43.5 1.9 %collective-permute-start.2 = (bf16[592,256]{1,0:T(8,128)(2,1)S(1)}, bf16[592,256]{1,0:T(8,128)(2,1)S(1)}, u32[]{:S(2)}, u32[]{:S(2)}) collective-permute-start(bf16[592,256]{1,0:T(8,128)(2,1)S(1)} %shard_map.140.own_ref), channel_id=1, source_target_pairs={{0,8},{8,16},{16,24},{24,32},{32,40},{40,48},{48,56},{56,64},{64,7... | collective-permute-start | bytes 909320 | tf_op jit(solution)/shard_map/ppermute | solution.py:318
  45.4 0.0 all-to-all-done
  45.4 0.1 convert_reduce_fusion
  45.6 0.0 copy-start.8
  45.6 13.5 %all_gather.3.stream_ref = bf16[1536,256]{1,0:T(8,128)(2,1)S(1)} all-gather(bf16[192,256]{1,0:T(8,128)(2,1)S(1)} %add_convert_fusion), channel_id=1, replica_groups=mesh['ctx'=64,'head'=8] {'head'}, dimensions={0}, use_global_device_ids=true | all-gather | bytes 884736 | tf_op jit(solution)/shard_map/all_gather | solution.py:386
  59.0 0.0 collective-permute-done.4.far_ref
  59.0 0.0 collective-permute-done.3.two_ref
  59.0 1.3 %collective-permute-done.2.one_ref = bf16[592,256]{1,0:T(8,128)(2,1)S(1)} collective-permute-done((bf16[592,256]{1,0:T(8,128)(2,1)S(1)}, bf16[592,256]{1,0:T(8,128)(2,1)S(1)}, u32[]{:S(2)}, u32[]{:S(2)}) %collective-permute-start.2) | collective-permute-done | bytes 303136 | tf_op jit(solution)/shard_map/ppermute | solution.py:318
  60.4 2.1 %shard_map.141 = (bf16[208,256]{1,0:T(8,128)(2,1)S(1)}, f32[12,256,256]{2,1,0:T(8,128)S(1)}, f32[8,256]{1,0:T(8,128)S(1)}) custom-call(bf16[192,1536]{1,0:T(8,128)(2,1)S(1)} %copy-done.1, bf16[1536,256]{1,0:T(8,128)(2,1)S(1)} %all_gather.3.stream_ref, bf16[592,256]{1,0:T(8,128)(2,1)S(1)} %shard_map.140.own_ref, ...), custom_call_target="tpu_custom_call" | custom-call | flops 352321536 | bytes 1376256 | tf_op jit(solution)/shard_map/pallas_call | solution.py:31
  62.5 5.9 %collective-permute-start.7 = (bf16[208,256]{1,0:T(8,128)(2,1)S(1)}, bf16[208,256]{1,0:T(8,128)(2,1)S(1)}, u32[]{:S(2)}, u32[]{:S(2)}) collective-permute-start(bf16[208,256]{1,0:T(8,128)(2,1)S(1)} %get-tuple-element.19.grad_ref), channel_id=1, source_target_pairs={{0,504},{8,0},{16,8},{24,16},{32,24},{40,32},{48,40},{56,48},{64,5... | collective-permute-start | bytes 319496 | tf_op jit(solution)/shard_map/ppermute | solution.py:318
  68.5 1.9 %collective-permute-start.6 = (bf16[208,256]{1,0:T(8,128)(2,1)S(1)}, bf16[208,256]{1,0:T(8,128)(2,1)S(1)}, u32[]{:S(2)}, u32[]{:S(2)}) collective-permute-start(bf16[208,256]{1,0:T(8,128)(2,1)S(1)} %get-tuple-element.19.grad_ref), channel_id=1, source_target_pairs={{0,8},{8,16},{16,24},{24,32},{32,40},{40,48},{48,56},{56,64},{64,7... | collective-permute-start | bytes 319496 | tf_op jit(solution)/shard_map/ppermute | solution.py:318
  70.4 4.0 %collective-permute-start.5 = (bf16[208,256]{1,0:T(8,128)(2,1)S(1)}, bf16[208,256]{1,0:T(8,128)(2,1)S(1)}, u32[]{:S(2)}, u32[]{:S(2)}) collective-permute-start(bf16[208,256]{1,0:T(8,128)(2,1)S(1)} %get-tuple-element.19.grad_ref), channel_id=1, source_target_pairs={{0,256},{8,264},{16,272},{24,280},{32,288},{40,296},{48,304},{56,3... | collective-permute-start | bytes 319496 | tf_op jit(solution)/shard_map/ppermute | solution.py:318
  74.4 2.7 %shard_map.142 = (bf16[192,256]{1,0:T(8,128)(2,1)}, f32[384,256]{1,0:T(8,128)S(1)}) custom-call(bf16[592,256]{1,0:T(8,128)(2,1)S(1)} %shard_map.140.own_ref, bf16[592,256]{1,0:T(8,128)(2,1)S(1)} %collective-permute-done.2.one_ref, bf16[592,256]{1,0:T(8,128)(2,1)S(1)} %collective-permute-done.3.two_ref, bf16[592,256]{1,0:T(8,128)(2,1)S(1)} %collective-permute-done.4.far_ref, ...), custom_call_target="tpu_custom_call" | custom-call | flops 301989888 | bytes 1212416 | tf_op jit(solution)/shard_map/pallas_call | solution.py:31
  77.1 0.0 collective-permute-done.7.grad_two_ref
  77.1 6.0 %collective-permute-done.6.grad_one_ref = bf16[208,256]{1,0:T(8,128)(2,1)S(1)} collective-permute-done((bf16[208,256]{1,0:T(8,128)(2,1)S(1)}, bf16[208,256]{1,0:T(8,128)(2,1)S(1)}, u32[]{:S(2)}, u32[]{:S(2)}) %collective-permute-start.6) | collective-permute-done | bytes 106528 | tf_op jit(solution)/shard_map/ppermute | solution.py:318
  83.2 1.3 %shard_map.143.acc_ref = f32[384,256]{1,0:T(8,128)S(1)} custom-call(bf16[592,256]{1,0:T(8,128)(2,1)S(1)} %shard_map.140.own_ref, bf16[592,256]{1,0:T(8,128)(2,1)S(1)} %collective-permute-done.2.one_ref, bf16[592,256]{1,0:T(8,128)(2,1)S(1)} %collective-permute-done.3.two_ref, bf16[208,256]{1,0:T(8,128)(2,1)S(1)} %collective-permute-done.6.grad_one_ref, ...), custom_call_target="tpu_custom_call" | custom-call | flops 201326592 | bytes 1212416 | tf_op jit(solution)/shard_map/pallas_call | solution.py:31
  84.5 1.5 %shard_map.144 = (bf16[192,256]{1,0:T(8,128)(2,1)}, bf16[192,256]{1,0:T(8,128)(2,1)}) custom-call(bf16[592,256]{1,0:T(8,128)(2,1)S(1)} %shard_map.140.own_ref, bf16[592,256]{1,0:T(8,128)(2,1)S(1)} %collective-permute-done.4.far_ref, bf16[208,256]{1,0:T(8,128)(2,1)S(1)} %collective-permute-done.5.grad_far_ref, f32[384,256]{1,0:T(8,128)S(1)} %shard_map.143.acc_ref), custom_call_target="tpu_custom_call" | custom-call | flops 100663296 | bytes 1212416 | tf_op jit(solution)/shard_map/pallas_call | solution.py:31
  (19 shorter events, 0.1 us)
Async XLA Ops:
  0.6 9.6 %collective-permute-start = (bf16[192,256]{1,0:T(8,128)(2,1)}, bf16[192,256]{1,0:T(8,128)(2,1)S(1)}, u32[]{:S(2)}, u32[]{:S(2)}) collective-permute-start(bf16[192,256]{1,0:T(8,128)(2,1)} %g_ref.1), channel_id=1, source_target_pairs={{0,8},{8,16},{16,24},{24,32},{32,40},{40,48},{48,56},{56,64},{64,7... | collective-permute-start | bytes 294920 | tf_op jit(solution)/shard_map/ppermute | solution.py:334
  4.9 7.1 %collective-permute-start.1 = (bf16[192,256]{1,0:T(8,128)(2,1)}, bf16[192,256]{1,0:T(8,128)(2,1)S(1)}, u32[]{:S(2)}, u32[]{:S(2)}) collective-permute-start(bf16[192,256]{1,0:T(8,128)(2,1)} %g_ref.1), channel_id=1, source_target_pairs={{8,0},{16,8},{24,16},{32,24},{40,32},{48,40},{56,48},{64,56},{72,6... | collective-permute-start | bytes 294920 | tf_op jit(solution)/shard_map/ppermute | solution.py:335
  12.0 1.4 %copy-start = (bf16[2,1536,192]{2,1,0:T(8,128)(2,1)S(1)}, bf16[2,1536,192]{2,1,0:T(8,128)(2,1)}, u32[]{:S(2)}) copy-start(bf16[2,1536,192]{2,1,0:T(8,128)(2,1)} %get-tuple-element.17.w_ref) | copy-start | bytes 3538948
  13.4 1.0 %copy-start.2 = (f32[2,256,192]{2,1,0:T(8,128)S(1)}, f32[2,256,192]{2,1,0:T(8,128)}, u32[]{:S(2)}) copy-start(f32[2,256,192]{2,1,0:T(8,128)} %get-tuple-element.16.gate_ref) | copy-start | bytes 1179652
  14.4 0.9 %copy-start.3 = (f32[256,192]{1,0:T(8,128)S(1)}, f32[256,192]{1,0:T(8,128)}, u32[]{:S(2)}) copy-start(f32[256,192]{1,0:T(8,128)} %get-tuple-element.15.sum_ref) | copy-start | bytes 589828
  15.4 0.8 copy-start.4
  17.8 6.9 %copy-start.10 = (s32[2,4,2]{1,2,0:T(2,128)S(1)}, s32[2,4,2]{1,2,0:T(2,128)}, u32[]{:S(2)}) copy-start(s32[2,4,2]{1,2,0:T(2,128)} %param.20) | copy-start | bytes 196
  17.8 7.0 %copy-start.5 = (bf16[256,192]{0,1:T(8,128)(2,1)S(1)}, bf16[256,192]{0,1:T(8,128)(2,1)}, u32[]{:S(2)}) copy-start(bf16[256,192]{0,1:T(8,128)(2,1)} %param.18) | copy-start | bytes 294916
  17.8 7.0 %copy-start.6 = (bf16[256,192]{0,1:T(8,128)(2,1)S(1)}, bf16[256,192]{0,1:T(8,128)(2,1)}, u32[]{:S(2)}) copy-start(bf16[256,192]{0,1:T(8,128)(2,1)} %param.19) | copy-start | bytes 294916
  17.8 7.0 %copy-start.7 = (bf16[256,192]{0,1:T(8,128)(2,1)S(1)}, bf16[256,192]{0,1:T(8,128)(2,1)}, u32[]{:S(2)}) copy-start(bf16[256,192]{0,1:T(8,128)(2,1)} %param.17) | copy-start | bytes 294916
  17.8 27.7 %copy-start.9 = (bf16[192,256]{1,0:T(8,128)(2,1)S(1)}, bf16[192,256]{1,0:T(8,128)(2,1)}, u32[]{:S(2)}) copy-start(bf16[192,256]{1,0:T(8,128)(2,1)} %param.15) | copy-start | bytes 294916
  17.8 27.6 %all-to-all-start = ((bf16[8,192,256]{2,1,0:T(8,128)(2,1)}), bf16[8,192,256]{2,1,0:T(8,128)(2,1)S(1)}, u32[]{:S(2)}, u32[]{:S(2)}) async-start(bf16[8,192,256]{2,1,0:T(8,128)(2,1)} %bitcast), calls=%async_computation | async-start | bytes 1572864 | tf_op jit(solution)/shard_map/all_to_all | solution.py:379
  24.0 36.4 %copy-start.1 = (bf16[192,1536]{1,0:T(8,128)(2,1)S(1)}, bf16[192,1536]{1,0:T(8,128)(2,1)}, u32[]{:S(2)}) copy-start(bf16[192,1536]{1,0:T(8,128)(2,1)} %w_ref.3) | copy-start | bytes 1769476
  25.5 33.6 %collective-permute-start.4 = (bf16[592,256]{1,0:T(8,128)(2,1)S(1)}, bf16[592,256]{1,0:T(8,128)(2,1)S(1)}, u32[]{:S(2)}, u32[]{:S(2)}) collective-permute-start(bf16[592,256]{1,0:T(8,128)(2,1)S(1)} %shard_map.140.own_ref), channel_id=1, source_target_pairs={{0,256},{8,264},{16,272},{24,280},{32,288},{40,296},{48,304},{56,3... | collective-permute-start | bytes 909320 | tf_op jit(solution)/shard_map/ppermute | solution.py:318
  37.5 21.6 %collective-permute-start.3 = (bf16[592,256]{1,0:T(8,128)(2,1)S(1)}, bf16[592,256]{1,0:T(8,128)(2,1)S(1)}, u32[]{:S(2)}, u32[]{:S(2)}) collective-permute-start(bf16[592,256]{1,0:T(8,128)(2,1)S(1)} %shard_map.140.own_ref), channel_id=1, source_target_pairs={{0,504},{8,0},{16,8},{24,16},{32,24},{40,32},{48,40},{56,48},{64,5... | collective-permute-start | bytes 909320 | tf_op jit(solution)/shard_map/ppermute | solution.py:318
  43.5 16.9 %collective-permute-start.2 = (bf16[592,256]{1,0:T(8,128)(2,1)S(1)}, bf16[592,256]{1,0:T(8,128)(2,1)S(1)}, u32[]{:S(2)}, u32[]{:S(2)}) collective-permute-start(bf16[592,256]{1,0:T(8,128)(2,1)S(1)} %shard_map.140.own_ref), channel_id=1, source_target_pairs={{0,8},{8,16},{16,24},{24,32},{32,40},{40,48},{48,56},{56,64},{64,7... | collective-permute-start | bytes 909320 | tf_op jit(solution)/shard_map/ppermute | solution.py:318
  45.6 17.0 %copy-start.8 = (bf16[192,256]{1,0:T(8,128)(2,1)}, bf16[192,256]{1,0:T(8,128)(2,1)S(1)}, u32[]{:S(2)}) copy-start(bf16[192,256]{1,0:T(8,128)(2,1)S(1)} %add_convert_fusion) | copy-start | bytes 294916
  62.5 14.6 %collective-permute-start.7 = (bf16[208,256]{1,0:T(8,128)(2,1)S(1)}, bf16[208,256]{1,0:T(8,128)(2,1)S(1)}, u32[]{:S(2)}, u32[]{:S(2)}) collective-permute-start(bf16[208,256]{1,0:T(8,128)(2,1)S(1)} %get-tuple-element.19.grad_ref), channel_id=1, source_target_pairs={{0,504},{8,0},{16,8},{24,16},{32,24},{40,32},{48,40},{56,48},{64,5... | collective-permute-start | bytes 319496 | tf_op jit(solution)/shard_map/ppermute | solution.py:318
  68.5 14.7 %collective-permute-start.6 = (bf16[208,256]{1,0:T(8,128)(2,1)S(1)}, bf16[208,256]{1,0:T(8,128)(2,1)S(1)}, u32[]{:S(2)}, u32[]{:S(2)}) collective-permute-start(bf16[208,256]{1,0:T(8,128)(2,1)S(1)} %get-tuple-element.19.grad_ref), channel_id=1, source_target_pairs={{0,8},{8,16},{16,24},{24,32},{32,40},{40,48},{48,56},{56,64},{64,7... | collective-permute-start | bytes 319496 | tf_op jit(solution)/shard_map/ppermute | solution.py:318
  70.4 14.1 %collective-permute-start.5 = (bf16[208,256]{1,0:T(8,128)(2,1)S(1)}, bf16[208,256]{1,0:T(8,128)(2,1)S(1)}, u32[]{:S(2)}, u32[]{:S(2)}) collective-permute-start(bf16[208,256]{1,0:T(8,128)(2,1)S(1)} %get-tuple-element.19.grad_ref), channel_id=1, source_target_pairs={{0,256},{8,264},{16,272},{24,280},{32,288},{40,296},{48,304},{56,3... | collective-permute-start | bytes 319496 | tf_op jit(solution)/shard_map/ppermute | solution.py:318

commit v5 on v4

--- a/solution.py
+++ b/solution.py
@@ -19,7 +19,6 @@
 NEG = -1e30
 SCALE = 1.0 / math.sqrt(HEAD_DIM)
 SCALE2 = SCALE * math.log2(math.e)
-MIRROR = (0, 2, 1, 3)
 VMEM = pl.BlockSpec(memory_space=pltpu.VMEM)
 HBM = pl.BlockSpec(memory_space=pltpu.HBM)
 SMEM = pl.BlockSpec(memory_space=pltpu.SMEM)
@@ -51,7 +50,7 @@
     return lax.dot_general(a, b, (((1,), (0,)), ((), ())), preferred_element_type=F32)
 
 
-def pack_body(mask_ref, count_ref, keys_ref, values_ref, queries_ref, out_ref):
+def pack_body(odd_ref, mask_ref, count_ref, keys_ref, values_ref, queries_ref, out_ref):
     columns, rows = keys_ref.shape
     out_ref[0:columns, :] = keys_ref[...]
     out_ref[columns : 2 * columns, :] = values_ref[...]
@@ -59,16 +58,17 @@
     row = lax.broadcasted_iota(jnp.int32, (META, rows), 0)
     first = lax.broadcasted_iota(jnp.int32, (META, rows), 1) < rows // 2
     meta = jnp.where(row == 0, count_ref[0].astype(F32), 0.0)
-    for j in range(LINKS):
+    links = (0, 2 - odd_ref[0], 1 + odd_ref[0], 3)
+    for slot, link in enumerate(links):
         for kb in range(2):
             picked = []
             for qb in range(2):
-                bit = (mask_ref[qb, j, kb] > 0).astype(F32)
-                if j == 0 and qb == kb:
+                bit = (mask_ref[qb, link, kb] > 0).astype(F32)
+                if slot == 0 and qb == kb:
                     bit = jnp.maximum(bit, 1.0)
                 picked.append(bit)
             meta = jnp.where(
-                row == 1 + 2 * j + kb, jnp.where(first, picked[0], picked[1]), meta
+                row == 1 + 2 * slot + kb, jnp.where(first, picked[0], picked[1]), meta
             )
     out_ref[3 * columns :, :] = meta.astype(BF16)
 
@@ -83,6 +83,7 @@
     w_out,
     x_ref,
     moved_ref,
+    sum_ref,
     g_low,
     pre_low,
     taps_low,
@@ -113,55 +114,93 @@
         for k in range(KW):
             a, shift = divmod(PAD + HALF - k, 8)
             acc = acc + taps_low[k : k + 1, :] * moved_ref[shift, pl.ds(at + 8 * a, step), :]
-        sum_out[pl.ds(at, step), :] = acc
+        sum_ref[pl.ds(at, step), :] = acc
         return carry
 
     lax.fori_loop(0, rows // step, block, 0)
+    sum_out[...] = sum_ref[...].T
     copies[2].wait()
     value = pre_low[0].astype(F32)
     gate = jax.nn.sigmoid(pre_low[1].astype(F32))
-    gate_out[0] = gate.T
-    gate_out[1] = (value * gate * (1.0 - gate)).T
+    gate_out[0] = gate
+    gate_out[1] = value * gate * (1.0 - gate)
     copies[3].wait()
-    for half in range(2):
-        for at in range(0, w_ref.shape[2], LANES):
-            w_out[half, at : at + LANES, :] = w_low[half, :, at : at + LANES].T
-
-
-def edge_body(before_ref, after_ref, sum_ref, gate_ref, taps_ref, w_ref, out_ref, head, tail):
-    rows, columns = sum_ref.shape
+    for at in range(0, w_ref.shape[1], LANES):
+        w_out[at : at + LANES, :] = w_low[:, at : at + LANES].T
+
+
+def edge_body(
+    odd_ref,
+    two_ref,
+    one_ref,
+    taps_ref,
+    sum_ref,
+    gate_ref,
+    w_ref,
+    out_ref,
+    head,
+    tail,
+    two_low,
+    one_low,
+    taps_low,
+    sum_low,
+    gate_low,
+    w_low,
+    sems,
+):
+    copies = [
+        pltpu.make_async_copy(ref, low, sems.at[i])
+        for i, (ref, low) in enumerate(
+            (
+                (two_ref, two_low),
+                (one_ref, one_low),
+                (taps_ref, taps_low),
+                (sum_ref, sum_low),
+                (gate_ref, gate_low),
+                (w_ref, w_low),
+            )
+        )
+    ]
+    for copy in copies:
+        copy.start()
+    columns, rows = sum_ref.shape
+    odd = odd_ref[0] > 0
+    for copy in copies[:3]:
+        copy.wait()
+    before = jnp.where(odd, one_low[:, rows - LANES :], two_low[:, rows - LANES :]).astype(F32)
+    after = jnp.where(odd, two_low[:, :LANES], one_low[:, :LANES]).astype(F32)
     blank = jnp.zeros((PAD, columns), F32)
-    head[0:PAD, :] = before_ref[:, rows - LANES :].astype(F32).T[LANES - PAD :, :]
+    head[0:PAD, :] = before.T[LANES - PAD :, :]
     head[PAD:, :] = blank
     tail[0:PAD, :] = blank
-    tail[PAD:, :] = after_ref[:, :LANES].astype(F32).T[:PAD, :]
+    tail[PAD:, :] = after.T[:PAD, :]
     first, last = blank, blank
     for d in range(1, HALF + 1):
-        first = first + taps_ref[HALF + d : HALF + d + 1, :] * head[PAD - d : 2 * PAD - d, :]
-        last = last + taps_ref[HALF - d : HALF - d + 1, :] * tail[d : PAD + d, :]
-    grad = jnp.concatenate(
-        [sum_ref[0:PAD, :] + first, sum_ref[PAD : rows - PAD, :], sum_ref[rows - PAD :, :] + last],
-        axis=0,
-    )
-    low = [(grad * gate_ref[half]).astype(BF16) for half in range(2)]
-    model = w_ref.shape[1]
+        first = first + taps_low[HALF + d : HALF + d + 1, :] * head[PAD - d : 2 * PAD - d, :]
+        last = last + taps_low[HALF - d : HALF - d + 1, :] * tail[d : PAD + d, :]
+    rest = jnp.zeros((LANES - PAD, columns), F32)
+    left = jnp.concatenate([first, rest], axis=0).T
+    right = jnp.concatenate([rest, last], axis=0).T
+    copies[3].wait()
+    grad = sum_low[...] + jnp.concatenate([left, right], axis=1)
+    copies[4].wait()
+    low = jnp.concatenate([(grad * gate_low[half]).astype(BF16) for half in range(2)], axis=0)
+    copies[5].wait()
+    model = w_ref.shape[0]
     chunk = 256 if model % 256 == 0 else LANES
     for at in range(0, model, chunk):
-        here = slice(at, at + chunk)
-        out_ref[here, :] = (
-            dot_nt(w_ref[0, here, :], low[0]) + dot_nt(w_ref[1, here, :], low[1])
-        ).astype(BF16)
+        out_ref[at : at + chunk, :] = dot_nn(w_low[at : at + chunk, :], low).astype(BF16)
 
 
 def meta_of(ref, columns):
     return ref[3 * columns : 3 * columns + META, :].astype(F32)
 
 
-def limits(query_meta, key_count, link):
+def limits(query_meta, key_count, slot):
     lane = lax.broadcasted_iota(jnp.int32, query_meta[0:1].shape, 1).astype(F32)
     valid = lane < query_meta[0:1]
     return [
-        jnp.where(valid & (query_meta[1 + 2 * link + kb : 2 + 2 * link + kb] > 0.5), key_count, 0.0)
+        jnp.where(valid & (query_meta[1 + 2 * slot + kb : 2 + 2 * slot + kb] > 0.5), key_count, 0.0)
         for kb in range(2)
     ]
 
@@ -188,7 +227,7 @@
 
 
 def grad_body(
-    columns, w_ref, stream_ref, own_ref, one_ref, two_ref, far_ref, out_ref, tile_out, inverse_out
+    columns, w_ref, stream_ref, own_ref, one_ref, far_ref, two_ref, out_ref, tile_out, inverse_out
 ):
     refs = (own_ref, one_ref, two_ref, far_ref)
     own_meta = meta_of(own_ref, columns)
@@ -270,51 +309,51 @@
         query_out[lo:hi, :] = (total * SCALE).astype(BF16)
 
 
-def remote_terms(columns, links, own_ref, span_refs, grad_refs, h):
+def remote_terms(columns, slots, own_ref, span_refs, grad_refs, h):
     lo, hi = h * HEAD_DIM, (h + 1) * HEAD_DIM
     key = own_ref[lo:hi, :]
     value = own_ref[columns + lo : columns + hi, :]
     count = meta_of(own_ref, columns)[0:1]
     key_term = value_term = 0.0
-    for link, span_ref, grad_ref in zip(links, span_refs, grad_refs):
+    for slot, span_ref, grad_ref in zip(slots, span_refs, grad_refs):
         query = span_ref[2 * columns + lo : 2 * columns + hi, :]
         grad = grad_ref[lo:hi, :]
         lse, delta = stats_of(grad_ref, columns, h)
-        limit = limits(meta_of(span_ref, columns), count, link)
+        limit = limits(meta_of(span_ref, columns), count, slot)
         probs, dscore = tile(key, value, query, grad, lse, delta, limit)
         key_term = key_term + dot_nt(query, dscore)
         value_term = value_term + dot_nt(grad, probs)
     return key_term, value_term
 
 
-def near_body(columns, own_ref, one_ref, two_ref, grad_one_ref, grad_two_ref, acc_ref, acc_out):
+def middle_body(columns, own_ref, two_ref, far_ref, grad_two_ref, grad_far_ref, acc_ref, acc_out):
     for h in range(columns // HEAD_DIM):
         lo, hi = h * HEAD_DIM, (h + 1) * HEAD_DIM
         key_term, value_term = remote_terms(
-            columns,
-            (MIRROR[1], MIRROR[2]),
-            own_ref,
-            (one_ref, two_ref),
-            (grad_one_ref, grad_two_ref),
-            h,
+            columns, (2, 3), own_ref, (two_ref, far_ref), (grad_two_ref, grad_far_ref), h
         )
         acc_out[lo:hi, :] = acc_ref[lo:hi, :] + key_term
         acc_out[columns + lo : columns + hi, :] = acc_ref[columns + lo : columns + hi, :] + value_term
 
 
-def far_body(columns, own_ref, far_ref, grad_far_ref, acc_ref, key_out, value_out):
+def last_body(columns, own_ref, one_ref, grad_one_ref, acc_ref, key_out, value_out):
     for h in range(columns // HEAD_DIM):
         lo, hi = h * HEAD_DIM, (h + 1) * HEAD_DIM
         key_term, value_term = remote_terms(
-            columns, (MIRROR[3],), own_ref, (far_ref,), (grad_far_ref,), h
+            columns, (1,), own_ref, (one_ref,), (grad_one_ref,), h
         )
         key_out[lo:hi, :] = ((acc_ref[lo:hi, :] + key_term) * SCALE).astype(BF16)
         value_out[lo:hi, :] = (acc_ref[columns + lo : columns + hi, :] + value_term).astype(BF16)
 
 
-def shifted(value, steps):
+def exchange(value, slot, closed=True):
     count = lax.axis_size("ctx")
-    pairs = [(source, (source + steps) % count) for source in range(count)]
+    if slot == 3:
+        pairs = [(c, (c + count // 2) % count) for c in range(count)]
+    else:
+        pairs = [(c, (c + (1 if (c + slot) % 2 else -1)) % count) for c in range(count)]
+    if not closed:
+        pairs = [(i, j) for i, j in pairs if abs(i - j) == 1]
     return lax.ppermute(value, "ctx", pairs)
 
 
@@ -324,33 +363,26 @@
     columns, row_count = g_conv.shape
     model = w_point.shape[2]
     groups = lax.axis_size("head")
-    spans = lax.axis_size("ctx")
     shape = jax.ShapeDtypeStruct
     queries, keys, values = (queries.T, keys.T, values.T)
     message = 3 * columns + META
     square = 2 * columns * row_count * row_count
 
-    up = [(i, i + 1) for i in range(spans - 1)]
-    before = lax.ppermute(g_conv, "ctx", up)
-    after = lax.ppermute(g_conv, "ctx", [(j, i) for i, j in up])
+    odd = (lax.axis_index("ctx") % 2).astype(jnp.int32).reshape(1)
+    near = [exchange(g_conv, slot, closed=False) for slot in (2, 1)]
     flat = (columns, row_count)
     own = call(
         pack_body,
         shape((message, row_count), BF16),
-        (block_mask, counts, keys, values, queries),
-        [SMEM] * 2 + [VMEM] * 3,
+        (odd, block_mask, counts, keys, values, queries),
+        [SMEM] * 3 + [VMEM] * 3,
         0,
         4 * message * row_count,
     )
-    offsets = [0, 1, -1, spans // 2]
     conv, gate, w_turned = call(
         own_conv_body,
-        (
-            shape((row_count, columns), F32),
-            shape((2, row_count, columns), F32),
-            shape((2, model, columns), BF16),
-        ),
-        (g_conv, pre, kernel, w_point),
+        (shape(flat, F32), shape((2,) + flat, F32), shape((model, 2 * columns), BF16)),
+        (g_conv, pre, kernel, w_point.reshape(2 * columns, model)),
         [HBM] * 4,
         2 * KW * columns * row_count,
         8 * columns * model,
@@ -358,10 +390,11 @@
         (
             pltpu.VMEM((row_count + 2 * PAD, columns), F32),
             pltpu.VMEM((8, row_count + 24, columns), F32),
+            pltpu.VMEM((row_count, columns), F32),
             pltpu.VMEM(flat, BF16),
             pltpu.VMEM((2,) + flat, BF16),
             pltpu.VMEM((KW, columns), F32),
-            pltpu.VMEM((2, columns, model), BF16),
+            pltpu.VMEM((2 * columns, model), BF16),
             pltpu.SemaphoreType.DMA((4,)),
         ),
         mib=BIG,
@@ -369,18 +402,30 @@
     point_grad = call(
         edge_body,
         shape((model, row_count), BF16),
-        (before, after, conv, gate, kernel, w_turned),
-        [VMEM] * 6,
+        (odd, *near, kernel, conv, gate, w_turned),
+        [SMEM] + [HBM] * 6,
         4 * columns * model * row_count,
         4 * columns * model,
         0,
-        (pltpu.VMEM((2 * PAD, columns), F32), pltpu.VMEM((2 * PAD, columns), F32)),
+        (
+            pltpu.VMEM((2 * PAD, columns), F32),
+            pltpu.VMEM((2 * PAD, columns), F32),
+            pltpu.VMEM(flat, BF16),
+            pltpu.VMEM(flat, BF16),
+            pltpu.VMEM((KW, columns), F32),
+            pltpu.VMEM(flat, F32),
+            pltpu.VMEM((2,) + flat, F32),
+            pltpu.VMEM((model, 2 * columns), BF16),
+            pltpu.SemaphoreType.DMA((6,)),
+        ),
+        mib=BIG,
     )
     parts = lax.all_to_all(
         point_grad.reshape(groups, columns, row_count), "head", 0, 0, tiled=False
     )
     own, _ = lax.optimization_barrier((own, point_grad))
-    one, two, far = [shifted(own, offset) for offset in offsets[1:]]
+    one, two = [exchange(own, slot) for slot in (1, 2)]
+    far = exchange(own, 3)
     piece = jnp.sum(parts.astype(F32), axis=0)
     stream_grad = (g_out.astype(F32) + piece).astype(BF16)
     stream_full = lax.all_gather(stream_grad, "head", axis=0, tiled=True)
@@ -388,13 +433,13 @@
     grad, tile, inverse = call(
         functools.partial(grad_body, columns),
         (shape((columns + META, row_count), BF16), shape(tiles, F32), shape((8, row_count), F32)),
-        (w_out, stream_full, own, one, two, far),
+        (w_out, stream_full, own, one, far, two),
         [VMEM] * 6,
         2 * columns * model * row_count + 2 * LINKS * square,
         2 * model * (columns + row_count),
         LINKS * columns // HEAD_DIM * row_count * row_count,
     )
-    grad_one, grad_two, grad_far = [shifted(grad, offset) for offset in offsets[1:]]
+    grad_one, grad_two, grad_far = [exchange(grad, slot) for slot in (1, 2, 3)]
     grad_queries, acc = call(
         functools.partial(local_body, columns),
         (shape((columns, row_count), BF16), shape((2 * columns, row_count), F32)),
@@ -404,18 +449,18 @@
         8 * message * row_count,
     )
     acc = call(
-        functools.partial(near_body, columns),
+        functools.partial(middle_body, columns),
         shape((2 * columns, row_count), F32),
-        (own, one, two, grad_one, grad_two, acc),
+        (own, two, far, grad_two, grad_far, acc),
         [VMEM] * 6,
         8 * square,
         8 * message * row_count,
         2 * columns // HEAD_DIM * row_count * row_count,
     )
     grad_keys, grad_values = call(
-        functools.partial(far_body, columns),
+        functools.partial(last_body, columns),
         (shape((columns, row_count), BF16), shape((columns, row_count), BF16)),
-        (own, far, grad_far, acc),
+        (own, one, grad_one, acc),
         [VMEM] * 4,
         4 * square,
         8 * message * row_count,

time: 86.6 us -> 79.1 us (0.913)
  the two profiles are of different devices: /device:TPU:2 before, /device:TPU:1 now
where the time goes in v5:
time: 79.1 us; the launch traced here: 78.7 us
  starting transfers between devices  43.4 us (55%)
  Pallas kernels  15.3 us (19%)
  blocking collectives  14.6 us (18%)
  waiting for transfers between devices  2.88 us (4%)
  between operations  1.56 us (2%)
    ppermute x8, starting transfers between devices, exchange(): return lax.ppermute(value, 'ctx', pairs)  37.7 us
    pallas_call x7, Pallas kernels, call(): pl.pallas_call(body, out_shape=out_shapes, in_specs=specs, out_specs=jax....  15.3 us
    all_gather x1, blocking collectives, per_device(): stream_full = lax.all_gather(stream_grad, 'head', axis=0, tiled=True)  14.6 us
    all_to_all x1, starting transfers between devices, per_device(): lax.all_to_all(point_grad.reshape(groups, columns, row_count), 'head', 0,...  5.67 us
    ppermute x8, waiting for transfers between devices, exchange(): return lax.ppermute(value, 'ctx', pairs)  2.88 us
  transfers between devices with their start and end apart: 9, of which 2 were waited for; matrix products, arithmetic and copies ran while one was open for 0% of the time, Pallas kernels for 11%

profile of v5, /device:TPU:1, one launch (start us, length us, event | category | flops | bytes accessed | tf_op | source)
XLA Modules:
  0.0 78.7 jit_solution(16386462730006651963)
XLA Ops:
  0.6 0.7 collective-permute-start
  1.3 8.2 %collective-permute-start.1 = (bf16[192,256]{1,0:T(8,128)(2,1)}, bf16[192,256]{1,0:T(8,128)(2,1)S(1)}, u32[]{:S(2)}, u32[]{:S(2)}) collective-permute-start(bf16[192,256]{1,0:T(8,128)(2,1)} %g_ref.1), channel_id=1, source_target_pairs={{0,8},{8,0},{16,24},{24,16},{32,40},{40,32},{48,56},{56,48},{64,72... | collective-permute-start | bytes 294920 | tf_op jit(solution)/shard_map/ppermute | solution.py:357
  9.5 3.8 %shard_map.138 = (f32[192,256]{1,0:T(8,128)}, f32[2,192,256]{2,1,0:T(8,128)}, bf16[1536,384]{1,0:T(8,128)(2,1)}) custom-call(bf16[192,256]{1,0:T(8,128)(2,1)} %g_ref.1, bf16[2,192,256]{2,1,0:T(8,128)(2,1)} %pre_ref.1, f32[31,192]{1,0:T(8,128)} %taps_ref.3, bf16[384,1536]{1,0:T(8,128)(2,1)} %bitcast.14), custom_call_target="tpu_custom_call" | custom-call | flops 3047424 | bytes 2359296 | tf_op jit(solution)/shard_map/pallas_call | solution.py:30
  13.3 0.0 collective-permute-done.two_ref
  13.3 0.0 copy-start.5
  13.3 0.0 collective-permute-done.1.one_ref
  13.3 0.0 copy-start.6
  13.3 0.6 copy-done.5
  13.9 0.0 copy-done.6
  14.0 3.2 %shard_map.139 = bf16[1536,256]{1,0:T(8,128)(2,1)} custom-call(s32[1]{0:T(128)} %bitcast.odd_ref, bf16[192,256]{1,0:T(8,128)(2,1)} %copy-done.5, bf16[192,256]{1,0:T(8,128)(2,1)} %copy-done.6, f32[31,192]{1,0:T(8,128)} %taps_ref.3, f32[192,256]{1,0:T(8,128)} %get-tuple-element.15.sum_ref, f32[2,192,256]{2,1,0:T(8,128)} %get-tuple-element.16.gate_ref, ...), custom_call_target="tpu_custom_call" | custom-call | flops 301989888 | bytes 1179648 | tf_op jit(solution)/shard_map/pallas_call | solution.py:30
  17.1 0.0 copy-start.7
  17.2 5.7 %all-to-all-start = ((bf16[8,192,256]{2,1,0:T(8,128)(2,1)}), bf16[8,192,256]{2,1,0:T(8,128)(2,1)S(1)}, u32[]{:S(2)}, u32[]{:S(2)}) async-start(bf16[8,192,256]{2,1,0:T(8,128)(2,1)} %bitcast.13), calls=%async_computation | async-start | bytes 1572864 | tf_op jit(solution)/shard_map/all_to_all | solution.py:423
  23.5 0.1 copy.15.mask_ref
  23.7 0.6 shard_map.140.own_ref
  24.3 12.6 %collective-permute-start.4 = (bf16[592,256]{1,0:T(8,128)(2,1)S(1)}, bf16[592,256]{1,0:T(8,128)(2,1)S(1)}, u32[]{:S(2)}, u32[]{:S(2)}) collective-permute-start(bf16[592,256]{1,0:T(8,128)(2,1)S(1)} %shard_map.140.own_ref), channel_id=1, source_target_pairs={{0,256},{8,264},{16,272},{24,280},{32,288},{40,296},{48,304},{56,3... | collective-permute-start | bytes 909320 | tf_op jit(solution)/shard_map/ppermute | solution.py:357
  36.9 3.1 %collective-permute-start.3 = (bf16[592,256]{1,0:T(8,128)(2,1)S(1)}, bf16[592,256]{1,0:T(8,128)(2,1)S(1)}, u32[]{:S(2)}, u32[]{:S(2)}) collective-permute-start(bf16[592,256]{1,0:T(8,128)(2,1)S(1)} %shard_map.140.own_ref), channel_id=1, source_target_pairs={{0,504},{8,16},{16,8},{24,32},{32,24},{40,48},{48,40},{56,64},{64,... | collective-permute-start | bytes 909320 | tf_op jit(solution)/shard_map/ppermute | solution.py:357
  40.0 1.9 %collective-permute-start.2 = (bf16[592,256]{1,0:T(8,128)(2,1)S(1)}, bf16[592,256]{1,0:T(8,128)(2,1)S(1)}, u32[]{:S(2)}, u32[]{:S(2)}) collective-permute-start(bf16[592,256]{1,0:T(8,128)(2,1)S(1)} %shard_map.140.own_ref), channel_id=1, source_target_pairs={{0,8},{8,0},{16,24},{24,16},{32,40},{40,32},{48,56},{56,48},{64,72... | collective-permute-start | bytes 909320 | tf_op jit(solution)/shard_map/ppermute | solution.py:357
  41.9 0.0 all-to-all-done
  41.9 0.1 convert_reduce_fusion
  42.1 0.0 copy-start.4
  42.1 14.6 %all_gather.3.stream_ref = bf16[1536,256]{1,0:T(8,128)(2,1)S(1)} all-gather(bf16[192,256]{1,0:T(8,128)(2,1)S(1)} %add_convert_fusion), channel_id=1, replica_groups=mesh['ctx'=64,'head'=8] {'head'}, dimensions={0}, use_global_device_ids=true | all-gather | bytes 884736 | tf_op jit(solution)/shard_map/all_gather | solution.py:431
  56.7 1.1 %collective-permute-done.3.two_ref = bf16[592,256]{1,0:T(8,128)(2,1)S(1)} collective-permute-done((bf16[592,256]{1,0:T(8,128)(2,1)S(1)}, bf16[592,256]{1,0:T(8,128)(2,1)S(1)}, u32[]{:S(2)}, u32[]{:S(2)}) %collective-permute-start.3) | collective-permute-done | bytes 303136 | tf_op jit(solution)/shard_map/ppermute | solution.py:357
  57.8 2.1 %shard_map.141 = (bf16[208,256]{1,0:T(8,128)(2,1)S(1)}, f32[12,256,256]{2,1,0:T(8,128)S(1)}, f32[8,256]{1,0:T(8,128)S(1)}) custom-call(bf16[192,1536]{1,0:T(8,128)(2,1)S(1)} %copy-done, bf16[1536,256]{1,0:T(8,128)(2,1)S(1)} %all_gather.3.stream_ref, bf16[592,256]{1,0:T(8,128)(2,1)S(1)} %shard_map.140.own_ref, ...), custom_call_target="tpu_custom_call" | custom-call | flops 352321536 | bytes 1376256 | tf_op jit(solution)/shard_map/pallas_call | solution.py:30
  60.0 5.2 %collective-permute-start.7 = (bf16[208,256]{1,0:T(8,128)(2,1)S(1)}, bf16[208,256]{1,0:T(8,128)(2,1)S(1)}, u32[]{:S(2)}, u32[]{:S(2)}) collective-permute-start(bf16[208,256]{1,0:T(8,128)(2,1)S(1)} %get-tuple-element.19.grad_ref), channel_id=1, source_target_pairs={{0,256},{8,264},{16,272},{24,280},{32,288},{40,296},{48,304},{56,3... | collective-permute-start | bytes 319496 | tf_op jit(solution)/shard_map/ppermute | solution.py:357
  65.2 4.1 %collective-permute-start.6 = (bf16[208,256]{1,0:T(8,128)(2,1)S(1)}, bf16[208,256]{1,0:T(8,128)(2,1)S(1)}, u32[]{:S(2)}, u32[]{:S(2)}) collective-permute-start(bf16[208,256]{1,0:T(8,128)(2,1)S(1)} %get-tuple-element.19.grad_ref), channel_id=1, source_target_pairs={{0,504},{8,16},{16,8},{24,32},{32,24},{40,48},{48,40},{56,64},{64,... | collective-permute-start | bytes 319496 | tf_op jit(solution)/shard_map/ppermute | solution.py:357
  69.3 1.9 %collective-permute-start.5 = (bf16[208,256]{1,0:T(8,128)(2,1)S(1)}, bf16[208,256]{1,0:T(8,128)(2,1)S(1)}, u32[]{:S(2)}, u32[]{:S(2)}) collective-permute-start(bf16[208,256]{1,0:T(8,128)(2,1)S(1)} %get-tuple-element.19.grad_ref), channel_id=1, source_target_pairs={{0,8},{8,0},{16,24},{24,16},{32,40},{40,32},{48,56},{56,48},{64,72... | collective-permute-start | bytes 319496 | tf_op jit(solution)/shard_map/ppermute | solution.py:357
  71.3 2.7 %shard_map.142 = (bf16[192,256]{1,0:T(8,128)(2,1)}, f32[384,256]{1,0:T(8,128)S(1)}) custom-call(bf16[592,256]{1,0:T(8,128)(2,1)S(1)} %shard_map.140.own_ref, bf16[592,256]{1,0:T(8,128)(2,1)S(1)} %collective-permute-done.2.one_ref, bf16[592,256]{1,0:T(8,128)(2,1)S(1)} %collective-permute-done.3.two_ref, bf16[592,256]{1,0:T(8,128)(2,1)S(1)} %collective-permute-done.4.far_ref, ...), custom_call_target="tpu_custom_call" | custom-call | flops 301989888 | bytes 1212416 | tf_op jit(solution)/shard_map/pallas_call | solution.py:30
  74.0 0.0 collective-permute-done.7.grad_far_ref
  74.0 1.8 %collective-permute-done.6.grad_two_ref = bf16[208,256]{1,0:T(8,128)(2,1)S(1)} collective-permute-done((bf16[208,256]{1,0:T(8,128)(2,1)S(1)}, bf16[208,256]{1,0:T(8,128)(2,1)S(1)}, u32[]{:S(2)}, u32[]{:S(2)}) %collective-permute-start.6) | collective-permute-done | bytes 106528 | tf_op jit(solution)/shard_map/ppermute | solution.py:357
  75.8 1.3 %shard_map.143.acc_ref = f32[384,256]{1,0:T(8,128)S(1)} custom-call(bf16[592,256]{1,0:T(8,128)(2,1)S(1)} %shard_map.140.own_ref, bf16[592,256]{1,0:T(8,128)(2,1)S(1)} %collective-permute-done.3.two_ref, bf16[592,256]{1,0:T(8,128)(2,1)S(1)} %collective-permute-done.4.far_ref, bf16[208,256]{1,0:T(8,128)(2,1)S(1)} %collective-permute-done.6.grad_two_ref, ...), custom_call_target="tpu_custom_call" | custom-call | flops 201326592 | bytes 1212416 | tf_op jit(solution)/shard_map/pallas_call | solution.py:30
  77.1 0.0 collective-permute-done.5.grad_one_ref
  77.1 1.5 %shard_map.144 = (bf16[192,256]{1,0:T(8,128)(2,1)}, bf16[192,256]{1,0:T(8,128)(2,1)}) custom-call(bf16[592,256]{1,0:T(8,128)(2,1)S(1)} %shard_map.140.own_ref, bf16[592,256]{1,0:T(8,128)(2,1)S(1)} %collective-permute-done.2.one_ref, bf16[208,256]{1,0:T(8,128)(2,1)S(1)} %collective-permute-done.5.grad_one_ref, f32[384,256]{1,0:T(8,128)S(1)} %shard_map.143.acc_ref), custom_call_target="tpu_custom_call" | custom-call | flops 100663296 | bytes 1212416 | tf_op jit(solution)/shard_map/pallas_call | solution.py:30
  (15 shorter events, 0.0 us)
Async XLA Ops:
  0.6 12.6 %collective-permute-start = (bf16[192,256]{1,0:T(8,128)(2,1)}, bf16[192,256]{1,0:T(8,128)(2,1)S(1)}, u32[]{:S(2)}, u32[]{:S(2)}) collective-permute-start(bf16[192,256]{1,0:T(8,128)(2,1)} %g_ref.1), channel_id=1, source_target_pairs={{8,16},{16,8},{24,32},{32,24},{40,48},{48,40},{56,64},{64,56},{72,... | collective-permute-start | bytes 294920 | tf_op jit(solution)/shard_map/ppermute | solution.py:357
  1.3 12.0 %collective-permute-start.1 = (bf16[192,256]{1,0:T(8,128)(2,1)}, bf16[192,256]{1,0:T(8,128)(2,1)S(1)}, u32[]{:S(2)}, u32[]{:S(2)}) collective-permute-start(bf16[192,256]{1,0:T(8,128)(2,1)} %g_ref.1), channel_id=1, source_target_pairs={{0,8},{8,0},{16,24},{24,16},{32,40},{40,32},{48,56},{56,48},{64,72... | collective-permute-start | bytes 294920 | tf_op jit(solution)/shard_map/ppermute | solution.py:357
  13.3 0.6 copy-start.5
  13.3 0.7 copy-start.6
  14.0 9.6 %copy-start.8 = (s32[2,4,2]{1,2,0:T(2,128)S(1)}, s32[2,4,2]{1,2,0:T(2,128)}, u32[]{:S(2)}) copy-start(s32[2,4,2]{1,2,0:T(2,128)} %param.20) | copy-start | bytes 196
  14.0 9.7 %copy-start.1 = (bf16[256,192]{0,1:T(8,128)(2,1)S(1)}, bf16[256,192]{0,1:T(8,128)(2,1)}, u32[]{:S(2)}) copy-start(bf16[256,192]{0,1:T(8,128)(2,1)} %param.18) | copy-start | bytes 294916
  14.0 9.7 %copy-start.2 = (bf16[256,192]{0,1:T(8,128)(2,1)S(1)}, bf16[256,192]{0,1:T(8,128)(2,1)}, u32[]{:S(2)}) copy-start(bf16[256,192]{0,1:T(8,128)(2,1)} %param.19) | copy-start | bytes 294916
  14.0 9.7 %copy-start.3 = (bf16[256,192]{0,1:T(8,128)(2,1)S(1)}, bf16[256,192]{0,1:T(8,128)(2,1)}, u32[]{:S(2)}) copy-start(bf16[256,192]{0,1:T(8,128)(2,1)} %param.17) | copy-start | bytes 294916
  17.1 24.9 %copy-start.7 = (bf16[192,256]{1,0:T(8,128)(2,1)S(1)}, bf16[192,256]{1,0:T(8,128)(2,1)}, u32[]{:S(2)}) copy-start(bf16[192,256]{1,0:T(8,128)(2,1)} %param.15) | copy-start | bytes 294916
  17.2 24.8 %all-to-all-start = ((bf16[8,192,256]{2,1,0:T(8,128)(2,1)}), bf16[8,192,256]{2,1,0:T(8,128)(2,1)S(1)}, u32[]{:S(2)}, u32[]{:S(2)}) async-start(bf16[8,192,256]{2,1,0:T(8,128)(2,1)} %bitcast.13), calls=%async_computation | async-start | bytes 1572864 | tf_op jit(solution)/shard_map/all_to_all | solution.py:423
  22.8 35.0 %copy-start = (bf16[192,1536]{1,0:T(8,128)(2,1)S(1)}, bf16[192,1536]{1,0:T(8,128)(2,1)}, u32[]{:S(2)}) copy-start(bf16[192,1536]{1,0:T(8,128)(2,1)} %w_ref.1) | copy-start | bytes 1769476
  24.3 32.4 %collective-permute-start.4 = (bf16[592,256]{1,0:T(8,128)(2,1)S(1)}, bf16[592,256]{1,0:T(8,128)(2,1)S(1)}, u32[]{:S(2)}, u32[]{:S(2)}) collective-permute-start(bf16[592,256]{1,0:T(8,128)(2,1)S(1)} %shard_map.140.own_ref), channel_id=1, source_target_pairs={{0,256},{8,264},{16,272},{24,280},{32,288},{40,296},{48,304},{56,3... | collective-permute-start | bytes 909320 | tf_op jit(solution)/shard_map/ppermute | solution.py:357
  36.9 20.9 %collective-permute-start.3 = (bf16[592,256]{1,0:T(8,128)(2,1)S(1)}, bf16[592,256]{1,0:T(8,128)(2,1)S(1)}, u32[]{:S(2)}, u32[]{:S(2)}) collective-permute-start(bf16[592,256]{1,0:T(8,128)(2,1)S(1)} %shard_map.140.own_ref), channel_id=1, source_target_pairs={{0,504},{8,16},{16,8},{24,32},{32,24},{40,48},{48,40},{56,64},{64,... | collective-permute-start | bytes 909320 | tf_op jit(solution)/shard_map/ppermute | solution.py:357
  40.0 17.8 %collective-permute-start.2 = (bf16[592,256]{1,0:T(8,128)(2,1)S(1)}, bf16[592,256]{1,0:T(8,128)(2,1)S(1)}, u32[]{:S(2)}, u32[]{:S(2)}) collective-permute-start(bf16[592,256]{1,0:T(8,128)(2,1)S(1)} %shard_map.140.own_ref), channel_id=1, source_target_pairs={{0,8},{8,0},{16,24},{24,16},{32,40},{40,32},{48,56},{56,48},{64,72... | collective-permute-start | bytes 909320 | tf_op jit(solution)/shard_map/ppermute | solution.py:357
  42.1 17.9 %copy-start.4 = (bf16[192,256]{1,0:T(8,128)(2,1)}, bf16[192,256]{1,0:T(8,128)(2,1)S(1)}, u32[]{:S(2)}) copy-start(bf16[192,256]{1,0:T(8,128)(2,1)S(1)} %add_convert_fusion) | copy-start | bytes 294916
  60.0 14.0 %collective-permute-start.7 = (bf16[208,256]{1,0:T(8,128)(2,1)S(1)}, bf16[208,256]{1,0:T(8,128)(2,1)S(1)}, u32[]{:S(2)}, u32[]{:S(2)}) collective-permute-start(bf16[208,256]{1,0:T(8,128)(2,1)S(1)} %get-tuple-element.19.grad_ref), channel_id=1, source_target_pairs={{0,256},{8,264},{16,272},{24,280},{32,288},{40,296},{48,304},{56,3... | collective-permute-start | bytes 319496 | tf_op jit(solution)/shard_map/ppermute | solution.py:357
  65.2 10.6 %collective-permute-start.6 = (bf16[208,256]{1,0:T(8,128)(2,1)S(1)}, bf16[208,256]{1,0:T(8,128)(2,1)S(1)}, u32[]{:S(2)}, u32[]{:S(2)}) collective-permute-start(bf16[208,256]{1,0:T(8,128)(2,1)S(1)} %get-tuple-element.19.grad_ref), channel_id=1, source_target_pairs={{0,504},{8,16},{16,8},{24,32},{32,24},{40,48},{48,40},{56,64},{64,... | collective-permute-start | bytes 319496 | tf_op jit(solution)/shard_map/ppermute | solution.py:357
  69.3 7.8 %collective-permute-start.5 = (bf16[208,256]{1,0:T(8,128)(2,1)S(1)}, bf16[208,256]{1,0:T(8,128)(2,1)S(1)}, u32[]{:S(2)}, u32[]{:S(2)}) collective-permute-start(bf16[208,256]{1,0:T(8,128)(2,1)S(1)} %get-tuple-element.19.grad_ref), channel_id=1, source_target_pairs={{0,8},{8,0},{16,24},{24,16},{32,40},{40,32},{48,56},{56,48},{64,72... | collective-permute-start | bytes 319496 | tf_op jit(solution)/shard_map/ppermute | solution.py:357

commit v6 on v5

--- a/solution.py
+++ b/solution.py
@@ -14,26 +14,24 @@
 HALF = 15
 LANES = 128
 META = 16
-BIG = 58
 PAD = 16
 NEG = -1e30
 SCALE = 1.0 / math.sqrt(HEAD_DIM)
 SCALE2 = SCALE * math.log2(math.e)
 VMEM = pl.BlockSpec(memory_space=pltpu.VMEM)
-HBM = pl.BlockSpec(memory_space=pltpu.HBM)
 SMEM = pl.BlockSpec(memory_space=pltpu.SMEM)
 F32 = jnp.float32
 BF16 = jnp.bfloat16
 
 
-def call(body, out_shapes, args, specs, flops, moved, exps=0, scratch=(), mib=24):
+def call(body, out_shapes, args, specs, flops, moved, exps=0, scratch=()):
     return pl.pallas_call(
         body,
         out_shape=out_shapes,
         in_specs=specs,
         out_specs=jax.tree.map(lambda _: VMEM, out_shapes),
         scratch_shapes=list(scratch),
-        compiler_params=pltpu.CompilerParams(vmem_limit_bytes=mib * 1024 * 1024),
+        compiler_params=pltpu.CompilerParams(vmem_limit_bytes=24 * 1024 * 1024),
         cost_estimate=pl.CostEstimate(flops=flops, bytes_accessed=moved, transcendentals=exps),
     )(*args)
 
@@ -73,37 +71,11 @@
     out_ref[3 * columns :, :] = meta.astype(BF16)
 
 
-def own_conv_body(
-    g_ref,
-    pre_ref,
-    taps_ref,
-    w_ref,
-    sum_out,
-    gate_out,
-    w_out,
-    x_ref,
-    moved_ref,
-    sum_ref,
-    g_low,
-    pre_low,
-    taps_low,
-    w_low,
-    sems,
-):
-    copies = [
-        pltpu.make_async_copy(g_ref, g_low, sems.at[0]),
-        pltpu.make_async_copy(taps_ref, taps_low, sems.at[1]),
-        pltpu.make_async_copy(pre_ref, pre_low, sems.at[2]),
-        pltpu.make_async_copy(w_ref, w_low, sems.at[3]),
-    ]
-    for copy in copies:
-        copy.start()
+def own_conv_body(g_ref, taps_ref, sum_out, x_ref, moved_ref, sum_ref):
     columns, rows = g_ref.shape
     x_ref[0:PAD, :] = jnp.zeros((PAD, columns), F32)
     x_ref[PAD + rows :, :] = jnp.zeros((PAD, columns), F32)
-    copies[0].wait()
-    copies[1].wait()
-    x_ref[PAD : PAD + rows, :] = g_low[...].astype(F32).T
+    x_ref[PAD : PAD + rows, :] = g_ref[...].astype(F32).T
     for shift in range(8):
         moved_ref[shift] = x_ref[shift : shift + rows + 24, :]
     step = 32
@@ -113,62 +85,21 @@
         acc = jnp.zeros((step, columns), F32)
         for k in range(KW):
             a, shift = divmod(PAD + HALF - k, 8)
-            acc = acc + taps_low[k : k + 1, :] * moved_ref[shift, pl.ds(at + 8 * a, step), :]
+            acc = acc + taps_ref[k : k + 1, :] * moved_ref[shift, pl.ds(at + 8 * a, step), :]
         sum_ref[pl.ds(at, step), :] = acc
         return carry
 
     lax.fori_loop(0, rows // step, block, 0)
     sum_out[...] = sum_ref[...].T
-    copies[2].wait()
-    value = pre_low[0].astype(F32)
-    gate = jax.nn.sigmoid(pre_low[1].astype(F32))
-    gate_out[0] = gate
-    gate_out[1] = value * gate * (1.0 - gate)
-    copies[3].wait()
-    for at in range(0, w_ref.shape[1], LANES):
-        w_out[at : at + LANES, :] = w_low[:, at : at + LANES].T
 
 
 def edge_body(
-    odd_ref,
-    two_ref,
-    one_ref,
-    taps_ref,
-    sum_ref,
-    gate_ref,
-    w_ref,
-    out_ref,
-    head,
-    tail,
-    two_low,
-    one_low,
-    taps_low,
-    sum_low,
-    gate_low,
-    w_low,
-    sems,
+    odd_ref, two_ref, one_ref, taps_ref, sum_ref, value_ref, gate_ref, w_ref, out_ref, head, tail
 ):
-    copies = [
-        pltpu.make_async_copy(ref, low, sems.at[i])
-        for i, (ref, low) in enumerate(
-            (
-                (two_ref, two_low),
-                (one_ref, one_low),
-                (taps_ref, taps_low),
-                (sum_ref, sum_low),
-                (gate_ref, gate_low),
-                (w_ref, w_low),
-            )
-        )
-    ]
-    for copy in copies:
-        copy.start()
     columns, rows = sum_ref.shape
     odd = odd_ref[0] > 0
-    for copy in copies[:3]:
-        copy.wait()
-    before = jnp.where(odd, one_low[:, rows - LANES :], two_low[:, rows - LANES :]).astype(F32)
-    after = jnp.where(odd, two_low[:, :LANES], one_low[:, :LANES]).astype(F32)
+    before = jnp.where(odd, one_ref[:, rows - LANES :], two_ref[:, rows - LANES :]).astype(F32)
+    after = jnp.where(odd, two_ref[:, :LANES], one_ref[:, :LANES]).astype(F32)
     blank = jnp.zeros((PAD, columns), F32)
     head[0:PAD, :] = before.T[LANES - PAD :, :]
     head[PAD:, :] = blank
@@ -176,20 +107,19 @@
     tail[PAD:, :] = after.T[:PAD, :]
     first, last = blank, blank
     for d in range(1, HALF + 1):
-        first = first + taps_low[HALF + d : HALF + d + 1, :] * head[PAD - d : 2 * PAD - d, :]
-        last = last + taps_low[HALF - d : HALF - d + 1, :] * tail[d : PAD + d, :]
+        first = first + taps_ref[HALF + d : HALF + d + 1, :] * head[PAD - d : 2 * PAD - d, :]
+        last = last + taps_ref[HALF - d : HALF - d + 1, :] * tail[d : PAD + d, :]
     rest = jnp.zeros((LANES - PAD, columns), F32)
     left = jnp.concatenate([first, rest], axis=0).T
     right = jnp.concatenate([rest, last], axis=0).T
-    copies[3].wait()
-    grad = sum_low[...] + jnp.concatenate([left, right], axis=1)
-    copies[4].wait()
-    low = jnp.concatenate([(grad * gate_low[half]).astype(BF16) for half in range(2)], axis=0)
-    copies[5].wait()
+    grad = sum_ref[...] + jnp.concatenate([left, right], axis=1)
+    low = jnp.concatenate(
+        [(grad * value_ref[...]).astype(BF16), (grad * gate_ref[...]).astype(BF16)], axis=0
+    )
     model = w_ref.shape[0]
     chunk = 256 if model % 256 == 0 else LANES
     for at in range(0, model, chunk):
-        out_ref[at : at + chunk, :] = dot_nn(w_low[at : at + chunk, :], low).astype(BF16)
+        out_ref[at : at + chunk, :] = dot_nn(w_ref[at : at + chunk, :], low).astype(BF16)
 
 
 def meta_of(ref, columns):
@@ -326,21 +256,21 @@
     return key_term, value_term
 
 
-def middle_body(columns, own_ref, two_ref, far_ref, grad_two_ref, grad_far_ref, acc_ref, acc_out):
+def middle_body(columns, own_ref, one_ref, far_ref, grad_one_ref, grad_far_ref, acc_ref, acc_out):
     for h in range(columns // HEAD_DIM):
         lo, hi = h * HEAD_DIM, (h + 1) * HEAD_DIM
         key_term, value_term = remote_terms(
-            columns, (2, 3), own_ref, (two_ref, far_ref), (grad_two_ref, grad_far_ref), h
+            columns, (1, 3), own_ref, (one_ref, far_ref), (grad_one_ref, grad_far_ref), h
         )
         acc_out[lo:hi, :] = acc_ref[lo:hi, :] + key_term
         acc_out[columns + lo : columns + hi, :] = acc_ref[columns + lo : columns + hi, :] + value_term
 
 
-def last_body(columns, own_ref, one_ref, grad_one_ref, acc_ref, key_out, value_out):
+def last_body(columns, own_ref, two_ref, grad_two_ref, acc_ref, key_out, value_out):
     for h in range(columns // HEAD_DIM):
         lo, hi = h * HEAD_DIM, (h + 1) * HEAD_DIM
         key_term, value_term = remote_terms(
-            columns, (1,), own_ref, (one_ref,), (grad_one_ref,), h
+            columns, (2,), own_ref, (two_ref,), (grad_two_ref,), h
         )
         key_out[lo:hi, :] = ((acc_ref[lo:hi, :] + key_term) * SCALE).astype(BF16)
         value_out[lo:hi, :] = (acc_ref[columns + lo : columns + hi, :] + value_term).astype(BF16)
@@ -379,46 +309,33 @@
         0,
         4 * message * row_count,
     )
-    conv, gate, w_turned = call(
+    conv = call(
         own_conv_body,
-        (shape(flat, F32), shape((2,) + flat, F32), shape((model, 2 * columns), BF16)),
-        (g_conv, pre, kernel, w_point.reshape(2 * columns, model)),
-        [HBM] * 4,
+        shape(flat, F32),
+        (g_conv, kernel),
+        [VMEM] * 2,
         2 * KW * columns * row_count,
-        8 * columns * model,
-        columns * row_count,
+        6 * columns * row_count,
+        0,
         (
             pltpu.VMEM((row_count + 2 * PAD, columns), F32),
             pltpu.VMEM((8, row_count + 24, columns), F32),
             pltpu.VMEM((row_count, columns), F32),
-            pltpu.VMEM(flat, BF16),
-            pltpu.VMEM((2,) + flat, BF16),
-            pltpu.VMEM((KW, columns), F32),
-            pltpu.VMEM((2 * columns, model), BF16),
-            pltpu.SemaphoreType.DMA((4,)),
         ),
-        mib=BIG,
-    )
+    )
+    wide = pre.astype(F32)
+    gate = jax.nn.sigmoid(wide[1])
+    slope = wide[0] * gate * (1.0 - gate)
+    w_turned = w_point.reshape(2 * columns, model).T
     point_grad = call(
         edge_body,
         shape((model, row_count), BF16),
-        (odd, *near, kernel, conv, gate, w_turned),
-        [SMEM] + [HBM] * 6,
+        (odd, *near, kernel, conv, gate, slope, w_turned),
+        [SMEM] + [VMEM] * 7,
         4 * columns * model * row_count,
         4 * columns * model,
         0,
-        (
-            pltpu.VMEM((2 * PAD, columns), F32),
-            pltpu.VMEM((2 * PAD, columns), F32),
-            pltpu.VMEM(flat, BF16),
-            pltpu.VMEM(flat, BF16),
-            pltpu.VMEM((KW, columns), F32),
-            pltpu.VMEM(flat, F32),
-            pltpu.VMEM((2,) + flat, F32),
-            pltpu.VMEM((model, 2 * columns), BF16),
-            pltpu.SemaphoreType.DMA((6,)),
-        ),
-        mib=BIG,
+        (pltpu.VMEM((2 * PAD, columns), F32), pltpu.VMEM((2 * PAD, columns), F32)),
     )
     parts = lax.all_to_all(
         point_grad.reshape(groups, columns, row_count), "head", 0, 0, tiled=False
@@ -451,7 +368,7 @@
     acc = call(
         functools.partial(middle_body, columns),
         shape((2 * columns, row_count), F32),
-        (own, two, far, grad_two, grad_far, acc),
+        (own, one, far, grad_one, grad_far, acc),
         [VMEM] * 6,
         8 * square,
         8 * message * row_count,
@@ -460,7 +377,7 @@
     grad_keys, grad_values = call(
         functools.partial(last_body, columns),
         (shape((columns, row_count), BF16), shape((columns, row_count), BF16)),
-        (own, one, grad_one, acc),
+        (own, two, grad_two, acc),
         [VMEM] * 4,
         4 * square,
         8 * message * row_count,

time: 79.1 us -> 76.5 us (0.967)
  Pallas kernels: 15.3 us -> 11.4 us
  other arithmetic: 0.12 us -> 1.2 us
  waiting for transfers between devices: 2.88 us -> 2.05 us
    pallas_call x7, Pallas kernels: 15.3 us -> 11.4 us  [call(): pl.pallas_call(body, out_shape=out_shapes, in_specs=specs, out_specs=jax....]
    convert_element_type x0 -> x1, other arithmetic: none -> 0.95 us  [per_device(): wide = pre.astype(F32)]
    ppermute x8, waiting for transfers between devices: 2.88 us -> 2.05 us  [exchange(): return lax.ppermute(value, 'ctx', pairs)]
  transfers between devices with their start and end apart: 9 -> 9, of which waited for: 2 -> 2; matrix products, arithmetic and copies ran while one was open for 0% -> 3% of each run, Pallas kernels for 11% -> 8%
where the time goes in v6:
time: 76.5 us; the launch traced here: 75.8 us
  starting transfers between devices  44 us (58%)
  blocking collectives  14.6 us (19%)
  Pallas kernels  11.4 us (15%)
  waiting for transfers between devices  2.05 us (3%)
  between operations  1.63 us (2%)
  other arithmetic  1.2 us (2%)
  local copies, waits for them, and re-layouts  0.89 us (1%)
    ppermute x8, starting transfers between devices, exchange(): return lax.ppermute(value, 'ctx', pairs)  38.3 us
    all_gather x1, blocking collectives, per_device(): stream_full = lax.all_gather(stream_grad, 'head', axis=0, tiled=True)  14.6 us
    pallas_call x7, Pallas kernels, call(): pl.pallas_call(body, out_shape=out_shapes, in_specs=specs, out_specs=jax....  11.4 us
    all_to_all x1, starting transfers between devices, per_device(): lax.all_to_all(point_grad.reshape(groups, columns, row_count), 'head', 0,...  5.73 us
    ppermute x8, waiting for transfers between devices, exchange(): return lax.ppermute(value, 'ctx', pairs)  2.05 us
  transfers between devices with their start and end apart: 9, of which 2 were waited for; matrix products, arithmetic and copies ran while one was open for 3% of the time, Pallas kernels for 8%

profile of v6, /device:TPU:1, one launch (start us, length us, event | category | flops | bytes accessed | tf_op | source)
XLA Modules:
  0.0 75.8 jit_solution(15326277832867056218)
XLA Ops:
  0.6 0.8 %collective-permute-start = (bf16[192,256]{1,0:T(8,128)(2,1)}, bf16[192,256]{1,0:T(8,128)(2,1)S(1)}, u32[]{:S(2)}, u32[]{:S(2)}) collective-permute-start(bf16[192,256]{1,0:T(8,128)(2,1)} %g_ref.1), channel_id=1, source_target_pairs={{8,16},{16,8},{24,32},{32,24},{40,48},{48,40},{56,64},{64,56},{72,... | collective-permute-start | bytes 294920 | tf_op jit(solution)/shard_map/ppermute | solution.py:287
  1.4 8.2 %collective-permute-start.1 = (bf16[192,256]{1,0:T(8,128)(2,1)}, bf16[192,256]{1,0:T(8,128)(2,1)S(1)}, u32[]{:S(2)}, u32[]{:S(2)}) collective-permute-start(bf16[192,256]{1,0:T(8,128)(2,1)} %g_ref.1), channel_id=1, source_target_pairs={{0,8},{8,0},{16,24},{24,16},{32,40},{40,32},{48,56},{56,48},{64,72... | collective-permute-start | bytes 294920 | tf_op jit(solution)/shard_map/ppermute | solution.py:287
  9.6 1.0 %convert_element_type.13 = f32[2,192,256]{2,1,0:T(8,128)S(1)} convert(bf16[2,192,256]{2,1,0:T(8,128)(2,1)} %param.12) | non-fusion elementwise | flops 98304 | bytes 589824 | tf_op jit(solution)/shard_map/convert_element_type | solution.py:326
  10.6 0.0 copy-start.1
  10.6 0.0 copy-start.5
  10.6 0.1 fusion.1.gate_ref
  10.7 0.1 fusion.5.value_ref
  10.8 0.7 copy.17
  11.5 1.3 %shard_map.138.sum_ref = f32[192,256]{1,0:T(8,128)S(1)} custom-call(bf16[192,256]{1,0:T(8,128)(2,1)S(1)} %copy-done.5, f32[31,192]{1,0:T(8,128)S(1)} %copy-done.1), custom_call_target="tpu_custom_call" | custom-call | flops 3047424 | bytes 294912 | tf_op jit(solution)/shard_map/pallas_call | solution.py:28
  12.9 0.0 copy-start.9
  12.9 0.0 copy-start.2
  12.9 0.0 copy-start.3
  12.9 0.0 copy-start.4
  12.9 1.7 %shard_map.139 = bf16[1536,256]{1,0:T(8,128)(2,1)} custom-call(s32[1]{0:T(128)} %bitcast.odd_ref, bf16[192,256]{1,0:T(8,128)(2,1)S(1)} %collective-permute-done.two_ref, bf16[192,256]{1,0:T(8,128)(2,1)S(1)} %collective-permute-done.1.one_ref, f32[31,192]{1,0:T(8,128)S(1)} %copy-done.1, f32[192,256]{1,0:T(8,128)S(1)} %shard_map.138.sum_ref, ...), custom_call_target="tpu_custom_call" | custom-call | flops 301989888 | bytes 1179648 | tf_op jit(solution)/shard_map/pallas_call | solution.py:28
  14.6 5.7 %all-to-all-start = ((bf16[8,192,256]{2,1,0:T(8,128)(2,1)}), bf16[8,192,256]{2,1,0:T(8,128)(2,1)S(1)}, u32[]{:S(2)}, u32[]{:S(2)}) async-start(bf16[8,192,256]{2,1,0:T(8,128)(2,1)} %bitcast.5), calls=%async_computation | async-start | bytes 1572864 | tf_op jit(solution)/shard_map/all_to_all | solution.py:340
  21.1 0.1 copy.18.mask_ref
  21.2 0.6 shard_map.140.own_ref
  21.8 13.1 %collective-permute-start.4 = (bf16[592,256]{1,0:T(8,128)(2,1)S(1)}, bf16[592,256]{1,0:T(8,128)(2,1)S(1)}, u32[]{:S(2)}, u32[]{:S(2)}) collective-permute-start(bf16[592,256]{1,0:T(8,128)(2,1)S(1)} %shard_map.140.own_ref), channel_id=1, source_target_pairs={{0,256},{8,264},{16,272},{24,280},{32,288},{40,296},{48,304},{56,3... | collective-permute-start | bytes 909320 | tf_op jit(solution)/shard_map/ppermute | solution.py:287
  34.9 3.0 %collective-permute-start.3 = (bf16[592,256]{1,0:T(8,128)(2,1)S(1)}, bf16[592,256]{1,0:T(8,128)(2,1)S(1)}, u32[]{:S(2)}, u32[]{:S(2)}) collective-permute-start(bf16[592,256]{1,0:T(8,128)(2,1)S(1)} %shard_map.140.own_ref), channel_id=1, source_target_pairs={{0,504},{8,16},{16,8},{24,32},{32,24},{40,48},{48,40},{56,64},{64,... | collective-permute-start | bytes 909320 | tf_op jit(solution)/shard_map/ppermute | solution.py:287
  38.0 1.9 %collective-permute-start.2 = (bf16[592,256]{1,0:T(8,128)(2,1)S(1)}, bf16[592,256]{1,0:T(8,128)(2,1)S(1)}, u32[]{:S(2)}, u32[]{:S(2)}) collective-permute-start(bf16[592,256]{1,0:T(8,128)(2,1)S(1)} %shard_map.140.own_ref), channel_id=1, source_target_pairs={{0,8},{8,0},{16,24},{24,16},{32,40},{40,32},{48,56},{56,48},{64,72... | collective-permute-start | bytes 909320 | tf_op jit(solution)/shard_map/ppermute | solution.py:287
  39.9 0.1 convert_reduce_fusion
  40.0 0.0 copy-start.7
  40.1 14.6 %all_gather.3.stream_ref = bf16[1536,256]{1,0:T(8,128)(2,1)S(1)} all-gather(bf16[192,256]{1,0:T(8,128)(2,1)S(1)} %add_convert_fusion), channel_id=1, replica_groups=mesh['ctx'=64,'head'=8] {'head'}, dimensions={0}, use_global_device_ids=true | all-gather | bytes 884736 | tf_op jit(solution)/shard_map/all_gather | solution.py:348
  54.7 1.1 %collective-permute-done.3.two_ref = bf16[592,256]{1,0:T(8,128)(2,1)S(1)} collective-permute-done((bf16[592,256]{1,0:T(8,128)(2,1)S(1)}, bf16[592,256]{1,0:T(8,128)(2,1)S(1)}, u32[]{:S(2)}, u32[]{:S(2)}) %collective-permute-start.3) | collective-permute-done | bytes 303136 | tf_op jit(solution)/shard_map/ppermute | solution.py:287
  55.8 2.1 %shard_map.141 = (bf16[208,256]{1,0:T(8,128)(2,1)S(1)}, f32[12,256,256]{2,1,0:T(8,128)S(1)}, f32[8,256]{1,0:T(8,128)S(1)}) custom-call(bf16[192,1536]{1,0:T(8,128)(2,1)S(1)} %copy-done, bf16[1536,256]{1,0:T(8,128)(2,1)S(1)} %all_gather.3.stream_ref, bf16[592,256]{1,0:T(8,128)(2,1)S(1)} %shard_map.140.own_ref, ...), custom_call_target="tpu_custom_call" | custom-call | flops 352321536 | bytes 1376256 | tf_op jit(solution)/shard_map/pallas_call | solution.py:28
  58.0 5.2 %collective-permute-start.7 = (bf16[208,256]{1,0:T(8,128)(2,1)S(1)}, bf16[208,256]{1,0:T(8,128)(2,1)S(1)}, u32[]{:S(2)}, u32[]{:S(2)}) collective-permute-start(bf16[208,256]{1,0:T(8,128)(2,1)S(1)} %get-tuple-element.13.grad_ref), channel_id=1, source_target_pairs={{0,256},{8,264},{16,272},{24,280},{32,288},{40,296},{48,304},{56,3... | collective-permute-start | bytes 319496 | tf_op jit(solution)/shard_map/ppermute | solution.py:287
  63.2 1.9 %collective-permute-start.6 = (bf16[208,256]{1,0:T(8,128)(2,1)S(1)}, bf16[208,256]{1,0:T(8,128)(2,1)S(1)}, u32[]{:S(2)}, u32[]{:S(2)}) collective-permute-start(bf16[208,256]{1,0:T(8,128)(2,1)S(1)} %get-tuple-element.13.grad_ref), channel_id=1, source_target_pairs={{0,8},{8,0},{16,24},{24,16},{32,40},{40,32},{48,56},{56,48},{64,72... | collective-permute-start | bytes 319496 | tf_op jit(solution)/shard_map/ppermute | solution.py:287
  65.1 4.1 %collective-permute-start.5 = (bf16[208,256]{1,0:T(8,128)(2,1)S(1)}, bf16[208,256]{1,0:T(8,128)(2,1)S(1)}, u32[]{:S(2)}, u32[]{:S(2)}) collective-permute-start(bf16[208,256]{1,0:T(8,128)(2,1)S(1)} %get-tuple-element.13.grad_ref), channel_id=1, source_target_pairs={{0,504},{8,16},{16,8},{24,32},{32,24},{40,48},{48,40},{56,64},{64,... | collective-permute-start | bytes 319496 | tf_op jit(solution)/shard_map/ppermute | solution.py:287
  69.3 2.7 %shard_map.142 = (bf16[192,256]{1,0:T(8,128)(2,1)}, f32[384,256]{1,0:T(8,128)S(1)}) custom-call(bf16[592,256]{1,0:T(8,128)(2,1)S(1)} %shard_map.140.own_ref, bf16[592,256]{1,0:T(8,128)(2,1)S(1)} %collective-permute-done.2.one_ref, bf16[592,256]{1,0:T(8,128)(2,1)S(1)} %collective-permute-done.3.two_ref, bf16[592,256]{1,0:T(8,128)(2,1)S(1)} %collective-permute-done.4.far_ref, ...), custom_call_target="tpu_custom_call" | custom-call | flops 301989888 | bytes 1212416 | tf_op jit(solution)/shard_map/pallas_call | solution.py:28
  72.0 1.3 %shard_map.143.acc_ref = f32[384,256]{1,0:T(8,128)S(1)} custom-call(bf16[592,256]{1,0:T(8,128)(2,1)S(1)} %shard_map.140.own_ref, bf16[592,256]{1,0:T(8,128)(2,1)S(1)} %collective-permute-done.2.one_ref, bf16[592,256]{1,0:T(8,128)(2,1)S(1)} %collective-permute-done.4.far_ref, bf16[208,256]{1,0:T(8,128)(2,1)S(1)} %collective-permute-done.6.grad_one_ref, ...), custom_call_target="tpu_custom_call" | custom-call | flops 201326592 | bytes 1212416 | tf_op jit(solution)/shard_map/pallas_call | solution.py:28
  73.4 0.9 %collective-permute-done.5.grad_two_ref = bf16[208,256]{1,0:T(8,128)(2,1)S(1)} collective-permute-done((bf16[208,256]{1,0:T(8,128)(2,1)S(1)}, bf16[208,256]{1,0:T(8,128)(2,1)S(1)}, u32[]{:S(2)}, u32[]{:S(2)}) %collective-permute-start.5) | collective-permute-done | bytes 106528 | tf_op jit(solution)/shard_map/ppermute | solution.py:287
  74.3 1.5 %shard_map.144 = (bf16[192,256]{1,0:T(8,128)(2,1)}, bf16[192,256]{1,0:T(8,128)(2,1)}) custom-call(bf16[592,256]{1,0:T(8,128)(2,1)S(1)} %shard_map.140.own_ref, bf16[592,256]{1,0:T(8,128)(2,1)S(1)} %collective-permute-done.3.two_ref, bf16[208,256]{1,0:T(8,128)(2,1)S(1)} %collective-permute-done.5.grad_two_ref, f32[384,256]{1,0:T(8,128)S(1)} %shard_map.143.acc_ref), custom_call_target="tpu_custom_call" | custom-call | flops 100663296 | bytes 1212416 | tf_op jit(solution)/shard_map/pallas_call | solution.py:28
  (21 shorter events, 0.1 us)
Async XLA Ops:
  0.6 10.1 %copy-start.6 = (bf16[2,192,1536]{2,1,0:T(8,128)(2,1)S(1)}, bf16[2,192,1536]{2,1,0:T(8,128)(2,1)}, u32[]{:S(2)}) copy-start(bf16[2,192,1536]{2,1,0:T(8,128)(2,1)} %param.14) | copy-start | bytes 3538948
  0.6 12.2 %collective-permute-start = (bf16[192,256]{1,0:T(8,128)(2,1)}, bf16[192,256]{1,0:T(8,128)(2,1)S(1)}, u32[]{:S(2)}, u32[]{:S(2)}) collective-permute-start(bf16[192,256]{1,0:T(8,128)(2,1)} %g_ref.1), channel_id=1, source_target_pairs={{8,16},{16,8},{24,32},{32,24},{40,48},{48,40},{56,64},{64,56},{72,... | collective-permute-start | bytes 294920 | tf_op jit(solution)/shard_map/ppermute | solution.py:287
  1.4 11.4 %collective-permute-start.1 = (bf16[192,256]{1,0:T(8,128)(2,1)}, bf16[192,256]{1,0:T(8,128)(2,1)S(1)}, u32[]{:S(2)}, u32[]{:S(2)}) collective-permute-start(bf16[192,256]{1,0:T(8,128)(2,1)} %g_ref.1), channel_id=1, source_target_pairs={{0,8},{8,0},{16,24},{24,16},{32,40},{40,32},{48,56},{56,48},{64,72... | collective-permute-start | bytes 294920 | tf_op jit(solution)/shard_map/ppermute | solution.py:287
  10.6 0.9 %copy-start.1 = (f32[31,192]{1,0:T(8,128)S(1)}, f32[31,192]{1,0:T(8,128)}, u32[]{:S(2)}) copy-start(f32[31,192]{1,0:T(8,128)} %taps_ref.3) | copy-start | bytes 71428
  10.6 0.9 %copy-start.5 = (bf16[192,256]{1,0:T(8,128)(2,1)S(1)}, bf16[192,256]{1,0:T(8,128)(2,1)}, u32[]{:S(2)}) copy-start(bf16[192,256]{1,0:T(8,128)(2,1)} %g_ref.1) | copy-start | bytes 294916
  12.9 8.2 %copy-start.9 = (s32[2,4,2]{1,2,0:T(2,128)S(1)}, s32[2,4,2]{1,2,0:T(2,128)}, u32[]{:S(2)}) copy-start(s32[2,4,2]{1,2,0:T(2,128)} %param.20) | copy-start | bytes 196
  12.9 8.3 %copy-start.2 = (bf16[256,192]{0,1:T(8,128)(2,1)S(1)}, bf16[256,192]{0,1:T(8,128)(2,1)}, u32[]{:S(2)}) copy-start(bf16[256,192]{0,1:T(8,128)(2,1)} %param.18) | copy-start | bytes 294916
  12.9 8.3 %copy-start.3 = (bf16[256,192]{0,1:T(8,128)(2,1)S(1)}, bf16[256,192]{0,1:T(8,128)(2,1)}, u32[]{:S(2)}) copy-start(bf16[256,192]{0,1:T(8,128)(2,1)} %param.19) | copy-start | bytes 294916
  12.9 8.3 %copy-start.4 = (bf16[256,192]{0,1:T(8,128)(2,1)S(1)}, bf16[256,192]{0,1:T(8,128)(2,1)}, u32[]{:S(2)}) copy-start(bf16[256,192]{0,1:T(8,128)(2,1)} %param.17) | copy-start | bytes 294916
  14.6 25.4 %copy-start.8 = (bf16[192,256]{1,0:T(8,128)(2,1)S(1)}, bf16[192,256]{1,0:T(8,128)(2,1)}, u32[]{:S(2)}) copy-start(bf16[192,256]{1,0:T(8,128)(2,1)} %param.15) | copy-start | bytes 294916
  14.6 25.3 %all-to-all-start = ((bf16[8,192,256]{2,1,0:T(8,128)(2,1)}), bf16[8,192,256]{2,1,0:T(8,128)(2,1)S(1)}, u32[]{:S(2)}, u32[]{:S(2)}) async-start(bf16[8,192,256]{2,1,0:T(8,128)(2,1)} %bitcast.5), calls=%async_computation | async-start | bytes 1572864 | tf_op jit(solution)/shard_map/all_to_all | solution.py:340
  20.3 35.5 %copy-start = (bf16[192,1536]{1,0:T(8,128)(2,1)S(1)}, bf16[192,1536]{1,0:T(8,128)(2,1)}, u32[]{:S(2)}) copy-start(bf16[192,1536]{1,0:T(8,128)(2,1)} %w_ref.1) | copy-start | bytes 1769476
  21.8 32.9 %collective-permute-start.4 = (bf16[592,256]{1,0:T(8,128)(2,1)S(1)}, bf16[592,256]{1,0:T(8,128)(2,1)S(1)}, u32[]{:S(2)}, u32[]{:S(2)}) collective-permute-start(bf16[592,256]{1,0:T(8,128)(2,1)S(1)} %shard_map.140.own_ref), channel_id=1, source_target_pairs={{0,256},{8,264},{16,272},{24,280},{32,288},{40,296},{48,304},{56,3... | collective-permute-start | bytes 909320 | tf_op jit(solution)/shard_map/ppermute | solution.py:287
  34.9 20.9 %collective-permute-start.3 = (bf16[592,256]{1,0:T(8,128)(2,1)S(1)}, bf16[592,256]{1,0:T(8,128)(2,1)S(1)}, u32[]{:S(2)}, u32[]{:S(2)}) collective-permute-start(bf16[592,256]{1,0:T(8,128)(2,1)S(1)} %shard_map.140.own_ref), channel_id=1, source_target_pairs={{0,504},{8,16},{16,8},{24,32},{32,24},{40,48},{48,40},{56,64},{64,... | collective-permute-start | bytes 909320 | tf_op jit(solution)/shard_map/ppermute | solution.py:287
  38.0 17.9 %collective-permute-start.2 = (bf16[592,256]{1,0:T(8,128)(2,1)S(1)}, bf16[592,256]{1,0:T(8,128)(2,1)S(1)}, u32[]{:S(2)}, u32[]{:S(2)}) collective-permute-start(bf16[592,256]{1,0:T(8,128)(2,1)S(1)} %shard_map.140.own_ref), channel_id=1, source_target_pairs={{0,8},{8,0},{16,24},{24,16},{32,40},{40,32},{48,56},{56,48},{64,72... | collective-permute-start | bytes 909320 | tf_op jit(solution)/shard_map/ppermute | solution.py:287
  40.0 17.9 %copy-start.7 = (bf16[192,256]{1,0:T(8,128)(2,1)}, bf16[192,256]{1,0:T(8,128)(2,1)S(1)}, u32[]{:S(2)}) copy-start(bf16[192,256]{1,0:T(8,128)(2,1)S(1)} %add_convert_fusion) | copy-start | bytes 294916
  58.0 14.0 %collective-permute-start.7 = (bf16[208,256]{1,0:T(8,128)(2,1)S(1)}, bf16[208,256]{1,0:T(8,128)(2,1)S(1)}, u32[]{:S(2)}, u32[]{:S(2)}) collective-permute-start(bf16[208,256]{1,0:T(8,128)(2,1)S(1)} %get-tuple-element.13.grad_ref), channel_id=1, source_target_pairs={{0,256},{8,264},{16,272},{24,280},{32,288},{40,296},{48,304},{56,3... | collective-permute-start | bytes 319496 | tf_op jit(solution)/shard_map/ppermute | solution.py:287
  63.2 8.8 %collective-permute-start.6 = (bf16[208,256]{1,0:T(8,128)(2,1)S(1)}, bf16[208,256]{1,0:T(8,128)(2,1)S(1)}, u32[]{:S(2)}, u32[]{:S(2)}) collective-permute-start(bf16[208,256]{1,0:T(8,128)(2,1)S(1)} %get-tuple-element.13.grad_ref), channel_id=1, source_target_pairs={{0,8},{8,0},{16,24},{24,16},{32,40},{40,32},{48,56},{56,48},{64,72... | collective-permute-start | bytes 319496 | tf_op jit(solution)/shard_map/ppermute | solution.py:287
  65.1 9.1 %collective-permute-start.5 = (bf16[208,256]{1,0:T(8,128)(2,1)S(1)}, bf16[208,256]{1,0:T(8,128)(2,1)S(1)}, u32[]{:S(2)}, u32[]{:S(2)}) collective-permute-start(bf16[208,256]{1,0:T(8,128)(2,1)S(1)} %get-tuple-element.13.grad_ref), channel_id=1, source_target_pairs={{0,504},{8,16},{16,8},{24,32},{32,24},{40,48},{48,40},{56,64},{64,... | collective-permute-start | bytes 319496 | tf_op jit(solution)/shard_map/ppermute | solution.py:287

commit v7 on v6

--- a/solution.py
+++ b/solution.py
@@ -48,8 +48,30 @@
     return lax.dot_general(a, b, (((1,), (0,)), ((), ())), preferred_element_type=F32)
 
 
-def pack_body(odd_ref, mask_ref, count_ref, keys_ref, values_ref, queries_ref, out_ref):
-    columns, rows = keys_ref.shape
+def own_body(
+    odd_ref,
+    mask_ref,
+    count_ref,
+    keys_ref,
+    values_ref,
+    queries_ref,
+    g_ref,
+    pre_ref,
+    taps_ref,
+    out_ref,
+    sum_out,
+    gate_out,
+    slope_out,
+    x_ref,
+    moved_ref,
+    sum_ref,
+):
+    columns, rows = g_ref.shape
+    x_ref[0:PAD, :] = jnp.zeros((PAD, columns), F32)
+    x_ref[PAD + rows :, :] = jnp.zeros((PAD, columns), F32)
+    x_ref[PAD : PAD + rows, :] = g_ref[...].astype(F32).T
+    for shift in range(8):
+        moved_ref[shift] = x_ref[shift : shift + rows + 24, :]
     out_ref[0:columns, :] = keys_ref[...]
     out_ref[columns : 2 * columns, :] = values_ref[...]
     out_ref[2 * columns : 3 * columns, :] = queries_ref[...]
@@ -69,15 +91,6 @@
                 row == 1 + 2 * slot + kb, jnp.where(first, picked[0], picked[1]), meta
             )
     out_ref[3 * columns :, :] = meta.astype(BF16)
-
-
-def own_conv_body(g_ref, taps_ref, sum_out, x_ref, moved_ref, sum_ref):
-    columns, rows = g_ref.shape
-    x_ref[0:PAD, :] = jnp.zeros((PAD, columns), F32)
-    x_ref[PAD + rows :, :] = jnp.zeros((PAD, columns), F32)
-    x_ref[PAD : PAD + rows, :] = g_ref[...].astype(F32).T
-    for shift in range(8):
-        moved_ref[shift] = x_ref[shift : shift + rows + 24, :]
     step = 32
 
     def block(i, carry):
@@ -91,10 +104,13 @@
 
     lax.fori_loop(0, rows // step, block, 0)
     sum_out[...] = sum_ref[...].T
+    gate = jax.nn.sigmoid(pre_ref[1].astype(F32))
+    gate_out[...] = gate
+    slope_out[...] = pre_ref[0].astype(F32) * gate * (1.0 - gate)
 
 
 def edge_body(
-    odd_ref, two_ref, one_ref, taps_ref, sum_ref, value_ref, gate_ref, w_ref, out_ref, head, tail
+    odd_ref, two_ref, one_ref, taps_ref, sum_ref, gate_ref, slope_ref, w_ref, out_ref, head, tail
 ):
     columns, rows = sum_ref.shape
     odd = odd_ref[0] > 0
@@ -114,7 +130,7 @@
     right = jnp.concatenate([rest, last], axis=0).T
     grad = sum_ref[...] + jnp.concatenate([left, right], axis=1)
     low = jnp.concatenate(
-        [(grad * value_ref[...]).astype(BF16), (grad * gate_ref[...]).astype(BF16)], axis=0
+        [(grad * gate_ref[...]).astype(BF16), (grad * slope_ref[...]).astype(BF16)], axis=0
     )
     model = w_ref.shape[0]
     chunk = 256 if model % 256 == 0 else LANES
@@ -301,31 +317,20 @@
     odd = (lax.axis_index("ctx") % 2).astype(jnp.int32).reshape(1)
     near = [exchange(g_conv, slot, closed=False) for slot in (2, 1)]
     flat = (columns, row_count)
-    own = call(
-        pack_body,
-        shape((message, row_count), BF16),
-        (odd, block_mask, counts, keys, values, queries),
-        [SMEM] * 3 + [VMEM] * 3,
-        0,
-        4 * message * row_count,
-    )
-    conv = call(
-        own_conv_body,
-        shape(flat, F32),
-        (g_conv, kernel),
-        [VMEM] * 2,
+    own, conv, gate, slope = call(
+        own_body,
+        (shape((message, row_count), BF16),) + (shape(flat, F32),) * 3,
+        (odd, block_mask, counts, keys, values, queries, g_conv, pre, kernel),
+        [SMEM] * 3 + [VMEM] * 6,
         2 * KW * columns * row_count,
-        6 * columns * row_count,
-        0,
+        6 * message * row_count,
+        columns * row_count,
         (
             pltpu.VMEM((row_count + 2 * PAD, columns), F32),
             pltpu.VMEM((8, row_count + 24, columns), F32),
             pltpu.VMEM((row_count, columns), F32),
         ),
     )
-    wide = pre.astype(F32)
-    gate = jax.nn.sigmoid(wide[1])
-    slope = wide[0] * gate * (1.0 - gate)
     w_turned = w_point.reshape(2 * columns, model).T
     point_grad = call(
         edge_body,
@@ -341,8 +346,7 @@
         point_grad.reshape(groups, columns, row_count), "head", 0, 0, tiled=False
     )
     own, _ = lax.optimization_barrier((own, point_grad))
-    one, two = [exchange(own, slot) for slot in (1, 2)]
-    far = exchange(own, 3)
+    two, one, far = [exchange(own, slot) for slot in (2, 1, 3)]
     piece = jnp.sum(parts.astype(F32), axis=0)
     stream_grad = (g_out.astype(F32) + piece).astype(BF16)
     stream_full = lax.all_gather(stream_grad, "head", axis=0, tiled=True)

time: 76.5 us -> 77.1 us (level)
  waiting for transfers between devices: 2.05 us -> 3.67 us
  local copies, waits for them, and re-layouts: 0.89 us -> 2.51 us
  starting transfers between devices: 44 us -> 42.8 us
  other arithmetic: 1.2 us -> 0.12 us
    ppermute x8, waiting for transfers between devices: 2.05 us -> 3.67 us  [exchange(): return lax.ppermute(value, 'ctx', pairs)]
    ppermute x8, starting transfers between devices: 38.3 us -> 37.1 us  [exchange(): return lax.ppermute(value, 'ctx', pairs)]
    reshape x1, local copies, waits for them, and re-layouts: 0.74 us -> 1.7 us  [per_device(): w_turned = w_point.reshape(2 * columns, model).T]
    convert_element_type x1 -> x0, other arithmetic: 0.95 us -> none  [per_device(): wide = pre.astype(F32)]
    pallas_call x7 -> x6, Pallas kernels: 11.4 us -> 11.4 us  [call(): pl.pallas_call(body, out_shape=out_shapes, in_specs=specs, out_specs=jax....]
where the time goes in v7:
time: 77.1 us; the launch traced here: 76.7 us
  starting transfers between devices  42.8 us (56%)
  blocking collectives  14.6 us (19%)
  Pallas kernels  11.4 us (15%)
  waiting for transfers between devices  3.67 us (5%)
  local copies, waits for them, and re-layouts  2.51 us (3%)
  between operations  1.54 us (2%)
    ppermute x8, starting transfers between devices, exchange(): return lax.ppermute(value, 'ctx', pairs)  37.1 us
    all_gather x1, blocking collectives, per_device(): stream_full = lax.all_gather(stream_grad, 'head', axis=0, tiled=True)  14.6 us
    pallas_call x6, Pallas kernels, call(): pl.pallas_call(body, out_shape=out_shapes, in_specs=specs, out_specs=jax....  11.4 us
    all_to_all x1, starting transfers between devices, per_device(): lax.all_to_all(point_grad.reshape(groups, columns, row_count), 'head', 0,...  5.66 us
    ppermute x8, waiting for transfers between devices, exchange(): return lax.ppermute(value, 'ctx', pairs)  3.67 us
    reshape x1, local copies, waits for them, and re-layouts, per_device(): w_turned = w_point.reshape(2 * columns, model).T  1.7 us
  transfers between devices with their start and end apart: 9, of which 2 were waited for; matrix products, arithmetic and copies ran while one was open for 3% of the time, Pallas kernels for 8%

profile of v7, /device:TPU:1, one launch (start us, length us, event | category | flops | bytes accessed | tf_op | source)
XLA Modules:
  0.0 76.7 jit_solution(18067668373816044426)
XLA Ops:
  0.7 0.8 %collective-permute-start = (bf16[192,256]{1,0:T(8,128)(2,1)}, bf16[192,256]{1,0:T(8,128)(2,1)S(1)}, u32[]{:S(2)}, u32[]{:S(2)}) collective-permute-start(bf16[192,256]{1,0:T(8,128)(2,1)} %g_ref.1), channel_id=1, source_target_pairs={{8,16},{16,8},{24,32},{32,24},{40,48},{48,40},{56,64},{64,56},{72,... | collective-permute-start | bytes 294920 | tf_op jit(solution)/shard_map/ppermute | solution.py:303
  1.5 8.2 %collective-permute-start.1 = (bf16[192,256]{1,0:T(8,128)(2,1)}, bf16[192,256]{1,0:T(8,128)(2,1)S(1)}, u32[]{:S(2)}, u32[]{:S(2)}) collective-permute-start(bf16[192,256]{1,0:T(8,128)(2,1)} %g_ref.1), channel_id=1, source_target_pairs={{0,8},{8,0},{16,24},{24,16},{32,40},{40,32},{48,56},{56,48},{64,72... | collective-permute-start | bytes 294920 | tf_op jit(solution)/shard_map/ppermute | solution.py:303
  10.3 0.8 %copy.17.mask_ref = s32[2,4,2]{2,1,0:T(4,128)S(1)} copy(s32[2,4,2]{1,2,0:T(2,128)} %param.20) | data formatting | bytes 128 | tf_op args[9]
  11.1 1.7 %copy.18 = bf16[384,1536]{0,1:T(8,128)(2,1)S(1)} copy(bf16[384,1536]{1,0:T(8,128)(2,1)} %bitcast.15) | data formatting | bytes 2359296 | tf_op jit(solution)/shard_map/reshape | solution.py:334
  12.8 0.0 copy-done.6
  12.8 0.0 copy-done.2
  12.8 0.0 copy-done.4
  12.9 2.0 %shard_map.138 = (bf16[592,256]{1,0:T(8,128)(2,1)S(1)}, f32[192,256]{1,0:T(8,128)S(1)}, f32[192,256]{1,0:T(8,128)S(1)}, f32[192,256]{1,0:T(8,128)S(1)}) custom-call(s32[1]{0:T(128)} %bitcast.odd_ref, s32[2,4,2]{2,1,0:T(4,128)S(1)} %copy.17.mask_ref, s32[1]{0:T(128)S(6)} %copy.19.count_ref, bf16[192,256]{1,0:T(8,128)(2,1)S(1)} %bitcast.12, ...), custom_call_target="tpu_custom_call" | custom-call | flops 3047424 | bytes 909312 | tf_op jit(solution)/shard_map/pallas_call | solution.py:28
  14.8 0.0 collective-permute-done.two_ref
  14.9 0.0 collective-permute-done.1.one_ref
  14.9 1.7 %shard_map.139 = bf16[1536,256]{1,0:T(8,128)(2,1)} custom-call(s32[1]{0:T(128)} %bitcast.odd_ref, bf16[192,256]{1,0:T(8,128)(2,1)S(1)} %collective-permute-done.two_ref, bf16[192,256]{1,0:T(8,128)(2,1)S(1)} %collective-permute-done.1.one_ref, f32[31,192]{1,0:T(8,128)S(1)} %copy-done.2, f32[192,256]{1,0:T(8,128)S(1)} %get-tuple-element.16.sum_ref, ...), custom_call_target="tpu_custom_call" | custom-call | flops 301989888 | bytes 1179648 | tf_op jit(solution)/shard_map/pallas_call | solution.py:28
  16.6 5.7 %all-to-all-start = ((bf16[8,192,256]{2,1,0:T(8,128)(2,1)}), bf16[8,192,256]{2,1,0:T(8,128)(2,1)S(1)}, u32[]{:S(2)}, u32[]{:S(2)}) async-start(bf16[8,192,256]{2,1,0:T(8,128)(2,1)} %bitcast.6), calls=%async_computation | async-start | bytes 1572864 | tf_op jit(solution)/shard_map/all_to_all | solution.py:345
  22.2 11.6 %collective-permute-start.4 = (bf16[592,256]{1,0:T(8,128)(2,1)S(1)}, bf16[592,256]{1,0:T(8,128)(2,1)S(1)}, u32[]{:S(2)}, u32[]{:S(2)}) collective-permute-start(bf16[592,256]{1,0:T(8,128)(2,1)S(1)} %get-tuple-element.20.own_ref), channel_id=1, source_target_pairs={{0,256},{8,264},{16,272},{24,280},{32,288},{40,296},{48,304},{56,3... | collective-permute-start | bytes 909320 | tf_op jit(solution)/shard_map/ppermute | solution.py:303
  33.9 2.7 %collective-permute-start.3 = (bf16[592,256]{1,0:T(8,128)(2,1)S(1)}, bf16[592,256]{1,0:T(8,128)(2,1)S(1)}, u32[]{:S(2)}, u32[]{:S(2)}) collective-permute-start(bf16[592,256]{1,0:T(8,128)(2,1)S(1)} %get-tuple-element.20.own_ref), channel_id=1, source_target_pairs={{0,504},{8,16},{16,8},{24,32},{32,24},{40,48},{48,40},{56,64},{64,... | collective-permute-start | bytes 909320 | tf_op jit(solution)/shard_map/ppermute | solution.py:303
  36.6 2.8 %collective-permute-start.2 = (bf16[592,256]{1,0:T(8,128)(2,1)S(1)}, bf16[592,256]{1,0:T(8,128)(2,1)S(1)}, u32[]{:S(2)}, u32[]{:S(2)}) collective-permute-start(bf16[592,256]{1,0:T(8,128)(2,1)S(1)} %get-tuple-element.20.own_ref), channel_id=1, source_target_pairs={{0,8},{8,0},{16,24},{24,16},{32,40},{40,32},{48,56},{56,48},{64,72... | collective-permute-start | bytes 909320 | tf_op jit(solution)/shard_map/ppermute | solution.py:303
  39.5 0.0 all-to-all-done
  39.5 0.1 convert_reduce_fusion
  39.6 0.0 copy-start.7
  39.6 14.6 %all_gather.3.stream_ref = bf16[1536,256]{1,0:T(8,128)(2,1)S(1)} all-gather(bf16[192,256]{1,0:T(8,128)(2,1)S(1)} %add_convert_fusion), channel_id=1, replica_groups=mesh['ctx'=64,'head'=8] {'head'}, dimensions={0}, use_global_device_ids=true | all-gather | bytes 884736 | tf_op jit(solution)/shard_map/all_gather | solution.py:352
  54.3 0.0 collective-permute-done.4.far_ref
  54.3 0.9 %collective-permute-done.3.two_ref = bf16[592,256]{1,0:T(8,128)(2,1)S(1)} collective-permute-done((bf16[592,256]{1,0:T(8,128)(2,1)S(1)}, bf16[592,256]{1,0:T(8,128)(2,1)S(1)}, u32[]{:S(2)}, u32[]{:S(2)}) %collective-permute-start.3) | collective-permute-done | bytes 303136 | tf_op jit(solution)/shard_map/ppermute | solution.py:303
  55.2 0.0 collective-permute-done.2.one_ref
  55.2 2.1 %shard_map.140 = (bf16[208,256]{1,0:T(8,128)(2,1)S(1)}, f32[12,256,256]{2,1,0:T(8,128)S(1)}, f32[8,256]{1,0:T(8,128)S(1)}) custom-call(bf16[192,1536]{1,0:T(8,128)(2,1)S(1)} %copy-done, bf16[1536,256]{1,0:T(8,128)(2,1)S(1)} %all_gather.3.stream_ref, bf16[592,256]{1,0:T(8,128)(2,1)S(1)} %get-tuple-element.20.own_ref, ...), custom_call_target="tpu_custom_call" | custom-call | flops 352321536 | bytes 1376256 | tf_op jit(solution)/shard_map/pallas_call | solution.py:28
  57.3 5.7 %collective-permute-start.7 = (bf16[208,256]{1,0:T(8,128)(2,1)S(1)}, bf16[208,256]{1,0:T(8,128)(2,1)S(1)}, u32[]{:S(2)}, u32[]{:S(2)}) collective-permute-start(bf16[208,256]{1,0:T(8,128)(2,1)S(1)} %get-tuple-element.21.grad_ref), channel_id=1, source_target_pairs={{0,256},{8,264},{16,272},{24,280},{32,288},{40,296},{48,304},{56,3... | collective-permute-start | bytes 319496 | tf_op jit(solution)/shard_map/ppermute | solution.py:303
  63.1 3.3 %collective-permute-start.6 = (bf16[208,256]{1,0:T(8,128)(2,1)S(1)}, bf16[208,256]{1,0:T(8,128)(2,1)S(1)}, u32[]{:S(2)}, u32[]{:S(2)}) collective-permute-start(bf16[208,256]{1,0:T(8,128)(2,1)S(1)} %get-tuple-element.21.grad_ref), channel_id=1, source_target_pairs={{0,8},{8,0},{16,24},{24,16},{32,40},{40,32},{48,56},{56,48},{64,72... | collective-permute-start | bytes 319496 | tf_op jit(solution)/shard_map/ppermute | solution.py:303
  66.3 1.9 %collective-permute-start.5 = (bf16[208,256]{1,0:T(8,128)(2,1)S(1)}, bf16[208,256]{1,0:T(8,128)(2,1)S(1)}, u32[]{:S(2)}, u32[]{:S(2)}) collective-permute-start(bf16[208,256]{1,0:T(8,128)(2,1)S(1)} %get-tuple-element.21.grad_ref), channel_id=1, source_target_pairs={{0,504},{8,16},{16,8},{24,32},{32,24},{40,48},{48,40},{56,64},{64,... | collective-permute-start | bytes 319496 | tf_op jit(solution)/shard_map/ppermute | solution.py:303
  68.3 2.7 %shard_map.141 = (bf16[192,256]{1,0:T(8,128)(2,1)}, f32[384,256]{1,0:T(8,128)S(1)}) custom-call(bf16[592,256]{1,0:T(8,128)(2,1)S(1)} %get-tuple-element.20.own_ref, bf16[592,256]{1,0:T(8,128)(2,1)S(1)} %collective-permute-done.2.one_ref, bf16[592,256]{1,0:T(8,128)(2,1)S(1)} %collective-permute-done.3.two_ref, ...), custom_call_target="tpu_custom_call" | custom-call | flops 301989888 | bytes 1212416 | tf_op jit(solution)/shard_map/pallas_call | solution.py:28
  71.0 0.0 collective-permute-done.7.grad_far_ref
  71.0 0.0 collective-permute-done.6.grad_one_ref
  71.0 1.3 %shard_map.142.acc_ref = f32[384,256]{1,0:T(8,128)S(1)} custom-call(bf16[592,256]{1,0:T(8,128)(2,1)S(1)} %get-tuple-element.20.own_ref, bf16[592,256]{1,0:T(8,128)(2,1)S(1)} %collective-permute-done.2.one_ref, bf16[592,256]{1,0:T(8,128)(2,1)S(1)} %collective-permute-done.4.far_ref, bf16[208,256]{1,0:T(8,128)(2,1)S(1)} %collective-permute-done.6.grad_one_ref, ...), custom_call_target="tpu_custom_call" | custom-call | flops 201326592 | bytes 1212416 | tf_op jit(solution)/shard_map/pallas_call | solution.py:28
  72.4 2.8 %collective-permute-done.5.grad_two_ref = bf16[208,256]{1,0:T(8,128)(2,1)S(1)} collective-permute-done((bf16[208,256]{1,0:T(8,128)(2,1)S(1)}, bf16[208,256]{1,0:T(8,128)(2,1)S(1)}, u32[]{:S(2)}, u32[]{:S(2)}) %collective-permute-start.5) | collective-permute-done | bytes 106528 | tf_op jit(solution)/shard_map/ppermute | solution.py:303
  75.1 1.5 %shard_map.143 = (bf16[192,256]{1,0:T(8,128)(2,1)}, bf16[192,256]{1,0:T(8,128)(2,1)}) custom-call(bf16[592,256]{1,0:T(8,128)(2,1)S(1)} %get-tuple-element.20.own_ref, bf16[592,256]{1,0:T(8,128)(2,1)S(1)} %collective-permute-done.3.two_ref, bf16[208,256]{1,0:T(8,128)(2,1)S(1)} %collective-permute-done.5.grad_two_ref, f32[384,256]{1,0:T(8,128)S(1)} %shard_map.142.acc_ref), custom_call_target="tpu_custom_call" | custom-call | flops 100663296 | bytes 1212416 | tf_op jit(solution)/shard_map/pallas_call | solution.py:28
  (15 shorter events, 0.0 us)
Async XLA Ops:
  0.6 12.2 %copy-start.6 = (bf16[192,256]{1,0:T(8,128)(2,1)S(1)}, bf16[192,256]{1,0:T(8,128)(2,1)}, u32[]{:S(2)}) copy-start(bf16[192,256]{1,0:T(8,128)(2,1)} %g_ref.1) | copy-start | bytes 294916
  0.6 12.2 %copy-start.2 = (f32[31,192]{1,0:T(8,128)S(1)}, f32[31,192]{1,0:T(8,128)}, u32[]{:S(2)}) copy-start(f32[31,192]{1,0:T(8,128)} %taps_ref.3) | copy-start | bytes 71428
  0.7 12.2 %copy-start.4 = (bf16[256,192]{0,1:T(8,128)(2,1)S(1)}, bf16[256,192]{0,1:T(8,128)(2,1)}, u32[]{:S(2)}) copy-start(bf16[256,192]{0,1:T(8,128)(2,1)} %param.19) | copy-start | bytes 294916
  0.7 12.2 %copy-start.3 = (bf16[256,192]{0,1:T(8,128)(2,1)S(1)}, bf16[256,192]{0,1:T(8,128)(2,1)}, u32[]{:S(2)}) copy-start(bf16[256,192]{0,1:T(8,128)(2,1)} %param.18) | copy-start | bytes 294916
  0.7 12.2 %copy-start.5 = (bf16[256,192]{0,1:T(8,128)(2,1)S(1)}, bf16[256,192]{0,1:T(8,128)(2,1)}, u32[]{:S(2)}) copy-start(bf16[256,192]{0,1:T(8,128)(2,1)} %param.17) | copy-start | bytes 294916
  0.7 12.2 %copy-start.1 = (bf16[2,192,256]{2,1,0:T(8,128)(2,1)S(1)}, bf16[2,192,256]{2,1,0:T(8,128)(2,1)}, u32[]{:S(2)}) copy-start(bf16[2,192,256]{2,1,0:T(8,128)(2,1)} %pre_ref.1) | copy-start | bytes 589828
  0.7 14.2 %collective-permute-start = (bf16[192,256]{1,0:T(8,128)(2,1)}, bf16[192,256]{1,0:T(8,128)(2,1)S(1)}, u32[]{:S(2)}, u32[]{:S(2)}) collective-permute-start(bf16[192,256]{1,0:T(8,128)(2,1)} %g_ref.1), channel_id=1, source_target_pairs={{8,16},{16,8},{24,32},{32,24},{40,48},{48,40},{56,64},{64,56},{72,... | collective-permute-start | bytes 294920 | tf_op jit(solution)/shard_map/ppermute | solution.py:303
  1.5 13.4 %collective-permute-start.1 = (bf16[192,256]{1,0:T(8,128)(2,1)}, bf16[192,256]{1,0:T(8,128)(2,1)S(1)}, u32[]{:S(2)}, u32[]{:S(2)}) collective-permute-start(bf16[192,256]{1,0:T(8,128)(2,1)} %g_ref.1), channel_id=1, source_target_pairs={{0,8},{8,0},{16,24},{24,16},{32,40},{40,32},{48,56},{56,48},{64,72... | collective-permute-start | bytes 294920 | tf_op jit(solution)/shard_map/ppermute | solution.py:303
  16.6 23.0 %copy-start.8 = (bf16[192,256]{1,0:T(8,128)(2,1)S(1)}, bf16[192,256]{1,0:T(8,128)(2,1)}, u32[]{:S(2)}) copy-start(bf16[192,256]{1,0:T(8,128)(2,1)} %param.15) | copy-start | bytes 294916
  16.6 38.6 %copy-start = (bf16[192,1536]{1,0:T(8,128)(2,1)S(1)}, bf16[192,1536]{1,0:T(8,128)(2,1)}, u32[]{:S(2)}) copy-start(bf16[192,1536]{1,0:T(8,128)(2,1)} %w_ref.1) | copy-start | bytes 1769476
  16.6 22.9 %all-to-all-start = ((bf16[8,192,256]{2,1,0:T(8,128)(2,1)}), bf16[8,192,256]{2,1,0:T(8,128)(2,1)S(1)}, u32[]{:S(2)}, u32[]{:S(2)}) async-start(bf16[8,192,256]{2,1,0:T(8,128)(2,1)} %bitcast.6), calls=%async_computation | async-start | bytes 1572864 | tf_op jit(solution)/shard_map/all_to_all | solution.py:345
  22.2 32.0 %collective-permute-start.4 = (bf16[592,256]{1,0:T(8,128)(2,1)S(1)}, bf16[592,256]{1,0:T(8,128)(2,1)S(1)}, u32[]{:S(2)}, u32[]{:S(2)}) collective-permute-start(bf16[592,256]{1,0:T(8,128)(2,1)S(1)} %get-tuple-element.20.own_ref), channel_id=1, source_target_pairs={{0,256},{8,264},{16,272},{24,280},{32,288},{40,296},{48,304},{56,3... | collective-permute-start | bytes 909320 | tf_op jit(solution)/shard_map/ppermute | solution.py:303
  33.9 21.3 %collective-permute-start.3 = (bf16[592,256]{1,0:T(8,128)(2,1)S(1)}, bf16[592,256]{1,0:T(8,128)(2,1)S(1)}, u32[]{:S(2)}, u32[]{:S(2)}) collective-permute-start(bf16[592,256]{1,0:T(8,128)(2,1)S(1)} %get-tuple-element.20.own_ref), channel_id=1, source_target_pairs={{0,504},{8,16},{16,8},{24,32},{32,24},{40,48},{48,40},{56,64},{64,... | collective-permute-start | bytes 909320 | tf_op jit(solution)/shard_map/ppermute | solution.py:303
  36.6 18.6 %collective-permute-start.2 = (bf16[592,256]{1,0:T(8,128)(2,1)S(1)}, bf16[592,256]{1,0:T(8,128)(2,1)S(1)}, u32[]{:S(2)}, u32[]{:S(2)}) collective-permute-start(bf16[592,256]{1,0:T(8,128)(2,1)S(1)} %get-tuple-element.20.own_ref), channel_id=1, source_target_pairs={{0,8},{8,0},{16,24},{24,16},{32,40},{40,32},{48,56},{56,48},{64,72... | collective-permute-start | bytes 909320 | tf_op jit(solution)/shard_map/ppermute | solution.py:303
  39.6 17.7 %copy-start.7 = (bf16[192,256]{1,0:T(8,128)(2,1)}, bf16[192,256]{1,0:T(8,128)(2,1)S(1)}, u32[]{:S(2)}) copy-start(bf16[192,256]{1,0:T(8,128)(2,1)S(1)} %add_convert_fusion) | copy-start | bytes 294916
  57.3 13.7 %collective-permute-start.7 = (bf16[208,256]{1,0:T(8,128)(2,1)S(1)}, bf16[208,256]{1,0:T(8,128)(2,1)S(1)}, u32[]{:S(2)}, u32[]{:S(2)}) collective-permute-start(bf16[208,256]{1,0:T(8,128)(2,1)S(1)} %get-tuple-element.21.grad_ref), channel_id=1, source_target_pairs={{0,256},{8,264},{16,272},{24,280},{32,288},{40,296},{48,304},{56,3... | collective-permute-start | bytes 319496 | tf_op jit(solution)/shard_map/ppermute | solution.py:303
  63.1 8.0 %collective-permute-start.6 = (bf16[208,256]{1,0:T(8,128)(2,1)S(1)}, bf16[208,256]{1,0:T(8,128)(2,1)S(1)}, u32[]{:S(2)}, u32[]{:S(2)}) collective-permute-start(bf16[208,256]{1,0:T(8,128)(2,1)S(1)} %get-tuple-element.21.grad_ref), channel_id=1, source_target_pairs={{0,8},{8,0},{16,24},{24,16},{32,40},{40,32},{48,56},{56,48},{64,72... | collective-permute-start | bytes 319496 | tf_op jit(solution)/shard_map/ppermute | solution.py:303
  66.3 8.8 %collective-permute-start.5 = (bf16[208,256]{1,0:T(8,128)(2,1)S(1)}, bf16[208,256]{1,0:T(8,128)(2,1)S(1)}, u32[]{:S(2)}, u32[]{:S(2)}) collective-permute-start(bf16[208,256]{1,0:T(8,128)(2,1)S(1)} %get-tuple-element.21.grad_ref), channel_id=1, source_target_pairs={{0,504},{8,16},{16,8},{24,32},{32,24},{40,48},{48,40},{56,64},{64,... | collective-permute-start | bytes 319496 | tf_op jit(solution)/shard_map/ppermute | solution.py:303

commit v8 on v7

--- a/solution.py
+++ b/solution.py
@@ -19,7 +19,6 @@
 SCALE = 1.0 / math.sqrt(HEAD_DIM)
 SCALE2 = SCALE * math.log2(math.e)
 VMEM = pl.BlockSpec(memory_space=pltpu.VMEM)
-SMEM = pl.BlockSpec(memory_space=pltpu.SMEM)
 F32 = jnp.float32
 BF16 = jnp.bfloat16
 
@@ -77,18 +76,26 @@
     out_ref[2 * columns : 3 * columns, :] = queries_ref[...]
     row = lax.broadcasted_iota(jnp.int32, (META, rows), 0)
     first = lax.broadcasted_iota(jnp.int32, (META, rows), 1) < rows // 2
-    meta = jnp.where(row == 0, count_ref[0].astype(F32), 0.0)
-    links = (0, 2 - odd_ref[0], 1 + odd_ref[0], 3)
-    for slot, link in enumerate(links):
-        for kb in range(2):
-            picked = []
-            for qb in range(2):
-                bit = (mask_ref[qb, link, kb] > 0).astype(F32)
-                if slot == 0 and qb == kb:
-                    bit = jnp.maximum(bit, 1.0)
-                picked.append(bit)
+    odd = odd_ref[...] > 0
+    meta = jnp.where(row == 0, count_ref[...].astype(F32), 0.0)
+    for kb in range(2):
+        bits = []
+        for qb in range(2):
+            given = [
+                (mask_ref[qb, kb : kb + 1, j : j + 1] > 0).astype(F32) for j in range(LINKS)
+            ]
+            own_bit = jnp.ones_like(given[0]) if qb == kb else given[0]
+            bits.append(
+                (
+                    own_bit,
+                    jnp.where(odd, given[1], given[2]),
+                    jnp.where(odd, given[2], given[1]),
+                    given[3],
+                )
+            )
+        for slot in range(LINKS):
             meta = jnp.where(
-                row == 1 + 2 * slot + kb, jnp.where(first, picked[0], picked[1]), meta
+                row == 1 + 2 * slot + kb, jnp.where(first, bits[0][slot], bits[1][slot]), meta
             )
     out_ref[3 * columns :, :] = meta.astype(BF16)
     step = 32
@@ -113,7 +120,7 @@
     odd_ref, two_ref, one_ref, taps_ref, sum_ref, gate_ref, slope_ref, w_ref, out_ref, head, tail
 ):
     columns, rows = sum_ref.shape
-    odd = odd_ref[0] > 0
+    odd = jnp.broadcast_to(odd_ref[...] > 0, (columns, LANES))
     before = jnp.where(odd, one_ref[:, rows - LANES :], two_ref[:, rows - LANES :]).astype(F32)
     after = jnp.where(odd, two_ref[:, :LANES], one_ref[:, :LANES]).astype(F32)
     blank = jnp.zeros((PAD, columns), F32)
@@ -192,15 +199,17 @@
         ]
         top = functools.reduce(jnp.maximum, [jnp.max(s, axis=0, keepdims=True) for s in scores])
         total = jnp.zeros_like(top)
-        mixed = jnp.zeros((HEAD_DIM, own_ref.shape[1]), F32)
+        mixed = jnp.zeros_like(top)
         for j in range(LINKS):
             expo = jnp.exp2(scores[j] - top)
-            tile_out[LINKS * h + j] = expo
+            dprob = dot_tn(refs[j][columns + lo : columns + hi, :], low[lo:hi])
+            tile_out[2 * (LINKS * h + j)] = expo
+            tile_out[2 * (LINKS * h + j) + 1] = dprob
             total = total + jnp.sum(expo, axis=0, keepdims=True)
-            mixed = mixed + dot_nn(refs[j][columns + lo : columns + hi, :], expo.astype(BF16))
+            mixed = mixed + jnp.sum(expo * dprob, axis=0, keepdims=True)
         inverse = jnp.where(valid, 1.0 / total, 0.0)
         inverse_out[h : h + 1, :] = inverse
-        delta = jnp.sum(low[lo:hi].astype(F32) * mixed, axis=0, keepdims=True) * inverse
+        delta = mixed * inverse
         rows += pieces(jnp.where(valid, top + jnp.log2(total), -NEG), 3)
         rows += pieces(delta, 2)
     index = lax.broadcasted_iota(jnp.int32, (META, own_meta.shape[1]), 0)
@@ -244,9 +253,8 @@
         _, delta = stats_of(grad_ref, columns, h)
         total = jnp.zeros((HEAD_DIM, own_ref.shape[1]), F32)
         for j in range(LINKS):
-            value = refs[j][columns + lo : columns + hi, :]
-            probs = tile_ref[LINKS * h + j] * inverse
-            dscore = (probs * (dot_tn(value, grad) - delta)).astype(BF16)
+            probs = tile_ref[2 * (LINKS * h + j)] * inverse
+            dscore = (probs * (tile_ref[2 * (LINKS * h + j) + 1] - delta)).astype(BF16)
             total = total + dot_nn(refs[j][lo:hi, :], dscore)
             if j == 0:
                 query = own_ref[2 * columns + lo : 2 * columns + hi, :]
@@ -314,14 +322,24 @@
     message = 3 * columns + META
     square = 2 * columns * row_count * row_count
 
-    odd = (lax.axis_index("ctx") % 2).astype(jnp.int32).reshape(1)
+    odd = (lax.axis_index("ctx") % 2).astype(jnp.int32).reshape(1, 1)
     near = [exchange(g_conv, slot, closed=False) for slot in (2, 1)]
     flat = (columns, row_count)
     own, conv, gate, slope = call(
         own_body,
         (shape((message, row_count), BF16),) + (shape(flat, F32),) * 3,
-        (odd, block_mask, counts, keys, values, queries, g_conv, pre, kernel),
-        [SMEM] * 3 + [VMEM] * 6,
+        (
+            odd,
+            block_mask.transpose(0, 2, 1),
+            counts.reshape(1, 1),
+            keys,
+            values,
+            queries,
+            g_conv,
+            pre,
+            kernel,
+        ),
+        [VMEM] * 9,
         2 * KW * columns * row_count,
         6 * message * row_count,
         columns * row_count,
@@ -336,7 +354,7 @@
         edge_body,
         shape((model, row_count), BF16),
         (odd, *near, kernel, conv, gate, slope, w_turned),
-        [SMEM] + [VMEM] * 7,
+        [VMEM] * 8,
         4 * columns * model * row_count,
         4 * columns * model,
         0,
@@ -350,7 +368,7 @@
     piece = jnp.sum(parts.astype(F32), axis=0)
     stream_grad = (g_out.astype(F32) + piece).astype(BF16)
     stream_full = lax.all_gather(stream_grad, "head", axis=0, tiled=True)
-    tiles = (LINKS * columns // HEAD_DIM, row_count, row_count)
+    tiles = (2 * LINKS * columns // HEAD_DIM, row_count, row_count)
     grad, tile, inverse = call(
         functools.partial(grad_body, columns),
         (shape((columns + META, row_count), BF16), shape(tiles, F32), shape((8, row_count), F32)),

time: 77.1 us -> 75.3 us (0.977)
  Pallas kernels: 11.4 us -> 8.98 us
  waiting for transfers between devices: 3.67 us -> 4.5 us
    pallas_call x6, Pallas kernels: 11.4 us -> 8.98 us  [call(): pl.pallas_call(body, out_shape=out_shapes, in_specs=specs, out_specs=jax....]
    ppermute x8, waiting for transfers between devices: 3.67 us -> 4.5 us  [exchange(): return lax.ppermute(value, 'ctx', pairs)]
  transfers between devices with their start and end apart: 9 -> 9, of which waited for: 2 -> 2; matrix products, arithmetic and copies ran while one was open for 3% -> 2% of each run, Pallas kernels for 8% -> 5%
where the time goes in v8:
time: 75.3 us; the launch traced here: 74.9 us
  starting transfers between devices  43.4 us (58%)
  blocking collectives  14.6 us (19%)
  Pallas kernels  8.98 us (12%)
  waiting for transfers between devices  4.5 us (6%)
  local copies, waits for them, and re-layouts  1.75 us (2%)
  between operations  1.55 us (2%)
    ppermute x8, starting transfers between devices, exchange(): return lax.ppermute(value, 'ctx', pairs)  37.7 us
    all_gather x1, blocking collectives, per_device(): stream_full = lax.all_gather(stream_grad, 'head', axis=0, tiled=True)  14.6 us
    pallas_call x6, Pallas kernels, call(): pl.pallas_call(body, out_shape=out_shapes, in_specs=specs, out_specs=jax....  8.98 us
    all_to_all x1, starting transfers between devices, per_device(): lax.all_to_all(point_grad.reshape(groups, columns, row_count), 'head', 0,...  5.66 us
    ppermute x8, waiting for transfers between devices, exchange(): return lax.ppermute(value, 'ctx', pairs)  4.5 us
    reshape x1, local copies, waits for them, and re-layouts, per_device(): w_turned = w_point.reshape(2 * columns, model).T  1.7 us
  transfers between devices with their start and end apart: 9, of which 2 were waited for; matrix products, arithmetic and copies ran while one was open for 2% of the time, Pallas kernels for 5%

profile of v8, /device:TPU:1, one launch (start us, length us, event | category | flops | bytes accessed | tf_op | source)
XLA Modules:
  0.0 74.9 jit_solution(648061018865208762)
XLA Ops:
  0.6 0.0 copy-start.6
  0.6 0.0 copy-start.2
  0.7 0.0 copy-start.7
  0.7 0.0 copy-start.4
  0.7 0.8 %collective-permute-start = (bf16[192,256]{1,0:T(8,128)(2,1)}, bf16[192,256]{1,0:T(8,128)(2,1)S(1)}, u32[]{:S(2)}, u32[]{:S(2)}) collective-permute-start(bf16[192,256]{1,0:T(8,128)(2,1)} %g_ref.1), channel_id=1, source_target_pairs={{8,16},{16,8},{24,32},{32,24},{40,48},{48,40},{56,64},{64,56},{72,... | collective-permute-start | bytes 294920 | tf_op jit(solution)/shard_map/ppermute | solution.py:311
  1.5 8.2 %collective-permute-start.1 = (bf16[192,256]{1,0:T(8,128)(2,1)}, bf16[192,256]{1,0:T(8,128)(2,1)S(1)}, u32[]{:S(2)}, u32[]{:S(2)}) collective-permute-start(bf16[192,256]{1,0:T(8,128)(2,1)} %g_ref.1), channel_id=1, source_target_pairs={{0,8},{8,0},{16,24},{24,16},{32,40},{40,32},{48,56},{56,48},{64,72... | collective-permute-start | bytes 294920 | tf_op jit(solution)/shard_map/ppermute | solution.py:311
  10.3 1.7 %copy.16 = bf16[384,1536]{0,1:T(8,128)(2,1)S(1)} copy(bf16[384,1536]{1,0:T(8,128)(2,1)} %bitcast.19) | data formatting | bytes 2359296 | tf_op jit(solution)/shard_map/reshape | solution.py:352
  12.1 1.4 %shard_map.138 = (bf16[592,256]{1,0:T(8,128)(2,1)S(1)}, f32[192,256]{1,0:T(8,128)S(1)}, f32[192,256]{1,0:T(8,128)S(1)}, f32[192,256]{1,0:T(8,128)S(1)}) custom-call(s32[1,1]{1,0:T(1,128)} %bitcast.odd_ref, s32[2,2,4]{2,1,0:T(2,128)S(1)} %bitcast.18, s32[1,1]{1,0:T(1,128)} %bitcast.13.count_ref, bf16[192,256]{1,0:T(8,128)(2,1)S(1)} %bitcast.15, ...), custom_call_target="tpu_custom_call" | custom-call | flops 3047424 | bytes 909312 | tf_op jit(solution)/shard_map/pallas_call | solution.py:27
  13.6 0.0 collective-permute-done.two_ref
  13.6 0.0 collective-permute-done.1.one_ref
  13.6 1.8 %shard_map.139 = bf16[1536,256]{1,0:T(8,128)(2,1)} custom-call(s32[1,1]{1,0:T(1,128)} %bitcast.odd_ref, bf16[192,256]{1,0:T(8,128)(2,1)S(1)} %collective-permute-done.two_ref, bf16[192,256]{1,0:T(8,128)(2,1)S(1)} %collective-permute-done.1.one_ref, f32[31,192]{1,0:T(8,128)S(1)} %copy-done.2, f32[192,256]{1,0:T(8,128)S(1)} %get-tuple-element.16.sum_ref, ...), custom_call_target="tpu_custom_call" | custom-call | flops 301989888 | bytes 1179648 | tf_op jit(solution)/shard_map/pallas_call | solution.py:27
  15.4 5.7 %all-to-all-start = ((bf16[8,192,256]{2,1,0:T(8,128)(2,1)}), bf16[8,192,256]{2,1,0:T(8,128)(2,1)S(1)}, u32[]{:S(2)}, u32[]{:S(2)}) async-start(bf16[8,192,256]{2,1,0:T(8,128)(2,1)} %bitcast.8), calls=%async_computation | async-start | bytes 1572864 | tf_op jit(solution)/shard_map/all_to_all | solution.py:363
  21.0 12.5 %collective-permute-start.4 = (bf16[592,256]{1,0:T(8,128)(2,1)S(1)}, bf16[592,256]{1,0:T(8,128)(2,1)S(1)}, u32[]{:S(2)}, u32[]{:S(2)}) collective-permute-start(bf16[592,256]{1,0:T(8,128)(2,1)S(1)} %get-tuple-element.20.own_ref), channel_id=1, source_target_pairs={{0,256},{8,264},{16,272},{24,280},{32,288},{40,296},{48,304},{56,3... | collective-permute-start | bytes 909320 | tf_op jit(solution)/shard_map/ppermute | solution.py:311
  33.5 3.0 %collective-permute-start.3 = (bf16[592,256]{1,0:T(8,128)(2,1)S(1)}, bf16[592,256]{1,0:T(8,128)(2,1)S(1)}, u32[]{:S(2)}, u32[]{:S(2)}) collective-permute-start(bf16[592,256]{1,0:T(8,128)(2,1)S(1)} %get-tuple-element.20.own_ref), channel_id=1, source_target_pairs={{0,504},{8,16},{16,8},{24,32},{32,24},{40,48},{48,40},{56,64},{64,... | collective-permute-start | bytes 909320 | tf_op jit(solution)/shard_map/ppermute | solution.py:311
  36.6 1.9 %collective-permute-start.2 = (bf16[592,256]{1,0:T(8,128)(2,1)S(1)}, bf16[592,256]{1,0:T(8,128)(2,1)S(1)}, u32[]{:S(2)}, u32[]{:S(2)}) collective-permute-start(bf16[592,256]{1,0:T(8,128)(2,1)S(1)} %get-tuple-element.20.own_ref), channel_id=1, source_target_pairs={{0,8},{8,0},{16,24},{24,16},{32,40},{40,32},{48,56},{56,48},{64,72... | collective-permute-start | bytes 909320 | tf_op jit(solution)/shard_map/ppermute | solution.py:311
  38.5 0.0 all-to-all-done
  38.5 0.1 convert_reduce_fusion
  38.7 0.0 copy-start.8
  38.7 14.6 %all_gather.3.stream_ref = bf16[1536,256]{1,0:T(8,128)(2,1)S(1)} all-gather(bf16[192,256]{1,0:T(8,128)(2,1)S(1)} %add_convert_fusion), channel_id=1, replica_groups=mesh['ctx'=64,'head'=8] {'head'}, dimensions={0}, use_global_device_ids=true | all-gather | bytes 884736 | tf_op jit(solution)/shard_map/all_gather | solution.py:370
  53.3 0.0 collective-permute-done.4.far_ref
  53.3 1.1 %collective-permute-done.3.two_ref = bf16[592,256]{1,0:T(8,128)(2,1)S(1)} collective-permute-done((bf16[592,256]{1,0:T(8,128)(2,1)S(1)}, bf16[592,256]{1,0:T(8,128)(2,1)S(1)}, u32[]{:S(2)}, u32[]{:S(2)}) %collective-permute-start.3) | collective-permute-done | bytes 303136 | tf_op jit(solution)/shard_map/ppermute | solution.py:311
  54.5 0.0 collective-permute-done.2.one_ref
  54.5 1.6 %shard_map.140 = (bf16[208,256]{1,0:T(8,128)(2,1)S(1)}, f32[24,256,256]{2,1,0:T(8,128)S(1)}, f32[8,256]{1,0:T(8,128)S(1)}) custom-call(bf16[192,1536]{1,0:T(8,128)(2,1)S(1)} %copy-done, bf16[1536,256]{1,0:T(8,128)(2,1)S(1)} %all_gather.3.stream_ref, bf16[592,256]{1,0:T(8,128)(2,1)S(1)} %get-tuple-element.20.own_ref, ...), custom_call_target="tpu_custom_call" | custom-call | flops 352321536 | bytes 1376256 | tf_op jit(solution)/shard_map/pallas_call | solution.py:27
  56.1 5.7 %collective-permute-start.7 = (bf16[208,256]{1,0:T(8,128)(2,1)S(1)}, bf16[208,256]{1,0:T(8,128)(2,1)S(1)}, u32[]{:S(2)}, u32[]{:S(2)}) collective-permute-start(bf16[208,256]{1,0:T(8,128)(2,1)S(1)} %get-tuple-element.21.grad_ref), channel_id=1, source_target_pairs={{0,256},{8,264},{16,272},{24,280},{32,288},{40,296},{48,304},{56,3... | collective-permute-start | bytes 319496 | tf_op jit(solution)/shard_map/ppermute | solution.py:311
  61.8 2.8 %collective-permute-start.6 = (bf16[208,256]{1,0:T(8,128)(2,1)S(1)}, bf16[208,256]{1,0:T(8,128)(2,1)S(1)}, u32[]{:S(2)}, u32[]{:S(2)}) collective-permute-start(bf16[208,256]{1,0:T(8,128)(2,1)S(1)} %get-tuple-element.21.grad_ref), channel_id=1, source_target_pairs={{0,8},{8,0},{16,24},{24,16},{32,40},{40,32},{48,56},{56,48},{64,72... | collective-permute-start | bytes 319496 | tf_op jit(solution)/shard_map/ppermute | solution.py:311
  64.6 2.8 %collective-permute-start.5 = (bf16[208,256]{1,0:T(8,128)(2,1)S(1)}, bf16[208,256]{1,0:T(8,128)(2,1)S(1)}, u32[]{:S(2)}, u32[]{:S(2)}) collective-permute-start(bf16[208,256]{1,0:T(8,128)(2,1)S(1)} %get-tuple-element.21.grad_ref), channel_id=1, source_target_pairs={{0,504},{8,16},{16,8},{24,32},{32,24},{40,48},{48,40},{56,64},{64,... | collective-permute-start | bytes 319496 | tf_op jit(solution)/shard_map/ppermute | solution.py:311
  67.4 1.3 %shard_map.141 = (bf16[192,256]{1,0:T(8,128)(2,1)}, f32[384,256]{1,0:T(8,128)S(1)}) custom-call(bf16[592,256]{1,0:T(8,128)(2,1)S(1)} %get-tuple-element.20.own_ref, bf16[592,256]{1,0:T(8,128)(2,1)S(1)} %collective-permute-done.2.one_ref, bf16[592,256]{1,0:T(8,128)(2,1)S(1)} %collective-permute-done.3.two_ref, ...), custom_call_target="tpu_custom_call" | custom-call | flops 301989888 | bytes 1212416 | tf_op jit(solution)/shard_map/pallas_call | solution.py:27
  68.7 0.0 collective-permute-done.7.grad_far_ref
  68.7 0.0 collective-permute-done.6.grad_one_ref
  68.7 1.3 %shard_map.142.acc_ref = f32[384,256]{1,0:T(8,128)S(1)} custom-call(bf16[592,256]{1,0:T(8,128)(2,1)S(1)} %get-tuple-element.20.own_ref, bf16[592,256]{1,0:T(8,128)(2,1)S(1)} %collective-permute-done.2.one_ref, bf16[592,256]{1,0:T(8,128)(2,1)S(1)} %collective-permute-done.4.far_ref, bf16[208,256]{1,0:T(8,128)(2,1)S(1)} %collective-permute-done.6.grad_one_ref, ...), custom_call_target="tpu_custom_call" | custom-call | flops 201326592 | bytes 1212416 | tf_op jit(solution)/shard_map/pallas_call | solution.py:27
  70.0 3.4 %collective-permute-done.5.grad_two_ref = bf16[208,256]{1,0:T(8,128)(2,1)S(1)} collective-permute-done((bf16[208,256]{1,0:T(8,128)(2,1)S(1)}, bf16[208,256]{1,0:T(8,128)(2,1)S(1)}, u32[]{:S(2)}, u32[]{:S(2)}) %collective-permute-start.5) | collective-permute-done | bytes 106528 | tf_op jit(solution)/shard_map/ppermute | solution.py:311
  73.4 1.5 %shard_map.143 = (bf16[192,256]{1,0:T(8,128)(2,1)}, bf16[192,256]{1,0:T(8,128)(2,1)}) custom-call(bf16[592,256]{1,0:T(8,128)(2,1)S(1)} %get-tuple-element.20.own_ref, bf16[592,256]{1,0:T(8,128)(2,1)S(1)} %collective-permute-done.3.two_ref, bf16[208,256]{1,0:T(8,128)(2,1)S(1)} %collective-permute-done.5.grad_two_ref, f32[384,256]{1,0:T(8,128)S(1)} %shard_map.142.acc_ref), custom_call_target="tpu_custom_call" | custom-call | flops 100663296 | bytes 1212416 | tf_op jit(solution)/shard_map/pallas_call | solution.py:27
  (16 shorter events, 0.1 us)
Async XLA Ops:
  0.6 11.4 %copy-start.6 = (bf16[192,256]{1,0:T(8,128)(2,1)S(1)}, bf16[192,256]{1,0:T(8,128)(2,1)}, u32[]{:S(2)}) copy-start(bf16[192,256]{1,0:T(8,128)(2,1)} %g_ref.1) | copy-start | bytes 294916
  0.6 11.4 %copy-start.2 = (f32[31,192]{1,0:T(8,128)S(1)}, f32[31,192]{1,0:T(8,128)}, u32[]{:S(2)}) copy-start(f32[31,192]{1,0:T(8,128)} %taps_ref.3) | copy-start | bytes 71428
  0.7 11.4 %copy-start.7 = (s32[2,4,2]{1,2,0:T(2,128)S(1)}, s32[2,4,2]{1,2,0:T(2,128)}, u32[]{:S(2)}) copy-start(s32[2,4,2]{1,2,0:T(2,128)} %param.20) | copy-start | bytes 196
  0.7 11.4 %copy-start.4 = (bf16[256,192]{0,1:T(8,128)(2,1)S(1)}, bf16[256,192]{0,1:T(8,128)(2,1)}, u32[]{:S(2)}) copy-start(bf16[256,192]{0,1:T(8,128)(2,1)} %param.19) | copy-start | bytes 294916
  0.7 11.4 %copy-start.3 = (bf16[256,192]{0,1:T(8,128)(2,1)S(1)}, bf16[256,192]{0,1:T(8,128)(2,1)}, u32[]{:S(2)}) copy-start(bf16[256,192]{0,1:T(8,128)(2,1)} %param.18) | copy-start | bytes 294916
  0.7 11.4 %copy-start.5 = (bf16[256,192]{0,1:T(8,128)(2,1)S(1)}, bf16[256,192]{0,1:T(8,128)(2,1)}, u32[]{:S(2)}) copy-start(bf16[256,192]{0,1:T(8,128)(2,1)} %param.17) | copy-start | bytes 294916
  0.7 11.4 %copy-start.1 = (bf16[2,192,256]{2,1,0:T(8,128)(2,1)S(1)}, bf16[2,192,256]{2,1,0:T(8,128)(2,1)}, u32[]{:S(2)}) copy-start(bf16[2,192,256]{2,1,0:T(8,128)(2,1)} %pre_ref.1) | copy-start | bytes 589828
  0.7 12.9 %collective-permute-start = (bf16[192,256]{1,0:T(8,128)(2,1)}, bf16[192,256]{1,0:T(8,128)(2,1)S(1)}, u32[]{:S(2)}, u32[]{:S(2)}) collective-permute-start(bf16[192,256]{1,0:T(8,128)(2,1)} %g_ref.1), channel_id=1, source_target_pairs={{8,16},{16,8},{24,32},{32,24},{40,48},{48,40},{56,64},{64,56},{72,... | collective-permute-start | bytes 294920 | tf_op jit(solution)/shard_map/ppermute | solution.py:311
  1.5 12.1 %collective-permute-start.1 = (bf16[192,256]{1,0:T(8,128)(2,1)}, bf16[192,256]{1,0:T(8,128)(2,1)S(1)}, u32[]{:S(2)}, u32[]{:S(2)}) collective-permute-start(bf16[192,256]{1,0:T(8,128)(2,1)} %g_ref.1), channel_id=1, source_target_pairs={{0,8},{8,0},{16,24},{24,16},{32,40},{40,32},{48,56},{56,48},{64,72... | collective-permute-start | bytes 294920 | tf_op jit(solution)/shard_map/ppermute | solution.py:311
  15.3 23.3 %copy-start.9 = (bf16[192,256]{1,0:T(8,128)(2,1)S(1)}, bf16[192,256]{1,0:T(8,128)(2,1)}, u32[]{:S(2)}) copy-start(bf16[192,256]{1,0:T(8,128)(2,1)} %param.15) | copy-start | bytes 294916
  15.3 39.1 %copy-start = (bf16[192,1536]{1,0:T(8,128)(2,1)S(1)}, bf16[192,1536]{1,0:T(8,128)(2,1)}, u32[]{:S(2)}) copy-start(bf16[192,1536]{1,0:T(8,128)(2,1)} %w_ref.1) | copy-start | bytes 1769476
  15.4 23.2 %all-to-all-start = ((bf16[8,192,256]{2,1,0:T(8,128)(2,1)}), bf16[8,192,256]{2,1,0:T(8,128)(2,1)S(1)}, u32[]{:S(2)}, u32[]{:S(2)}) async-start(bf16[8,192,256]{2,1,0:T(8,128)(2,1)} %bitcast.8), calls=%async_computation | async-start | bytes 1572864 | tf_op jit(solution)/shard_map/all_to_all | solution.py:363
  21.0 32.3 %collective-permute-start.4 = (bf16[592,256]{1,0:T(8,128)(2,1)S(1)}, bf16[592,256]{1,0:T(8,128)(2,1)S(1)}, u32[]{:S(2)}, u32[]{:S(2)}) collective-permute-start(bf16[592,256]{1,0:T(8,128)(2,1)S(1)} %get-tuple-element.20.own_ref), channel_id=1, source_target_pairs={{0,256},{8,264},{16,272},{24,280},{32,288},{40,296},{48,304},{56,3... | collective-permute-start | bytes 909320 | tf_op jit(solution)/shard_map/ppermute | solution.py:311
  33.5 20.9 %collective-permute-start.3 = (bf16[592,256]{1,0:T(8,128)(2,1)S(1)}, bf16[592,256]{1,0:T(8,128)(2,1)S(1)}, u32[]{:S(2)}, u32[]{:S(2)}) collective-permute-start(bf16[592,256]{1,0:T(8,128)(2,1)S(1)} %get-tuple-element.20.own_ref), channel_id=1, source_target_pairs={{0,504},{8,16},{16,8},{24,32},{32,24},{40,48},{48,40},{56,64},{64,... | collective-permute-start | bytes 909320 | tf_op jit(solution)/shard_map/ppermute | solution.py:311
  36.6 17.9 %collective-permute-start.2 = (bf16[592,256]{1,0:T(8,128)(2,1)S(1)}, bf16[592,256]{1,0:T(8,128)(2,1)S(1)}, u32[]{:S(2)}, u32[]{:S(2)}) collective-permute-start(bf16[592,256]{1,0:T(8,128)(2,1)S(1)} %get-tuple-element.20.own_ref), channel_id=1, source_target_pairs={{0,8},{8,0},{16,24},{24,16},{32,40},{40,32},{48,56},{56,48},{64,72... | collective-permute-start | bytes 909320 | tf_op jit(solution)/shard_map/ppermute | solution.py:311
  38.7 17.4 %copy-start.8 = (bf16[192,256]{1,0:T(8,128)(2,1)}, bf16[192,256]{1,0:T(8,128)(2,1)S(1)}, u32[]{:S(2)}) copy-start(bf16[192,256]{1,0:T(8,128)(2,1)S(1)} %add_convert_fusion) | copy-start | bytes 294916
  56.1 12.6 %collective-permute-start.7 = (bf16[208,256]{1,0:T(8,128)(2,1)S(1)}, bf16[208,256]{1,0:T(8,128)(2,1)S(1)}, u32[]{:S(2)}, u32[]{:S(2)}) collective-permute-start(bf16[208,256]{1,0:T(8,128)(2,1)S(1)} %get-tuple-element.21.grad_ref), channel_id=1, source_target_pairs={{0,256},{8,264},{16,272},{24,280},{32,288},{40,296},{48,304},{56,3... | collective-permute-start | bytes 319496 | tf_op jit(solution)/shard_map/ppermute | solution.py:311
  61.8 6.9 %collective-permute-start.6 = (bf16[208,256]{1,0:T(8,128)(2,1)S(1)}, bf16[208,256]{1,0:T(8,128)(2,1)S(1)}, u32[]{:S(2)}, u32[]{:S(2)}) collective-permute-start(bf16[208,256]{1,0:T(8,128)(2,1)S(1)} %get-tuple-element.21.grad_ref), channel_id=1, source_target_pairs={{0,8},{8,0},{16,24},{24,16},{32,40},{40,32},{48,56},{56,48},{64,72... | collective-permute-start | bytes 319496 | tf_op jit(solution)/shard_map/ppermute | solution.py:311
  64.6 8.8 %collective-permute-start.5 = (bf16[208,256]{1,0:T(8,128)(2,1)S(1)}, bf16[208,256]{1,0:T(8,128)(2,1)S(1)}, u32[]{:S(2)}, u32[]{:S(2)}) collective-permute-start(bf16[208,256]{1,0:T(8,128)(2,1)S(1)} %get-tuple-element.21.grad_ref), channel_id=1, source_target_pairs={{0,504},{8,16},{16,8},{24,32},{32,24},{40,48},{48,40},{56,64},{64,... | collective-permute-start | bytes 319496 | tf_op jit(solution)/shard_map/ppermute | solution.py:311

commit v9 on v8

--- a/solution.py
+++ b/solution.py
@@ -77,7 +77,7 @@
     row = lax.broadcasted_iota(jnp.int32, (META, rows), 0)
     first = lax.broadcasted_iota(jnp.int32, (META, rows), 1) < rows // 2
     odd = odd_ref[...] > 0
-    meta = jnp.where(row == 0, count_ref[...].astype(F32), 0.0)
+    meta = jnp.where(row == 0, count_ref[...].astype(F32).reshape(1, 1), 0.0)
     for kb in range(2):
         bits = []
         for qb in range(2):
@@ -179,39 +179,66 @@
     return found
 
 
-def grad_body(
-    columns, w_ref, stream_ref, own_ref, one_ref, far_ref, two_ref, out_ref, tile_out, inverse_out
-):
-    refs = (own_ref, one_ref, two_ref, far_ref)
+def part_of(refs, slots, own_ref, own_meta, low, columns, h, top, tile_out):
+    lo, hi = h * HEAD_DIM, (h + 1) * HEAD_DIM
+    query = own_ref[2 * columns + lo : 2 * columns + hi, :]
+    scores = []
+    for ref, slot in zip(refs, slots):
+        limit = limits(own_meta, meta_of(ref, columns)[0:1], slot)
+        scores.append(masked(dot_tn(ref[lo:hi, :], query) * SCALE2, limit))
+    top = functools.reduce(jnp.maximum, [jnp.max(s, axis=0, keepdims=True) for s in scores], top)
+    total = jnp.zeros_like(top)
+    mixed = jnp.zeros_like(top)
+    for i, ref in enumerate(refs):
+        expo = jnp.exp2(scores[i] - top)
+        dprob = dot_tn(ref[columns + lo : columns + hi, :], low[lo:hi])
+        at = 2 * (len(refs) * h + i)
+        tile_out[at] = expo
+        tile_out[at + 1] = dprob
+        total = total + jnp.sum(expo, axis=0, keepdims=True)
+        mixed = mixed + jnp.sum(expo * dprob, axis=0, keepdims=True)
+    return top, total, mixed
+
+
+def valid_of(meta):
+    return lax.broadcasted_iota(jnp.int32, meta[0:1].shape, 1).astype(F32) < meta[0:1]
+
+
+def near_body(
+    columns, w_ref, stream_ref, own_ref, one_ref, two_ref, low_out, tile_out, part_out
+):
     own_meta = meta_of(own_ref, columns)
-    lane = lax.broadcasted_iota(jnp.int32, own_meta[0:1].shape, 1).astype(F32)
-    valid = lane < own_meta[0:1]
-    limit = [limits(own_meta, meta_of(refs[j], columns)[0:1], j) for j in range(LINKS)]
-    low = jnp.where(valid, dot_nn(w_ref[...], stream_ref[...]), 0.0).astype(BF16)
+    low = jnp.where(valid_of(own_meta), dot_nn(w_ref[...], stream_ref[...]), 0.0).astype(BF16)
+    low_out[...] = low
+    start = jnp.full(own_meta[0:1].shape, NEG, F32)
+    part_out[...] = jnp.zeros(part_out.shape, F32)
+    for h in range(columns // HEAD_DIM):
+        found = part_of(
+            (own_ref, one_ref, two_ref), (0, 1, 2), own_ref, own_meta, low, columns, h, start, tile_out
+        )
+        for i, row in enumerate(found):
+            part_out[3 * h + i : 3 * h + i + 1, :] = row
+
+
+def grad_body(columns, own_ref, far_ref, low_ref, part_ref, out_ref, tile_out, factor_out):
+    own_meta = meta_of(own_ref, columns)
+    valid = valid_of(own_meta)
+    low = low_ref[...]
     out_ref[0:columns, :] = low
+    factor_out[...] = jnp.zeros(factor_out.shape, F32)
     rows = []
-    inverse_out[...] = jnp.zeros(inverse_out.shape, F32)
     for h in range(columns // HEAD_DIM):
-        lo, hi = h * HEAD_DIM, (h + 1) * HEAD_DIM
-        query = own_ref[2 * columns + lo : 2 * columns + hi, :]
-        scores = [
-            masked(dot_tn(refs[j][lo:hi, :], query) * SCALE2, limit[j]) for j in range(LINKS)
-        ]
-        top = functools.reduce(jnp.maximum, [jnp.max(s, axis=0, keepdims=True) for s in scores])
-        total = jnp.zeros_like(top)
-        mixed = jnp.zeros_like(top)
-        for j in range(LINKS):
-            expo = jnp.exp2(scores[j] - top)
-            dprob = dot_tn(refs[j][columns + lo : columns + hi, :], low[lo:hi])
-            tile_out[2 * (LINKS * h + j)] = expo
-            tile_out[2 * (LINKS * h + j) + 1] = dprob
-            total = total + jnp.sum(expo, axis=0, keepdims=True)
-            mixed = mixed + jnp.sum(expo * dprob, axis=0, keepdims=True)
+        old = [part_ref[3 * h + i : 3 * h + i + 1, :] for i in range(3)]
+        top, total, mixed = part_of(
+            (far_ref,), (3,), own_ref, own_meta, low, columns, h, old[0], tile_out
+        )
+        scale = jnp.exp2(old[0] - top)
+        total = total + scale * old[1]
         inverse = jnp.where(valid, 1.0 / total, 0.0)
-        inverse_out[h : h + 1, :] = inverse
-        delta = mixed * inverse
+        factor_out[2 * h : 2 * h + 1, :] = inverse * scale
+        factor_out[2 * h + 1 : 2 * h + 2, :] = inverse
         rows += pieces(jnp.where(valid, top + jnp.log2(total), -NEG), 3)
-        rows += pieces(delta, 2)
+        rows += pieces((mixed + scale * old[2]) * inverse, 2)
     index = lax.broadcasted_iota(jnp.int32, (META, own_meta.shape[1]), 0)
     meta = jnp.zeros((META, own_meta.shape[1]), F32)
     for i, row in enumerate(rows):
@@ -240,8 +267,9 @@
     two_ref,
     far_ref,
     grad_ref,
-    tile_ref,
-    inverse_ref,
+    near_tile_ref,
+    far_tile_ref,
+    factor_ref,
     query_out,
     acc_out,
 ):
@@ -249,12 +277,13 @@
     for h in range(columns // HEAD_DIM):
         lo, hi = h * HEAD_DIM, (h + 1) * HEAD_DIM
         grad = grad_ref[lo:hi, :]
-        inverse = inverse_ref[h : h + 1, :]
         _, delta = stats_of(grad_ref, columns, h)
         total = jnp.zeros((HEAD_DIM, own_ref.shape[1]), F32)
         for j in range(LINKS):
-            probs = tile_ref[2 * (LINKS * h + j)] * inverse
-            dscore = (probs * (tile_ref[2 * (LINKS * h + j) + 1] - delta)).astype(BF16)
+            tiles, at = (near_tile_ref, 2 * (3 * h + j)) if j < 3 else (far_tile_ref, 2 * h)
+            row = 2 * h + (j == 3)
+            probs = tiles[at] * factor_ref[row : row + 1, :]
+            dscore = (probs * (tiles[at + 1] - delta)).astype(BF16)
             total = total + dot_nn(refs[j][lo:hi, :], dscore)
             if j == 0:
                 query = own_ref[2 * columns + lo : 2 * columns + hi, :]
@@ -280,21 +309,23 @@
     return key_term, value_term
 
 
-def middle_body(columns, own_ref, one_ref, far_ref, grad_one_ref, grad_far_ref, acc_ref, acc_out):
+def middle_body(columns, own_ref, far_ref, grad_far_ref, acc_ref, acc_out):
     for h in range(columns // HEAD_DIM):
         lo, hi = h * HEAD_DIM, (h + 1) * HEAD_DIM
         key_term, value_term = remote_terms(
-            columns, (1, 3), own_ref, (one_ref, far_ref), (grad_one_ref, grad_far_ref), h
+            columns, (3,), own_ref, (far_ref,), (grad_far_ref,), h
         )
         acc_out[lo:hi, :] = acc_ref[lo:hi, :] + key_term
         acc_out[columns + lo : columns + hi, :] = acc_ref[columns + lo : columns + hi, :] + value_term
 
 
-def last_body(columns, own_ref, two_ref, grad_two_ref, acc_ref, key_out, value_out):
+def last_body(
+    columns, own_ref, one_ref, two_ref, grad_one_ref, grad_two_ref, acc_ref, key_out, value_out
+):
     for h in range(columns // HEAD_DIM):
         lo, hi = h * HEAD_DIM, (h + 1) * HEAD_DIM
         key_term, value_term = remote_terms(
-            columns, (2,), own_ref, (two_ref,), (grad_two_ref,), h
+            columns, (1, 2), own_ref, (one_ref, two_ref), (grad_one_ref, grad_two_ref), h
         )
         key_out[lo:hi, :] = ((acc_ref[lo:hi, :] + key_term) * SCALE).astype(BF16)
         value_out[lo:hi, :] = (acc_ref[columns + lo : columns + hi, :] + value_term).astype(BF16)
@@ -331,7 +362,7 @@
         (
             odd,
             block_mask.transpose(0, 2, 1),
-            counts.reshape(1, 1),
+            counts,
             keys,
             values,
             queries,
@@ -368,42 +399,59 @@
     piece = jnp.sum(parts.astype(F32), axis=0)
     stream_grad = (g_out.astype(F32) + piece).astype(BF16)
     stream_full = lax.all_gather(stream_grad, "head", axis=0, tiled=True)
-    tiles = (2 * LINKS * columns // HEAD_DIM, row_count, row_count)
-    grad, tile, inverse = call(
+    heads = columns // HEAD_DIM
+    low, near_tiles, part = call(
+        functools.partial(near_body, columns),
+        (
+            shape(flat, BF16),
+            shape((6 * heads, row_count, row_count), F32),
+            shape((3 * heads, row_count), F32),
+        ),
+        (w_out, stream_full, own, one, two),
+        [VMEM] * 5,
+        2 * columns * model * row_count + 6 * square,
+        2 * model * (columns + row_count),
+        3 * heads * row_count * row_count,
+    )
+    grad, far_tiles, factor = call(
         functools.partial(grad_body, columns),
-        (shape((columns + META, row_count), BF16), shape(tiles, F32), shape((8, row_count), F32)),
-        (w_out, stream_full, own, one, far, two),
-        [VMEM] * 6,
-        2 * columns * model * row_count + 2 * LINKS * square,
-        2 * model * (columns + row_count),
-        LINKS * columns // HEAD_DIM * row_count * row_count,
+        (
+            shape((columns + META, row_count), BF16),
+            shape((2 * heads, row_count, row_count), F32),
+            shape((2 * heads, row_count), F32),
+        ),
+        (own, far, low, part),
+        [VMEM] * 4,
+        2 * square,
+        4 * message * row_count,
+        heads * row_count * row_count,
     )
     grad_one, grad_two, grad_far = [exchange(grad, slot) for slot in (1, 2, 3)]
     grad_queries, acc = call(
         functools.partial(local_body, columns),
-        (shape((columns, row_count), BF16), shape((2 * columns, row_count), F32)),
-        (own, one, two, far, grad, tile, inverse),
-        [VMEM] * 7,
+        (shape(flat, BF16), shape((2 * columns, row_count), F32)),
+        (own, one, two, far, grad, near_tiles, far_tiles, factor),
+        [VMEM] * 8,
         3 * LINKS * square,
         8 * message * row_count,
     )
     acc = call(
         functools.partial(middle_body, columns),
         shape((2 * columns, row_count), F32),
-        (own, one, far, grad_one, grad_far, acc),
+        (own, far, grad_far, acc),
+        [VMEM] * 4,
+        4 * square,
+        6 * message * row_count,
+        heads * row_count * row_count,
+    )
+    grad_keys, grad_values = call(
+        functools.partial(last_body, columns),
+        (shape(flat, BF16), shape(flat, BF16)),
+        (own, one, two, grad_one, grad_two, acc),
         [VMEM] * 6,
         8 * square,
         8 * message * row_count,
-        2 * columns // HEAD_DIM * row_count * row_count,
-    )
-    grad_keys, grad_values = call(
-        functools.partial(last_body, columns),
-        (shape((columns, row_count), BF16), shape((columns, row_count), BF16)),
-        (own, two, grad_two, acc),
-        [VMEM] * 4,
-        4 * square,
-        8 * message * row_count,
-        columns // HEAD_DIM * row_count * row_count,
+        2 * heads * row_count * row_count,
     )
     return (stream_grad.T, grad_queries.T, grad_keys.T, grad_values.T)
 

time: 75.3 us -> 74.8 us (level)
  waiting for transfers between devices: 4.5 us -> 3.34 us
    ppermute x8, waiting for transfers between devices: 4.5 us -> 3.34 us  [exchange(): return lax.ppermute(value, 'ctx', pairs)]
    pallas_call x6 -> x7, Pallas kernels: 8.98 us -> 9.45 us  [call(): pl.pallas_call(body, out_shape=out_shapes, in_specs=specs, out_specs=jax....]
  transfers between devices with their start and end apart: 9 -> 9, of which waited for: 2 -> 2; matrix products, arithmetic and copies ran while one was open for 2% -> 2% of each run, Pallas kernels for 5% -> 7%
where the time goes in v9:
time: 74.8 us; the launch traced here: 74.2 us
  starting transfers between devices  43.4 us (58%)
  blocking collectives  14.6 us (20%)
  Pallas kernels  9.45 us (13%)
  waiting for transfers between devices  3.34 us (4%)
  local copies, waits for them, and re-layouts  1.75 us (2%)
  between operations  1.56 us (2%)
    ppermute x8, starting transfers between devices, exchange(): return lax.ppermute(value, 'ctx', pairs)  37.7 us
    all_gather x1, blocking collectives, per_device(): stream_full = lax.all_gather(stream_grad, 'head', axis=0, tiled=True)  14.6 us
    pallas_call x7, Pallas kernels, call(): pl.pallas_call(body, out_shape=out_shapes, in_specs=specs, out_specs=jax....  9.45 us
    all_to_all x1, starting transfers between devices, per_device(): lax.all_to_all(point_grad.reshape(groups, columns, row_count), 'head', 0,...  5.66 us
    ppermute x8, waiting for transfers between devices, exchange(): return lax.ppermute(value, 'ctx', pairs)  3.34 us
    reshape x1, local copies, waits for them, and re-layouts, per_device(): w_turned = w_point.reshape(2 * columns, model).T  1.7 us
  transfers between devices with their start and end apart: 9, of which 2 were waited for; matrix products, arithmetic and copies ran while one was open for 2% of the time, Pallas kernels for 7%

profile of v9, /device:TPU:1, one launch (start us, length us, event | category | flops | bytes accessed | tf_op | source)
XLA Modules:
  0.0 74.2 jit_solution(2675689449814262119)
XLA Ops:
  0.6 0.0 copy-start.6
  0.6 0.0 copy-start.2
  0.7 0.0 copy-start.7
  0.7 0.8 %collective-permute-start = (bf16[192,256]{1,0:T(8,128)(2,1)}, bf16[192,256]{1,0:T(8,128)(2,1)S(1)}, u32[]{:S(2)}, u32[]{:S(2)}) collective-permute-start(bf16[192,256]{1,0:T(8,128)(2,1)} %g_ref.1), channel_id=1, source_target_pairs={{8,16},{16,8},{24,32},{32,24},{40,48},{48,40},{56,64},{64,56},{72,... | collective-permute-start | bytes 294920 | tf_op jit(solution)/shard_map/ppermute | solution.py:342
  1.5 8.2 %collective-permute-start.1 = (bf16[192,256]{1,0:T(8,128)(2,1)}, bf16[192,256]{1,0:T(8,128)(2,1)S(1)}, u32[]{:S(2)}, u32[]{:S(2)}) collective-permute-start(bf16[192,256]{1,0:T(8,128)(2,1)} %g_ref.1), channel_id=1, source_target_pairs={{0,8},{8,0},{16,24},{24,16},{32,40},{40,32},{48,56},{56,48},{64,72... | collective-permute-start | bytes 294920 | tf_op jit(solution)/shard_map/ppermute | solution.py:342
  10.3 1.7 %copy.16 = bf16[384,1536]{0,1:T(8,128)(2,1)S(1)} copy(bf16[384,1536]{1,0:T(8,128)(2,1)} %bitcast.17) | data formatting | bytes 2359296 | tf_op jit(solution)/shard_map/reshape | solution.py:383
  12.1 1.4 %shard_map.138 = (bf16[592,256]{1,0:T(8,128)(2,1)S(1)}, f32[192,256]{1,0:T(8,128)S(1)}, f32[192,256]{1,0:T(8,128)S(1)}, f32[192,256]{1,0:T(8,128)S(1)}) custom-call(s32[1,1]{1,0:T(1,128)} %bitcast.odd_ref, s32[2,2,4]{2,1,0:T(2,128)S(1)} %bitcast.16, s32[1]{0:T(128)S(6)} %copy.17.count_ref, bf16[192,256]{1,0:T(8,128)(2,1)S(1)} %bitcast.13, ...), custom_call_target="tpu_custom_call" | custom-call | flops 3047424 | bytes 909312 | tf_op jit(solution)/shard_map/pallas_call | solution.py:27
  13.6 0.0 collective-permute-done.two_ref
  13.6 0.0 collective-permute-done.1.one_ref
  13.6 1.8 %shard_map.139 = bf16[1536,256]{1,0:T(8,128)(2,1)} custom-call(s32[1,1]{1,0:T(1,128)} %bitcast.odd_ref, bf16[192,256]{1,0:T(8,128)(2,1)S(1)} %collective-permute-done.two_ref, bf16[192,256]{1,0:T(8,128)(2,1)S(1)} %collective-permute-done.1.one_ref, f32[31,192]{1,0:T(8,128)S(1)} %copy-done.2, f32[192,256]{1,0:T(8,128)S(1)} %get-tuple-element.19.sum_ref, ...), custom_call_target="tpu_custom_call" | custom-call | flops 301989888 | bytes 1179648 | tf_op jit(solution)/shard_map/pallas_call | solution.py:27
  15.4 5.7 %all-to-all-start = ((bf16[8,192,256]{2,1,0:T(8,128)(2,1)}), bf16[8,192,256]{2,1,0:T(8,128)(2,1)S(1)}, u32[]{:S(2)}, u32[]{:S(2)}) async-start(bf16[8,192,256]{2,1,0:T(8,128)(2,1)} %bitcast.7), calls=%async_computation | async-start | bytes 1572864 | tf_op jit(solution)/shard_map/all_to_all | solution.py:394
  21.0 12.5 %collective-permute-start.4 = (bf16[592,256]{1,0:T(8,128)(2,1)S(1)}, bf16[592,256]{1,0:T(8,128)(2,1)S(1)}, u32[]{:S(2)}, u32[]{:S(2)}) collective-permute-start(bf16[592,256]{1,0:T(8,128)(2,1)S(1)} %get-tuple-element.23.own_ref), channel_id=1, source_target_pairs={{0,256},{8,264},{16,272},{24,280},{32,288},{40,296},{48,304},{56,3... | collective-permute-start | bytes 909320 | tf_op jit(solution)/shard_map/ppermute | solution.py:342
  33.6 3.0 %collective-permute-start.3 = (bf16[592,256]{1,0:T(8,128)(2,1)S(1)}, bf16[592,256]{1,0:T(8,128)(2,1)S(1)}, u32[]{:S(2)}, u32[]{:S(2)}) collective-permute-start(bf16[592,256]{1,0:T(8,128)(2,1)S(1)} %get-tuple-element.23.own_ref), channel_id=1, source_target_pairs={{0,504},{8,16},{16,8},{24,32},{32,24},{40,48},{48,40},{56,64},{64,... | collective-permute-start | bytes 909320 | tf_op jit(solution)/shard_map/ppermute | solution.py:342
  36.6 1.9 %collective-permute-start.2 = (bf16[592,256]{1,0:T(8,128)(2,1)S(1)}, bf16[592,256]{1,0:T(8,128)(2,1)S(1)}, u32[]{:S(2)}, u32[]{:S(2)}) collective-permute-start(bf16[592,256]{1,0:T(8,128)(2,1)S(1)} %get-tuple-element.23.own_ref), channel_id=1, source_target_pairs={{0,8},{8,0},{16,24},{24,16},{32,40},{40,32},{48,56},{56,48},{64,72... | collective-permute-start | bytes 909320 | tf_op jit(solution)/shard_map/ppermute | solution.py:342
  38.5 0.0 all-to-all-done
  38.5 0.1 convert_reduce_fusion
  38.7 0.0 copy-start.8
  38.7 14.6 %all_gather.3.stream_ref = bf16[1536,256]{1,0:T(8,128)(2,1)S(1)} all-gather(bf16[192,256]{1,0:T(8,128)(2,1)S(1)} %add_convert_fusion), channel_id=1, replica_groups=mesh['ctx'=64,'head'=8] {'head'}, dimensions={0}, use_global_device_ids=true | all-gather | bytes 884736 | tf_op jit(solution)/shard_map/all_gather | solution.py:401
  53.3 1.1 %collective-permute-done.3.two_ref = bf16[592,256]{1,0:T(8,128)(2,1)S(1)} collective-permute-done((bf16[592,256]{1,0:T(8,128)(2,1)S(1)}, bf16[592,256]{1,0:T(8,128)(2,1)S(1)}, u32[]{:S(2)}, u32[]{:S(2)}) %collective-permute-start.3) | collective-permute-done | bytes 303136 | tf_op jit(solution)/shard_map/ppermute | solution.py:342
  54.5 0.0 collective-permute-done.2.one_ref
  54.5 1.5 %shard_map.140 = (bf16[192,256]{1,0:T(8,128)(2,1)S(1)}, f32[18,256,256]{2,1,0:T(8,128)S(1)}, f32[9,256]{1,0:T(8,128)S(1)}) custom-call(bf16[192,1536]{1,0:T(8,128)(2,1)S(1)} %copy-done, bf16[1536,256]{1,0:T(8,128)(2,1)S(1)} %all_gather.3.stream_ref, bf16[592,256]{1,0:T(8,128)(2,1)S(1)} %get-tuple-element.23.own_ref, ...), custom_call_target="tpu_custom_call" | custom-call | flops 301989888 | bytes 1376256 | tf_op jit(solution)/shard_map/pallas_call | solution.py:27
  55.9 0.0 collective-permute-done.4.far_ref
  56.0 0.6 shard_map.141
  56.5 5.7 %collective-permute-start.7 = (bf16[208,256]{1,0:T(8,128)(2,1)S(1)}, bf16[208,256]{1,0:T(8,128)(2,1)S(1)}, u32[]{:S(2)}, u32[]{:S(2)}) collective-permute-start(bf16[208,256]{1,0:T(8,128)(2,1)S(1)} %get-tuple-element.26.grad_ref), channel_id=1, source_target_pairs={{0,256},{8,264},{16,272},{24,280},{32,288},{40,296},{48,304},{56,3... | collective-permute-start | bytes 319496 | tf_op jit(solution)/shard_map/ppermute | solution.py:342
  62.3 3.6 %collective-permute-start.6 = (bf16[208,256]{1,0:T(8,128)(2,1)S(1)}, bf16[208,256]{1,0:T(8,128)(2,1)S(1)}, u32[]{:S(2)}, u32[]{:S(2)}) collective-permute-start(bf16[208,256]{1,0:T(8,128)(2,1)S(1)} %get-tuple-element.26.grad_ref), channel_id=1, source_target_pairs={{0,504},{8,16},{16,8},{24,32},{32,24},{40,48},{48,40},{56,64},{64,... | collective-permute-start | bytes 319496 | tf_op jit(solution)/shard_map/ppermute | solution.py:342
  65.9 1.9 %collective-permute-start.5 = (bf16[208,256]{1,0:T(8,128)(2,1)S(1)}, bf16[208,256]{1,0:T(8,128)(2,1)S(1)}, u32[]{:S(2)}, u32[]{:S(2)}) collective-permute-start(bf16[208,256]{1,0:T(8,128)(2,1)S(1)} %get-tuple-element.26.grad_ref), channel_id=1, source_target_pairs={{0,8},{8,0},{16,24},{24,16},{32,40},{40,32},{48,56},{56,48},{64,72... | collective-permute-start | bytes 319496 | tf_op jit(solution)/shard_map/ppermute | solution.py:342
  67.8 1.3 %shard_map.142 = (bf16[192,256]{1,0:T(8,128)(2,1)}, f32[384,256]{1,0:T(8,128)S(1)}) custom-call(bf16[592,256]{1,0:T(8,128)(2,1)S(1)} %get-tuple-element.23.own_ref, bf16[592,256]{1,0:T(8,128)(2,1)S(1)} %collective-permute-done.2.one_ref, bf16[592,256]{1,0:T(8,128)(2,1)S(1)} %collective-permute-done.3.two_ref, ...), custom_call_target="tpu_custom_call" | custom-call | flops 301989888 | bytes 1212416 | tf_op jit(solution)/shard_map/pallas_call | solution.py:27
  69.2 0.0 collective-permute-done.7.grad_far_ref
  69.2 0.9 %shard_map.143.acc_ref = f32[384,256]{1,0:T(8,128)S(1)} custom-call(bf16[592,256]{1,0:T(8,128)(2,1)S(1)} %get-tuple-element.23.own_ref, bf16[592,256]{1,0:T(8,128)(2,1)S(1)} %collective-permute-done.4.far_ref, bf16[208,256]{1,0:T(8,128)(2,1)S(1)} %collective-permute-done.7.grad_far_ref, f32[384,256]{1,0:T(8,128)S(1)} %get-tuple-element.31.acc_ref), custom_call_target="tpu_custom_call" | custom-call | flops 100663296 | bytes 909312 | tf_op jit(solution)/shard_map/pallas_call | solution.py:27
  70.0 2.2 %collective-permute-done.6.grad_two_ref = bf16[208,256]{1,0:T(8,128)(2,1)S(1)} collective-permute-done((bf16[208,256]{1,0:T(8,128)(2,1)S(1)}, bf16[208,256]{1,0:T(8,128)(2,1)S(1)}, u32[]{:S(2)}, u32[]{:S(2)}) %collective-permute-start.6) | collective-permute-done | bytes 106528 | tf_op jit(solution)/shard_map/ppermute | solution.py:342
  72.2 0.0 collective-permute-done.5.grad_one_ref
  72.2 2.0 %shard_map.144 = (bf16[192,256]{1,0:T(8,128)(2,1)}, bf16[192,256]{1,0:T(8,128)(2,1)}) custom-call(bf16[592,256]{1,0:T(8,128)(2,1)S(1)} %get-tuple-element.23.own_ref, bf16[592,256]{1,0:T(8,128)(2,1)S(1)} %collective-permute-done.2.one_ref, bf16[592,256]{1,0:T(8,128)(2,1)S(1)} %collective-permute-done.3.two_ref, ...), custom_call_target="tpu_custom_call" | custom-call | flops 201326592 | bytes 1212416 | tf_op jit(solution)/shard_map/pallas_call | solution.py:27
  (17 shorter events, 0.1 us)
Async XLA Ops:
  0.6 11.4 %copy-start.6 = (bf16[192,256]{1,0:T(8,128)(2,1)S(1)}, bf16[192,256]{1,0:T(8,128)(2,1)}, u32[]{:S(2)}) copy-start(bf16[192,256]{1,0:T(8,128)(2,1)} %g_ref.1) | copy-start | bytes 294916
  0.6 11.4 %copy-start.2 = (f32[31,192]{1,0:T(8,128)S(1)}, f32[31,192]{1,0:T(8,128)}, u32[]{:S(2)}) copy-start(f32[31,192]{1,0:T(8,128)} %taps_ref.3) | copy-start | bytes 71428
  0.7 11.4 %copy-start.7 = (s32[2,4,2]{1,2,0:T(2,128)S(1)}, s32[2,4,2]{1,2,0:T(2,128)}, u32[]{:S(2)}) copy-start(s32[2,4,2]{1,2,0:T(2,128)} %param.20) | copy-start | bytes 196
  0.7 11.4 %copy-start.4 = (bf16[256,192]{0,1:T(8,128)(2,1)S(1)}, bf16[256,192]{0,1:T(8,128)(2,1)}, u32[]{:S(2)}) copy-start(bf16[256,192]{0,1:T(8,128)(2,1)} %param.19) | copy-start | bytes 294916
  0.7 11.4 %copy-start.3 = (bf16[256,192]{0,1:T(8,128)(2,1)S(1)}, bf16[256,192]{0,1:T(8,128)(2,1)}, u32[]{:S(2)}) copy-start(bf16[256,192]{0,1:T(8,128)(2,1)} %param.18) | copy-start | bytes 294916
  0.7 11.4 %copy-start.5 = (bf16[256,192]{0,1:T(8,128)(2,1)S(1)}, bf16[256,192]{0,1:T(8,128)(2,1)}, u32[]{:S(2)}) copy-start(bf16[256,192]{0,1:T(8,128)(2,1)} %param.17) | copy-start | bytes 294916
  0.7 11.4 %copy-start.1 = (bf16[2,192,256]{2,1,0:T(8,128)(2,1)S(1)}, bf16[2,192,256]{2,1,0:T(8,128)(2,1)}, u32[]{:S(2)}) copy-start(bf16[2,192,256]{2,1,0:T(8,128)(2,1)} %pre_ref.1) | copy-start | bytes 589828
  0.7 12.9 %collective-permute-start = (bf16[192,256]{1,0:T(8,128)(2,1)}, bf16[192,256]{1,0:T(8,128)(2,1)S(1)}, u32[]{:S(2)}, u32[]{:S(2)}) collective-permute-start(bf16[192,256]{1,0:T(8,128)(2,1)} %g_ref.1), channel_id=1, source_target_pairs={{8,16},{16,8},{24,32},{32,24},{40,48},{48,40},{56,64},{64,56},{72,... | collective-permute-start | bytes 294920 | tf_op jit(solution)/shard_map/ppermute | solution.py:342
  1.5 12.1 %collective-permute-start.1 = (bf16[192,256]{1,0:T(8,128)(2,1)}, bf16[192,256]{1,0:T(8,128)(2,1)S(1)}, u32[]{:S(2)}, u32[]{:S(2)}) collective-permute-start(bf16[192,256]{1,0:T(8,128)(2,1)} %g_ref.1), channel_id=1, source_target_pairs={{0,8},{8,0},{16,24},{24,16},{32,40},{40,32},{48,56},{56,48},{64,72... | collective-permute-start | bytes 294920 | tf_op jit(solution)/shard_map/ppermute | solution.py:342
  15.4 23.3 %copy-start.9 = (bf16[192,256]{1,0:T(8,128)(2,1)S(1)}, bf16[192,256]{1,0:T(8,128)(2,1)}, u32[]{:S(2)}) copy-start(bf16[192,256]{1,0:T(8,128)(2,1)} %param.15) | copy-start | bytes 294916
  15.4 39.1 %copy-start = (bf16[192,1536]{1,0:T(8,128)(2,1)S(1)}, bf16[192,1536]{1,0:T(8,128)(2,1)}, u32[]{:S(2)}) copy-start(bf16[192,1536]{1,0:T(8,128)(2,1)} %w_ref.1) | copy-start | bytes 1769476
  15.4 23.2 %all-to-all-start = ((bf16[8,192,256]{2,1,0:T(8,128)(2,1)}), bf16[8,192,256]{2,1,0:T(8,128)(2,1)S(1)}, u32[]{:S(2)}, u32[]{:S(2)}) async-start(bf16[8,192,256]{2,1,0:T(8,128)(2,1)} %bitcast.7), calls=%async_computation | async-start | bytes 1572864 | tf_op jit(solution)/shard_map/all_to_all | solution.py:394
  21.0 34.9 %collective-permute-start.4 = (bf16[592,256]{1,0:T(8,128)(2,1)S(1)}, bf16[592,256]{1,0:T(8,128)(2,1)S(1)}, u32[]{:S(2)}, u32[]{:S(2)}) collective-permute-start(bf16[592,256]{1,0:T(8,128)(2,1)S(1)} %get-tuple-element.23.own_ref), channel_id=1, source_target_pairs={{0,256},{8,264},{16,272},{24,280},{32,288},{40,296},{48,304},{56,3... | collective-permute-start | bytes 909320 | tf_op jit(solution)/shard_map/ppermute | solution.py:342
  33.6 20.9 %collective-permute-start.3 = (bf16[592,256]{1,0:T(8,128)(2,1)S(1)}, bf16[592,256]{1,0:T(8,128)(2,1)S(1)}, u32[]{:S(2)}, u32[]{:S(2)}) collective-permute-start(bf16[592,256]{1,0:T(8,128)(2,1)S(1)} %get-tuple-element.23.own_ref), channel_id=1, source_target_pairs={{0,504},{8,16},{16,8},{24,32},{32,24},{40,48},{48,40},{56,64},{64,... | collective-permute-start | bytes 909320 | tf_op jit(solution)/shard_map/ppermute | solution.py:342
  36.6 17.9 %collective-permute-start.2 = (bf16[592,256]{1,0:T(8,128)(2,1)S(1)}, bf16[592,256]{1,0:T(8,128)(2,1)S(1)}, u32[]{:S(2)}, u32[]{:S(2)}) collective-permute-start(bf16[592,256]{1,0:T(8,128)(2,1)S(1)} %get-tuple-element.23.own_ref), channel_id=1, source_target_pairs={{0,8},{8,0},{16,24},{24,16},{32,40},{40,32},{48,56},{56,48},{64,72... | collective-permute-start | bytes 909320 | tf_op jit(solution)/shard_map/ppermute | solution.py:342
  38.7 17.3 %copy-start.8 = (bf16[192,256]{1,0:T(8,128)(2,1)}, bf16[192,256]{1,0:T(8,128)(2,1)S(1)}, u32[]{:S(2)}) copy-start(bf16[192,256]{1,0:T(8,128)(2,1)S(1)} %add_convert_fusion) | copy-start | bytes 294916
  56.5 12.6 %collective-permute-start.7 = (bf16[208,256]{1,0:T(8,128)(2,1)S(1)}, bf16[208,256]{1,0:T(8,128)(2,1)S(1)}, u32[]{:S(2)}, u32[]{:S(2)}) collective-permute-start(bf16[208,256]{1,0:T(8,128)(2,1)S(1)} %get-tuple-element.26.grad_ref), channel_id=1, source_target_pairs={{0,256},{8,264},{16,272},{24,280},{32,288},{40,296},{48,304},{56,3... | collective-permute-start | bytes 319496 | tf_op jit(solution)/shard_map/ppermute | solution.py:342
  62.3 9.9 %collective-permute-start.6 = (bf16[208,256]{1,0:T(8,128)(2,1)S(1)}, bf16[208,256]{1,0:T(8,128)(2,1)S(1)}, u32[]{:S(2)}, u32[]{:S(2)}) collective-permute-start(bf16[208,256]{1,0:T(8,128)(2,1)S(1)} %get-tuple-element.26.grad_ref), channel_id=1, source_target_pairs={{0,504},{8,16},{16,8},{24,32},{32,24},{40,48},{48,40},{56,64},{64,... | collective-permute-start | bytes 319496 | tf_op jit(solution)/shard_map/ppermute | solution.py:342
  65.9 6.3 %collective-permute-start.5 = (bf16[208,256]{1,0:T(8,128)(2,1)S(1)}, bf16[208,256]{1,0:T(8,128)(2,1)S(1)}, u32[]{:S(2)}, u32[]{:S(2)}) collective-permute-start(bf16[208,256]{1,0:T(8,128)(2,1)S(1)} %get-tuple-element.26.grad_ref), channel_id=1, source_target_pairs={{0,8},{8,0},{16,24},{24,16},{32,40},{40,32},{48,56},{56,48},{64,72... | collective-permute-start | bytes 319496 | tf_op jit(solution)/shard_map/ppermute | solution.py:342

commit v10 on v9

--- a/solution.py
+++ b/solution.py
@@ -205,7 +205,7 @@
 
 
 def near_body(
-    columns, w_ref, stream_ref, own_ref, one_ref, two_ref, low_out, tile_out, part_out
+    columns, w_ref, stream_ref, own_ref, one_ref, low_out, tile_out, part_out
 ):
     own_meta = meta_of(own_ref, columns)
     low = jnp.where(valid_of(own_meta), dot_nn(w_ref[...], stream_ref[...]), 0.0).astype(BF16)
@@ -214,13 +214,15 @@
     part_out[...] = jnp.zeros(part_out.shape, F32)
     for h in range(columns // HEAD_DIM):
         found = part_of(
-            (own_ref, one_ref, two_ref), (0, 1, 2), own_ref, own_meta, low, columns, h, start, tile_out
+            (own_ref, one_ref), (0, 1), own_ref, own_meta, low, columns, h, start, tile_out
         )
         for i, row in enumerate(found):
             part_out[3 * h + i : 3 * h + i + 1, :] = row
 
 
-def grad_body(columns, own_ref, far_ref, low_ref, part_ref, out_ref, tile_out, factor_out):
+def grad_body(
+    columns, own_ref, two_ref, far_ref, low_ref, part_ref, out_ref, tile_out, factor_out
+):
     own_meta = meta_of(own_ref, columns)
     valid = valid_of(own_meta)
     low = low_ref[...]
@@ -230,7 +232,7 @@
     for h in range(columns // HEAD_DIM):
         old = [part_ref[3 * h + i : 3 * h + i + 1, :] for i in range(3)]
         top, total, mixed = part_of(
-            (far_ref,), (3,), own_ref, own_meta, low, columns, h, old[0], tile_out
+            (two_ref, far_ref), (2, 3), own_ref, own_meta, low, columns, h, old[0], tile_out
         )
         scale = jnp.exp2(old[0] - top)
         total = total + scale * old[1]
@@ -267,8 +269,8 @@
     two_ref,
     far_ref,
     grad_ref,
-    near_tile_ref,
-    far_tile_ref,
+    first_tile_ref,
+    other_tile_ref,
     factor_ref,
     query_out,
     acc_out,
@@ -280,8 +282,9 @@
         _, delta = stats_of(grad_ref, columns, h)
         total = jnp.zeros((HEAD_DIM, own_ref.shape[1]), F32)
         for j in range(LINKS):
-            tiles, at = (near_tile_ref, 2 * (3 * h + j)) if j < 3 else (far_tile_ref, 2 * h)
-            row = 2 * h + (j == 3)
+            tiles = first_tile_ref if j < 2 else other_tile_ref
+            at = 2 * (2 * h + j % 2)
+            row = 2 * h + j // 2
             probs = tiles[at] * factor_ref[row : row + 1, :]
             dscore = (probs * (tiles[at + 1] - delta)).astype(BF16)
             total = total + dot_nn(refs[j][lo:hi, :], dscore)
@@ -309,23 +312,23 @@
     return key_term, value_term
 
 
-def middle_body(columns, own_ref, far_ref, grad_far_ref, acc_ref, acc_out):
+def middle_body(columns, own_ref, two_ref, grad_two_ref, acc_ref, acc_out):
     for h in range(columns // HEAD_DIM):
         lo, hi = h * HEAD_DIM, (h + 1) * HEAD_DIM
         key_term, value_term = remote_terms(
-            columns, (3,), own_ref, (far_ref,), (grad_far_ref,), h
+            columns, (2,), own_ref, (two_ref,), (grad_two_ref,), h
         )
         acc_out[lo:hi, :] = acc_ref[lo:hi, :] + key_term
         acc_out[columns + lo : columns + hi, :] = acc_ref[columns + lo : columns + hi, :] + value_term
 
 
 def last_body(
-    columns, own_ref, one_ref, two_ref, grad_one_ref, grad_two_ref, acc_ref, key_out, value_out
+    columns, own_ref, one_ref, far_ref, grad_one_ref, grad_far_ref, acc_ref, key_out, value_out
 ):
     for h in range(columns // HEAD_DIM):
         lo, hi = h * HEAD_DIM, (h + 1) * HEAD_DIM
         key_term, value_term = remote_terms(
-            columns, (1, 2), own_ref, (one_ref, two_ref), (grad_one_ref, grad_two_ref), h
+            columns, (1, 3), own_ref, (one_ref, far_ref), (grad_one_ref, grad_far_ref), h
         )
         key_out[lo:hi, :] = ((acc_ref[lo:hi, :] + key_term) * SCALE).astype(BF16)
         value_out[lo:hi, :] = (acc_ref[columns + lo : columns + hi, :] + value_term).astype(BF16)
@@ -400,37 +403,37 @@
     stream_grad = (g_out.astype(F32) + piece).astype(BF16)
     stream_full = lax.all_gather(stream_grad, "head", axis=0, tiled=True)
     heads = columns // HEAD_DIM
-    low, near_tiles, part = call(
+    low, first_tiles, part = call(
         functools.partial(near_body, columns),
         (
             shape(flat, BF16),
-            shape((6 * heads, row_count, row_count), F32),
+            shape((4 * heads, row_count, row_count), F32),
             shape((3 * heads, row_count), F32),
         ),
-        (w_out, stream_full, own, one, two),
-        [VMEM] * 5,
-        2 * columns * model * row_count + 6 * square,
+        (w_out, stream_full, own, one),
+        [VMEM] * 4,
+        2 * columns * model * row_count + 4 * square,
         2 * model * (columns + row_count),
-        3 * heads * row_count * row_count,
-    )
-    grad, far_tiles, factor = call(
+        2 * heads * row_count * row_count,
+    )
+    grad, other_tiles, factor = call(
         functools.partial(grad_body, columns),
         (
             shape((columns + META, row_count), BF16),
-            shape((2 * heads, row_count, row_count), F32),
+            shape((4 * heads, row_count, row_count), F32),
             shape((2 * heads, row_count), F32),
         ),
-        (own, far, low, part),
-        [VMEM] * 4,
-        2 * square,
-        4 * message * row_count,
-        heads * row_count * row_count,
+        (own, two, far, low, part),
+        [VMEM] * 5,
+        4 * square,
+        6 * message * row_count,
+        2 * heads * row_count * row_count,
     )
     grad_one, grad_two, grad_far = [exchange(grad, slot) for slot in (1, 2, 3)]
     grad_queries, acc = call(
         functools.partial(local_body, columns),
         (shape(flat, BF16), shape((2 * columns, row_count), F32)),
-        (own, one, two, far, grad, near_tiles, far_tiles, factor),
+        (own, one, two, far, grad, first_tiles, other_tiles, factor),
         [VMEM] * 8,
         3 * LINKS * square,
         8 * message * row_count,
@@ -438,7 +441,7 @@
     acc = call(
         functools.partial(middle_body, columns),
         shape((2 * columns, row_count), F32),
-        (own, far, grad_far, acc),
+        (own, two, grad_two, acc),
         [VMEM] * 4,
         4 * square,
         6 * message * row_count,
@@ -447,7 +450,7 @@
     grad_keys, grad_values = call(
         functools.partial(last_body, columns),
         (shape(flat, BF16), shape(flat, BF16)),
-        (own, one, two, grad_one, grad_two, acc),
+        (own, one, far, grad_one, grad_far, acc),
         [VMEM] * 6,
         8 * square,
         8 * message * row_count,

time: 74.8 us -> 76.2 us (1.019)
  waiting for transfers between devices: 3.34 us -> 4.23 us
    ppermute x8, waiting for transfers between devices: 3.34 us -> 4.23 us  [exchange(): return lax.ppermute(value, 'ctx', pairs)]
  transfers between devices with their start and end apart: 9 -> 9, of which waited for: 2 -> 1; matrix products, arithmetic and copies ran while one was open for 2% -> 2% of each run, Pallas kernels for 7% -> 6%
where the time goes in v10:
time: 76.2 us; the launch traced here: 75.8 us
  starting transfers between devices  43.9 us (58%)
  blocking collectives  14.6 us (19%)
  Pallas kernels  9.53 us (13%)
  waiting for transfers between devices  4.23 us (6%)
  local copies, waits for them, and re-layouts  1.75 us (2%)
  between operations  1.57 us (2%)
    ppermute x8, starting transfers between devices, exchange(): return lax.ppermute(value, 'ctx', pairs)  38.3 us
    all_gather x1, blocking collectives, per_device(): stream_full = lax.all_gather(stream_grad, 'head', axis=0, tiled=True)  14.6 us
    pallas_call x7, Pallas kernels, call(): pl.pallas_call(body, out_shape=out_shapes, in_specs=specs, out_specs=jax....  9.53 us
    all_to_all x1, starting transfers between devices, per_device(): lax.all_to_all(point_grad.reshape(groups, columns, row_count), 'head', 0,...  5.66 us
    ppermute x8, waiting for transfers between devices, exchange(): return lax.ppermute(value, 'ctx', pairs)  4.23 us
    reshape x1, local copies, waits for them, and re-layouts, per_device(): w_turned = w_point.reshape(2 * columns, model).T  1.7 us
  transfers between devices with their start and end apart: 9, of which 1 were waited for; matrix products, arithmetic and copies ran while one was open for 2% of the time, Pallas kernels for 6%

profile of v10, /device:TPU:1, one launch (start us, length us, event | category | flops | bytes accessed | tf_op | source)
XLA Modules:
  0.0 75.8 jit_solution(12970748874686022906)
XLA Ops:
  0.6 0.0 copy-start.6
  0.6 0.0 copy-start.2
  0.7 0.0 copy-start.7
  0.7 0.8 %collective-permute-start = (bf16[192,256]{1,0:T(8,128)(2,1)}, bf16[192,256]{1,0:T(8,128)(2,1)S(1)}, u32[]{:S(2)}, u32[]{:S(2)}) collective-permute-start(bf16[192,256]{1,0:T(8,128)(2,1)} %g_ref.1), channel_id=1, source_target_pairs={{8,16},{16,8},{24,32},{32,24},{40,48},{48,40},{56,64},{64,56},{72,... | collective-permute-start | bytes 294920 | tf_op jit(solution)/shard_map/ppermute | solution.py:345
  1.5 8.2 %collective-permute-start.1 = (bf16[192,256]{1,0:T(8,128)(2,1)}, bf16[192,256]{1,0:T(8,128)(2,1)S(1)}, u32[]{:S(2)}, u32[]{:S(2)}) collective-permute-start(bf16[192,256]{1,0:T(8,128)(2,1)} %g_ref.1), channel_id=1, source_target_pairs={{0,8},{8,0},{16,24},{24,16},{32,40},{40,32},{48,56},{56,48},{64,72... | collective-permute-start | bytes 294920 | tf_op jit(solution)/shard_map/ppermute | solution.py:345
  10.3 1.7 %copy.16 = bf16[384,1536]{0,1:T(8,128)(2,1)S(1)} copy(bf16[384,1536]{1,0:T(8,128)(2,1)} %bitcast.17) | data formatting | bytes 2359296 | tf_op jit(solution)/shard_map/reshape | solution.py:386
  12.1 1.4 %shard_map.138 = (bf16[592,256]{1,0:T(8,128)(2,1)S(1)}, f32[192,256]{1,0:T(8,128)S(1)}, f32[192,256]{1,0:T(8,128)S(1)}, f32[192,256]{1,0:T(8,128)S(1)}) custom-call(s32[1,1]{1,0:T(1,128)} %bitcast.odd_ref, s32[2,2,4]{2,1,0:T(2,128)S(1)} %bitcast.16, s32[1]{0:T(128)S(6)} %copy.17.count_ref, bf16[192,256]{1,0:T(8,128)(2,1)S(1)} %bitcast.13, ...), custom_call_target="tpu_custom_call" | custom-call | flops 3047424 | bytes 909312 | tf_op jit(solution)/shard_map/pallas_call | solution.py:27
  13.6 0.0 collective-permute-done.two_ref
  13.6 0.0 collective-permute-done.1.one_ref
  13.6 1.8 %shard_map.139 = bf16[1536,256]{1,0:T(8,128)(2,1)} custom-call(s32[1,1]{1,0:T(1,128)} %bitcast.odd_ref, bf16[192,256]{1,0:T(8,128)(2,1)S(1)} %collective-permute-done.two_ref, bf16[192,256]{1,0:T(8,128)(2,1)S(1)} %collective-permute-done.1.one_ref, f32[31,192]{1,0:T(8,128)S(1)} %copy-done.2, f32[192,256]{1,0:T(8,128)S(1)} %get-tuple-element.19.sum_ref, ...), custom_call_target="tpu_custom_call" | custom-call | flops 301989888 | bytes 1179648 | tf_op jit(solution)/shard_map/pallas_call | solution.py:27
  15.4 5.7 %all-to-all-start = ((bf16[8,192,256]{2,1,0:T(8,128)(2,1)}), bf16[8,192,256]{2,1,0:T(8,128)(2,1)S(1)}, u32[]{:S(2)}, u32[]{:S(2)}) async-start(bf16[8,192,256]{2,1,0:T(8,128)(2,1)} %bitcast.7), calls=%async_computation | async-start | bytes 1572864 | tf_op jit(solution)/shard_map/all_to_all | solution.py:397
  21.0 12.5 %collective-permute-start.4 = (bf16[592,256]{1,0:T(8,128)(2,1)S(1)}, bf16[592,256]{1,0:T(8,128)(2,1)S(1)}, u32[]{:S(2)}, u32[]{:S(2)}) collective-permute-start(bf16[592,256]{1,0:T(8,128)(2,1)S(1)} %get-tuple-element.23.own_ref), channel_id=1, source_target_pairs={{0,256},{8,264},{16,272},{24,280},{32,288},{40,296},{48,304},{56,3... | collective-permute-start | bytes 909320 | tf_op jit(solution)/shard_map/ppermute | solution.py:345
  33.6 3.0 %collective-permute-start.3 = (bf16[592,256]{1,0:T(8,128)(2,1)S(1)}, bf16[592,256]{1,0:T(8,128)(2,1)S(1)}, u32[]{:S(2)}, u32[]{:S(2)}) collective-permute-start(bf16[592,256]{1,0:T(8,128)(2,1)S(1)} %get-tuple-element.23.own_ref), channel_id=1, source_target_pairs={{0,504},{8,16},{16,8},{24,32},{32,24},{40,48},{48,40},{56,64},{64,... | collective-permute-start | bytes 909320 | tf_op jit(solution)/shard_map/ppermute | solution.py:345
  36.6 1.9 %collective-permute-start.2 = (bf16[592,256]{1,0:T(8,128)(2,1)S(1)}, bf16[592,256]{1,0:T(8,128)(2,1)S(1)}, u32[]{:S(2)}, u32[]{:S(2)}) collective-permute-start(bf16[592,256]{1,0:T(8,128)(2,1)S(1)} %get-tuple-element.23.own_ref), channel_id=1, source_target_pairs={{0,8},{8,0},{16,24},{24,16},{32,40},{40,32},{48,56},{56,48},{64,72... | collective-permute-start | bytes 909320 | tf_op jit(solution)/shard_map/ppermute | solution.py:345
  38.5 0.0 all-to-all-done
  38.5 0.1 convert_reduce_fusion
  38.7 0.0 copy-start.8
  38.7 14.6 %all_gather.3.stream_ref = bf16[1536,256]{1,0:T(8,128)(2,1)S(1)} all-gather(bf16[192,256]{1,0:T(8,128)(2,1)S(1)} %add_convert_fusion), channel_id=1, replica_groups=mesh['ctx'=64,'head'=8] {'head'}, dimensions={0}, use_global_device_ids=true | all-gather | bytes 884736 | tf_op jit(solution)/shard_map/all_gather | solution.py:404
  53.3 0.0 collective-permute-done.2.one_ref
  53.3 1.2 %shard_map.140 = (bf16[192,256]{1,0:T(8,128)(2,1)S(1)}, f32[12,256,256]{2,1,0:T(8,128)S(1)}, f32[9,256]{1,0:T(8,128)S(1)}) custom-call(bf16[192,1536]{1,0:T(8,128)(2,1)S(1)} %copy-done, bf16[1536,256]{1,0:T(8,128)(2,1)S(1)} %all_gather.3.stream_ref, bf16[592,256]{1,0:T(8,128)(2,1)S(1)} %get-tuple-element.23.own_ref, ...), custom_call_target="tpu_custom_call" | custom-call | flops 251658240 | bytes 1376256 | tf_op jit(solution)/shard_map/pallas_call | solution.py:27
  54.5 0.0 collective-permute-done.4.far_ref
  54.5 0.0 collective-permute-done.3.two_ref
  54.5 0.9 %shard_map.141 = (bf16[208,256]{1,0:T(8,128)(2,1)S(1)}, f32[12,256,256]{2,1,0:T(8,128)S(1)}, f32[6,256]{1,0:T(8,128)S(1)}) custom-call(bf16[592,256]{1,0:T(8,128)(2,1)S(1)} %get-tuple-element.23.own_ref, bf16[592,256]{1,0:T(8,128)(2,1)S(1)} %collective-permute-done.3.two_ref, bf16[592,256]{1,0:T(8,128)(2,1)S(1)} %collective-permute-done.4.far_ref, ...), custom_call_target="tpu_custom_call" | custom-call | flops 100663296 | bytes 909312 | tf_op jit(solution)/shard_map/pallas_call | solution.py:27
  55.5 7.4 %collective-permute-start.7 = (bf16[208,256]{1,0:T(8,128)(2,1)S(1)}, bf16[208,256]{1,0:T(8,128)(2,1)S(1)}, u32[]{:S(2)}, u32[]{:S(2)}) collective-permute-start(bf16[208,256]{1,0:T(8,128)(2,1)S(1)} %get-tuple-element.26.grad_ref), channel_id=1, source_target_pairs={{0,504},{8,16},{16,8},{24,32},{32,24},{40,48},{48,40},{56,64},{64,... | collective-permute-start | bytes 319496 | tf_op jit(solution)/shard_map/ppermute | solution.py:345
  62.8 2.5 %collective-permute-start.6 = (bf16[208,256]{1,0:T(8,128)(2,1)S(1)}, bf16[208,256]{1,0:T(8,128)(2,1)S(1)}, u32[]{:S(2)}, u32[]{:S(2)}) collective-permute-start(bf16[208,256]{1,0:T(8,128)(2,1)S(1)} %get-tuple-element.26.grad_ref), channel_id=1, source_target_pairs={{0,256},{8,264},{16,272},{24,280},{32,288},{40,296},{48,304},{56,3... | collective-permute-start | bytes 319496 | tf_op jit(solution)/shard_map/ppermute | solution.py:345
  65.4 1.9 %collective-permute-start.5 = (bf16[208,256]{1,0:T(8,128)(2,1)S(1)}, bf16[208,256]{1,0:T(8,128)(2,1)S(1)}, u32[]{:S(2)}, u32[]{:S(2)}) collective-permute-start(bf16[208,256]{1,0:T(8,128)(2,1)S(1)} %get-tuple-element.26.grad_ref), channel_id=1, source_target_pairs={{0,8},{8,0},{16,24},{24,16},{32,40},{40,32},{48,56},{56,48},{64,72... | collective-permute-start | bytes 319496 | tf_op jit(solution)/shard_map/ppermute | solution.py:345
  67.3 1.3 %shard_map.142 = (bf16[192,256]{1,0:T(8,128)(2,1)}, f32[384,256]{1,0:T(8,128)S(1)}) custom-call(bf16[592,256]{1,0:T(8,128)(2,1)S(1)} %get-tuple-element.23.own_ref, bf16[592,256]{1,0:T(8,128)(2,1)S(1)} %collective-permute-done.2.one_ref, bf16[592,256]{1,0:T(8,128)(2,1)S(1)} %collective-permute-done.3.two_ref, ...), custom_call_target="tpu_custom_call" | custom-call | flops 301989888 | bytes 1212416 | tf_op jit(solution)/shard_map/pallas_call | solution.py:27
  68.7 0.0 collective-permute-done.7.grad_two_ref
  68.7 0.9 %shard_map.143.acc_ref = f32[384,256]{1,0:T(8,128)S(1)} custom-call(bf16[592,256]{1,0:T(8,128)(2,1)S(1)} %get-tuple-element.23.own_ref, bf16[592,256]{1,0:T(8,128)(2,1)S(1)} %collective-permute-done.3.two_ref, bf16[208,256]{1,0:T(8,128)(2,1)S(1)} %collective-permute-done.7.grad_two_ref, f32[384,256]{1,0:T(8,128)S(1)} %get-tuple-element.31.acc_ref), custom_call_target="tpu_custom_call" | custom-call | flops 100663296 | bytes 909312 | tf_op jit(solution)/shard_map/pallas_call | solution.py:27
  69.5 4.2 %collective-permute-done.6.grad_far_ref = bf16[208,256]{1,0:T(8,128)(2,1)S(1)} collective-permute-done((bf16[208,256]{1,0:T(8,128)(2,1)S(1)}, bf16[208,256]{1,0:T(8,128)(2,1)S(1)}, u32[]{:S(2)}, u32[]{:S(2)}) %collective-permute-start.6) | collective-permute-done | bytes 106528 | tf_op jit(solution)/shard_map/ppermute | solution.py:345
  73.7 0.0 collective-permute-done.5.grad_one_ref
  73.7 2.0 %shard_map.144 = (bf16[192,256]{1,0:T(8,128)(2,1)}, bf16[192,256]{1,0:T(8,128)(2,1)}) custom-call(bf16[592,256]{1,0:T(8,128)(2,1)S(1)} %get-tuple-element.23.own_ref, bf16[592,256]{1,0:T(8,128)(2,1)S(1)} %collective-permute-done.2.one_ref, bf16[592,256]{1,0:T(8,128)(2,1)S(1)} %collective-permute-done.4.far_ref, ...), custom_call_target="tpu_custom_call" | custom-call | flops 201326592 | bytes 1212416 | tf_op jit(solution)/shard_map/pallas_call | solution.py:27
  (17 shorter events, 0.1 us)
Async XLA Ops:
  0.6 11.4 %copy-start.6 = (bf16[192,256]{1,0:T(8,128)(2,1)S(1)}, bf16[192,256]{1,0:T(8,128)(2,1)}, u32[]{:S(2)}) copy-start(bf16[192,256]{1,0:T(8,128)(2,1)} %g_ref.1) | copy-start | bytes 294916
  0.6 11.4 %copy-start.2 = (f32[31,192]{1,0:T(8,128)S(1)}, f32[31,192]{1,0:T(8,128)}, u32[]{:S(2)}) copy-start(f32[31,192]{1,0:T(8,128)} %taps_ref.3) | copy-start | bytes 71428
  0.7 11.4 %copy-start.7 = (s32[2,4,2]{1,2,0:T(2,128)S(1)}, s32[2,4,2]{1,2,0:T(2,128)}, u32[]{:S(2)}) copy-start(s32[2,4,2]{1,2,0:T(2,128)} %param.20) | copy-start | bytes 196
  0.7 11.4 %copy-start.4 = (bf16[256,192]{0,1:T(8,128)(2,1)S(1)}, bf16[256,192]{0,1:T(8,128)(2,1)}, u32[]{:S(2)}) copy-start(bf16[256,192]{0,1:T(8,128)(2,1)} %param.19) | copy-start | bytes 294916
  0.7 11.4 %copy-start.3 = (bf16[256,192]{0,1:T(8,128)(2,1)S(1)}, bf16[256,192]{0,1:T(8,128)(2,1)}, u32[]{:S(2)}) copy-start(bf16[256,192]{0,1:T(8,128)(2,1)} %param.18) | copy-start | bytes 294916
  0.7 11.4 %copy-start.5 = (bf16[256,192]{0,1:T(8,128)(2,1)S(1)}, bf16[256,192]{0,1:T(8,128)(2,1)}, u32[]{:S(2)}) copy-start(bf16[256,192]{0,1:T(8,128)(2,1)} %param.17) | copy-start | bytes 294916
  0.7 11.4 %copy-start.1 = (bf16[2,192,256]{2,1,0:T(8,128)(2,1)S(1)}, bf16[2,192,256]{2,1,0:T(8,128)(2,1)}, u32[]{:S(2)}) copy-start(bf16[2,192,256]{2,1,0:T(8,128)(2,1)} %pre_ref.1) | copy-start | bytes 589828
  0.7 12.9 %collective-permute-start = (bf16[192,256]{1,0:T(8,128)(2,1)}, bf16[192,256]{1,0:T(8,128)(2,1)S(1)}, u32[]{:S(2)}, u32[]{:S(2)}) collective-permute-start(bf16[192,256]{1,0:T(8,128)(2,1)} %g_ref.1), channel_id=1, source_target_pairs={{8,16},{16,8},{24,32},{32,24},{40,48},{48,40},{56,64},{64,56},{72,... | collective-permute-start | bytes 294920 | tf_op jit(solution)/shard_map/ppermute | solution.py:345
  1.5 12.1 %collective-permute-start.1 = (bf16[192,256]{1,0:T(8,128)(2,1)}, bf16[192,256]{1,0:T(8,128)(2,1)S(1)}, u32[]{:S(2)}, u32[]{:S(2)}) collective-permute-start(bf16[192,256]{1,0:T(8,128)(2,1)} %g_ref.1), channel_id=1, source_target_pairs={{0,8},{8,0},{16,24},{24,16},{32,40},{40,32},{48,56},{56,48},{64,72... | collective-permute-start | bytes 294920 | tf_op jit(solution)/shard_map/ppermute | solution.py:345
  15.4 23.3 %copy-start.9 = (bf16[192,256]{1,0:T(8,128)(2,1)S(1)}, bf16[192,256]{1,0:T(8,128)(2,1)}, u32[]{:S(2)}) copy-start(bf16[192,256]{1,0:T(8,128)(2,1)} %param.15) | copy-start | bytes 294916
  15.4 38.0 %copy-start = (bf16[192,1536]{1,0:T(8,128)(2,1)S(1)}, bf16[192,1536]{1,0:T(8,128)(2,1)}, u32[]{:S(2)}) copy-start(bf16[192,1536]{1,0:T(8,128)(2,1)} %w_ref.1) | copy-start | bytes 1769476
  15.4 23.2 %all-to-all-start = ((bf16[8,192,256]{2,1,0:T(8,128)(2,1)}), bf16[8,192,256]{2,1,0:T(8,128)(2,1)S(1)}, u32[]{:S(2)}, u32[]{:S(2)}) async-start(bf16[8,192,256]{2,1,0:T(8,128)(2,1)} %bitcast.7), calls=%async_computation | async-start | bytes 1572864 | tf_op jit(solution)/shard_map/all_to_all | solution.py:397
  21.0 33.5 %collective-permute-start.4 = (bf16[592,256]{1,0:T(8,128)(2,1)S(1)}, bf16[592,256]{1,0:T(8,128)(2,1)S(1)}, u32[]{:S(2)}, u32[]{:S(2)}) collective-permute-start(bf16[592,256]{1,0:T(8,128)(2,1)S(1)} %get-tuple-element.23.own_ref), channel_id=1, source_target_pairs={{0,256},{8,264},{16,272},{24,280},{32,288},{40,296},{48,304},{56,3... | collective-permute-start | bytes 909320 | tf_op jit(solution)/shard_map/ppermute | solution.py:345
  33.6 21.0 %collective-permute-start.3 = (bf16[592,256]{1,0:T(8,128)(2,1)S(1)}, bf16[592,256]{1,0:T(8,128)(2,1)S(1)}, u32[]{:S(2)}, u32[]{:S(2)}) collective-permute-start(bf16[592,256]{1,0:T(8,128)(2,1)S(1)} %get-tuple-element.23.own_ref), channel_id=1, source_target_pairs={{0,504},{8,16},{16,8},{24,32},{32,24},{40,48},{48,40},{56,64},{64,... | collective-permute-start | bytes 909320 | tf_op jit(solution)/shard_map/ppermute | solution.py:345
  36.6 16.7 %collective-permute-start.2 = (bf16[592,256]{1,0:T(8,128)(2,1)S(1)}, bf16[592,256]{1,0:T(8,128)(2,1)S(1)}, u32[]{:S(2)}, u32[]{:S(2)}) collective-permute-start(bf16[592,256]{1,0:T(8,128)(2,1)S(1)} %get-tuple-element.23.own_ref), channel_id=1, source_target_pairs={{0,8},{8,0},{16,24},{24,16},{32,40},{40,32},{48,56},{56,48},{64,72... | collective-permute-start | bytes 909320 | tf_op jit(solution)/shard_map/ppermute | solution.py:345
  38.7 16.8 %copy-start.8 = (bf16[192,256]{1,0:T(8,128)(2,1)}, bf16[192,256]{1,0:T(8,128)(2,1)S(1)}, u32[]{:S(2)}) copy-start(bf16[192,256]{1,0:T(8,128)(2,1)S(1)} %add_convert_fusion) | copy-start | bytes 294916
  55.5 13.2 %collective-permute-start.7 = (bf16[208,256]{1,0:T(8,128)(2,1)S(1)}, bf16[208,256]{1,0:T(8,128)(2,1)S(1)}, u32[]{:S(2)}, u32[]{:S(2)}) collective-permute-start(bf16[208,256]{1,0:T(8,128)(2,1)S(1)} %get-tuple-element.26.grad_ref), channel_id=1, source_target_pairs={{0,504},{8,16},{16,8},{24,32},{32,24},{40,48},{48,40},{56,64},{64,... | collective-permute-start | bytes 319496 | tf_op jit(solution)/shard_map/ppermute | solution.py:345
  62.8 10.9 %collective-permute-start.6 = (bf16[208,256]{1,0:T(8,128)(2,1)S(1)}, bf16[208,256]{1,0:T(8,128)(2,1)S(1)}, u32[]{:S(2)}, u32[]{:S(2)}) collective-permute-start(bf16[208,256]{1,0:T(8,128)(2,1)S(1)} %get-tuple-element.26.grad_ref), channel_id=1, source_target_pairs={{0,256},{8,264},{16,272},{24,280},{32,288},{40,296},{48,304},{56,3... | collective-permute-start | bytes 319496 | tf_op jit(solution)/shard_map/ppermute | solution.py:345
  65.4 8.4 %collective-permute-start.5 = (bf16[208,256]{1,0:T(8,128)(2,1)S(1)}, bf16[208,256]{1,0:T(8,128)(2,1)S(1)}, u32[]{:S(2)}, u32[]{:S(2)}) collective-permute-start(bf16[208,256]{1,0:T(8,128)(2,1)S(1)} %get-tuple-element.26.grad_ref), channel_id=1, source_target_pairs={{0,8},{8,0},{16,24},{24,16},{32,40},{40,32},{48,56},{56,48},{64,72... | collective-permute-start | bytes 319496 | tf_op jit(solution)/shard_map/ppermute | solution.py:345

commit v11 on v10

--- a/solution.py
+++ b/solution.py
@@ -312,23 +312,23 @@
     return key_term, value_term
 
 
-def middle_body(columns, own_ref, two_ref, grad_two_ref, acc_ref, acc_out):
+def middle_body(columns, own_ref, far_ref, grad_far_ref, acc_ref, acc_out):
     for h in range(columns // HEAD_DIM):
         lo, hi = h * HEAD_DIM, (h + 1) * HEAD_DIM
         key_term, value_term = remote_terms(
-            columns, (2,), own_ref, (two_ref,), (grad_two_ref,), h
+            columns, (3,), own_ref, (far_ref,), (grad_far_ref,), h
         )
         acc_out[lo:hi, :] = acc_ref[lo:hi, :] + key_term
         acc_out[columns + lo : columns + hi, :] = acc_ref[columns + lo : columns + hi, :] + value_term
 
 
 def last_body(
-    columns, own_ref, one_ref, far_ref, grad_one_ref, grad_far_ref, acc_ref, key_out, value_out
+    columns, own_ref, one_ref, two_ref, grad_one_ref, grad_two_ref, acc_ref, key_out, value_out
 ):
     for h in range(columns // HEAD_DIM):
         lo, hi = h * HEAD_DIM, (h + 1) * HEAD_DIM
         key_term, value_term = remote_terms(
-            columns, (1, 3), own_ref, (one_ref, far_ref), (grad_one_ref, grad_far_ref), h
+            columns, (1, 2), own_ref, (one_ref, two_ref), (grad_one_ref, grad_two_ref), h
         )
         key_out[lo:hi, :] = ((acc_ref[lo:hi, :] + key_term) * SCALE).astype(BF16)
         value_out[lo:hi, :] = (acc_ref[columns + lo : columns + hi, :] + value_term).astype(BF16)
@@ -441,7 +441,7 @@
     acc = call(
         functools.partial(middle_body, columns),
         shape((2 * columns, row_count), F32),
-        (own, two, grad_two, acc),
+        (own, far, grad_far, acc),
         [VMEM] * 4,
         4 * square,
         6 * message * row_count,
@@ -450,7 +450,7 @@
     grad_keys, grad_values = call(
         functools.partial(last_body, columns),
         (shape(flat, BF16), shape(flat, BF16)),
-        (own, one, far, grad_one, grad_far, acc),
+        (own, one, two, grad_one, grad_two, acc),
         [VMEM] * 6,
         8 * square,
         8 * message * row_count,

time: 76.2 us -> 75.2 us (0.987)
  waiting for transfers between devices: 4.23 us -> 3.21 us
    ppermute x8, waiting for transfers between devices: 4.23 us -> 3.21 us  [exchange(): return lax.ppermute(value, 'ctx', pairs)]
where the time goes in v11:
time: 75.2 us; the launch traced here: 74.7 us
  starting transfers between devices  43.9 us (58%)
  blocking collectives  14.6 us (19%)
  Pallas kernels  9.53 us (13%)
  waiting for transfers between devices  3.21 us (4%)
  local copies, waits for them, and re-layouts  1.75 us (2%)
  between operations  1.57 us (2%)
    ppermute x8, starting transfers between devices, exchange(): return lax.ppermute(value, 'ctx', pairs)  38.3 us
    all_gather x1, blocking collectives, per_device(): stream_full = lax.all_gather(stream_grad, 'head', axis=0, tiled=True)  14.6 us
    pallas_call x7, Pallas kernels, call(): pl.pallas_call(body, out_shape=out_shapes, in_specs=specs, out_specs=jax....  9.53 us
    all_to_all x1, starting transfers between devices, per_device(): lax.all_to_all(point_grad.reshape(groups, columns, row_count), 'head', 0,...  5.66 us
    ppermute x8, waiting for transfers between devices, exchange(): return lax.ppermute(value, 'ctx', pairs)  3.21 us
    reshape x1, local copies, waits for them, and re-layouts, per_device(): w_turned = w_point.reshape(2 * columns, model).T  1.7 us
  transfers between devices with their start and end apart: 9, of which 1 were waited for; matrix products, arithmetic and copies ran while one was open for 2% of the time, Pallas kernels for 6%

profile of v11, /device:TPU:1, one launch (start us, length us, event | category | flops | bytes accessed | tf_op | source)
XLA Modules:
  0.0 74.7 jit_solution(2502946384807930995)
XLA Ops:
  0.6 0.0 copy-start.6
  0.6 0.0 copy-start.2
  0.7 0.0 copy-start.7
  0.7 0.8 %collective-permute-start = (bf16[192,256]{1,0:T(8,128)(2,1)}, bf16[192,256]{1,0:T(8,128)(2,1)S(1)}, u32[]{:S(2)}, u32[]{:S(2)}) collective-permute-start(bf16[192,256]{1,0:T(8,128)(2,1)} %g_ref.1), channel_id=1, source_target_pairs={{8,16},{16,8},{24,32},{32,24},{40,48},{48,40},{56,64},{64,56},{72,... | collective-permute-start | bytes 294920 | tf_op jit(solution)/shard_map/ppermute | solution.py:345
  1.5 8.2 %collective-permute-start.1 = (bf16[192,256]{1,0:T(8,128)(2,1)}, bf16[192,256]{1,0:T(8,128)(2,1)S(1)}, u32[]{:S(2)}, u32[]{:S(2)}) collective-permute-start(bf16[192,256]{1,0:T(8,128)(2,1)} %g_ref.1), channel_id=1, source_target_pairs={{0,8},{8,0},{16,24},{24,16},{32,40},{40,32},{48,56},{56,48},{64,72... | collective-permute-start | bytes 294920 | tf_op jit(solution)/shard_map/ppermute | solution.py:345
  10.3 1.7 %copy.16 = bf16[384,1536]{0,1:T(8,128)(2,1)S(1)} copy(bf16[384,1536]{1,0:T(8,128)(2,1)} %bitcast.17) | data formatting | bytes 2359296 | tf_op jit(solution)/shard_map/reshape | solution.py:386
  12.1 1.4 %shard_map.138 = (bf16[592,256]{1,0:T(8,128)(2,1)S(1)}, f32[192,256]{1,0:T(8,128)S(1)}, f32[192,256]{1,0:T(8,128)S(1)}, f32[192,256]{1,0:T(8,128)S(1)}) custom-call(s32[1,1]{1,0:T(1,128)} %bitcast.odd_ref, s32[2,2,4]{2,1,0:T(2,128)S(1)} %bitcast.16, s32[1]{0:T(128)S(6)} %copy.17.count_ref, bf16[192,256]{1,0:T(8,128)(2,1)S(1)} %bitcast.13, ...), custom_call_target="tpu_custom_call" | custom-call | flops 3047424 | bytes 909312 | tf_op jit(solution)/shard_map/pallas_call | solution.py:27
  13.6 0.0 collective-permute-done.two_ref
  13.6 0.0 collective-permute-done.1.one_ref
  13.6 1.8 %shard_map.139 = bf16[1536,256]{1,0:T(8,128)(2,1)} custom-call(s32[1,1]{1,0:T(1,128)} %bitcast.odd_ref, bf16[192,256]{1,0:T(8,128)(2,1)S(1)} %collective-permute-done.two_ref, bf16[192,256]{1,0:T(8,128)(2,1)S(1)} %collective-permute-done.1.one_ref, f32[31,192]{1,0:T(8,128)S(1)} %copy-done.2, f32[192,256]{1,0:T(8,128)S(1)} %get-tuple-element.19.sum_ref, ...), custom_call_target="tpu_custom_call" | custom-call | flops 301989888 | bytes 1179648 | tf_op jit(solution)/shard_map/pallas_call | solution.py:27
  15.4 5.7 %all-to-all-start = ((bf16[8,192,256]{2,1,0:T(8,128)(2,1)}), bf16[8,192,256]{2,1,0:T(8,128)(2,1)S(1)}, u32[]{:S(2)}, u32[]{:S(2)}) async-start(bf16[8,192,256]{2,1,0:T(8,128)(2,1)} %bitcast.7), calls=%async_computation | async-start | bytes 1572864 | tf_op jit(solution)/shard_map/all_to_all | solution.py:397
  21.0 12.5 %collective-permute-start.4 = (bf16[592,256]{1,0:T(8,128)(2,1)S(1)}, bf16[592,256]{1,0:T(8,128)(2,1)S(1)}, u32[]{:S(2)}, u32[]{:S(2)}) collective-permute-start(bf16[592,256]{1,0:T(8,128)(2,1)S(1)} %get-tuple-element.23.own_ref), channel_id=1, source_target_pairs={{0,256},{8,264},{16,272},{24,280},{32,288},{40,296},{48,304},{56,3... | collective-permute-start | bytes 909320 | tf_op jit(solution)/shard_map/ppermute | solution.py:345
  33.6 3.0 %collective-permute-start.3 = (bf16[592,256]{1,0:T(8,128)(2,1)S(1)}, bf16[592,256]{1,0:T(8,128)(2,1)S(1)}, u32[]{:S(2)}, u32[]{:S(2)}) collective-permute-start(bf16[592,256]{1,0:T(8,128)(2,1)S(1)} %get-tuple-element.23.own_ref), channel_id=1, source_target_pairs={{0,504},{8,16},{16,8},{24,32},{32,24},{40,48},{48,40},{56,64},{64,... | collective-permute-start | bytes 909320 | tf_op jit(solution)/shard_map/ppermute | solution.py:345
  36.6 1.9 %collective-permute-start.2 = (bf16[592,256]{1,0:T(8,128)(2,1)S(1)}, bf16[592,256]{1,0:T(8,128)(2,1)S(1)}, u32[]{:S(2)}, u32[]{:S(2)}) collective-permute-start(bf16[592,256]{1,0:T(8,128)(2,1)S(1)} %get-tuple-element.23.own_ref), channel_id=1, source_target_pairs={{0,8},{8,0},{16,24},{24,16},{32,40},{40,32},{48,56},{56,48},{64,72... | collective-permute-start | bytes 909320 | tf_op jit(solution)/shard_map/ppermute | solution.py:345
  38.5 0.0 all-to-all-done
  38.5 0.1 convert_reduce_fusion
  38.7 0.0 copy-start.8
  38.7 14.6 %all_gather.3.stream_ref = bf16[1536,256]{1,0:T(8,128)(2,1)S(1)} all-gather(bf16[192,256]{1,0:T(8,128)(2,1)S(1)} %add_convert_fusion), channel_id=1, replica_groups=mesh['ctx'=64,'head'=8] {'head'}, dimensions={0}, use_global_device_ids=true | all-gather | bytes 884736 | tf_op jit(solution)/shard_map/all_gather | solution.py:404
  53.3 0.0 collective-permute-done.2.one_ref
  53.3 1.2 %shard_map.140 = (bf16[192,256]{1,0:T(8,128)(2,1)S(1)}, f32[12,256,256]{2,1,0:T(8,128)S(1)}, f32[9,256]{1,0:T(8,128)S(1)}) custom-call(bf16[192,1536]{1,0:T(8,128)(2,1)S(1)} %copy-done, bf16[1536,256]{1,0:T(8,128)(2,1)S(1)} %all_gather.3.stream_ref, bf16[592,256]{1,0:T(8,128)(2,1)S(1)} %get-tuple-element.23.own_ref, ...), custom_call_target="tpu_custom_call" | custom-call | flops 251658240 | bytes 1376256 | tf_op jit(solution)/shard_map/pallas_call | solution.py:27
  54.5 0.0 collective-permute-done.4.far_ref
  54.5 0.0 collective-permute-done.3.two_ref
  54.5 0.9 %shard_map.141 = (bf16[208,256]{1,0:T(8,128)(2,1)S(1)}, f32[12,256,256]{2,1,0:T(8,128)S(1)}, f32[6,256]{1,0:T(8,128)S(1)}) custom-call(bf16[592,256]{1,0:T(8,128)(2,1)S(1)} %get-tuple-element.23.own_ref, bf16[592,256]{1,0:T(8,128)(2,1)S(1)} %collective-permute-done.3.two_ref, bf16[592,256]{1,0:T(8,128)(2,1)S(1)} %collective-permute-done.4.far_ref, ...), custom_call_target="tpu_custom_call" | custom-call | flops 100663296 | bytes 909312 | tf_op jit(solution)/shard_map/pallas_call | solution.py:27
  55.5 6.8 %collective-permute-start.7 = (bf16[208,256]{1,0:T(8,128)(2,1)S(1)}, bf16[208,256]{1,0:T(8,128)(2,1)S(1)}, u32[]{:S(2)}, u32[]{:S(2)}) collective-permute-start(bf16[208,256]{1,0:T(8,128)(2,1)S(1)} %get-tuple-element.26.grad_ref), channel_id=1, source_target_pairs={{0,256},{8,264},{16,272},{24,280},{32,288},{40,296},{48,304},{56,3... | collective-permute-start | bytes 319496 | tf_op jit(solution)/shard_map/ppermute | solution.py:345
  62.3 3.1 %collective-permute-start.6 = (bf16[208,256]{1,0:T(8,128)(2,1)S(1)}, bf16[208,256]{1,0:T(8,128)(2,1)S(1)}, u32[]{:S(2)}, u32[]{:S(2)}) collective-permute-start(bf16[208,256]{1,0:T(8,128)(2,1)S(1)} %get-tuple-element.26.grad_ref), channel_id=1, source_target_pairs={{0,504},{8,16},{16,8},{24,32},{32,24},{40,48},{48,40},{56,64},{64,... | collective-permute-start | bytes 319496 | tf_op jit(solution)/shard_map/ppermute | solution.py:345
  65.4 1.9 %collective-permute-start.5 = (bf16[208,256]{1,0:T(8,128)(2,1)S(1)}, bf16[208,256]{1,0:T(8,128)(2,1)S(1)}, u32[]{:S(2)}, u32[]{:S(2)}) collective-permute-start(bf16[208,256]{1,0:T(8,128)(2,1)S(1)} %get-tuple-element.26.grad_ref), channel_id=1, source_target_pairs={{0,8},{8,0},{16,24},{24,16},{32,40},{40,32},{48,56},{56,48},{64,72... | collective-permute-start | bytes 319496 | tf_op jit(solution)/shard_map/ppermute | solution.py:345
  67.3 1.3 %shard_map.142 = (bf16[192,256]{1,0:T(8,128)(2,1)}, f32[384,256]{1,0:T(8,128)S(1)}) custom-call(bf16[592,256]{1,0:T(8,128)(2,1)S(1)} %get-tuple-element.23.own_ref, bf16[592,256]{1,0:T(8,128)(2,1)S(1)} %collective-permute-done.2.one_ref, bf16[592,256]{1,0:T(8,128)(2,1)S(1)} %collective-permute-done.3.two_ref, ...), custom_call_target="tpu_custom_call" | custom-call | flops 301989888 | bytes 1212416 | tf_op jit(solution)/shard_map/pallas_call | solution.py:27
  68.7 0.0 collective-permute-done.7.grad_far_ref
  68.7 0.9 %shard_map.143.acc_ref = f32[384,256]{1,0:T(8,128)S(1)} custom-call(bf16[592,256]{1,0:T(8,128)(2,1)S(1)} %get-tuple-element.23.own_ref, bf16[592,256]{1,0:T(8,128)(2,1)S(1)} %collective-permute-done.4.far_ref, bf16[208,256]{1,0:T(8,128)(2,1)S(1)} %collective-permute-done.7.grad_far_ref, f32[384,256]{1,0:T(8,128)S(1)} %get-tuple-element.31.acc_ref), custom_call_target="tpu_custom_call" | custom-call | flops 100663296 | bytes 909312 | tf_op jit(solution)/shard_map/pallas_call | solution.py:27
  69.5 3.2 %collective-permute-done.6.grad_two_ref = bf16[208,256]{1,0:T(8,128)(2,1)S(1)} collective-permute-done((bf16[208,256]{1,0:T(8,128)(2,1)S(1)}, bf16[208,256]{1,0:T(8,128)(2,1)S(1)}, u32[]{:S(2)}, u32[]{:S(2)}) %collective-permute-start.6) | collective-permute-done | bytes 106528 | tf_op jit(solution)/shard_map/ppermute | solution.py:345
  72.7 0.0 collective-permute-done.5.grad_one_ref
  72.7 2.0 %shard_map.144 = (bf16[192,256]{1,0:T(8,128)(2,1)}, bf16[192,256]{1,0:T(8,128)(2,1)}) custom-call(bf16[592,256]{1,0:T(8,128)(2,1)S(1)} %get-tuple-element.23.own_ref, bf16[592,256]{1,0:T(8,128)(2,1)S(1)} %collective-permute-done.2.one_ref, bf16[592,256]{1,0:T(8,128)(2,1)S(1)} %collective-permute-done.3.two_ref, ...), custom_call_target="tpu_custom_call" | custom-call | flops 201326592 | bytes 1212416 | tf_op jit(solution)/shard_map/pallas_call | solution.py:27
  (17 shorter events, 0.1 us)
Async XLA Ops:
  0.6 11.4 %copy-start.6 = (bf16[192,256]{1,0:T(8,128)(2,1)S(1)}, bf16[192,256]{1,0:T(8,128)(2,1)}, u32[]{:S(2)}) copy-start(bf16[192,256]{1,0:T(8,128)(2,1)} %g_ref.1) | copy-start | bytes 294916
  0.6 11.4 %copy-start.2 = (f32[31,192]{1,0:T(8,128)S(1)}, f32[31,192]{1,0:T(8,128)}, u32[]{:S(2)}) copy-start(f32[31,192]{1,0:T(8,128)} %taps_ref.3) | copy-start | bytes 71428
  0.7 11.4 %copy-start.7 = (s32[2,4,2]{1,2,0:T(2,128)S(1)}, s32[2,4,2]{1,2,0:T(2,128)}, u32[]{:S(2)}) copy-start(s32[2,4,2]{1,2,0:T(2,128)} %param.20) | copy-start | bytes 196
  0.7 11.4 %copy-start.4 = (bf16[256,192]{0,1:T(8,128)(2,1)S(1)}, bf16[256,192]{0,1:T(8,128)(2,1)}, u32[]{:S(2)}) copy-start(bf16[256,192]{0,1:T(8,128)(2,1)} %param.19) | copy-start | bytes 294916
  0.7 11.4 %copy-start.3 = (bf16[256,192]{0,1:T(8,128)(2,1)S(1)}, bf16[256,192]{0,1:T(8,128)(2,1)}, u32[]{:S(2)}) copy-start(bf16[256,192]{0,1:T(8,128)(2,1)} %param.18) | copy-start | bytes 294916
  0.7 11.4 %copy-start.5 = (bf16[256,192]{0,1:T(8,128)(2,1)S(1)}, bf16[256,192]{0,1:T(8,128)(2,1)}, u32[]{:S(2)}) copy-start(bf16[256,192]{0,1:T(8,128)(2,1)} %param.17) | copy-start | bytes 294916
  0.7 11.4 %copy-start.1 = (bf16[2,192,256]{2,1,0:T(8,128)(2,1)S(1)}, bf16[2,192,256]{2,1,0:T(8,128)(2,1)}, u32[]{:S(2)}) copy-start(bf16[2,192,256]{2,1,0:T(8,128)(2,1)} %pre_ref.1) | copy-start | bytes 589828
  0.7 12.9 %collective-permute-start = (bf16[192,256]{1,0:T(8,128)(2,1)}, bf16[192,256]{1,0:T(8,128)(2,1)S(1)}, u32[]{:S(2)}, u32[]{:S(2)}) collective-permute-start(bf16[192,256]{1,0:T(8,128)(2,1)} %g_ref.1), channel_id=1, source_target_pairs={{8,16},{16,8},{24,32},{32,24},{40,48},{48,40},{56,64},{64,56},{72,... | collective-permute-start | bytes 294920 | tf_op jit(solution)/shard_map/ppermute | solution.py:345
  1.5 12.1 %collective-permute-start.1 = (bf16[192,256]{1,0:T(8,128)(2,1)}, bf16[192,256]{1,0:T(8,128)(2,1)S(1)}, u32[]{:S(2)}, u32[]{:S(2)}) collective-permute-start(bf16[192,256]{1,0:T(8,128)(2,1)} %g_ref.1), channel_id=1, source_target_pairs={{0,8},{8,0},{16,24},{24,16},{32,40},{40,32},{48,56},{56,48},{64,72... | collective-permute-start | bytes 294920 | tf_op jit(solution)/shard_map/ppermute | solution.py:345
  15.4 23.3 %copy-start.9 = (bf16[192,256]{1,0:T(8,128)(2,1)S(1)}, bf16[192,256]{1,0:T(8,128)(2,1)}, u32[]{:S(2)}) copy-start(bf16[192,256]{1,0:T(8,128)(2,1)} %param.15) | copy-start | bytes 294916
  15.4 38.0 %copy-start = (bf16[192,1536]{1,0:T(8,128)(2,1)S(1)}, bf16[192,1536]{1,0:T(8,128)(2,1)}, u32[]{:S(2)}) copy-start(bf16[192,1536]{1,0:T(8,128)(2,1)} %w_ref.1) | copy-start | bytes 1769476
  15.4 23.2 %all-to-all-start = ((bf16[8,192,256]{2,1,0:T(8,128)(2,1)}), bf16[8,192,256]{2,1,0:T(8,128)(2,1)S(1)}, u32[]{:S(2)}, u32[]{:S(2)}) async-start(bf16[8,192,256]{2,1,0:T(8,128)(2,1)} %bitcast.7), calls=%async_computation | async-start | bytes 1572864 | tf_op jit(solution)/shard_map/all_to_all | solution.py:397
  21.0 33.5 %collective-permute-start.4 = (bf16[592,256]{1,0:T(8,128)(2,1)S(1)}, bf16[592,256]{1,0:T(8,128)(2,1)S(1)}, u32[]{:S(2)}, u32[]{:S(2)}) collective-permute-start(bf16[592,256]{1,0:T(8,128)(2,1)S(1)} %get-tuple-element.23.own_ref), channel_id=1, source_target_pairs={{0,256},{8,264},{16,272},{24,280},{32,288},{40,296},{48,304},{56,3... | collective-permute-start | bytes 909320 | tf_op jit(solution)/shard_map/ppermute | solution.py:345
  33.6 21.0 %collective-permute-start.3 = (bf16[592,256]{1,0:T(8,128)(2,1)S(1)}, bf16[592,256]{1,0:T(8,128)(2,1)S(1)}, u32[]{:S(2)}, u32[]{:S(2)}) collective-permute-start(bf16[592,256]{1,0:T(8,128)(2,1)S(1)} %get-tuple-element.23.own_ref), channel_id=1, source_target_pairs={{0,504},{8,16},{16,8},{24,32},{32,24},{40,48},{48,40},{56,64},{64,... | collective-permute-start | bytes 909320 | tf_op jit(solution)/shard_map/ppermute | solution.py:345
  36.6 16.7 %collective-permute-start.2 = (bf16[592,256]{1,0:T(8,128)(2,1)S(1)}, bf16[592,256]{1,0:T(8,128)(2,1)S(1)}, u32[]{:S(2)}, u32[]{:S(2)}) collective-permute-start(bf16[592,256]{1,0:T(8,128)(2,1)S(1)} %get-tuple-element.23.own_ref), channel_id=1, source_target_pairs={{0,8},{8,0},{16,24},{24,16},{32,40},{40,32},{48,56},{56,48},{64,72... | collective-permute-start | bytes 909320 | tf_op jit(solution)/shard_map/ppermute | solution.py:345
  38.7 16.8 %copy-start.8 = (bf16[192,256]{1,0:T(8,128)(2,1)}, bf16[192,256]{1,0:T(8,128)(2,1)S(1)}, u32[]{:S(2)}) copy-start(bf16[192,256]{1,0:T(8,128)(2,1)S(1)} %add_convert_fusion) | copy-start | bytes 294916
  55.5 13.2 %collective-permute-start.7 = (bf16[208,256]{1,0:T(8,128)(2,1)S(1)}, bf16[208,256]{1,0:T(8,128)(2,1)S(1)}, u32[]{:S(2)}, u32[]{:S(2)}) collective-permute-start(bf16[208,256]{1,0:T(8,128)(2,1)S(1)} %get-tuple-element.26.grad_ref), channel_id=1, source_target_pairs={{0,256},{8,264},{16,272},{24,280},{32,288},{40,296},{48,304},{56,3... | collective-permute-start | bytes 319496 | tf_op jit(solution)/shard_map/ppermute | solution.py:345
  62.3 10.4 %collective-permute-start.6 = (bf16[208,256]{1,0:T(8,128)(2,1)S(1)}, bf16[208,256]{1,0:T(8,128)(2,1)S(1)}, u32[]{:S(2)}, u32[]{:S(2)}) collective-permute-start(bf16[208,256]{1,0:T(8,128)(2,1)S(1)} %get-tuple-element.26.grad_ref), channel_id=1, source_target_pairs={{0,504},{8,16},{16,8},{24,32},{32,24},{40,48},{48,40},{56,64},{64,... | collective-permute-start | bytes 319496 | tf_op jit(solution)/shard_map/ppermute | solution.py:345
  65.4 7.3 %collective-permute-start.5 = (bf16[208,256]{1,0:T(8,128)(2,1)S(1)}, bf16[208,256]{1,0:T(8,128)(2,1)S(1)}, u32[]{:S(2)}, u32[]{:S(2)}) collective-permute-start(bf16[208,256]{1,0:T(8,128)(2,1)S(1)} %get-tuple-element.26.grad_ref), channel_id=1, source_target_pairs={{0,8},{8,0},{16,24},{24,16},{32,40},{40,32},{48,56},{56,48},{64,72... | collective-permute-start | bytes 319496 | tf_op jit(solution)/shard_map/ppermute | solution.py:345

commit v12 on v8

--- a/solution.py
+++ b/solution.py
@@ -77,7 +77,7 @@
     row = lax.broadcasted_iota(jnp.int32, (META, rows), 0)
     first = lax.broadcasted_iota(jnp.int32, (META, rows), 1) < rows // 2
     odd = odd_ref[...] > 0
-    meta = jnp.where(row == 0, count_ref[...].astype(F32), 0.0)
+    meta = jnp.where(row == 0, count_ref[...].astype(F32).reshape(1, 1), 0.0)
     for kb in range(2):
         bits = []
         for qb in range(2):
@@ -280,21 +280,23 @@
     return key_term, value_term
 
 
-def middle_body(columns, own_ref, one_ref, far_ref, grad_one_ref, grad_far_ref, acc_ref, acc_out):
+def middle_body(columns, own_ref, far_ref, grad_far_ref, acc_ref, acc_out):
     for h in range(columns // HEAD_DIM):
         lo, hi = h * HEAD_DIM, (h + 1) * HEAD_DIM
         key_term, value_term = remote_terms(
-            columns, (1, 3), own_ref, (one_ref, far_ref), (grad_one_ref, grad_far_ref), h
+            columns, (3,), own_ref, (far_ref,), (grad_far_ref,), h
         )
         acc_out[lo:hi, :] = acc_ref[lo:hi, :] + key_term
         acc_out[columns + lo : columns + hi, :] = acc_ref[columns + lo : columns + hi, :] + value_term
 
 
-def last_body(columns, own_ref, two_ref, grad_two_ref, acc_ref, key_out, value_out):
+def last_body(
+    columns, own_ref, one_ref, two_ref, grad_one_ref, grad_two_ref, acc_ref, key_out, value_out
+):
     for h in range(columns // HEAD_DIM):
         lo, hi = h * HEAD_DIM, (h + 1) * HEAD_DIM
         key_term, value_term = remote_terms(
-            columns, (2,), own_ref, (two_ref,), (grad_two_ref,), h
+            columns, (1, 2), own_ref, (one_ref, two_ref), (grad_one_ref, grad_two_ref), h
         )
         key_out[lo:hi, :] = ((acc_ref[lo:hi, :] + key_term) * SCALE).astype(BF16)
         value_out[lo:hi, :] = (acc_ref[columns + lo : columns + hi, :] + value_term).astype(BF16)
@@ -331,7 +333,7 @@
         (
             odd,
             block_mask.transpose(0, 2, 1),
-            counts.reshape(1, 1),
+            counts,
             keys,
             values,
             queries,
@@ -368,6 +370,7 @@
     piece = jnp.sum(parts.astype(F32), axis=0)
     stream_grad = (g_out.astype(F32) + piece).astype(BF16)
     stream_full = lax.all_gather(stream_grad, "head", axis=0, tiled=True)
+    heads = columns // HEAD_DIM
     tiles = (2 * LINKS * columns // HEAD_DIM, row_count, row_count)
     grad, tile, inverse = call(
         functools.partial(grad_body, columns),
@@ -390,20 +393,20 @@
     acc = call(
         functools.partial(middle_body, columns),
         shape((2 * columns, row_count), F32),
-        (own, one, far, grad_one, grad_far, acc),
+        (own, far, grad_far, acc),
+        [VMEM] * 4,
+        4 * square,
+        6 * message * row_count,
+        heads * row_count * row_count,
+    )
+    grad_keys, grad_values = call(
+        functools.partial(last_body, columns),
+        (shape(flat, BF16), shape(flat, BF16)),
+        (own, one, two, grad_one, grad_two, acc),
         [VMEM] * 6,
         8 * square,
         8 * message * row_count,
-        2 * columns // HEAD_DIM * row_count * row_count,
-    )
-    grad_keys, grad_values = call(
-        functools.partial(last_body, columns),
-        (shape((columns, row_count), BF16), shape((columns, row_count), BF16)),
-        (own, two, grad_two, acc),
-        [VMEM] * 4,
-        4 * square,
-        8 * message * row_count,
-        columns // HEAD_DIM * row_count * row_count,
+        2 * heads * row_count * row_count,
     )
     return (stream_grad.T, grad_queries.T, grad_keys.T, grad_values.T)
 

time: 75.3 us -> 74.3 us (0.987)
  waiting for transfers between devices: 4.5 us -> 3.37 us
    ppermute x8, waiting for transfers between devices: 4.5 us -> 3.37 us  [exchange(): return lax.ppermute(value, 'ctx', pairs)]
where the time goes in v12:
time: 74.3 us; the launch traced here: 73.8 us
  starting transfers between devices  43.4 us (58%)
  blocking collectives  14.6 us (20%)
  Pallas kernels  9.01 us (12%)
  waiting for transfers between devices  3.37 us (5%)
  local copies, waits for them, and re-layouts  1.75 us (2%)
  between operations  1.55 us (2%)
    ppermute x8, starting transfers between devices, exchange(): return lax.ppermute(value, 'ctx', pairs)  37.7 us
    all_gather x1, blocking collectives, per_device(): stream_full = lax.all_gather(stream_grad, 'head', axis=0, tiled=True)  14.6 us
    pallas_call x6, Pallas kernels, call(): pl.pallas_call(body, out_shape=out_shapes, in_specs=specs, out_specs=jax....  9.01 us
    all_to_all x1, starting transfers between devices, per_device(): lax.all_to_all(point_grad.reshape(groups, columns, row_count), 'head', 0,...  5.66 us
    ppermute x8, waiting for transfers between devices, exchange(): return lax.ppermute(value, 'ctx', pairs)  3.37 us
    reshape x1, local copies, waits for them, and re-layouts, per_device(): w_turned = w_point.reshape(2 * columns, model).T  1.7 us
  transfers between devices with their start and end apart: 9, of which 2 were waited for; matrix products, arithmetic and copies ran while one was open for 2% of the time, Pallas kernels for 5%

profile of v12, /device:TPU:1, one launch (start us, length us, event | category | flops | bytes accessed | tf_op | source)
XLA Modules:
  0.0 73.8 jit_solution(11744017511969333583)
XLA Ops:
  0.6 0.0 copy-start.6
  0.6 0.0 copy-start.2
  0.7 0.0 copy-start.7
  0.7 0.8 %collective-permute-start = (bf16[192,256]{1,0:T(8,128)(2,1)}, bf16[192,256]{1,0:T(8,128)(2,1)S(1)}, u32[]{:S(2)}, u32[]{:S(2)}) collective-permute-start(bf16[192,256]{1,0:T(8,128)(2,1)} %g_ref.1), channel_id=1, source_target_pairs={{8,16},{16,8},{24,32},{32,24},{40,48},{48,40},{56,64},{64,56},{72,... | collective-permute-start | bytes 294920 | tf_op jit(solution)/shard_map/ppermute | solution.py:313
  1.5 8.2 %collective-permute-start.1 = (bf16[192,256]{1,0:T(8,128)(2,1)}, bf16[192,256]{1,0:T(8,128)(2,1)S(1)}, u32[]{:S(2)}, u32[]{:S(2)}) collective-permute-start(bf16[192,256]{1,0:T(8,128)(2,1)} %g_ref.1), channel_id=1, source_target_pairs={{0,8},{8,0},{16,24},{24,16},{32,40},{40,32},{48,56},{56,48},{64,72... | collective-permute-start | bytes 294920 | tf_op jit(solution)/shard_map/ppermute | solution.py:313
  10.3 1.7 %copy.16 = bf16[384,1536]{0,1:T(8,128)(2,1)S(1)} copy(bf16[384,1536]{1,0:T(8,128)(2,1)} %bitcast.17) | data formatting | bytes 2359296 | tf_op jit(solution)/shard_map/reshape | solution.py:354
  12.1 1.4 %shard_map.138 = (bf16[592,256]{1,0:T(8,128)(2,1)S(1)}, f32[192,256]{1,0:T(8,128)S(1)}, f32[192,256]{1,0:T(8,128)S(1)}, f32[192,256]{1,0:T(8,128)S(1)}) custom-call(s32[1,1]{1,0:T(1,128)} %bitcast.odd_ref, s32[2,2,4]{2,1,0:T(2,128)S(1)} %bitcast.16, s32[1]{0:T(128)S(6)} %copy.17.count_ref, bf16[192,256]{1,0:T(8,128)(2,1)S(1)} %bitcast.13, ...), custom_call_target="tpu_custom_call" | custom-call | flops 3047424 | bytes 909312 | tf_op jit(solution)/shard_map/pallas_call | solution.py:27
  13.6 0.0 collective-permute-done.two_ref
  13.6 0.0 collective-permute-done.1.one_ref
  13.6 1.8 %shard_map.139 = bf16[1536,256]{1,0:T(8,128)(2,1)} custom-call(s32[1,1]{1,0:T(1,128)} %bitcast.odd_ref, bf16[192,256]{1,0:T(8,128)(2,1)S(1)} %collective-permute-done.two_ref, bf16[192,256]{1,0:T(8,128)(2,1)S(1)} %collective-permute-done.1.one_ref, f32[31,192]{1,0:T(8,128)S(1)} %copy-done.2, f32[192,256]{1,0:T(8,128)S(1)} %get-tuple-element.16.sum_ref, ...), custom_call_target="tpu_custom_call" | custom-call | flops 301989888 | bytes 1179648 | tf_op jit(solution)/shard_map/pallas_call | solution.py:27
  15.4 5.7 %all-to-all-start = ((bf16[8,192,256]{2,1,0:T(8,128)(2,1)}), bf16[8,192,256]{2,1,0:T(8,128)(2,1)S(1)}, u32[]{:S(2)}, u32[]{:S(2)}) async-start(bf16[8,192,256]{2,1,0:T(8,128)(2,1)} %bitcast.7), calls=%async_computation | async-start | bytes 1572864 | tf_op jit(solution)/shard_map/all_to_all | solution.py:365
  21.0 12.5 %collective-permute-start.4 = (bf16[592,256]{1,0:T(8,128)(2,1)S(1)}, bf16[592,256]{1,0:T(8,128)(2,1)S(1)}, u32[]{:S(2)}, u32[]{:S(2)}) collective-permute-start(bf16[592,256]{1,0:T(8,128)(2,1)S(1)} %get-tuple-element.20.own_ref), channel_id=1, source_target_pairs={{0,256},{8,264},{16,272},{24,280},{32,288},{40,296},{48,304},{56,3... | collective-permute-start | bytes 909320 | tf_op jit(solution)/shard_map/ppermute | solution.py:313
  33.5 3.0 %collective-permute-start.3 = (bf16[592,256]{1,0:T(8,128)(2,1)S(1)}, bf16[592,256]{1,0:T(8,128)(2,1)S(1)}, u32[]{:S(2)}, u32[]{:S(2)}) collective-permute-start(bf16[592,256]{1,0:T(8,128)(2,1)S(1)} %get-tuple-element.20.own_ref), channel_id=1, source_target_pairs={{0,504},{8,16},{16,8},{24,32},{32,24},{40,48},{48,40},{56,64},{64,... | collective-permute-start | bytes 909320 | tf_op jit(solution)/shard_map/ppermute | solution.py:313
  36.6 1.9 %collective-permute-start.2 = (bf16[592,256]{1,0:T(8,128)(2,1)S(1)}, bf16[592,256]{1,0:T(8,128)(2,1)S(1)}, u32[]{:S(2)}, u32[]{:S(2)}) collective-permute-start(bf16[592,256]{1,0:T(8,128)(2,1)S(1)} %get-tuple-element.20.own_ref), channel_id=1, source_target_pairs={{0,8},{8,0},{16,24},{24,16},{32,40},{40,32},{48,56},{56,48},{64,72... | collective-permute-start | bytes 909320 | tf_op jit(solution)/shard_map/ppermute | solution.py:313
  38.5 0.0 all-to-all-done
  38.5 0.1 convert_reduce_fusion
  38.6 0.0 copy-done.9
  38.7 0.0 copy-start.8
  38.7 14.6 %all_gather.3.stream_ref = bf16[1536,256]{1,0:T(8,128)(2,1)S(1)} all-gather(bf16[192,256]{1,0:T(8,128)(2,1)S(1)} %add_convert_fusion), channel_id=1, replica_groups=mesh['ctx'=64,'head'=8] {'head'}, dimensions={0}, use_global_device_ids=true | all-gather | bytes 884736 | tf_op jit(solution)/shard_map/all_gather | solution.py:372
  53.3 0.0 collective-permute-done.4.far_ref
  53.3 1.1 %collective-permute-done.3.two_ref = bf16[592,256]{1,0:T(8,128)(2,1)S(1)} collective-permute-done((bf16[592,256]{1,0:T(8,128)(2,1)S(1)}, bf16[592,256]{1,0:T(8,128)(2,1)S(1)}, u32[]{:S(2)}, u32[]{:S(2)}) %collective-permute-start.3) | collective-permute-done | bytes 303136 | tf_op jit(solution)/shard_map/ppermute | solution.py:313
  54.5 0.0 collective-permute-done.2.one_ref
  54.5 1.6 %shard_map.140 = (bf16[208,256]{1,0:T(8,128)(2,1)S(1)}, f32[24,256,256]{2,1,0:T(8,128)S(1)}, f32[8,256]{1,0:T(8,128)S(1)}) custom-call(bf16[192,1536]{1,0:T(8,128)(2,1)S(1)} %copy-done, bf16[1536,256]{1,0:T(8,128)(2,1)S(1)} %all_gather.3.stream_ref, bf16[592,256]{1,0:T(8,128)(2,1)S(1)} %get-tuple-element.20.own_ref, ...), custom_call_target="tpu_custom_call" | custom-call | flops 352321536 | bytes 1376256 | tf_op jit(solution)/shard_map/pallas_call | solution.py:27
  56.1 5.7 %collective-permute-start.7 = (bf16[208,256]{1,0:T(8,128)(2,1)S(1)}, bf16[208,256]{1,0:T(8,128)(2,1)S(1)}, u32[]{:S(2)}, u32[]{:S(2)}) collective-permute-start(bf16[208,256]{1,0:T(8,128)(2,1)S(1)} %get-tuple-element.21.grad_ref), channel_id=1, source_target_pairs={{0,256},{8,264},{16,272},{24,280},{32,288},{40,296},{48,304},{56,3... | collective-permute-start | bytes 319496 | tf_op jit(solution)/shard_map/ppermute | solution.py:313
  61.9 3.6 %collective-permute-start.6 = (bf16[208,256]{1,0:T(8,128)(2,1)S(1)}, bf16[208,256]{1,0:T(8,128)(2,1)S(1)}, u32[]{:S(2)}, u32[]{:S(2)}) collective-permute-start(bf16[208,256]{1,0:T(8,128)(2,1)S(1)} %get-tuple-element.21.grad_ref), channel_id=1, source_target_pairs={{0,504},{8,16},{16,8},{24,32},{32,24},{40,48},{48,40},{56,64},{64,... | collective-permute-start | bytes 319496 | tf_op jit(solution)/shard_map/ppermute | solution.py:313
  65.5 1.9 %collective-permute-start.5 = (bf16[208,256]{1,0:T(8,128)(2,1)S(1)}, bf16[208,256]{1,0:T(8,128)(2,1)S(1)}, u32[]{:S(2)}, u32[]{:S(2)}) collective-permute-start(bf16[208,256]{1,0:T(8,128)(2,1)S(1)} %get-tuple-element.21.grad_ref), channel_id=1, source_target_pairs={{0,8},{8,0},{16,24},{24,16},{32,40},{40,32},{48,56},{56,48},{64,72... | collective-permute-start | bytes 319496 | tf_op jit(solution)/shard_map/ppermute | solution.py:313
  67.4 1.3 %shard_map.141 = (bf16[192,256]{1,0:T(8,128)(2,1)}, f32[384,256]{1,0:T(8,128)S(1)}) custom-call(bf16[592,256]{1,0:T(8,128)(2,1)S(1)} %get-tuple-element.20.own_ref, bf16[592,256]{1,0:T(8,128)(2,1)S(1)} %collective-permute-done.2.one_ref, bf16[592,256]{1,0:T(8,128)(2,1)S(1)} %collective-permute-done.3.two_ref, ...), custom_call_target="tpu_custom_call" | custom-call | flops 301989888 | bytes 1212416 | tf_op jit(solution)/shard_map/pallas_call | solution.py:27
  68.7 0.0 collective-permute-done.7.grad_far_ref
  68.7 0.9 %shard_map.142.acc_ref = f32[384,256]{1,0:T(8,128)S(1)} custom-call(bf16[592,256]{1,0:T(8,128)(2,1)S(1)} %get-tuple-element.20.own_ref, bf16[592,256]{1,0:T(8,128)(2,1)S(1)} %collective-permute-done.4.far_ref, bf16[208,256]{1,0:T(8,128)(2,1)S(1)} %collective-permute-done.7.grad_far_ref, f32[384,256]{1,0:T(8,128)S(1)} %get-tuple-element.25.acc_ref), custom_call_target="tpu_custom_call" | custom-call | flops 100663296 | bytes 909312 | tf_op jit(solution)/shard_map/pallas_call | solution.py:27
  69.6 2.2 %collective-permute-done.6.grad_two_ref = bf16[208,256]{1,0:T(8,128)(2,1)S(1)} collective-permute-done((bf16[208,256]{1,0:T(8,128)(2,1)S(1)}, bf16[208,256]{1,0:T(8,128)(2,1)S(1)}, u32[]{:S(2)}, u32[]{:S(2)}) %collective-permute-start.6) | collective-permute-done | bytes 106528 | tf_op jit(solution)/shard_map/ppermute | solution.py:313
  71.8 0.0 collective-permute-done.5.grad_one_ref
  71.8 2.0 %shard_map.143 = (bf16[192,256]{1,0:T(8,128)(2,1)}, bf16[192,256]{1,0:T(8,128)(2,1)}) custom-call(bf16[592,256]{1,0:T(8,128)(2,1)S(1)} %get-tuple-element.20.own_ref, bf16[592,256]{1,0:T(8,128)(2,1)S(1)} %collective-permute-done.2.one_ref, bf16[592,256]{1,0:T(8,128)(2,1)S(1)} %collective-permute-done.3.two_ref, ...), custom_call_target="tpu_custom_call" | custom-call | flops 201326592 | bytes 1212416 | tf_op jit(solution)/shard_map/pallas_call | solution.py:27
  (16 shorter events, 0.1 us)
Async XLA Ops:
  0.6 11.4 %copy-start.6 = (bf16[192,256]{1,0:T(8,128)(2,1)S(1)}, bf16[192,256]{1,0:T(8,128)(2,1)}, u32[]{:S(2)}) copy-start(bf16[192,256]{1,0:T(8,128)(2,1)} %g_ref.1) | copy-start | bytes 294916
  0.6 11.4 %copy-start.2 = (f32[31,192]{1,0:T(8,128)S(1)}, f32[31,192]{1,0:T(8,128)}, u32[]{:S(2)}) copy-start(f32[31,192]{1,0:T(8,128)} %taps_ref.3) | copy-start | bytes 71428
  0.7 11.4 %copy-start.7 = (s32[2,4,2]{1,2,0:T(2,128)S(1)}, s32[2,4,2]{1,2,0:T(2,128)}, u32[]{:S(2)}) copy-start(s32[2,4,2]{1,2,0:T(2,128)} %param.20) | copy-start | bytes 196
  0.7 11.4 %copy-start.4 = (bf16[256,192]{0,1:T(8,128)(2,1)S(1)}, bf16[256,192]{0,1:T(8,128)(2,1)}, u32[]{:S(2)}) copy-start(bf16[256,192]{0,1:T(8,128)(2,1)} %param.19) | copy-start | bytes 294916
  0.7 11.4 %copy-start.3 = (bf16[256,192]{0,1:T(8,128)(2,1)S(1)}, bf16[256,192]{0,1:T(8,128)(2,1)}, u32[]{:S(2)}) copy-start(bf16[256,192]{0,1:T(8,128)(2,1)} %param.18) | copy-start | bytes 294916
  0.7 11.4 %copy-start.5 = (bf16[256,192]{0,1:T(8,128)(2,1)S(1)}, bf16[256,192]{0,1:T(8,128)(2,1)}, u32[]{:S(2)}) copy-start(bf16[256,192]{0,1:T(8,128)(2,1)} %param.17) | copy-start | bytes 294916
  0.7 11.4 %copy-start.1 = (bf16[2,192,256]{2,1,0:T(8,128)(2,1)S(1)}, bf16[2,192,256]{2,1,0:T(8,128)(2,1)}, u32[]{:S(2)}) copy-start(bf16[2,192,256]{2,1,0:T(8,128)(2,1)} %pre_ref.1) | copy-start | bytes 589828
  0.7 12.9 %collective-permute-start = (bf16[192,256]{1,0:T(8,128)(2,1)}, bf16[192,256]{1,0:T(8,128)(2,1)S(1)}, u32[]{:S(2)}, u32[]{:S(2)}) collective-permute-start(bf16[192,256]{1,0:T(8,128)(2,1)} %g_ref.1), channel_id=1, source_target_pairs={{8,16},{16,8},{24,32},{32,24},{40,48},{48,40},{56,64},{64,56},{72,... | collective-permute-start | bytes 294920 | tf_op jit(solution)/shard_map/ppermute | solution.py:313
  1.5 12.1 %collective-permute-start.1 = (bf16[192,256]{1,0:T(8,128)(2,1)}, bf16[192,256]{1,0:T(8,128)(2,1)S(1)}, u32[]{:S(2)}, u32[]{:S(2)}) collective-permute-start(bf16[192,256]{1,0:T(8,128)(2,1)} %g_ref.1), channel_id=1, source_target_pairs={{0,8},{8,0},{16,24},{24,16},{32,40},{40,32},{48,56},{56,48},{64,72... | collective-permute-start | bytes 294920 | tf_op jit(solution)/shard_map/ppermute | solution.py:313
  15.3 23.3 %copy-start.9 = (bf16[192,256]{1,0:T(8,128)(2,1)S(1)}, bf16[192,256]{1,0:T(8,128)(2,1)}, u32[]{:S(2)}) copy-start(bf16[192,256]{1,0:T(8,128)(2,1)} %param.15) | copy-start | bytes 294916
  15.3 39.1 %copy-start = (bf16[192,1536]{1,0:T(8,128)(2,1)S(1)}, bf16[192,1536]{1,0:T(8,128)(2,1)}, u32[]{:S(2)}) copy-start(bf16[192,1536]{1,0:T(8,128)(2,1)} %w_ref.1) | copy-start | bytes 1769476
  15.4 23.2 %all-to-all-start = ((bf16[8,192,256]{2,1,0:T(8,128)(2,1)}), bf16[8,192,256]{2,1,0:T(8,128)(2,1)S(1)}, u32[]{:S(2)}, u32[]{:S(2)}) async-start(bf16[8,192,256]{2,1,0:T(8,128)(2,1)} %bitcast.7), calls=%async_computation | async-start | bytes 1572864 | tf_op jit(solution)/shard_map/all_to_all | solution.py:365
  21.0 32.3 %collective-permute-start.4 = (bf16[592,256]{1,0:T(8,128)(2,1)S(1)}, bf16[592,256]{1,0:T(8,128)(2,1)S(1)}, u32[]{:S(2)}, u32[]{:S(2)}) collective-permute-start(bf16[592,256]{1,0:T(8,128)(2,1)S(1)} %get-tuple-element.20.own_ref), channel_id=1, source_target_pairs={{0,256},{8,264},{16,272},{24,280},{32,288},{40,296},{48,304},{56,3... | collective-permute-start | bytes 909320 | tf_op jit(solution)/shard_map/ppermute | solution.py:313
  33.5 20.9 %collective-permute-start.3 = (bf16[592,256]{1,0:T(8,128)(2,1)S(1)}, bf16[592,256]{1,0:T(8,128)(2,1)S(1)}, u32[]{:S(2)}, u32[]{:S(2)}) collective-permute-start(bf16[592,256]{1,0:T(8,128)(2,1)S(1)} %get-tuple-element.20.own_ref), channel_id=1, source_target_pairs={{0,504},{8,16},{16,8},{24,32},{32,24},{40,48},{48,40},{56,64},{64,... | collective-permute-start | bytes 909320 | tf_op jit(solution)/shard_map/ppermute | solution.py:313
  36.6 17.9 %collective-permute-start.2 = (bf16[592,256]{1,0:T(8,128)(2,1)S(1)}, bf16[592,256]{1,0:T(8,128)(2,1)S(1)}, u32[]{:S(2)}, u32[]{:S(2)}) collective-permute-start(bf16[592,256]{1,0:T(8,128)(2,1)S(1)} %get-tuple-element.20.own_ref), channel_id=1, source_target_pairs={{0,8},{8,0},{16,24},{24,16},{32,40},{40,32},{48,56},{56,48},{64,72... | collective-permute-start | bytes 909320 | tf_op jit(solution)/shard_map/ppermute | solution.py:313
  38.7 17.4 %copy-start.8 = (bf16[192,256]{1,0:T(8,128)(2,1)}, bf16[192,256]{1,0:T(8,128)(2,1)S(1)}, u32[]{:S(2)}) copy-start(bf16[192,256]{1,0:T(8,128)(2,1)S(1)} %add_convert_fusion) | copy-start | bytes 294916
  56.1 12.6 %collective-permute-start.7 = (bf16[208,256]{1,0:T(8,128)(2,1)S(1)}, bf16[208,256]{1,0:T(8,128)(2,1)S(1)}, u32[]{:S(2)}, u32[]{:S(2)}) collective-permute-start(bf16[208,256]{1,0:T(8,128)(2,1)S(1)} %get-tuple-element.21.grad_ref), channel_id=1, source_target_pairs={{0,256},{8,264},{16,272},{24,280},{32,288},{40,296},{48,304},{56,3... | collective-permute-start | bytes 319496 | tf_op jit(solution)/shard_map/ppermute | solution.py:313
  61.9 9.9 %collective-permute-start.6 = (bf16[208,256]{1,0:T(8,128)(2,1)S(1)}, bf16[208,256]{1,0:T(8,128)(2,1)S(1)}, u32[]{:S(2)}, u32[]{:S(2)}) collective-permute-start(bf16[208,256]{1,0:T(8,128)(2,1)S(1)} %get-tuple-element.21.grad_ref), channel_id=1, source_target_pairs={{0,504},{8,16},{16,8},{24,32},{32,24},{40,48},{48,40},{56,64},{64,... | collective-permute-start | bytes 319496 | tf_op jit(solution)/shard_map/ppermute | solution.py:313
  65.5 6.3 %collective-permute-start.5 = (bf16[208,256]{1,0:T(8,128)(2,1)S(1)}, bf16[208,256]{1,0:T(8,128)(2,1)S(1)}, u32[]{:S(2)}, u32[]{:S(2)}) collective-permute-start(bf16[208,256]{1,0:T(8,128)(2,1)S(1)} %get-tuple-element.21.grad_ref), channel_id=1, source_target_pairs={{0,8},{8,0},{16,24},{24,16},{32,40},{40,32},{48,56},{56,48},{64,72... | collective-permute-start | bytes 319496 | tf_op jit(solution)/shard_map/ppermute | solution.py:313

commit v13 on v12

--- a/solution.py
+++ b/solution.py
@@ -109,7 +109,7 @@
         sum_ref[pl.ds(at, step), :] = acc
         return carry
 
-    lax.fori_loop(0, rows // step, block, 0)
+    lax.fori_loop(0, rows // step, block, 0, unroll=4)
     sum_out[...] = sum_ref[...].T
     gate = jax.nn.sigmoid(pre_ref[1].astype(F32))
     gate_out[...] = gate

time: 74.3 us -> 74.3 us (level)
  no operation moved by 1% of the time
where the time goes in v13:
time: 74.3 us; the launch traced here: 73.9 us
  starting transfers between devices  43.5 us (59%)
  blocking collectives  14.6 us (20%)
  Pallas kernels  8.84 us (12%)
  waiting for transfers between devices  3.41 us (5%)
  local copies, waits for them, and re-layouts  1.75 us (2%)
  between operations  1.55 us (2%)
    ppermute x8, starting transfers between devices, exchange(): return lax.ppermute(value, 'ctx', pairs)  37.9 us
    all_gather x1, blocking collectives, per_device(): stream_full = lax.all_gather(stream_grad, 'head', axis=0, tiled=True)  14.6 us
    pallas_call x6, Pallas kernels, call(): pl.pallas_call(body, out_shape=out_shapes, in_specs=specs, out_specs=jax....  8.84 us
    all_to_all x1, starting transfers between devices, per_device(): lax.all_to_all(point_grad.reshape(groups, columns, row_count), 'head', 0,...  5.66 us
    ppermute x8, waiting for transfers between devices, exchange(): return lax.ppermute(value, 'ctx', pairs)  3.41 us
    reshape x1, local copies, waits for them, and re-layouts, per_device(): w_turned = w_point.reshape(2 * columns, model).T  1.7 us
  transfers between devices with their start and end apart: 9, of which 2 were waited for; matrix products, arithmetic and copies ran while one was open for 2% of the time, Pallas kernels for 5%

profile of v13, /device:TPU:1, one launch (start us, length us, event | category | flops | bytes accessed | tf_op | source)
XLA Modules:
  0.0 73.9 jit_solution(5617103294753484031)
XLA Ops:
  0.6 0.0 copy-start.6
  0.6 0.0 copy-start.2
  0.7 0.0 copy-start.7
  0.7 0.8 %collective-permute-start = (bf16[192,256]{1,0:T(8,128)(2,1)}, bf16[192,256]{1,0:T(8,128)(2,1)S(1)}, u32[]{:S(2)}, u32[]{:S(2)}) collective-permute-start(bf16[192,256]{1,0:T(8,128)(2,1)} %g_ref.1), channel_id=1, source_target_pairs={{8,16},{16,8},{24,32},{32,24},{40,48},{48,40},{56,64},{64,56},{72,... | collective-permute-start | bytes 294920 | tf_op jit(solution)/shard_map/ppermute | solution.py:313
  1.5 8.2 %collective-permute-start.1 = (bf16[192,256]{1,0:T(8,128)(2,1)}, bf16[192,256]{1,0:T(8,128)(2,1)S(1)}, u32[]{:S(2)}, u32[]{:S(2)}) collective-permute-start(bf16[192,256]{1,0:T(8,128)(2,1)} %g_ref.1), channel_id=1, source_target_pairs={{0,8},{8,0},{16,24},{24,16},{32,40},{40,32},{48,56},{56,48},{64,72... | collective-permute-start | bytes 294920 | tf_op jit(solution)/shard_map/ppermute | solution.py:313
  10.3 1.7 %copy.16 = bf16[384,1536]{0,1:T(8,128)(2,1)S(1)} copy(bf16[384,1536]{1,0:T(8,128)(2,1)} %bitcast.17) | data formatting | bytes 2359296 | tf_op jit(solution)/shard_map/reshape | solution.py:354
  12.1 1.3 %shard_map.138 = (bf16[592,256]{1,0:T(8,128)(2,1)S(1)}, f32[192,256]{1,0:T(8,128)S(1)}, f32[192,256]{1,0:T(8,128)S(1)}, f32[192,256]{1,0:T(8,128)S(1)}) custom-call(s32[1,1]{1,0:T(1,128)} %bitcast.odd_ref, s32[2,2,4]{2,1,0:T(2,128)S(1)} %bitcast.16, s32[1]{0:T(128)S(6)} %copy.17.count_ref, bf16[192,256]{1,0:T(8,128)(2,1)S(1)} %bitcast.13, ...), custom_call_target="tpu_custom_call" | custom-call | flops 3047424 | bytes 909312 | tf_op jit(solution)/shard_map/pallas_call | solution.py:27
  13.4 0.0 collective-permute-done.two_ref
  13.4 0.0 collective-permute-done.1.one_ref
  13.4 1.8 %shard_map.139 = bf16[1536,256]{1,0:T(8,128)(2,1)} custom-call(s32[1,1]{1,0:T(1,128)} %bitcast.odd_ref, bf16[192,256]{1,0:T(8,128)(2,1)S(1)} %collective-permute-done.two_ref, bf16[192,256]{1,0:T(8,128)(2,1)S(1)} %collective-permute-done.1.one_ref, f32[31,192]{1,0:T(8,128)S(1)} %copy-done.2, f32[192,256]{1,0:T(8,128)S(1)} %get-tuple-element.16.sum_ref, ...), custom_call_target="tpu_custom_call" | custom-call | flops 301989888 | bytes 1179648 | tf_op jit(solution)/shard_map/pallas_call | solution.py:27
  15.2 5.7 %all-to-all-start = ((bf16[8,192,256]{2,1,0:T(8,128)(2,1)}), bf16[8,192,256]{2,1,0:T(8,128)(2,1)S(1)}, u32[]{:S(2)}, u32[]{:S(2)}) async-start(bf16[8,192,256]{2,1,0:T(8,128)(2,1)} %bitcast.7), calls=%async_computation | async-start | bytes 1572864 | tf_op jit(solution)/shard_map/all_to_all | solution.py:365
  20.8 12.7 %collective-permute-start.4 = (bf16[592,256]{1,0:T(8,128)(2,1)S(1)}, bf16[592,256]{1,0:T(8,128)(2,1)S(1)}, u32[]{:S(2)}, u32[]{:S(2)}) collective-permute-start(bf16[592,256]{1,0:T(8,128)(2,1)S(1)} %get-tuple-element.20.own_ref), channel_id=1, source_target_pairs={{0,256},{8,264},{16,272},{24,280},{32,288},{40,296},{48,304},{56,3... | collective-permute-start | bytes 909320 | tf_op jit(solution)/shard_map/ppermute | solution.py:313
  33.5 3.0 %collective-permute-start.3 = (bf16[592,256]{1,0:T(8,128)(2,1)S(1)}, bf16[592,256]{1,0:T(8,128)(2,1)S(1)}, u32[]{:S(2)}, u32[]{:S(2)}) collective-permute-start(bf16[592,256]{1,0:T(8,128)(2,1)S(1)} %get-tuple-element.20.own_ref), channel_id=1, source_target_pairs={{0,504},{8,16},{16,8},{24,32},{32,24},{40,48},{48,40},{56,64},{64,... | collective-permute-start | bytes 909320 | tf_op jit(solution)/shard_map/ppermute | solution.py:313
  36.6 1.9 %collective-permute-start.2 = (bf16[592,256]{1,0:T(8,128)(2,1)S(1)}, bf16[592,256]{1,0:T(8,128)(2,1)S(1)}, u32[]{:S(2)}, u32[]{:S(2)}) collective-permute-start(bf16[592,256]{1,0:T(8,128)(2,1)S(1)} %get-tuple-element.20.own_ref), channel_id=1, source_target_pairs={{0,8},{8,0},{16,24},{24,16},{32,40},{40,32},{48,56},{56,48},{64,72... | collective-permute-start | bytes 909320 | tf_op jit(solution)/shard_map/ppermute | solution.py:313
  38.5 0.0 all-to-all-done
  38.5 0.1 convert_reduce_fusion
  38.7 0.0 copy-start.8
  38.7 14.6 %all_gather.3.stream_ref = bf16[1536,256]{1,0:T(8,128)(2,1)S(1)} all-gather(bf16[192,256]{1,0:T(8,128)(2,1)S(1)} %add_convert_fusion), channel_id=1, replica_groups=mesh['ctx'=64,'head'=8] {'head'}, dimensions={0}, use_global_device_ids=true | all-gather | bytes 884736 | tf_op jit(solution)/shard_map/all_gather | solution.py:372
  53.3 0.0 collective-permute-done.4.far_ref
  53.3 1.1 %collective-permute-done.3.two_ref = bf16[592,256]{1,0:T(8,128)(2,1)S(1)} collective-permute-done((bf16[592,256]{1,0:T(8,128)(2,1)S(1)}, bf16[592,256]{1,0:T(8,128)(2,1)S(1)}, u32[]{:S(2)}, u32[]{:S(2)}) %collective-permute-start.3) | collective-permute-done | bytes 303136 | tf_op jit(solution)/shard_map/ppermute | solution.py:313
  54.5 0.0 collective-permute-done.2.one_ref
  54.5 1.6 %shard_map.140 = (bf16[208,256]{1,0:T(8,128)(2,1)S(1)}, f32[24,256,256]{2,1,0:T(8,128)S(1)}, f32[8,256]{1,0:T(8,128)S(1)}) custom-call(bf16[192,1536]{1,0:T(8,128)(2,1)S(1)} %copy-done, bf16[1536,256]{1,0:T(8,128)(2,1)S(1)} %all_gather.3.stream_ref, bf16[592,256]{1,0:T(8,128)(2,1)S(1)} %get-tuple-element.20.own_ref, ...), custom_call_target="tpu_custom_call" | custom-call | flops 352321536 | bytes 1376256 | tf_op jit(solution)/shard_map/pallas_call | solution.py:27
  56.1 0.0 copy-done.8
  56.1 5.7 %collective-permute-start.7 = (bf16[208,256]{1,0:T(8,128)(2,1)S(1)}, bf16[208,256]{1,0:T(8,128)(2,1)S(1)}, u32[]{:S(2)}, u32[]{:S(2)}) collective-permute-start(bf16[208,256]{1,0:T(8,128)(2,1)S(1)} %get-tuple-element.21.grad_ref), channel_id=1, source_target_pairs={{0,256},{8,264},{16,272},{24,280},{32,288},{40,296},{48,304},{56,3... | collective-permute-start | bytes 319496 | tf_op jit(solution)/shard_map/ppermute | solution.py:313
  61.9 3.6 %collective-permute-start.6 = (bf16[208,256]{1,0:T(8,128)(2,1)S(1)}, bf16[208,256]{1,0:T(8,128)(2,1)S(1)}, u32[]{:S(2)}, u32[]{:S(2)}) collective-permute-start(bf16[208,256]{1,0:T(8,128)(2,1)S(1)} %get-tuple-element.21.grad_ref), channel_id=1, source_target_pairs={{0,504},{8,16},{16,8},{24,32},{32,24},{40,48},{48,40},{56,64},{64,... | collective-permute-start | bytes 319496 | tf_op jit(solution)/shard_map/ppermute | solution.py:313
  65.5 1.9 %collective-permute-start.5 = (bf16[208,256]{1,0:T(8,128)(2,1)S(1)}, bf16[208,256]{1,0:T(8,128)(2,1)S(1)}, u32[]{:S(2)}, u32[]{:S(2)}) collective-permute-start(bf16[208,256]{1,0:T(8,128)(2,1)S(1)} %get-tuple-element.21.grad_ref), channel_id=1, source_target_pairs={{0,8},{8,0},{16,24},{24,16},{32,40},{40,32},{48,56},{56,48},{64,72... | collective-permute-start | bytes 319496 | tf_op jit(solution)/shard_map/ppermute | solution.py:313
  67.4 1.3 %shard_map.141 = (bf16[192,256]{1,0:T(8,128)(2,1)}, f32[384,256]{1,0:T(8,128)S(1)}) custom-call(bf16[592,256]{1,0:T(8,128)(2,1)S(1)} %get-tuple-element.20.own_ref, bf16[592,256]{1,0:T(8,128)(2,1)S(1)} %collective-permute-done.2.one_ref, bf16[592,256]{1,0:T(8,128)(2,1)S(1)} %collective-permute-done.3.two_ref, ...), custom_call_target="tpu_custom_call" | custom-call | flops 301989888 | bytes 1212416 | tf_op jit(solution)/shard_map/pallas_call | solution.py:27
  68.7 0.0 collective-permute-done.7.grad_far_ref
  68.7 0.9 %shard_map.142.acc_ref = f32[384,256]{1,0:T(8,128)S(1)} custom-call(bf16[592,256]{1,0:T(8,128)(2,1)S(1)} %get-tuple-element.20.own_ref, bf16[592,256]{1,0:T(8,128)(2,1)S(1)} %collective-permute-done.4.far_ref, bf16[208,256]{1,0:T(8,128)(2,1)S(1)} %collective-permute-done.7.grad_far_ref, f32[384,256]{1,0:T(8,128)S(1)} %get-tuple-element.25.acc_ref), custom_call_target="tpu_custom_call" | custom-call | flops 100663296 | bytes 909312 | tf_op jit(solution)/shard_map/pallas_call | solution.py:27
  69.6 2.3 %collective-permute-done.6.grad_two_ref = bf16[208,256]{1,0:T(8,128)(2,1)S(1)} collective-permute-done((bf16[208,256]{1,0:T(8,128)(2,1)S(1)}, bf16[208,256]{1,0:T(8,128)(2,1)S(1)}, u32[]{:S(2)}, u32[]{:S(2)}) %collective-permute-start.6) | collective-permute-done | bytes 106528 | tf_op jit(solution)/shard_map/ppermute | solution.py:313
  71.8 0.0 collective-permute-done.5.grad_one_ref
  71.8 2.0 %shard_map.143 = (bf16[192,256]{1,0:T(8,128)(2,1)}, bf16[192,256]{1,0:T(8,128)(2,1)}) custom-call(bf16[592,256]{1,0:T(8,128)(2,1)S(1)} %get-tuple-element.20.own_ref, bf16[592,256]{1,0:T(8,128)(2,1)S(1)} %collective-permute-done.2.one_ref, bf16[592,256]{1,0:T(8,128)(2,1)S(1)} %collective-permute-done.3.two_ref, ...), custom_call_target="tpu_custom_call" | custom-call | flops 201326592 | bytes 1212416 | tf_op jit(solution)/shard_map/pallas_call | solution.py:27
  (16 shorter events, 0.1 us)
Async XLA Ops:
  0.6 11.4 %copy-start.6 = (bf16[192,256]{1,0:T(8,128)(2,1)S(1)}, bf16[192,256]{1,0:T(8,128)(2,1)}, u32[]{:S(2)}) copy-start(bf16[192,256]{1,0:T(8,128)(2,1)} %g_ref.1) | copy-start | bytes 294916
  0.6 11.4 %copy-start.2 = (f32[31,192]{1,0:T(8,128)S(1)}, f32[31,192]{1,0:T(8,128)}, u32[]{:S(2)}) copy-start(f32[31,192]{1,0:T(8,128)} %taps_ref.3) | copy-start | bytes 71428
  0.7 11.4 %copy-start.7 = (s32[2,4,2]{1,2,0:T(2,128)S(1)}, s32[2,4,2]{1,2,0:T(2,128)}, u32[]{:S(2)}) copy-start(s32[2,4,2]{1,2,0:T(2,128)} %param.20) | copy-start | bytes 196
  0.7 11.4 %copy-start.4 = (bf16[256,192]{0,1:T(8,128)(2,1)S(1)}, bf16[256,192]{0,1:T(8,128)(2,1)}, u32[]{:S(2)}) copy-start(bf16[256,192]{0,1:T(8,128)(2,1)} %param.19) | copy-start | bytes 294916
  0.7 11.4 %copy-start.3 = (bf16[256,192]{0,1:T(8,128)(2,1)S(1)}, bf16[256,192]{0,1:T(8,128)(2,1)}, u32[]{:S(2)}) copy-start(bf16[256,192]{0,1:T(8,128)(2,1)} %param.18) | copy-start | bytes 294916
  0.7 11.4 %copy-start.5 = (bf16[256,192]{0,1:T(8,128)(2,1)S(1)}, bf16[256,192]{0,1:T(8,128)(2,1)}, u32[]{:S(2)}) copy-start(bf16[256,192]{0,1:T(8,128)(2,1)} %param.17) | copy-start | bytes 294916
  0.7 11.4 %copy-start.1 = (bf16[2,192,256]{2,1,0:T(8,128)(2,1)S(1)}, bf16[2,192,256]{2,1,0:T(8,128)(2,1)}, u32[]{:S(2)}) copy-start(bf16[2,192,256]{2,1,0:T(8,128)(2,1)} %pre_ref.1) | copy-start | bytes 589828
  0.7 12.7 %collective-permute-start = (bf16[192,256]{1,0:T(8,128)(2,1)}, bf16[192,256]{1,0:T(8,128)(2,1)S(1)}, u32[]{:S(2)}, u32[]{:S(2)}) collective-permute-start(bf16[192,256]{1,0:T(8,128)(2,1)} %g_ref.1), channel_id=1, source_target_pairs={{8,16},{16,8},{24,32},{32,24},{40,48},{48,40},{56,64},{64,56},{72,... | collective-permute-start | bytes 294920 | tf_op jit(solution)/shard_map/ppermute | solution.py:313
  1.5 11.9 %collective-permute-start.1 = (bf16[192,256]{1,0:T(8,128)(2,1)}, bf16[192,256]{1,0:T(8,128)(2,1)S(1)}, u32[]{:S(2)}, u32[]{:S(2)}) collective-permute-start(bf16[192,256]{1,0:T(8,128)(2,1)} %g_ref.1), channel_id=1, source_target_pairs={{0,8},{8,0},{16,24},{24,16},{32,40},{40,32},{48,56},{56,48},{64,72... | collective-permute-start | bytes 294920 | tf_op jit(solution)/shard_map/ppermute | solution.py:313
  15.2 23.5 %copy-start.9 = (bf16[192,256]{1,0:T(8,128)(2,1)S(1)}, bf16[192,256]{1,0:T(8,128)(2,1)}, u32[]{:S(2)}) copy-start(bf16[192,256]{1,0:T(8,128)(2,1)} %param.15) | copy-start | bytes 294916
  15.2 39.3 %copy-start = (bf16[192,1536]{1,0:T(8,128)(2,1)S(1)}, bf16[192,1536]{1,0:T(8,128)(2,1)}, u32[]{:S(2)}) copy-start(bf16[192,1536]{1,0:T(8,128)(2,1)} %w_ref.1) | copy-start | bytes 1769476
  15.2 23.3 %all-to-all-start = ((bf16[8,192,256]{2,1,0:T(8,128)(2,1)}), bf16[8,192,256]{2,1,0:T(8,128)(2,1)S(1)}, u32[]{:S(2)}, u32[]{:S(2)}) async-start(bf16[8,192,256]{2,1,0:T(8,128)(2,1)} %bitcast.7), calls=%async_computation | async-start | bytes 1572864 | tf_op jit(solution)/shard_map/all_to_all | solution.py:365
  20.8 32.5 %collective-permute-start.4 = (bf16[592,256]{1,0:T(8,128)(2,1)S(1)}, bf16[592,256]{1,0:T(8,128)(2,1)S(1)}, u32[]{:S(2)}, u32[]{:S(2)}) collective-permute-start(bf16[592,256]{1,0:T(8,128)(2,1)S(1)} %get-tuple-element.20.own_ref), channel_id=1, source_target_pairs={{0,256},{8,264},{16,272},{24,280},{32,288},{40,296},{48,304},{56,3... | collective-permute-start | bytes 909320 | tf_op jit(solution)/shard_map/ppermute | solution.py:313
  33.5 20.9 %collective-permute-start.3 = (bf16[592,256]{1,0:T(8,128)(2,1)S(1)}, bf16[592,256]{1,0:T(8,128)(2,1)S(1)}, u32[]{:S(2)}, u32[]{:S(2)}) collective-permute-start(bf16[592,256]{1,0:T(8,128)(2,1)S(1)} %get-tuple-element.20.own_ref), channel_id=1, source_target_pairs={{0,504},{8,16},{16,8},{24,32},{32,24},{40,48},{48,40},{56,64},{64,... | collective-permute-start | bytes 909320 | tf_op jit(solution)/shard_map/ppermute | solution.py:313
  36.6 17.9 %collective-permute-start.2 = (bf16[592,256]{1,0:T(8,128)(2,1)S(1)}, bf16[592,256]{1,0:T(8,128)(2,1)S(1)}, u32[]{:S(2)}, u32[]{:S(2)}) collective-permute-start(bf16[592,256]{1,0:T(8,128)(2,1)S(1)} %get-tuple-element.20.own_ref), channel_id=1, source_target_pairs={{0,8},{8,0},{16,24},{24,16},{32,40},{40,32},{48,56},{56,48},{64,72... | collective-permute-start | bytes 909320 | tf_op jit(solution)/shard_map/ppermute | solution.py:313
  38.7 17.4 %copy-start.8 = (bf16[192,256]{1,0:T(8,128)(2,1)}, bf16[192,256]{1,0:T(8,128)(2,1)S(1)}, u32[]{:S(2)}) copy-start(bf16[192,256]{1,0:T(8,128)(2,1)S(1)} %add_convert_fusion) | copy-start | bytes 294916
  56.1 12.6 %collective-permute-start.7 = (bf16[208,256]{1,0:T(8,128)(2,1)S(1)}, bf16[208,256]{1,0:T(8,128)(2,1)S(1)}, u32[]{:S(2)}, u32[]{:S(2)}) collective-permute-start(bf16[208,256]{1,0:T(8,128)(2,1)S(1)} %get-tuple-element.21.grad_ref), channel_id=1, source_target_pairs={{0,256},{8,264},{16,272},{24,280},{32,288},{40,296},{48,304},{56,3... | collective-permute-start | bytes 319496 | tf_op jit(solution)/shard_map/ppermute | solution.py:313
  61.9 10.0 %collective-permute-start.6 = (bf16[208,256]{1,0:T(8,128)(2,1)S(1)}, bf16[208,256]{1,0:T(8,128)(2,1)S(1)}, u32[]{:S(2)}, u32[]{:S(2)}) collective-permute-start(bf16[208,256]{1,0:T(8,128)(2,1)S(1)} %get-tuple-element.21.grad_ref), channel_id=1, source_target_pairs={{0,504},{8,16},{16,8},{24,32},{32,24},{40,48},{48,40},{56,64},{64,... | collective-permute-start | bytes 319496 | tf_op jit(solution)/shard_map/ppermute | solution.py:313
  65.5 6.4 %collective-permute-start.5 = (bf16[208,256]{1,0:T(8,128)(2,1)S(1)}, bf16[208,256]{1,0:T(8,128)(2,1)S(1)}, u32[]{:S(2)}, u32[]{:S(2)}) collective-permute-start(bf16[208,256]{1,0:T(8,128)(2,1)S(1)} %get-tuple-element.21.grad_ref), channel_id=1, source_target_pairs={{0,8},{8,0},{16,24},{24,16},{32,40},{40,32},{48,56},{56,48},{64,72... | collective-permute-start | bytes 319496 | tf_op jit(solution)/shard_map/ppermute | solution.py:313
